TPU v7x, 32 devices: a whole 2x2x4 slice. The times are simulated.
32 devices in a mesh: ctx: 8 (over z, y), head: 4 (over x, core).
Axes of the slice: x: 2, y: 2, z: 4, core: 2. Of those that a mesh axis runs over, the one named last changes fastest.
Arguments:
- queries: bfloat16 [8192, 4096], P('ctx', 'head'), may hold values from -6.4 to 6.4
- keys: bfloat16 [8192, 4096], P('ctx', 'head'), may hold values from -0.62 to 0.62
- values: bfloat16 [8192, 4096], P('ctx', 'head'), may hold values from -7.6 to 7.6
- log_decay: float32 [32, 8192], P('head', 'ctx'), may hold values from -1.6 to 0, as said below
- gain: float32 [4096], P('head'), may hold values from 0.1 to 1.9
Outputs:
- shift: float32 [4096], P('head')
- covariance: float32 [4096, 2048], P(('head', 'ctx'))
Inputs may be any that keep to these rules, and one draw needn't show every extreme that they name: log_decay is negative everywhere.
All inputs are finite; a program needn't handle non-finite values.
Results may differ from a plain program's by a relative error of at most 0.0045.
The roundings to bfloat16 on the way count: a program that leaves them out, or rounds other values in their place, can miss the bound.
Values may be sent and summed in bfloat16 or wider, within the bound.
No kernel may reach another device: no remote copies, remote signals or barrier semaphores. Data moves between devices by JAX's collectives and lax.ppermute only.
A program may use at most 128 MiB of HBM per device.

v0:
```python
import jax
import jax.numpy as jnp
from jax import lax
from jax.sharding import PartitionSpec as P

HEAD_DIM = 128
SPAN = 256


def entering(value, axis, join, neutral):
    count, mine = (lax.axis_size(axis), lax.axis_index(axis))
    pieces = jax.tree.map(lambda part: lax.all_gather(part, axis), value)
    total = jax.tree.map(
        lambda part, zero: jnp.full_like(part, 0) + jnp.asarray(zero, part.dtype), value, neutral
    )

    def turn(position, total):
        longer = join(total, jax.tree.map(lambda part: part[position], pieces))
        return jax.tree.map(lambda new, old: jnp.where(position < mine, new, old), longer, total)

    return lax.fori_loop(0, count - 1, turn, total)


def merged(value, axis, join):
    pieces = jax.tree.map(lambda part: lax.all_gather(part, axis), value)
    head = jax.tree.map(lambda part: part[0], pieces)
    tail = jax.tree.map(lambda part: part[1:], pieces)
    total, _ = lax.scan(lambda total, slab: (join(total, slab), None), head, tail)
    return total


def from_partner(value, axis, apart):
    mask = 2**apart
    pairs = [(source, source ^ mask) for source in range(lax.axis_size(axis))]
    return lax.ppermute(value, axis, pairs)


def block_step(state, inputs):
    query, key, value, decay = inputs
    cumul = jnp.cumsum(decay, axis=1)
    scores = jnp.einsum("thd,shd->hts", query, key, preferred_element_type=jnp.float32)
    length = query.shape[0]
    later = jnp.arange(length)[:, None] >= jnp.arange(length)[None, :]
    diff = cumul[:, :, None] - cumul[:, None, :]
    factor = jnp.where(later[None], jnp.exp(jnp.where(later[None], diff, 0.0)), 0.0)
    weights = (scores * factor).astype(jnp.bfloat16)
    inner = jnp.einsum("hts,shd->thd", weights, value, preferred_element_type=jnp.float32)
    scaled_q = query.astype(jnp.float32) * jnp.exp(cumul).T[:, :, None]
    outer = jnp.einsum("thd,hde->the", scaled_q, state, precision=lax.Precision.HIGHEST)
    scaled_k = key.astype(jnp.float32) * jnp.exp(cumul[:, -1:] - cumul).T[:, :, None]
    update = jnp.einsum(
        "shd,she->hde", scaled_k, value.astype(jnp.float32), precision=lax.Precision.HIGHEST
    )
    new_state = jnp.exp(cumul[:, -1])[:, None, None] * state + update
    return (new_state, inner + outer)


def run_blocks(start, query, key, value, decay):
    count, heads, size = query.shape
    blocks = count // SPAN
    shaped = (
        query.reshape(blocks, SPAN, heads, size),
        key.reshape(blocks, SPAN, heads, size),
        value.reshape(blocks, SPAN, heads, size),
        decay.reshape(heads, blocks, SPAN).transpose(1, 0, 2),
    )
    ending, raw = lax.scan(block_step, start, shaped)
    return (ending, raw.reshape(count, heads, size))


def chain_join(earlier, later):
    return (earlier[0] * later[0], later[0][:, None, None] * earlier[1] + later[1])


def incoming_state(total, ending):
    heads = total.shape[0]
    identity = (jnp.ones((heads,), jnp.float32), jnp.zeros_like(ending))
    carried = entering((total, ending), "ctx", chain_join, identity)
    return carried[1]


def extreme_join(first, second):
    return (jnp.maximum(first[0], second[0]), jnp.minimum(first[1], second[1]))


def body(queries, keys, values, log_decay, gain):
    count, width = queries.shape
    heads = width // HEAD_DIM
    query = queries.reshape(count, heads, HEAD_DIM)
    key = keys.reshape(count, heads, HEAD_DIM)
    value = values.reshape(count, heads, HEAD_DIM)
    cumul = jnp.cumsum(log_decay, axis=1)
    total = jnp.exp(cumul[:, -1])
    scaled_k = key.astype(jnp.float32) * jnp.exp(cumul[:, -1:] - cumul).T[:, :, None]
    ending = jnp.einsum(
        "shd,she->hde", scaled_k, value.astype(jnp.float32), precision=lax.Precision.HIGHEST
    )
    arrived = incoming_state(total, ending)
    _, raw = run_blocks(arrived, query, key, value, log_decay)
    scale = jnp.sqrt(jnp.mean(raw * raw, axis=-1, keepdims=True) + 1e-06)
    attended = (
        (raw / scale * gain.reshape(heads, HEAD_DIM)).reshape(count, width).astype(jnp.bfloat16)
    )
    top, bottom = merged(
        (jnp.max(attended, axis=0), jnp.min(attended, axis=0)), "ctx", extreme_join
    )
    shift = (top.astype(jnp.float32) + bottom.astype(jnp.float32)) / 2.0
    partner = from_partner(attended, "head", 0)
    own_means = jnp.mean(attended.astype(jnp.float32), axis=0)
    other_means = jnp.mean(partner.astype(jnp.float32), axis=0)
    own_centered = (attended.astype(jnp.float32) - own_means).astype(jnp.bfloat16)
    other_centered = (partner.astype(jnp.float32) - other_means).astype(jnp.bfloat16)
    parity = lax.axis_index("head") % 2
    lower = parity == 0
    pair_data = jnp.concatenate(
        [
            jnp.where(lower, own_centered, other_centered),
            jnp.where(lower, other_centered, own_centered),
        ],
        axis=1,
    )
    pair_means = jnp.concatenate(
        [jnp.where(lower, own_means, other_means), jnp.where(lower, other_means, own_means)]
    )
    offset = parity * width
    shards = lax.axis_size("ctx")
    rows = width // shards
    first_row = lax.axis_index("ctx") * rows
    every_mean = lax.all_gather(pair_means[None, :], "ctx", axis=0, tiled=True)
    channel_spread = every_mean - jnp.mean(every_mean, axis=0)
    spread_rows = lax.dynamic_slice_in_dim(channel_spread, offset + first_row, rows, 1)
    fix = count * jnp.dot(spread_rows.T, channel_spread, precision=lax.Precision.HIGHEST)
    gram = lax.psum_scatter(
        lax.dot_general(
            own_centered, pair_data, (((0,), (0,)), ((), ())), preferred_element_type=jnp.float32
        ),
        "ctx",
        scatter_dimension=0,
        tiled=True,
    )
    covariance = (gram + fix) / (count * shards)
    return (shift, covariance)


def solution(mesh):
    placed = (P("ctx", "head"), P("ctx", "head"), P("ctx", "head"), P("head", "ctx"), P("head"))
    return jax.shard_map(
        body,
        mesh=mesh,
        in_specs=placed,
        out_specs=(P("head"), P(("head", "ctx"), None)),
        check_vma=False,
    )
```

profile of v0, /device:TPU:0, one launch (start us, length us, event | category | flops | bytes accessed | tf_op | source)
XLA Modules:
  0.0 329.0 jit_solution(14172750126689939225)
XLA Ops:
  7.2 0.8 copy.69
  8.0 2.3 reduce-window.14
  10.9 4.1 %copy.83 = f32[1024,1024]{0,1:T(8,128)} copy(bf16[1024,1024]{1,0:T(8,128)(2,1)} %param.12) | data formatting | bytes 6291456 | tf_op jit(solution)/shard_map/convert_element_type | solution.py:94
  15.0 6.1 %fusion.24 = f32[8,128,128]{2,1,0:T(8,128)} fusion(f32[1024,8,128]{0,2,1:T(8,128)} %bitcast.142, f32[1024,8]{0,1:T(8,128)S(1)} %exponential_bitcast_fusion.2, bf16[1024,1024]{1,0:T(8,128)(2,1)} %param.13), kind=kOutput, calls=%fused_computation.51 | convolution fusion | flops 1611661312 | bytes 6848512 | tf_op jit(solution)/shard_map/shd,she->hde/dot_general | solution.py:95
  22.5 23.6 %all-reduce = f32[64]{0:T(128)S(1)} all-reduce(f32[64]{0:T(128)S(1)} %bitcast_dynamic-update-slice_fusion), channel_id=2, replica_groups=mesh['ctx'=8,'head'=4] {'ctx'}, use_global_device_ids=true, to_apply=%add | all-reduce | flops 64 | bytes 512
  46.3 2.0 copy.92
  48.3 1.9 copy.93
  50.2 2.0 copy.94
  52.2 45.4 %all-gather.7.cloned.1.call-done = f32[64,128,128]{2,1,0:T(8,128)} async-done(((f32[8,128,128]{2,1,0:T(8,128)}), f32[64,128,128]{2,1,0:T(8,128)}) %all-gather.7.cloned.1.call-update) | async-done | bytes 4194320 | tf_op jit(solution)/shard_map/all_gather | solution.py:12
  97.6 8.4 %while.40 = (s32[]{:T(128)}, f32[8,128,128]{2,1,0:T(8,128)S(1)}, s32[]{:T(128)}, f32[8,8]{1,0:T(8,128)S(1)}, f32[8,8,128,128]{3,2,1,0:T(8,128)}, /*index=5*/s32[]{:T(128)}, s32[]{:T(128)}) while((s32[]{:T(128)}, f32[8,128,128]{2,1,0:T(8,128)S(1)}, s32[]{:T(128)}, f32[8,8]{1,0:T(8,128)S(1)}, f32[8,8,128,128]{3,2,1,0:T(8,128)}, ...), condition=%wide.region_3.4_spmd.clone, body=%wide.region_2.3_spmd.clone.sunk | while | flops 524292 | bytes 1573065 | solution.py:21
  97.6 1.2 fusion.45
  98.8 1.2 fusion.45
  100.0 1.2 fusion.45
  101.2 1.2 fusion.45
  102.5 1.2 fusion.45
  103.7 1.2 fusion.45
  104.9 1.2 fusion.45
  106.1 36.9 %while.38 = (s32[]{:T(128)}, f32[8,128,128]{2,1,0:T(8,128)S(1)}, f32[4,256,8,128]{1,3,2,0:T(8,128)}, f32[4,8,256]{2,1,0:T(8,128)}, bf16[4,256,8,128]{3,2,1,0:T(8...) while((s32[]{:T(128)}, f32[8,128,128]{2,1,0:T(8,128)S(1)}, ...), condition=%wide.region_7.8_spmd, body=%wide.region_4.7_spmd.sunk | while | flops 1078265856 | bytes 11248913 | solution.py:67
  106.1 0.7 dynamic-slice_bitcast_fusion.4
  106.8 0.6 reduce-window.24
  107.6 1.3 constant_dynamic-slice_fusion.6
  108.9 1.4 convolution_bitcast_fusion.2
  110.3 1.1 constant_dynamic-slice_fusion.5
  111.4 2.0 fusion.44
  113.7 1.6 convolution_add_fusion.2
  115.3 0.7 dynamic-slice_bitcast_fusion.4
  116.0 0.6 reduce-window.24
  116.8 1.3 constant_dynamic-slice_fusion.6
  118.1 1.4 convolution_bitcast_fusion.2
  119.5 1.1 constant_dynamic-slice_fusion.5
  120.6 2.1 fusion.44
  123.0 1.6 convolution_add_fusion.2
  124.6 0.7 dynamic-slice_bitcast_fusion.4
  126.1 1.3 constant_dynamic-slice_fusion.6
  127.4 1.4 convolution_bitcast_fusion.2
  128.8 1.1 constant_dynamic-slice_fusion.5
  129.9 2.0 fusion.44
  132.2 1.6 convolution_add_fusion.2
  133.8 0.7 dynamic-slice_bitcast_fusion.4
  134.5 0.6 reduce-window.24
  135.3 1.3 constant_dynamic-slice_fusion.6
  136.6 1.4 convolution_bitcast_fusion.2
  138.0 1.1 constant_dynamic-slice_fusion.5
  139.1 2.0 fusion.44
  141.4 1.6 convolution_add_fusion.2
  143.0 2.6 multiply_reduce_fusion
  145.6 5.2 %copy.78 = f32[4,256,8,128]{3,2,1,0:T(8,128)} copy(f32[4,256,8,128]{1,3,2,0:T(8,128)} %get-tuple-element.162) | data formatting | bytes 8388608 | tf_op jit(solution)/shard_map/while | solution.py:67
  151.1 1.1 div.56
  152.2 1.0 copy-done
  153.3 2.2 fusion.19
  155.5 4.2 %convert_reduce_fusion.1 = (f32[8,128]{1,0:T(8,128)S(1)}, bf16[4,256,8,128]{1,3,2,0:T(8,128)(2,1)}) fusion(f32[8,128]{1,0:T(8,128)S(1)} %bitcast.156, f32[4,256,8,128]{1,3,2,0:T(8,128)} %get-tuple-element.162, f32[4,256,8]{1,2,0:T(8,128)S(1)} %add_sqrt_fusion), kind=kLoop, calls=%fused_computation.48 | loop fusion | flops 5241856 | bytes 6332416 | tf_op jit(solution)/shard_map/reduce_sum | solution.py:109
  159.8 2.0 convert_reduce_fusion
  161.8 2.8 broadcast_select_fusion.1
  164.5 7.2 %fusion.20 = f32[1024,2048]{1,0:T(8,128)} fusion(bf16[1024,1024]{1,0:T(8,128)(2,1)S(1)} %get-tuple-element.263, bf16[1024,1024]{1,0:T(8,128)(2,1)S(1)} %get-tuple-element.262, bf16[1024,1024]{1,0:T(8,128)(2,1)S(1)} %fusion.19, f32[1024]{0:T(1024)S(1)} %multiply_bitcast_fusion), kind=kOutput, calls=%fused_computation.43 | convolution fusion | flops 4306501632 | bytes 14684160 | tf_op jit(solution)/shard_map/dot_general | solution.py:134
  171.8 1.6 copy-done.3
  173.3 0.9 fusion.32
  174.2 31.5 %all-gather.4 = bf16[8,1,1024]{2,1,0:T(2,128)(2,1)S(1)} all-gather(bf16[1,1,1024]{2,1,0:T(2,128)(2,1)S(1)} %reshape.171), channel_id=1, replica_groups=mesh['ctx'=8,'head'=4] {'ctx'}, dimensions={0}, use_global_device_ids=true | all-gather | bytes 18432 | tf_op jit(solution)/shard_map/all_gather | solution.py:25
  205.7 31.5 %all-gather.3 = bf16[8,1,1024]{2,1,0:T(2,128)(2,1)S(1)} all-gather(bf16[1,1,1024]{2,1,0:T(2,128)(2,1)S(1)} %reshape.169), channel_id=1, replica_groups=mesh['ctx'=8,'head'=4] {'ctx'}, dimensions={0}, use_global_device_ids=true | all-gather | bytes 18432 | tf_op jit(solution)/shard_map/all_gather | solution.py:25
  237.4 0.6 while.39
  238.0 0.6 add_multiply_fusion.1
  238.6 30.8 %all-gather.2 = f32[16384]{0:T(1024)S(1)} all-gather(f32[2048]{0:T(1024)S(1)} %pad_maximum_fusion), channel_id=4, replica_groups=mesh['ctx'=8,'head'=4] {'ctx'}, dimensions={0}, use_global_device_ids=true | all-gather | bytes 73728 | tf_op jit(solution)/shard_map/all_gather | solution.py:129
  269.4 1.0 convolution_multiply_fusion
  270.4 49.5 %reduce-scatter.2.cloned.1.call-done = f32[128,2048]{1,0:T(8,128)} async-done(((f32[1024,2048]{1,0:T(8,128)}), f32[128,2048]{1,0:T(8,128)}) %reduce-scatter.2.cloned.1.call-update) | async-done | bytes 1048592 | tf_op jit(solution)/shard_map/reduce_scatter | solution.py:133
  319.9 2.3 add_multiply_fusion
  (109 shorter events, 5.5 us)
Async XLA Ops:
  7.2 90.4 %all-gather.7.cloned.1.call-start = ((), (), s32[]{:S(2)}) async-start(), calls=%async_computation.2 | async-start | bytes 4718592 | tf_op jit(solution)/shard_map/all_gather | solution.py:12
  15.0 6.2 %copy-start.6 = (u32[32]{0:T(128)S(1)}, u32[32]{0:T(128)}, u32[]{:S(2)}) copy-start(u32[32]{0:T(128)} %constant.110) | copy-start | bytes 388
  15.0 31.2 %copy-start.1 = (bf16[1024,1024]{1,0:T(8,128)(2,1)S(1)}, bf16[1024,1024]{1,0:T(8,128)(2,1)}, u32[]{:S(2)}) copy-start(bf16[1024,1024]{1,0:T(8,128)(2,1)} %param.12) | copy-start | bytes 6291460
  21.2 298.7 %reduce-scatter.2.cloned.1.call-start = ((), (), s32[]{:S(2)}) async-start(), calls=%async_computation.1 | async-start | bytes 9437184 | tf_op jit(solution)/shard_map/reduce_scatter | solution.py:133
  46.2 2.0 copy-start.2
  46.3 4.0 %copy-start.4 = (bf16[1024,1024]{1,0:T(8,128)(2,1)S(1)}, bf16[1024,1024]{1,0:T(8,128)(2,1)}, u32[]{:S(2)}) copy-start(bf16[1024,1024]{1,0:T(8,128)(2,1)} %param.11) | copy-start | bytes 6291460
  150.8 1.4 copy-start.5
  151.1 2.2 copy-start
  155.4 4.4 %collective-permute-start = (bf16[1024,1024]{1,0:T(8,128)(2,1)S(1)}, bf16[1024,1024]{1,0:T(8,128)(2,1)}, u32[]{:S(2)}, u32[]{:S(2)}) collective-permute-start(bf16[1024,1024]{1,0:T(8,128)(2,1)S(1)} %fusion.19), channel_id=1, source_target_pairs={{0,1},{1,0},{2,3},{3,2},{4,5},{5,4},{6,7},{7,6},{8,9},{9,8},{10,11... | collective-permute-start | bytes 6291464 | tf_op jit(solution)/shard_map/ppermute | solution.py:35
  171.7 1.6 copy-start.3
Sparse Core Ops, SparseCore 0:
  21.3 76.2 all-gather.6
  171.9 147.9 reduce-scatter.1
where the time goes:
time: 330 us; the launch traced here: 329 us
  blocking collectives  117 us (35%)
  waiting for transfers between devices  95 us (29%)
  local copies, waits for them, and re-layouts  35.2 us (11%)
  matrix products  34.3 us (10%)
  other arithmetic  31.6 us (10%)
  between operations  14.9 us (5%)
    all_gather x2, blocking collectives, merged(): pieces = jax.tree.map(lambda part: lax.all_gather(part, axis), value)  63 us
    reduce_scatter x1, waiting for transfers between devices, body(): lax.psum_scatter(lax.dot_general(own_centered, pair_data, (((0,), (0,)),...  49.5 us
    all_gather x1, waiting for transfers between devices, entering(): pieces = jax.tree.map(lambda part: lax.all_gather(part, axis), value)  45.4 us
    all_gather x1, blocking collectives, body(): every_mean = lax.all_gather(pair_means[None, :], 'ctx', axis=0, tiled=True)  30.8 us
    unnamed x1, blocking collectives  23.6 us
    dynamic_slice x8, local copies, waits for them, and re-layouts, run_blocks(): ending, raw = lax.scan(block_step, start, shaped)  9.43 us
    unnamed x26, local copies, waits for them, and re-layouts  9.33 us
    select_n x7, other arithmetic, turn(): jnp.where(position < mine, new, old)  8.2 us
  transfers between devices with their start and end apart: 3, of which 3 were waited for; matrix products, arithmetic and copies ran while one was open for 4% of the time, Pallas kernels for 0%

commit v1 on v0

v1 whole, which is shorter than its diff:
```python
import functools

import jax
import jax.numpy as jnp
from jax import lax
from jax.experimental import pallas as pl
from jax.experimental.pallas import tpu as pltpu
from jax.sharding import PartitionSpec as P

HEAD_DIM = 128
SPAN = 256
F32 = jnp.float32
BF16 = jnp.bfloat16
HIGHEST = lax.Precision.HIGHEST
MIB = 1 << 20


def params(limit_mib):
    return pltpu.CompilerParams(vmem_limit_bytes=limit_mib * MIB)


def cost(flops, moved, transcendentals=0):
    return pl.CostEstimate(
        flops=int(flops), bytes_accessed=int(moved), transcendentals=int(transcendentals)
    )


def whole(shape):
    return pl.BlockSpec(shape, lambda *_: (0,) * len(shape))


def struct(shape, dtype):
    return jax.ShapeDtypeStruct(shape, dtype)


def dot(a, b):
    return jnp.dot(a, b, preferred_element_type=F32)


def split(value):
    high = value.astype(BF16)
    return high, (value - high.astype(F32)).astype(BF16)


def running_sum(decay):
    rows = lax.broadcasted_iota(jnp.int32, (SPAN, SPAN), 0)
    columns = lax.broadcasted_iota(jnp.int32, (SPAN, SPAN), 1)
    ones = jnp.where(rows <= columns, 1.0, 0.0).astype(F32)
    return jnp.dot(decay, ones, precision=HIGHEST, preferred_element_type=F32)


def head_columns(head):
    return slice(head * HEAD_DIM, (head + 1) * HEAD_DIM)


def states_kernel(shards, me_ref, k_ref, v_ref, decay_ref, entering_ref, before_ref, *rest):
    pieces, (state, total) = rest[:shards], rest[shards:]
    heads = decay_ref.shape[0]
    step = pl.program_id(0)

    @pl.when(step == 0)
    def _():
        state[...] = jnp.zeros_like(state)
        total[...] = jnp.ones_like(total)

    entering_ref[0] = state[...]
    before_ref[0] = total[...]
    cumul = running_sum(decay_ref[...])
    last = cumul[:, SPAN - 1 :]
    weight = jnp.exp(last - cumul)
    drop = jnp.exp(last)
    for head in range(heads):
        cols = head_columns(head)
        scaled = k_ref[:, cols].T.astype(F32) * weight[head : head + 1, :]
        high, low = split(scaled)
        value = v_ref[:, cols]
        update = dot(high, value) + dot(low, value)
        state[cols, :] = state[cols, :] * drop[head : head + 1, :] + update
    total[...] = total[...] * drop

    @pl.when(step == pl.num_programs(0) - 1)
    def _():
        rows = heads * HEAD_DIM // shards
        for index in range(shards):
            start = pl.multiple_of((me_ref[0] ^ index) * rows, rows)
            pieces[index][:rows, :] = state[pl.ds(start, rows), :]
            piece_total = total[pl.ds(start // HEAD_DIM, 1), :]
            pieces[index][rows:, :] = jnp.broadcast_to(piece_total, (8, HEAD_DIM))


def local_states(me, keys, values, log_decay, shards):
    count, width = keys.shape
    heads = width // HEAD_DIM
    blocks = count // SPAN
    rows = width // shards
    piece = (rows + 8, HEAD_DIM)
    shapes = [(blocks, width, HEAD_DIM), (blocks, heads, HEAD_DIM)] + [piece] * shards
    tokens = pl.BlockSpec((SPAN, width), lambda i, me: (i, 0))
    out = pl.pallas_call(
        functools.partial(states_kernel, shards),
        grid_spec=pltpu.PrefetchScalarGridSpec(
            num_scalar_prefetch=1,
            grid=(blocks,),
            in_specs=[tokens, tokens, pl.BlockSpec((heads, SPAN), lambda i, me: (0, i))],
            out_specs=[
                pl.BlockSpec((1, width, HEAD_DIM), lambda i, me: (i, 0, 0)),
                pl.BlockSpec((1, heads, HEAD_DIM), lambda i, me: (i, 0, 0)),
            ]
            + [whole(piece)] * shards,
            scratch_shapes=[pltpu.VMEM((width, HEAD_DIM), F32), pltpu.VMEM((heads, HEAD_DIM), F32)],
        ),
        out_shape=[struct(shape, F32) for shape in shapes],
        compiler_params=params(24),
        cost_estimate=cost(4 * count * width * HEAD_DIM, 4 * count * width),
        name="local_states",
    )(me, keys, values, log_decay)
    return out[0], out[1], out[2:]


def chain_kernel(shards, me_ref, *refs):
    arrived, outs, (ordered, entering) = refs[:shards], refs[shards : 2 * shards], refs[2 * shards :]
    rows = outs[0].shape[0]
    for index in range(shards):
        ordered[me_ref[0] ^ index] = arrived[index][...]
    carried = jnp.zeros((rows, HEAD_DIM), F32)
    for shard in range(shards):
        entering[shard] = carried
        carried = carried * ordered[shard, rows : rows + 1, :] + ordered[shard, :rows, :]
    for index in range(shards):
        outs[index][...] = entering[me_ref[0] ^ index]


def chain(me, pieces):
    shards = len(pieces)
    rows = pieces[0].shape[0] - 8
    return pl.pallas_call(
        functools.partial(chain_kernel, shards),
        grid_spec=pltpu.PrefetchScalarGridSpec(
            num_scalar_prefetch=1,
            grid=(1,),
            in_specs=[whole((rows + 8, HEAD_DIM))] * shards,
            out_specs=[whole((rows, HEAD_DIM))] * shards,
            scratch_shapes=[
                pltpu.VMEM((shards, rows + 8, HEAD_DIM), F32),
                pltpu.VMEM((shards, rows, HEAD_DIM), F32),
            ],
        ),
        out_shape=[struct((rows, HEAD_DIM), F32)] * shards,
        compiler_params=params(16),
        name="chain",
    )(me, *pieces)


def inner_kernel(q_ref, k_ref, v_ref, decay_ref, raw_ref):
    heads = decay_ref.shape[0]
    cumul = running_sum(decay_ref[...])
    columns = cumul.T
    half = SPAN // 2
    for head in range(heads):
        cols = head_columns(head)
        for part in range(2):
            rows = slice(part * half, (part + 1) * half)
            width = (part + 1) * half
            scores = lax.dot_general(
                q_ref[rows, cols],
                k_ref[:width, cols],
                (((1,), (1,)), ((), ())),
                preferred_element_type=F32,
            )
            diff = columns[rows, head : head + 1] - cumul[head : head + 1, :width]
            token = lax.broadcasted_iota(jnp.int32, (half, width), 0) + part * half
            earlier = lax.broadcasted_iota(jnp.int32, (half, width), 1)
            factor = jnp.exp(jnp.where(token >= earlier, diff, -jnp.inf))
            weights = (scores * factor).astype(BF16)
            raw_ref[rows, cols] = dot(weights, v_ref[:width, cols])


def inner(queries, keys, values, log_decay):
    count, width = keys.shape
    heads = width // HEAD_DIM
    tokens = pl.BlockSpec((SPAN, width), lambda i: (i, 0))
    return pl.pallas_call(
        inner_kernel,
        grid=(count // SPAN,),
        in_specs=[tokens, tokens, tokens, pl.BlockSpec((heads, SPAN), lambda i: (0, i))],
        out_specs=tokens,
        out_shape=struct((count, width), F32),
        compiler_params=params(24),
        cost_estimate=cost(4 * count * width * SPAN, 10 * count * width, count * heads * SPAN),
        name="inner",
    )(queries, keys, values, log_decay)


def finish_kernel(
    shards, me_ref, q_ref, raw_ref, entering_ref, before_ref, decay_ref, gain_ref, *rest
):
    pieces, (centered_ref, stats_ref, arrived) = rest[:shards], rest[shards:]
    heads = decay_ref.shape[0]
    width = heads * HEAD_DIM
    rows = width // shards
    step = pl.program_id(0)
    blocks = pl.num_programs(0)
    count = centered_ref.shape[0]

    @pl.when(step == 0)
    def _():
        for index in range(shards):
            start = pl.multiple_of((me_ref[0] ^ index) * rows, rows)
            arrived[pl.ds(start, rows), :] = pieces[index][...]
        stats_ref[0:1, :] = jnp.zeros((1, width), F32)
        stats_ref[1:2, :] = jnp.full((1, width), -jnp.inf, F32)
        stats_ref[2:3, :] = jnp.full((1, width), jnp.inf, F32)
        stats_ref[3:, :] = jnp.zeros((5, width), F32)

    factor = jnp.exp(running_sum(decay_ref[...])).T
    first = pl.multiple_of(step * SPAN, SPAN)
    for head in range(heads):
        cols = head_columns(head)
        state = entering_ref[0, cols, :] + before_ref[0, head : head + 1, :] * arrived[cols, :]
        high, low = split(state)
        query = q_ref[:, cols]
        outer = dot(query, high) + dot(query, low)
        raw = raw_ref[:, cols] + outer * factor[:, head : head + 1]
        power = jnp.mean(raw * raw, axis=1, keepdims=True)
        attended = (raw / jnp.sqrt(power + 1e-06) * gain_ref[:, cols]).astype(BF16)
        centered_ref[pl.ds(first, SPAN), cols] = attended
        wide = attended.astype(F32)
        stats_ref[0:1, cols] += jnp.sum(wide, axis=0, keepdims=True)
        stats_ref[1:2, cols] = jnp.maximum(stats_ref[1:2, cols], jnp.max(wide, axis=0, keepdims=True))
        stats_ref[2:3, cols] = jnp.minimum(stats_ref[2:3, cols], jnp.min(wide, axis=0, keepdims=True))

    @pl.when(step == blocks - 1)
    def _():
        mean = stats_ref[0:1, :] / count
        stats_ref[0:1, :] = mean

        @pl.loop(0, count // 128)
        def _(index):
            part = pl.ds(pl.multiple_of(index * 128, 128), 128)
            centered_ref[part, :] = (centered_ref[part, :].astype(F32) - mean).astype(BF16)


def finish(me, queries, raw, entering, before, log_decay, gain, pieces):
    count, width = queries.shape
    heads = width // HEAD_DIM
    shards = len(pieces)
    tokens = pl.BlockSpec((SPAN, width), lambda i, me: (i, 0))
    return pl.pallas_call(
        functools.partial(finish_kernel, shards),
        grid_spec=pltpu.PrefetchScalarGridSpec(
            num_scalar_prefetch=1,
            grid=(count // SPAN,),
            in_specs=[
                tokens,
                tokens,
                pl.BlockSpec((1, width, HEAD_DIM), lambda i, me: (i, 0, 0)),
                pl.BlockSpec((1, heads, HEAD_DIM), lambda i, me: (i, 0, 0)),
                pl.BlockSpec((heads, SPAN), lambda i, me: (0, i)),
                whole((1, width)),
            ]
            + [whole(pieces[0].shape)] * shards,
            out_specs=[whole((count, width)), whole((8, width))],
            scratch_shapes=[pltpu.VMEM((width, HEAD_DIM), F32)],
        ),
        out_shape=[struct((count, width), BF16), struct((8, width), F32)],
        compiler_params=params(32),
        cost_estimate=cost(4 * count * width * HEAD_DIM, 10 * count * width),
        name="finish",
    )(me, queries, raw, entering, before, log_decay, gain, *pieces)


def gram_kernel(rows, ranges, me_ref, own_ref, other_ref, keep_ref, send_ref, both, sems):
    width = own_ref.shape[1]
    copies = [
        pltpu.make_async_copy(own_ref, both.at[:, :width], sems.at[0]),
        pltpu.make_async_copy(other_ref, both.at[:, width:], sems.at[1]),
    ]
    for copy in copies:
        copy.start()
    for copy in copies:
        copy.wait()
    low = me_ref[0] & 1
    for index in range(keep_ref.shape[0]):
        for out_ref, bit in ((send_ref, 1 - low), (keep_ref, low)):
            start = (2 * index + bit) * rows
            left = both[:, pl.ds(pl.multiple_of(start, rows), rows)].T
            place = 0
            for begin, end in ranges:
                size = (end - begin) * rows
                at = pl.multiple_of(start + begin * rows, rows)
                out = dot(left, both[:, pl.ds(at, size)])
                out_ref[index, :, place : place + size] = out.astype(out_ref.dtype)
                place += size


def gram_parts(me, own, other, rows, ranges):
    count, width = own.shape
    shards = width // rows
    size = sum(end - begin for begin, end in ranges) * rows
    if rows % 128:
        full = lax.dot_general(
            own,
            jnp.concatenate([own, other], axis=1),
            (((0,), (0,)), ((), ())),
            preferred_element_type=F32,
        )
        parts = []
        for shard in range(shards):
            line = full[shard * rows : (shard + 1) * rows]
            slabs = [line[:, (shard + a) * rows : (shard + b) * rows] for a, b in ranges]
            parts.append(jnp.concatenate(slabs, axis=1))
        parts = jnp.stack(parts).reshape(shards // 2, 2, rows, size)
        low = me[0] & 1
        keep = lax.dynamic_index_in_dim(parts, low, 1, False)
        send = lax.dynamic_index_in_dim(parts, 1 - low, 1, False)
        return keep, send.astype(BF16)
    shape = (shards // 2, rows, size)
    anywhere = pl.BlockSpec(memory_space=pl.ANY)
    return pl.pallas_call(
        functools.partial(gram_kernel, rows, ranges),
        grid_spec=pltpu.PrefetchScalarGridSpec(
            num_scalar_prefetch=1,
            grid=(1,),
            in_specs=[anywhere, anywhere],
            out_specs=[whole(shape), whole(shape)],
            scratch_shapes=[pltpu.VMEM((count, 2 * width), BF16), pltpu.SemaphoreType.DMA((2,))],
        ),
        out_shape=[struct(shape, F32), struct(shape, BF16)],
        compiler_params=params(32),
        cost_estimate=cost(2 * count * width * size, 4 * count * width),
        name="gram",
    )(me, own, other)


def cover_kernel(rows, shards, total, order, me_ref, means_ref, others_ref, *refs):
    chunk_count = len(order)
    chunks = refs[:chunk_count]
    mirrors = refs[chunk_count : chunk_count + shards - 1]
    out_ref, spread = refs[chunk_count + shards - 1 :]
    width = rows * shards
    mine, side = me_ref[0], me_ref[1]
    for ref, place in ((means_ref, side), (others_ref, 1 - side)):
        value = ref[...]
        centre = jnp.sum(value, axis=0, keepdims=True) / shards
        spread[:, pl.ds(pl.multiple_of(place * width, width), width)] = value - centre
    block = side * shards + mine
    left = spread[:, pl.ds(pl.multiple_of(block * rows, rows), rows)].T
    count = total // shards
    out_ref[...] = count * jnp.dot(left, spread[...], precision=HIGHEST, preferred_element_type=F32)

    def put(position, gram):
        position = lax.rem(position + 2 * shards, 2 * shards)
        at = pl.ds(pl.multiple_of(position * rows, rows), rows)
        out_ref[:, at] = (out_ref[:, at] + gram) / total

    for chunk, steps in zip(chunks, order):
        for index, step in enumerate(steps):
            put(block + step, chunk[:, index * rows : (index + 1) * rows])
    for index in range(shards - 1):
        put(block - (index + 1), mirrors[index][...].T.astype(F32))


def cover(me, means, others, chunks, mirrors, order, rows, shards, total):
    width = rows * shards
    if rows % 128:
        mine, side = me[0], me[1]
        pair = [jnp.where(side == 0, means, others), jnp.where(side == 0, others, means)]
        spread = jnp.concatenate(pair, axis=1)
        spread = spread - jnp.mean(spread, axis=0)
        block = side * shards + mine
        left = lax.dynamic_slice_in_dim(spread, block * rows, rows, 1)
        fix = (total // shards) * jnp.dot(left.T, spread, precision=HIGHEST)
        ahead = {}
        for chunk, steps in zip(chunks, order):
            for index, step in enumerate(steps):
                ahead[step] = chunk[:, index * rows : (index + 1) * rows]
        slabs = [mirrors[step - 1].T.astype(F32) for step in range(shards - 1, 0, -1)]
        slabs += [ahead[step] for step in range(shards + 1)]
        line = jnp.roll(jnp.concatenate(slabs, axis=1), (block - (shards - 1)) * rows, axis=1)
        return (line + fix) / total
    return pl.pallas_call(
        functools.partial(cover_kernel, rows, shards, total, order),
        grid_spec=pltpu.PrefetchScalarGridSpec(
            num_scalar_prefetch=1,
            grid=(1,),
            in_specs=[whole(value.shape) for value in (means, others, *chunks, *mirrors)],
            out_specs=whole((rows, 2 * width)),
            scratch_shapes=[pltpu.VMEM((shards, 2 * width), F32)],
        ),
        out_shape=struct((rows, 2 * width), F32),
        compiler_params=params(16),
        name="cover",
    )(me, means, others, *chunks, *mirrors)


def body(queries, keys, values, log_decay, gain):
    count, width = queries.shape
    shards = lax.axis_size("ctx")
    sides = lax.axis_size("head")
    rows = width // shards
    mine, head = lax.axis_index("ctx"), lax.axis_index("head")
    me = jnp.stack([mine, head % 2]).astype(jnp.int32)

    def to_shard(value, apart):
        return lax.ppermute(value, "ctx", [(a, a ^ apart) for a in range(shards)])

    def to_partner(value):
        return lax.ppermute(value, "head", [(a, a ^ 1) for a in range(sides)])

    def everywhere(values):
        return [values[0]] + [to_shard(values[k], k) for k in range(1, shards)]

    def forward(value, steps):
        pairs = []
        for shard in range(shards):
            for side in range(sides):
                block = (side % 2) * shards + shard + steps
                other = (block // shards) % 2
                target = (block % shards) * sides + (side // 2) * 2 + other
                pairs.append((shard * sides + side, target))
        return lax.ppermute(value, ("ctx", "head"), pairs)

    entering, before, pieces = local_states(me, keys, values, log_decay, shards)
    arrived = everywhere(pieces)
    raw = inner(queries, keys, values, log_decay)
    entry = everywhere(chain(me, arrived))
    centered, stats = finish(
        me, queries, raw, entering, before, log_decay, gain.reshape(1, width), entry
    )
    partner = to_partner(centered)

    third = (shards - 1) // 2
    order = [
        tuple(range(1, 1 + third)),
        tuple(range(1 + third, 1 + 2 * third)),
        tuple(range(1 + 2 * third, shards + 1)) + (0,),
    ]
    ranges = [
        ((1, 1 + third),),
        ((1 + third, 1 + 2 * third),),
        ((1 + 2 * third, shards + 1), (0, 1)),
    ]
    place = mine // 2
    chunks, mirrors = [], [None] * (shards - 1)
    for spans, steps in zip(ranges, order):
        keep, send = gram_parts(me, centered, partner, rows, spans)
        summed = keep + to_shard(send, 1).astype(F32)
        total = lax.dynamic_index_in_dim(summed, place, 0, False)
        for apart in range(1, shards // 2):
            slab = lax.dynamic_index_in_dim(summed, place ^ apart, 0, False).astype(BF16)
            total = total + to_shard(slab, 2 * apart).astype(F32)
        chunks.append(total)
        for index, step in enumerate(steps):
            if 0 < step < shards:
                slab = total[:, index * rows : (index + 1) * rows].astype(BF16)
                mirrors[step - 1] = forward(slab, step)

    small = stats[:3]
    gathered = jnp.stack(everywhere([small] * shards))
    means = gathered[:, 0]
    shift = (jnp.max(gathered[:, 1], axis=0) + jnp.min(gathered[:, 2], axis=0)) / 2.0
    others = to_partner(means)
    covariance = cover(me, means, others, chunks, mirrors, order, rows, shards, count * shards)
    return (shift, covariance)


def solution(mesh):
    placed = (P("ctx", "head"), P("ctx", "head"), P("ctx", "head"), P("head", "ctx"), P("head"))
    return jax.shard_map(
        body,
        mesh=mesh,
        in_specs=placed,
        out_specs=(P("head"), P(("head", "ctx"), None)),
        check_vma=False,
    )
```

time: 330 us -> 141 us (0.43)
  blocking collectives: 117 us -> 0 us
  starting transfers between devices: 0.15 us -> 60 us
  waiting for transfers between devices: 95 us -> 38.1 us
  matrix products: 34.3 us -> 0 us
  Pallas kernels: 0 us -> 32.3 us
  other arithmetic: 31.6 us -> 2.07 us
  local copies, waits for them, and re-layouts: 35.2 us -> 5.98 us
  between operations: 14.9 us -> 1 us
    all_gather x3 -> x0, blocking collectives: 93.8 us -> none  [the longest x2 63 us: merged(): pieces = jax.tree.map(lambda part: lax.all_gather(part, axis), value)]
    ppermute x1 -> x42, starting transfers between devices: 0.07 us -> 60 us  [the longest x33 49.7 us: to_shard(): return lax.ppermute(value, 'ctx', [(a, a ^ apart) for a in range(shards)])]
    reduce_scatter x1 -> x0, waiting for transfers between devices: 49.5 us -> none  [body(): lax.psum_scatter(lax.dot_general(own_centered, pair_data, (((0,), (0,)),...]
    all_gather x1 -> x0, waiting for transfers between devices: 45.4 us -> none  [entering(): pieces = jax.tree.map(lambda part: lax.all_gather(part, axis), value)]
    ppermute x1 -> x42, waiting for transfers between devices: 0.1 us -> 38.1 us  [the longest x33 30.9 us: to_shard(): return lax.ppermute(value, 'ctx', [(a, a ^ apart) for a in range(shards)])]
    dot_general x15 -> x0, matrix products: 34.3 us -> none  [the longest x4 8.1 us: block_step(): jnp.einsum('hts,shd->thd', weights, value, preferred_element_type=jnp.flo...]
    pallas_call x0 -> x8, Pallas kernels: none -> 32.3 us  [the longest x1 8.46 us: inner(): pl.pallas_call(inner_kernel, grid=(count // SPAN,), in_specs=[tokens, tok...]
    unnamed x1 -> x0, blocking collectives: 23.6 us -> none
  transfers between devices with their start and end apart: 3 -> 42, of which waited for: 3 -> 16; matrix products, arithmetic and copies ran while one was open for 4% -> 2% of each run, Pallas kernels for 0% -> 10%
where the time goes in v1:
time: 141 us; the launch traced here: 139 us
  starting transfers between devices  60 us (43%)
  waiting for transfers between devices  38.1 us (27%)
  Pallas kernels  32.3 us (23%)
  local copies, waits for them, and re-layouts  5.98 us (4%)
  other arithmetic  2.07 us (1%)
    ppermute x33, starting transfers between devices, to_shard(): return lax.ppermute(value, 'ctx', [(a, a ^ apart) for a in range(shards)])  49.7 us
    ppermute x33, waiting for transfers between devices, to_shard(): return lax.ppermute(value, 'ctx', [(a, a ^ apart) for a in range(shards)])  30.9 us
    ppermute x7, starting transfers between devices, forward(): return lax.ppermute(value, ('ctx', 'head'), pairs)  10.1 us
    pallas_call x1, Pallas kernels, inner(): pl.pallas_call(inner_kernel, grid=(count // SPAN,), in_specs=[tokens, tok...  8.46 us
    pallas_call x1, Pallas kernels, finish(): pl.pallas_call(functools.partial(finish_kernel, shards), grid_spec=pltpu....  8.02 us
    pallas_call x3, Pallas kernels, gram_parts(): pl.pallas_call(functools.partial(gram_kernel, rows, ranges), grid_spec=pl...  7.94 us
    unnamed x18, local copies, waits for them, and re-layouts  5.54 us
    pallas_call x1, Pallas kernels, local_states(): pl.pallas_call(functools.partial(states_kernel, shards), grid_spec=pltpu....  4.48 us
  transfers between devices with their start and end apart: 42, of which 16 were waited for; matrix products, arithmetic and copies ran while one was open for 2% of the time, Pallas kernels for 10%

profile of v1, /device:TPU:0, one launch (start us, length us, event | category | flops | bytes accessed | tf_op | source)
XLA Modules:
  0.0 139.4 jit_solution(15384855352343401272)
XLA Ops:
  0.6 0.1 pad_add_fusion.me_ref
  0.7 1.6 %copy-done.2 = bf16[1024,1024]{1,0:T(8,128)(2,1)S(1)} copy-done((bf16[1024,1024]{1,0:T(8,128)(2,1)S(1)}, bf16[1024,1024]{1,0:T(8,128)(2,1)}, u32[]{:S(2)}) %copy-start.2) | copy-done | bytes 2097176
  2.3 1.6 %copy-done.4 = bf16[1024,1024]{1,0:T(8,128)(2,1)S(1)} copy-done((bf16[1024,1024]{1,0:T(8,128)(2,1)S(1)}, bf16[1024,1024]{1,0:T(8,128)(2,1)}, u32[]{:S(2)}) %copy-start.4) | copy-done | bytes 2097176
  3.9 0.8 copy-done.6
  4.7 4.5 %local_states.1 = (f32[4,1024,128]{2,1,0:T(8,128)S(1)}, f32[4,8,128]{2,1,0:T(8,128)S(1)}, f32[136,128]{1,0:T(8,128)S(1)}, f32[136,128]{1,0:T(8,128)S(1)}, f32[13...) custom-call(s32[2]{0:T(128)S(1)} %pad_add_fusion.me_ref, ...), custom_call_target="tpu_custom_call" | custom-call | flops 536870912 | bytes 4194304 | tf_op jit(solution)/shard_map/local_states/pallas_call | solution.py:99
  9.2 3.0 %collective-permute-start = (f32[136,128]{1,0:T(8,128)S(1)}, f32[136,128]{1,0:T(8,128)S(1)}, u32[]{:S(2)}, u32[]{:S(2)}) collective-permute-start(f32[136,128]{1,0:T(8,128)S(1)} %get-tuple-element.31), channel_id=1, source_target_pairs={{0,4},{4,0},{8,12},{12,8},{16,20},{20,16},{24,28},{28,24},{1,5},{5... | collective-permute-start | bytes 208904 | tf_op jit(solution)/shard_map/ppermute | solution.py:405
  12.2 1.6 %collective-permute-start.1 = (f32[136,128]{1,0:T(8,128)S(1)}, f32[136,128]{1,0:T(8,128)S(1)}, u32[]{:S(2)}, u32[]{:S(2)}) collective-permute-start(f32[136,128]{1,0:T(8,128)S(1)} %get-tuple-element.32), channel_id=1, source_target_pairs={{0,8},{4,12},{8,0},{12,4},{16,24},{20,28},{24,16},{28,20},{1,9},{5... | collective-permute-start | bytes 208904 | tf_op jit(solution)/shard_map/ppermute | solution.py:405
  13.8 3.0 %collective-permute-start.3 = (f32[136,128]{1,0:T(8,128)S(1)}, f32[136,128]{1,0:T(8,128)S(1)}, u32[]{:S(2)}, u32[]{:S(2)}) collective-permute-start(f32[136,128]{1,0:T(8,128)S(1)} %get-tuple-element.34), channel_id=1, source_target_pairs={{0,16},{4,20},{8,24},{12,28},{16,0},{20,4},{24,8},{28,12},{1,17},{... | collective-permute-start | bytes 208904 | tf_op jit(solution)/shard_map/ppermute | solution.py:405
  16.7 1.3 collective-permute-start.4
  18.0 3.6 %collective-permute-start.5 = (f32[136,128]{1,0:T(8,128)S(1)}, f32[136,128]{1,0:T(8,128)S(1)}, u32[]{:S(2)}, u32[]{:S(2)}) collective-permute-start(f32[136,128]{1,0:T(8,128)S(1)} %get-tuple-element.36), channel_id=1, source_target_pairs={{0,24},{4,28},{8,16},{12,20},{16,8},{20,12},{24,0},{28,4},{1,25},{... | collective-permute-start | bytes 208904 | tf_op jit(solution)/shard_map/ppermute | solution.py:405
  21.7 5.8 %collective-permute-done.4.refs_5_ = f32[136,128]{1,0:T(8,128)S(1)} collective-permute-done((f32[136,128]{1,0:T(8,128)S(1)}, f32[136,128]{1,0:T(8,128)S(1)}, u32[]{:S(2)}, u32[]{:S(2)}) %collective-permute-start.4) | collective-permute-done | bytes 69664 | tf_op jit(solution)/shard_map/ppermute | solution.py:405
  27.5 1.3 collective-permute-done.6.refs_7_
  28.8 0.7 chain.1
  29.4 3.5 %collective-permute-start.10 = (f32[128,128]{1,0:T(8,128)S(1)}, f32[128,128]{1,0:T(8,128)S(1)}, u32[]{:S(2)}, u32[]{:S(2)}) collective-permute-start(f32[128,128]{1,0:T(8,128)S(1)} %get-tuple-element.42), channel_id=1, source_target_pairs={{0,16},{4,20},{8,24},{12,28},{16,0},{20,4},{24,8},{28,12},{1,17},{... | collective-permute-start | bytes 196616 | tf_op jit(solution)/shard_map/ppermute | solution.py:405
  32.9 1.5 %collective-permute-start.12 = (f32[128,128]{1,0:T(8,128)S(1)}, f32[128,128]{1,0:T(8,128)S(1)}, u32[]{:S(2)}, u32[]{:S(2)}) collective-permute-start(f32[128,128]{1,0:T(8,128)S(1)} %get-tuple-element.44), channel_id=1, source_target_pairs={{0,24},{4,28},{8,16},{12,20},{16,8},{20,12},{24,0},{28,4},{1,25},{... | collective-permute-start | bytes 196616 | tf_op jit(solution)/shard_map/ppermute | solution.py:405
  34.4 3.2 %collective-permute-start.13 = (f32[128,128]{1,0:T(8,128)S(1)}, f32[128,128]{1,0:T(8,128)S(1)}, u32[]{:S(2)}, u32[]{:S(2)}) collective-permute-start(f32[128,128]{1,0:T(8,128)S(1)} %get-tuple-element.45), channel_id=1, source_target_pairs={{0,28},{4,24},{8,20},{12,16},{16,12},{20,8},{24,4},{28,0},{1,29},{... | collective-permute-start | bytes 196616 | tf_op jit(solution)/shard_map/ppermute | solution.py:405
  37.7 0.5 collective-permute-start.7
  38.2 2.2 %collective-permute-done.10.rest_4_ = f32[128,128]{1,0:T(8,128)S(1)} collective-permute-done((f32[128,128]{1,0:T(8,128)S(1)}, f32[128,128]{1,0:T(8,128)S(1)}, u32[]{:S(2)}, u32[]{:S(2)}) %collective-permute-start.10) | collective-permute-done | bytes 65568 | tf_op jit(solution)/shard_map/ppermute | solution.py:405
  40.4 2.3 %collective-permute-done.11.rest_5_ = f32[128,128]{1,0:T(8,128)S(1)} collective-permute-done((f32[128,128]{1,0:T(8,128)S(1)}, f32[128,128]{1,0:T(8,128)S(1)}, u32[]{:S(2)}, u32[]{:S(2)}) %collective-permute-start.11) | collective-permute-done | bytes 65568 | tf_op jit(solution)/shard_map/ppermute | solution.py:405
  42.7 8.5 %inner.1.raw_ref = f32[1024,1024]{1,0:T(8,128)S(1)} custom-call(bf16[1024,1024]{1,0:T(8,128)(2,1)S(1)} %copy-done.5, bf16[1024,1024]{1,0:T(8,128)(2,1)S(1)} %copy-done.3, bf16[1024,1024]{1,0:T(8,128)(2,1)S(1)} %copy-done.4, f32[8,1024]{1,0:T(8,128)S(1)} %copy-done.6), custom_call_target="tpu_custom_call" | custom-call | flops 1073741824 | bytes 10485760 | tf_op jit(solution)/shard_map/inner/pallas_call | solution.py:182
  51.3 8.0 %finish.1 = (bf16[1024,1024]{1,0:T(8,128)(2,1)S(1)}, f32[8,1024]{1,0:T(8,128)S(1)}) custom-call(s32[2]{0:T(128)S(1)} %pad_add_fusion.me_ref, bf16[1024,1024]{1,0:T(8,128)(2,1)S(1)} %copy-done.5, f32[1024,1024]{1,0:T(8,128)S(1)} %inner.1.raw_ref, f32[4,1024,128]{2,1,0:T(8,128)S(1)} %get-tuple-element.28.entering_ref, ...), custom_call_target="tpu_custom_call" | custom-call | flops 536870912 | bytes 10485760 | tf_op jit(solution)/shard_map/finish/pallas_call | solution.py:248
  59.3 0.1 collective-permute-start.22
  59.4 4.1 %collective-permute-done.22.other_ref = bf16[1024,1024]{1,0:T(8,128)(2,1)S(1)} collective-permute-done((bf16[1024,1024]{1,0:T(8,128)(2,1)S(1)}, bf16[1024,1024]{1,0:T(8,128)(2,1)S(1)}, u32[]{:S(2)}, u32[]{:S(2)}) %collective-permute-start.22) | collective-permute-done | bytes 2097184 | tf_op jit(solution)/shard_map/ppermute | solution.py:408
  63.5 2.6 %gram.5 = (f32[4,128,384]{2,1,0:T(8,128)S(1)}, bf16[4,128,384]{2,1,0:T(8,128)(2,1)S(1)}) custom-call(s32[2]{0:T(128)S(1)} %pad_add_fusion.me_ref, bf16[1024,1024]{1,0:T(8,128)(2,1)S(1)} %get-tuple-element.47.own_ref, bf16[1024,1024]{1,0:T(8,128)(2,1)S(1)} %collective-permute-done.22.other_ref), custom_call_target="tpu_custom_call" | custom-call | flops 805306368 | bytes 4194304 | tf_op jit(solution)/shard_map/gram/pallas_call | solution.py:319
  66.1 1.3 collective-permute-start.31
  67.4 2.9 %collective-permute-start.16 = (f32[3,1024]{1,0:T(4,128)S(1)}, f32[3,1024]{1,0:T(4,128)S(1)}, u32[]{:S(2)}, u32[]{:S(2)}) collective-permute-start(f32[3,1024]{1,0:T(4,128)S(1)} %get-tuple-element.76), channel_id=1, source_target_pairs={{0,12},{4,8},{8,4},{12,0},{16,28},{20,24},{24,20},{28,16},{1,13},{... | collective-permute-start | bytes 36872 | tf_op jit(solution)/shard_map/ppermute | solution.py:405
  70.3 3.2 %collective-permute-start.18 = (f32[3,1024]{1,0:T(4,128)S(1)}, f32[3,1024]{1,0:T(4,128)S(1)}, u32[]{:S(2)}, u32[]{:S(2)}) collective-permute-start(f32[3,1024]{1,0:T(4,128)S(1)} %get-tuple-element.76), channel_id=1, source_target_pairs={{0,20},{4,16},{8,28},{12,24},{16,4},{20,0},{24,12},{28,8},{1,21},{... | collective-permute-start | bytes 36872 | tf_op jit(solution)/shard_map/ppermute | solution.py:405
  73.5 1.6 %collective-permute-start.19 = (f32[3,1024]{1,0:T(4,128)S(1)}, f32[3,1024]{1,0:T(4,128)S(1)}, u32[]{:S(2)}, u32[]{:S(2)}) collective-permute-start(f32[3,1024]{1,0:T(4,128)S(1)} %get-tuple-element.76), channel_id=1, source_target_pairs={{0,24},{4,28},{8,16},{12,20},{16,8},{20,12},{24,0},{28,4},{1,25},{... | collective-permute-start | bytes 36872 | tf_op jit(solution)/shard_map/ppermute | solution.py:405
  75.1 1.3 collective-permute-start.14
  76.4 2.5 %collective-permute-start.20 = (f32[3,1024]{1,0:T(4,128)S(1)}, f32[3,1024]{1,0:T(4,128)S(1)}, u32[]{:S(2)}, u32[]{:S(2)}) collective-permute-start(f32[3,1024]{1,0:T(4,128)S(1)} %get-tuple-element.76), channel_id=1, source_target_pairs={{0,28},{4,24},{8,20},{12,16},{16,12},{20,8},{24,4},{28,0},{1,29},{... | collective-permute-start | bytes 36872 | tf_op jit(solution)/shard_map/ppermute | solution.py:405
  78.9 0.2 collective-permute-done.19
  79.2 0.9 collective-permute-done.15
  80.1 2.8 %collective-permute-done.20 = f32[3,1024]{1,0:T(4,128)S(1)} collective-permute-done((f32[3,1024]{1,0:T(4,128)S(1)}, f32[3,1024]{1,0:T(4,128)S(1)}, u32[]{:S(2)}, u32[]{:S(2)}) %collective-permute-start.20) | collective-permute-done | bytes 12320 | tf_op jit(solution)/shard_map/ppermute | solution.py:405
  82.9 0.2 stack.47
  83.1 1.6 %copy-done.1 = bf16[1024,1024]{1,0:T(8,128)(2,1)S(1)} copy-done((bf16[1024,1024]{1,0:T(8,128)(2,1)S(1)}, bf16[1024,1024]{1,0:T(8,128)(2,1)}, u32[]{:S(2)}) %copy-start.1) | copy-done | bytes 2097176
  84.7 2.6 %gram.4 = (f32[4,128,384]{2,1,0:T(8,128)S(1)}, bf16[4,128,384]{2,1,0:T(8,128)(2,1)S(1)}) custom-call(s32[2]{0:T(128)S(1)} %pad_add_fusion.me_ref, bf16[1024,1024]{1,0:T(8,128)(2,1)S(1)} %get-tuple-element.47.own_ref, bf16[1024,1024]{1,0:T(8,128)(2,1)S(1)} %copy-done.1), custom_call_target="tpu_custom_call" | custom-call | flops 805306368 | bytes 4194304 | tf_op jit(solution)/shard_map/gram/pallas_call | solution.py:319
  87.3 0.8 collective-permute-start.27
  88.1 2.8 %gram.3 = (f32[4,128,384]{2,1,0:T(8,128)S(1)}, bf16[4,128,384]{2,1,0:T(8,128)(2,1)S(1)}) custom-call(s32[2]{0:T(128)S(1)} %pad_add_fusion.me_ref, bf16[1024,1024]{1,0:T(8,128)(2,1)S(1)} %get-tuple-element.47.own_ref, bf16[1024,1024]{1,0:T(8,128)(2,1)S(1)} %copy-done.1), custom_call_target="tpu_custom_call" | custom-call | flops 805306368 | bytes 4194304 | tf_op jit(solution)/shard_map/gram/pallas_call | solution.py:319
  90.9 1.3 collective-permute-start.23
  92.2 1.1 convert_add_fusion
  93.3 0.2 collective-permute-start.32
  93.5 2.6 %collective-permute-start.33 = (bf16[128,384]{1,0:T(8,128)(2,1)S(1)}, bf16[128,384]{1,0:T(8,128)(2,1)S(1)}, u32[]{:S(2)}, u32[]{:S(2)}) collective-permute-start(bf16[128,384]{1,0:T(8,128)(2,1)S(1)} %get-tuple-element.62), channel_id=1, source_target_pairs={{0,16},{4,20},{8,24},{12,28},{16,0},{20,4},{24,8},{28,12},{1,17},{... | collective-permute-start | bytes 294920 | tf_op jit(solution)/shard_map/ppermute | solution.py:405
  96.1 3.2 %collective-permute-done.27 = bf16[4,128,384]{2,1,0:T(8,128)(2,1)S(1)} collective-permute-done((bf16[4,128,384]{2,1,0:T(8,128)(2,1)S(1)}, bf16[4,128,384]{2,1,0:T(8,128)(2,1)S(1)}, u32[]{:S(2)}, u32[]{:S(2)}) %collective-permute-start.27) | collective-permute-done | bytes 393248 | tf_op jit(solution)/shard_map/ppermute | solution.py:405
  99.3 2.2 %collective-permute-start.34 = (bf16[128,384]{1,0:T(8,128)(2,1)S(1)}, bf16[128,384]{1,0:T(8,128)(2,1)S(1)}, u32[]{:S(2)}, u32[]{:S(2)}) collective-permute-start(bf16[128,384]{1,0:T(8,128)(2,1)S(1)} %get-tuple-element.61), channel_id=1, source_target_pairs={{0,24},{4,28},{8,16},{12,20},{16,8},{20,12},{24,0},{28,4},{1,25},{... | collective-permute-start | bytes 294920 | tf_op jit(solution)/shard_map/ppermute | solution.py:405
  101.6 5.7 %collective-permute-done.23 = bf16[4,128,384]{2,1,0:T(8,128)(2,1)S(1)} collective-permute-done((bf16[4,128,384]{2,1,0:T(8,128)(2,1)S(1)}, bf16[4,128,384]{2,1,0:T(8,128)(2,1)S(1)}, u32[]{:S(2)}, u32[]{:S(2)}) %collective-permute-start.23) | collective-permute-done | bytes 393248 | tf_op jit(solution)/shard_map/ppermute | solution.py:405
  107.3 0.2 collective-permute-start.28
  107.5 0.1 convert_add_fusion.2
  107.6 2.6 %collective-permute-start.29 = (bf16[128,384]{1,0:T(8,128)(2,1)S(1)}, bf16[128,384]{1,0:T(8,128)(2,1)S(1)}, u32[]{:S(2)}, u32[]{:S(2)}) collective-permute-start(bf16[128,384]{1,0:T(8,128)(2,1)S(1)} %get-tuple-element.65), channel_id=1, source_target_pairs={{0,16},{4,20},{8,24},{12,28},{16,0},{20,4},{24,8},{28,12},{1,17},{... | collective-permute-start | bytes 294920 | tf_op jit(solution)/shard_map/ppermute | solution.py:405
  110.3 1.7 %collective-permute-start.30 = (bf16[128,384]{1,0:T(8,128)(2,1)S(1)}, bf16[128,384]{1,0:T(8,128)(2,1)S(1)}, u32[]{:S(2)}, u32[]{:S(2)}) collective-permute-start(bf16[128,384]{1,0:T(8,128)(2,1)S(1)} %get-tuple-element.64), channel_id=1, source_target_pairs={{0,24},{4,28},{8,16},{12,20},{16,8},{20,12},{24,0},{28,4},{1,25},{... | collective-permute-start | bytes 294920 | tf_op jit(solution)/shard_map/ppermute | solution.py:405
  112.0 0.9 collective-permute-done.28
  112.9 1.9 %collective-permute-start.25 = (bf16[128,384]{1,0:T(8,128)(2,1)S(1)}, bf16[128,384]{1,0:T(8,128)(2,1)S(1)}, u32[]{:S(2)}, u32[]{:S(2)}) collective-permute-start(bf16[128,384]{1,0:T(8,128)(2,1)S(1)} %get-tuple-element.68), channel_id=1, source_target_pairs={{0,16},{4,20},{8,24},{12,28},{16,0},{20,4},{24,8},{28,12},{1,17},{... | collective-permute-start | bytes 294920 | tf_op jit(solution)/shard_map/ppermute | solution.py:405
  114.8 4.5 %collective-permute-done.29 = bf16[128,384]{1,0:T(8,128)(2,1)S(1)} collective-permute-done((bf16[128,384]{1,0:T(8,128)(2,1)S(1)}, bf16[128,384]{1,0:T(8,128)(2,1)S(1)}, u32[]{:S(2)}, u32[]{:S(2)}) %collective-permute-start.29) | collective-permute-done | bytes 98336 | tf_op jit(solution)/shard_map/ppermute | solution.py:405
  119.3 2.3 %collective-permute-start.26 = (bf16[128,384]{1,0:T(8,128)(2,1)S(1)}, bf16[128,384]{1,0:T(8,128)(2,1)S(1)}, u32[]{:S(2)}, u32[]{:S(2)}) collective-permute-start(bf16[128,384]{1,0:T(8,128)(2,1)S(1)} %get-tuple-element.67), channel_id=1, source_target_pairs={{0,24},{4,28},{8,16},{12,20},{16,8},{20,12},{24,0},{28,4},{1,25},{... | collective-permute-start | bytes 294920 | tf_op jit(solution)/shard_map/ppermute | solution.py:405
  121.6 1.6 %collective-permute-start.41 = (bf16[128,128]{1,0:T(8,128)(2,1)S(1)}, bf16[128,128]{1,0:T(8,128)(2,1)S(1)}, u32[]{:S(2)}, u32[]{:S(2)}) collective-permute-start(bf16[128,128]{1,0:T(8,128)(2,1)S(1)} %slice.66), channel_id=1, source_target_pairs={{0,28},{1,29},{2,30},{3,31},{4,1},{5,0},{6,3},{7,2},{8,5},{9,4},{1... | collective-permute-start | bytes 98312 | tf_op jit(solution)/shard_map/ppermute | solution.py:421
  123.3 2.1 %collective-permute-start.38 = (bf16[128,128]{1,0:T(8,128)(2,1)S(1)}, bf16[128,128]{1,0:T(8,128)(2,1)S(1)}, u32[]{:S(2)}, u32[]{:S(2)}) collective-permute-start(bf16[128,128]{1,0:T(8,128)(2,1)S(1)} %get-tuple-element.71), channel_id=1, source_target_pairs={{0,16},{1,17},{2,18},{3,19},{4,20},{5,21},{6,22},{7,23},{8,24},{9,... | collective-permute-start | bytes 98312 | tf_op jit(solution)/shard_map/ppermute | solution.py:421
  125.4 1.1 collective-permute-done.25
  126.6 2.9 %collective-permute-start.40 = (bf16[128,128]{1,0:T(8,128)(2,1)S(1)}, bf16[128,128]{1,0:T(8,128)(2,1)S(1)}, u32[]{:S(2)}, u32[]{:S(2)}) collective-permute-start(bf16[128,128]{1,0:T(8,128)(2,1)S(1)} %get-tuple-element.69), channel_id=1, source_target_pairs={{0,24},{1,25},{2,26},{3,27},{4,28},{5,29},{6,30},{7,31},{8,1},{9,0... | collective-permute-start | bytes 98312 | tf_op jit(solution)/shard_map/ppermute | solution.py:421
  129.5 1.5 %collective-permute-start.35 = (bf16[128,128]{1,0:T(8,128)(2,1)S(1)}, bf16[128,128]{1,0:T(8,128)(2,1)S(1)}, u32[]{:S(2)}, u32[]{:S(2)}) collective-permute-start(bf16[128,128]{1,0:T(8,128)(2,1)S(1)} %get-tuple-element.74), channel_id=1, source_target_pairs={{0,4},{1,5},{2,6},{3,7},{4,8},{5,9},{6,10},{7,11},{8,12},{9,13},{1... | collective-permute-start | bytes 98312 | tf_op jit(solution)/shard_map/ppermute | solution.py:421
  131.0 2.0 %collective-permute-start.37 = (bf16[128,128]{1,0:T(8,128)(2,1)S(1)}, bf16[128,128]{1,0:T(8,128)(2,1)S(1)}, u32[]{:S(2)}, u32[]{:S(2)}) collective-permute-start(bf16[128,128]{1,0:T(8,128)(2,1)S(1)} %get-tuple-element.72), channel_id=1, source_target_pairs={{0,12},{1,13},{2,14},{3,15},{4,16},{5,17},{6,18},{7,19},{8,20},{9,... | collective-permute-start | bytes 98312 | tf_op jit(solution)/shard_map/ppermute | solution.py:421
  133.0 0.6 add_multiply_fusion
  133.6 2.0 %collective-permute-done.35.refs_3_ = bf16[128,128]{1,0:T(8,128)(2,1)S(1)} collective-permute-done((bf16[128,128]{1,0:T(8,128)(2,1)S(1)}, bf16[128,128]{1,0:T(8,128)(2,1)S(1)}, u32[]{:S(2)}, u32[]{:S(2)}) %collective-permute-start.35) | collective-permute-done | bytes 32800 | tf_op jit(solution)/shard_map/ppermute | solution.py:421
  135.6 0.6 collective-permute-done.36.refs_4_
  136.2 0.5 collective-permute-done.37.refs_5_
  136.7 2.8 %cover.1 = f32[128,2048]{1,0:T(8,128)} custom-call(s32[2]{0:T(128)S(1)} %pad_add_fusion.me_ref, f32[8,1024]{1,0:T(8,128)S(1)} %get-tuple-element.75.means_ref, f32[8,1024]{1,0:T(8,128)S(1)} %collective-permute-done.21.others_ref, f32[128,384]{1,0:T(8,128)S(1)} %get-tuple-element.59.refs_0_, f32[128,384]{1,0:T(8,128)S(1)} %get-tuple-element.57.refs_1_, ...), custom_call_target="tpu_custom_call" | custom-call | tf_op jit(solution)/shard_map/cover/pallas_call | solution.py:381
  (71 shorter events, 0.8 us)
Async XLA Ops:
  0.7 1.6 %copy-start.2 = (bf16[1024,1024]{1,0:T(8,128)(2,1)S(1)}, bf16[1024,1024]{1,0:T(8,128)(2,1)}, u32[]{:S(2)}) copy-start(bf16[1024,1024]{1,0:T(8,128)(2,1)} %k_ref.3) | copy-start | bytes 6291460
  2.3 1.6 %copy-start.4 = (bf16[1024,1024]{1,0:T(8,128)(2,1)S(1)}, bf16[1024,1024]{1,0:T(8,128)(2,1)}, u32[]{:S(2)}) copy-start(bf16[1024,1024]{1,0:T(8,128)(2,1)} %v_ref.3) | copy-start | bytes 6291460
  3.9 0.8 copy-start.6
  4.7 38.1 %copy-start.3 = (bf16[1024,1024]{1,0:T(8,128)(2,1)S(1)}, bf16[1024,1024]{1,0:T(8,128)(2,1)}, u32[]{:S(2)}) copy-start(bf16[1024,1024]{1,0:T(8,128)(2,1)} %k_ref.3) | copy-start | bytes 6291460
  4.7 38.1 %copy-start.5 = (bf16[1024,1024]{1,0:T(8,128)(2,1)S(1)}, bf16[1024,1024]{1,0:T(8,128)(2,1)}, u32[]{:S(2)}) copy-start(bf16[1024,1024]{1,0:T(8,128)(2,1)} %q_ref.3) | copy-start | bytes 6291460
  9.2 8.9 %collective-permute-start = (f32[136,128]{1,0:T(8,128)S(1)}, f32[136,128]{1,0:T(8,128)S(1)}, u32[]{:S(2)}, u32[]{:S(2)}) collective-permute-start(f32[136,128]{1,0:T(8,128)S(1)} %get-tuple-element.31), channel_id=1, source_target_pairs={{0,4},{4,0},{8,12},{12,8},{16,20},{20,16},{24,28},{28,24},{1,5},{5... | collective-permute-start | bytes 208904 | tf_op jit(solution)/shard_map/ppermute | solution.py:405
  12.2 9.5 %collective-permute-start.1 = (f32[136,128]{1,0:T(8,128)S(1)}, f32[136,128]{1,0:T(8,128)S(1)}, u32[]{:S(2)}, u32[]{:S(2)}) collective-permute-start(f32[136,128]{1,0:T(8,128)S(1)} %get-tuple-element.32), channel_id=1, source_target_pairs={{0,8},{4,12},{8,0},{12,4},{16,24},{20,28},{24,16},{28,20},{1,9},{5... | collective-permute-start | bytes 208904 | tf_op jit(solution)/shard_map/ppermute | solution.py:405
  13.8 7.9 %collective-permute-start.2 = (f32[136,128]{1,0:T(8,128)S(1)}, f32[136,128]{1,0:T(8,128)S(1)}, u32[]{:S(2)}, u32[]{:S(2)}) collective-permute-start(f32[136,128]{1,0:T(8,128)S(1)} %get-tuple-element.33), channel_id=1, source_target_pairs={{0,12},{4,8},{8,4},{12,0},{16,28},{20,24},{24,20},{28,16},{1,13},{... | collective-permute-start | bytes 208904 | tf_op jit(solution)/shard_map/ppermute | solution.py:405
  13.8 7.9 %collective-permute-start.3 = (f32[136,128]{1,0:T(8,128)S(1)}, f32[136,128]{1,0:T(8,128)S(1)}, u32[]{:S(2)}, u32[]{:S(2)}) collective-permute-start(f32[136,128]{1,0:T(8,128)S(1)} %get-tuple-element.34), channel_id=1, source_target_pairs={{0,16},{4,20},{8,24},{12,28},{16,0},{20,4},{24,8},{28,12},{1,17},{... | collective-permute-start | bytes 208904 | tf_op jit(solution)/shard_map/ppermute | solution.py:405
  16.7 10.7 %collective-permute-start.4 = (f32[136,128]{1,0:T(8,128)S(1)}, f32[136,128]{1,0:T(8,128)S(1)}, u32[]{:S(2)}, u32[]{:S(2)}) collective-permute-start(f32[136,128]{1,0:T(8,128)S(1)} %get-tuple-element.35), channel_id=1, source_target_pairs={{0,20},{4,16},{8,28},{12,24},{16,4},{20,0},{24,12},{28,8},{1,21},{... | collective-permute-start | bytes 208904 | tf_op jit(solution)/shard_map/ppermute | solution.py:405
  18.0 9.4 %collective-permute-start.5 = (f32[136,128]{1,0:T(8,128)S(1)}, f32[136,128]{1,0:T(8,128)S(1)}, u32[]{:S(2)}, u32[]{:S(2)}) collective-permute-start(f32[136,128]{1,0:T(8,128)S(1)} %get-tuple-element.36), channel_id=1, source_target_pairs={{0,24},{4,28},{8,16},{12,20},{16,8},{20,12},{24,0},{28,4},{1,25},{... | collective-permute-start | bytes 208904 | tf_op jit(solution)/shard_map/ppermute | solution.py:405
  21.6 7.1 %collective-permute-start.6 = (f32[136,128]{1,0:T(8,128)S(1)}, f32[136,128]{1,0:T(8,128)S(1)}, u32[]{:S(2)}, u32[]{:S(2)}) collective-permute-start(f32[136,128]{1,0:T(8,128)S(1)} %get-tuple-element.37), channel_id=1, source_target_pairs={{0,28},{4,24},{8,20},{12,16},{16,12},{20,8},{24,4},{28,0},{1,29},{... | collective-permute-start | bytes 208904 | tf_op jit(solution)/shard_map/ppermute | solution.py:405
  29.4 11.0 %collective-permute-start.10 = (f32[128,128]{1,0:T(8,128)S(1)}, f32[128,128]{1,0:T(8,128)S(1)}, u32[]{:S(2)}, u32[]{:S(2)}) collective-permute-start(f32[128,128]{1,0:T(8,128)S(1)} %get-tuple-element.42), channel_id=1, source_target_pairs={{0,16},{4,20},{8,24},{12,28},{16,0},{20,4},{24,8},{28,12},{1,17},{... | collective-permute-start | bytes 196616 | tf_op jit(solution)/shard_map/ppermute | solution.py:405
  32.9 9.8 %collective-permute-start.11 = (f32[128,128]{1,0:T(8,128)S(1)}, f32[128,128]{1,0:T(8,128)S(1)}, u32[]{:S(2)}, u32[]{:S(2)}) collective-permute-start(f32[128,128]{1,0:T(8,128)S(1)} %get-tuple-element.43), channel_id=1, source_target_pairs={{0,20},{4,16},{8,28},{12,24},{16,4},{20,0},{24,12},{28,8},{1,21},{... | collective-permute-start | bytes 196616 | tf_op jit(solution)/shard_map/ppermute | solution.py:405
  32.9 18.3 %collective-permute-start.12 = (f32[128,128]{1,0:T(8,128)S(1)}, f32[128,128]{1,0:T(8,128)S(1)}, u32[]{:S(2)}, u32[]{:S(2)}) collective-permute-start(f32[128,128]{1,0:T(8,128)S(1)} %get-tuple-element.44), channel_id=1, source_target_pairs={{0,24},{4,28},{8,16},{12,20},{16,8},{20,12},{24,0},{28,4},{1,25},{... | collective-permute-start | bytes 196616 | tf_op jit(solution)/shard_map/ppermute | solution.py:405
  34.4 16.8 %collective-permute-start.13 = (f32[128,128]{1,0:T(8,128)S(1)}, f32[128,128]{1,0:T(8,128)S(1)}, u32[]{:S(2)}, u32[]{:S(2)}) collective-permute-start(f32[128,128]{1,0:T(8,128)S(1)} %get-tuple-element.45), channel_id=1, source_target_pairs={{0,28},{4,24},{8,20},{12,16},{16,12},{20,8},{24,4},{28,0},{1,29},{... | collective-permute-start | bytes 196616 | tf_op jit(solution)/shard_map/ppermute | solution.py:405
  37.7 13.5 %collective-permute-start.7 = (f32[128,128]{1,0:T(8,128)S(1)}, f32[128,128]{1,0:T(8,128)S(1)}, u32[]{:S(2)}, u32[]{:S(2)}) collective-permute-start(f32[128,128]{1,0:T(8,128)S(1)} %get-tuple-element.39), channel_id=1, source_target_pairs={{0,4},{4,0},{8,12},{12,8},{16,20},{20,16},{24,28},{28,24},{1,5},{5... | collective-permute-start | bytes 196616 | tf_op jit(solution)/shard_map/ppermute | solution.py:405
  40.4 10.8 %collective-permute-start.8 = (f32[128,128]{1,0:T(8,128)S(1)}, f32[128,128]{1,0:T(8,128)S(1)}, u32[]{:S(2)}, u32[]{:S(2)}) collective-permute-start(f32[128,128]{1,0:T(8,128)S(1)} %get-tuple-element.40), channel_id=1, source_target_pairs={{0,8},{4,12},{8,0},{12,4},{16,24},{20,28},{24,16},{28,20},{1,9},{5... | collective-permute-start | bytes 196616 | tf_op jit(solution)/shard_map/ppermute | solution.py:405
  42.7 8.5 %copy-start.7 = (f32[8,1024]{1,0:T(8,128)S(1)}, f32[8,1024]{1,0:T(8,128)}, u32[]{:S(2)}) copy-start(f32[8,1024]{1,0:T(8,128)} %decay_ref.5) | copy-start | bytes 98308
  42.7 8.6 %copy-start.8 = (f32[1024]{0:T(1024)S(1)}, f32[1024]{0:T(1024)}, u32[]{:S(2)}) copy-start(f32[1024]{0:T(1024)} %param.9) | copy-start | bytes 12292
  42.7 8.5 %collective-permute-start.9 = (f32[128,128]{1,0:T(8,128)S(1)}, f32[128,128]{1,0:T(8,128)S(1)}, u32[]{:S(2)}, u32[]{:S(2)}) collective-permute-start(f32[128,128]{1,0:T(8,128)S(1)} %get-tuple-element.41), channel_id=1, source_target_pairs={{0,12},{4,8},{8,4},{12,0},{16,28},{20,24},{24,20},{28,16},{1,13},{... | collective-permute-start | bytes 196616 | tf_op jit(solution)/shard_map/ppermute | solution.py:405
  59.3 4.2 %collective-permute-start.22 = (bf16[1024,1024]{1,0:T(8,128)(2,1)S(1)}, bf16[1024,1024]{1,0:T(8,128)(2,1)S(1)}, u32[]{:S(2)}, u32[]{:S(2)}) collective-permute-start(bf16[1024,1024]{1,0:T(8,128)(2,1)S(1)} %get-tuple-element.47.own_ref), channel_id=1, source_target_pairs={{0,1},{1,0},{2,3},{3,2},{4,5},{5,4},{6,7},{7,6},{8,9},{9,8},{10,11... | collective-permute-start | bytes 6291464 | tf_op jit(solution)/shard_map/ppermute | solution.py:408
  63.5 2.6 %copy-start = (bf16[1024,1024]{1,0:T(8,128)(2,1)}, bf16[1024,1024]{1,0:T(8,128)(2,1)S(1)}, u32[]{:S(2)}) copy-start(bf16[1024,1024]{1,0:T(8,128)(2,1)S(1)} %collective-permute-done.22.other_ref) | copy-start | bytes 6291460
  66.1 26.1 %collective-permute-start.31 = (bf16[4,128,384]{2,1,0:T(8,128)(2,1)S(1)}, bf16[4,128,384]{2,1,0:T(8,128)(2,1)}, u32[]{:S(2)}, u32[]{:S(2)}) collective-permute-start(bf16[4,128,384]{2,1,0:T(8,128)(2,1)S(1)} %get-tuple-element.53), channel_id=1, source_target_pairs={{0,4},{4,0},{8,12},{12,8},{16,20},{20,16},{24,28},{28,24},{1,5},{5... | collective-permute-start | bytes 1179656 | tf_op jit(solution)/shard_map/ppermute | solution.py:405
  67.4 7.7 %collective-permute-start.16 = (f32[3,1024]{1,0:T(4,128)S(1)}, f32[3,1024]{1,0:T(4,128)S(1)}, u32[]{:S(2)}, u32[]{:S(2)}) collective-permute-start(f32[3,1024]{1,0:T(4,128)S(1)} %get-tuple-element.76), channel_id=1, source_target_pairs={{0,12},{4,8},{8,4},{12,0},{16,28},{20,24},{24,20},{28,16},{1,13},{... | collective-permute-start | bytes 36872 | tf_op jit(solution)/shard_map/ppermute | solution.py:405
  70.3 6.1 %collective-permute-start.17 = (f32[3,1024]{1,0:T(4,128)S(1)}, f32[3,1024]{1,0:T(4,128)S(1)}, u32[]{:S(2)}, u32[]{:S(2)}) collective-permute-start(f32[3,1024]{1,0:T(4,128)S(1)} %get-tuple-element.76), channel_id=1, source_target_pairs={{0,16},{4,20},{8,24},{12,28},{16,0},{20,4},{24,8},{28,12},{1,17},{... | collective-permute-start | bytes 36872 | tf_op jit(solution)/shard_map/ppermute | solution.py:405
  70.3 6.1 %collective-permute-start.18 = (f32[3,1024]{1,0:T(4,128)S(1)}, f32[3,1024]{1,0:T(4,128)S(1)}, u32[]{:S(2)}, u32[]{:S(2)}) collective-permute-start(f32[3,1024]{1,0:T(4,128)S(1)} %get-tuple-element.76), channel_id=1, source_target_pairs={{0,20},{4,16},{8,28},{12,24},{16,4},{20,0},{24,12},{28,8},{1,21},{... | collective-permute-start | bytes 36872 | tf_op jit(solution)/shard_map/ppermute | solution.py:405
  73.5 5.6 %collective-permute-start.19 = (f32[3,1024]{1,0:T(4,128)S(1)}, f32[3,1024]{1,0:T(4,128)S(1)}, u32[]{:S(2)}, u32[]{:S(2)}) collective-permute-start(f32[3,1024]{1,0:T(4,128)S(1)} %get-tuple-element.76), channel_id=1, source_target_pairs={{0,24},{4,28},{8,16},{12,20},{16,8},{20,12},{24,0},{28,4},{1,25},{... | collective-permute-start | bytes 36872 | tf_op jit(solution)/shard_map/ppermute | solution.py:405
  75.1 4.1 %collective-permute-start.14 = (f32[3,1024]{1,0:T(4,128)S(1)}, f32[3,1024]{1,0:T(4,128)S(1)}, u32[]{:S(2)}, u32[]{:S(2)}) collective-permute-start(f32[3,1024]{1,0:T(4,128)S(1)} %get-tuple-element.76), channel_id=1, source_target_pairs={{0,4},{4,0},{8,12},{12,8},{16,20},{20,16},{24,28},{28,24},{1,5},{5... | collective-permute-start | bytes 36872 | tf_op jit(solution)/shard_map/ppermute | solution.py:405
  76.3 3.7 %collective-permute-start.15 = (f32[3,1024]{1,0:T(4,128)S(1)}, f32[3,1024]{1,0:T(4,128)S(1)}, u32[]{:S(2)}, u32[]{:S(2)}) collective-permute-start(f32[3,1024]{1,0:T(4,128)S(1)} %get-tuple-element.76), channel_id=1, source_target_pairs={{0,8},{4,12},{8,0},{12,4},{16,24},{20,28},{24,16},{28,20},{1,9},{5... | collective-permute-start | bytes 36872 | tf_op jit(solution)/shard_map/ppermute | solution.py:405
  76.4 6.5 %collective-permute-start.20 = (f32[3,1024]{1,0:T(4,128)S(1)}, f32[3,1024]{1,0:T(4,128)S(1)}, u32[]{:S(2)}, u32[]{:S(2)}) collective-permute-start(f32[3,1024]{1,0:T(4,128)S(1)} %get-tuple-element.76), channel_id=1, source_target_pairs={{0,28},{4,24},{8,20},{12,16},{16,12},{20,8},{24,4},{28,0},{1,29},{... | collective-permute-start | bytes 36872 | tf_op jit(solution)/shard_map/ppermute | solution.py:405
  83.1 46.4 %collective-permute-start.21 = (f32[8,1024]{1,0:T(8,128)S(1)}, f32[8,1024]{1,0:T(8,128)S(1)}, u32[]{:S(2)}, u32[]{:S(2)}) collective-permute-start(f32[8,1024]{1,0:T(8,128)S(1)} %get-tuple-element.75.means_ref), channel_id=1, source_target_pairs={{0,1},{1,0},{2,3},{3,2},{4,5},{5,4},{6,7},{7,6},{8,9},{9,8},{10,11... | collective-permute-start | bytes 98312 | tf_op jit(solution)/shard_map/ppermute | solution.py:408
  83.1 1.6 %copy-start.1 = (bf16[1024,1024]{1,0:T(8,128)(2,1)S(1)}, bf16[1024,1024]{1,0:T(8,128)(2,1)}, u32[]{:S(2)}) copy-start(bf16[1024,1024]{1,0:T(8,128)(2,1)} %copy-done) | copy-start | bytes 6291460
  87.3 12.0 %collective-permute-start.27 = (bf16[4,128,384]{2,1,0:T(8,128)(2,1)S(1)}, bf16[4,128,384]{2,1,0:T(8,128)(2,1)S(1)}, u32[]{:S(2)}, u32[]{:S(2)}) collective-permute-start(bf16[4,128,384]{2,1,0:T(8,128)(2,1)S(1)} %get-tuple-element.51), channel_id=1, source_target_pairs={{0,4},{4,0},{8,12},{12,8},{16,20},{20,16},{24,28},{28,24},{1,5},{5... | collective-permute-start | bytes 1179656 | tf_op jit(solution)/shard_map/ppermute | solution.py:405
  90.9 16.4 %collective-permute-start.23 = (bf16[4,128,384]{2,1,0:T(8,128)(2,1)S(1)}, bf16[4,128,384]{2,1,0:T(8,128)(2,1)S(1)}, u32[]{:S(2)}, u32[]{:S(2)}) collective-permute-start(bf16[4,128,384]{2,1,0:T(8,128)(2,1)S(1)} %get-tuple-element.49), channel_id=1, source_target_pairs={{0,4},{4,0},{8,12},{12,8},{16,20},{20,16},{24,28},{28,24},{1,5},{5... | collective-permute-start | bytes 1179656 | tf_op jit(solution)/shard_map/ppermute | solution.py:405
  93.3 14.3 %collective-permute-start.32 = (bf16[128,384]{1,0:T(8,128)(2,1)S(1)}, bf16[128,384]{1,0:T(8,128)(2,1)S(1)}, u32[]{:S(2)}, u32[]{:S(2)}) collective-permute-start(bf16[128,384]{1,0:T(8,128)(2,1)S(1)} %get-tuple-element.60), channel_id=1, source_target_pairs={{0,8},{4,12},{8,0},{12,4},{16,24},{20,28},{24,16},{28,20},{1,9},{5... | collective-permute-start | bytes 294920 | tf_op jit(solution)/shard_map/ppermute | solution.py:405
  93.5 16.7 %collective-permute-start.33 = (bf16[128,384]{1,0:T(8,128)(2,1)S(1)}, bf16[128,384]{1,0:T(8,128)(2,1)S(1)}, u32[]{:S(2)}, u32[]{:S(2)}) collective-permute-start(bf16[128,384]{1,0:T(8,128)(2,1)S(1)} %get-tuple-element.62), channel_id=1, source_target_pairs={{0,16},{4,20},{8,24},{12,28},{16,0},{20,4},{24,8},{28,12},{1,17},{... | collective-permute-start | bytes 294920 | tf_op jit(solution)/shard_map/ppermute | solution.py:405
  99.3 12.7 %collective-permute-start.34 = (bf16[128,384]{1,0:T(8,128)(2,1)S(1)}, bf16[128,384]{1,0:T(8,128)(2,1)S(1)}, u32[]{:S(2)}, u32[]{:S(2)}) collective-permute-start(bf16[128,384]{1,0:T(8,128)(2,1)S(1)} %get-tuple-element.61), channel_id=1, source_target_pairs={{0,24},{4,28},{8,16},{12,20},{16,8},{20,12},{24,0},{28,4},{1,25},{... | collective-permute-start | bytes 294920 | tf_op jit(solution)/shard_map/ppermute | solution.py:405
  107.3 5.6 %collective-permute-start.28 = (bf16[128,384]{1,0:T(8,128)(2,1)S(1)}, bf16[128,384]{1,0:T(8,128)(2,1)S(1)}, u32[]{:S(2)}, u32[]{:S(2)}) collective-permute-start(bf16[128,384]{1,0:T(8,128)(2,1)S(1)} %get-tuple-element.63), channel_id=1, source_target_pairs={{0,8},{4,12},{8,0},{12,4},{16,24},{20,28},{24,16},{28,20},{1,9},{5... | collective-permute-start | bytes 294920 | tf_op jit(solution)/shard_map/ppermute | solution.py:405
  107.6 11.6 %collective-permute-start.29 = (bf16[128,384]{1,0:T(8,128)(2,1)S(1)}, bf16[128,384]{1,0:T(8,128)(2,1)S(1)}, u32[]{:S(2)}, u32[]{:S(2)}) collective-permute-start(bf16[128,384]{1,0:T(8,128)(2,1)S(1)} %get-tuple-element.65), channel_id=1, source_target_pairs={{0,16},{4,20},{8,24},{12,28},{16,0},{20,4},{24,8},{28,12},{1,17},{... | collective-permute-start | bytes 294920 | tf_op jit(solution)/shard_map/ppermute | solution.py:405
  110.3 11.3 %collective-permute-start.30 = (bf16[128,384]{1,0:T(8,128)(2,1)S(1)}, bf16[128,384]{1,0:T(8,128)(2,1)S(1)}, u32[]{:S(2)}, u32[]{:S(2)}) collective-permute-start(bf16[128,384]{1,0:T(8,128)(2,1)S(1)} %get-tuple-element.64), channel_id=1, source_target_pairs={{0,24},{4,28},{8,16},{12,20},{16,8},{20,12},{24,0},{28,4},{1,25},{... | collective-permute-start | bytes 294920 | tf_op jit(solution)/shard_map/ppermute | solution.py:405
  111.9 11.4 %collective-permute-start.24 = (bf16[128,384]{1,0:T(8,128)(2,1)S(1)}, bf16[128,384]{1,0:T(8,128)(2,1)S(1)}, u32[]{:S(2)}, u32[]{:S(2)}) collective-permute-start(bf16[128,384]{1,0:T(8,128)(2,1)S(1)} %get-tuple-element.66), channel_id=1, source_target_pairs={{0,8},{4,12},{8,0},{12,4},{16,24},{20,28},{24,16},{28,20},{1,9},{5... | collective-permute-start | bytes 294920 | tf_op jit(solution)/shard_map/ppermute | solution.py:405
  112.9 13.6 %collective-permute-start.25 = (bf16[128,384]{1,0:T(8,128)(2,1)S(1)}, bf16[128,384]{1,0:T(8,128)(2,1)S(1)}, u32[]{:S(2)}, u32[]{:S(2)}) collective-permute-start(bf16[128,384]{1,0:T(8,128)(2,1)S(1)} %get-tuple-element.68), channel_id=1, source_target_pairs={{0,16},{4,20},{8,24},{12,28},{16,0},{20,4},{24,8},{28,12},{1,17},{... | collective-permute-start | bytes 294920 | tf_op jit(solution)/shard_map/ppermute | solution.py:405
  119.3 7.3 %collective-permute-start.26 = (bf16[128,384]{1,0:T(8,128)(2,1)S(1)}, bf16[128,384]{1,0:T(8,128)(2,1)S(1)}, u32[]{:S(2)}, u32[]{:S(2)}) collective-permute-start(bf16[128,384]{1,0:T(8,128)(2,1)S(1)} %get-tuple-element.67), channel_id=1, source_target_pairs={{0,24},{4,28},{8,16},{12,20},{16,8},{20,12},{24,0},{28,4},{1,25},{... | collective-permute-start | bytes 294920 | tf_op jit(solution)/shard_map/ppermute | solution.py:405
  121.6 9.5 %collective-permute-start.41 = (bf16[128,128]{1,0:T(8,128)(2,1)S(1)}, bf16[128,128]{1,0:T(8,128)(2,1)S(1)}, u32[]{:S(2)}, u32[]{:S(2)}) collective-permute-start(bf16[128,128]{1,0:T(8,128)(2,1)S(1)} %slice.66), channel_id=1, source_target_pairs={{0,28},{1,29},{2,30},{3,31},{4,1},{5,0},{6,3},{7,2},{8,5},{9,4},{1... | collective-permute-start | bytes 98312 | tf_op jit(solution)/shard_map/ppermute | solution.py:421
  123.3 7.7 %collective-permute-start.38 = (bf16[128,128]{1,0:T(8,128)(2,1)S(1)}, bf16[128,128]{1,0:T(8,128)(2,1)S(1)}, u32[]{:S(2)}, u32[]{:S(2)}) collective-permute-start(bf16[128,128]{1,0:T(8,128)(2,1)S(1)} %get-tuple-element.71), channel_id=1, source_target_pairs={{0,16},{1,17},{2,18},{3,19},{4,20},{5,21},{6,22},{7,23},{8,24},{9,... | collective-permute-start | bytes 98312 | tf_op jit(solution)/shard_map/ppermute | solution.py:421
  126.5 7.1 %collective-permute-start.39 = (bf16[128,128]{1,0:T(8,128)(2,1)S(1)}, bf16[128,128]{1,0:T(8,128)(2,1)S(1)}, u32[]{:S(2)}, u32[]{:S(2)}) collective-permute-start(bf16[128,128]{1,0:T(8,128)(2,1)S(1)} %get-tuple-element.70), channel_id=1, source_target_pairs={{0,20},{1,21},{2,22},{3,23},{4,24},{5,25},{6,26},{7,27},{8,28},{9,... | collective-permute-start | bytes 98312 | tf_op jit(solution)/shard_map/ppermute | solution.py:421
  126.6 7.1 %collective-permute-start.40 = (bf16[128,128]{1,0:T(8,128)(2,1)S(1)}, bf16[128,128]{1,0:T(8,128)(2,1)S(1)}, u32[]{:S(2)}, u32[]{:S(2)}) collective-permute-start(bf16[128,128]{1,0:T(8,128)(2,1)S(1)} %get-tuple-element.69), channel_id=1, source_target_pairs={{0,24},{1,25},{2,26},{3,27},{4,28},{5,29},{6,30},{7,31},{8,1},{9,0... | collective-permute-start | bytes 98312 | tf_op jit(solution)/shard_map/ppermute | solution.py:421
  129.5 6.1 %collective-permute-start.35 = (bf16[128,128]{1,0:T(8,128)(2,1)S(1)}, bf16[128,128]{1,0:T(8,128)(2,1)S(1)}, u32[]{:S(2)}, u32[]{:S(2)}) collective-permute-start(bf16[128,128]{1,0:T(8,128)(2,1)S(1)} %get-tuple-element.74), channel_id=1, source_target_pairs={{0,4},{1,5},{2,6},{3,7},{4,8},{5,9},{6,10},{7,11},{8,12},{9,13},{1... | collective-permute-start | bytes 98312 | tf_op jit(solution)/shard_map/ppermute | solution.py:421
  131.0 5.1 %collective-permute-start.36 = (bf16[128,128]{1,0:T(8,128)(2,1)S(1)}, bf16[128,128]{1,0:T(8,128)(2,1)S(1)}, u32[]{:S(2)}, u32[]{:S(2)}) collective-permute-start(bf16[128,128]{1,0:T(8,128)(2,1)S(1)} %get-tuple-element.73), channel_id=1, source_target_pairs={{0,8},{1,9},{2,10},{3,11},{4,12},{5,13},{6,14},{7,15},{8,16},{9,17... | collective-permute-start | bytes 98312 | tf_op jit(solution)/shard_map/ppermute | solution.py:421
  131.0 5.6 %collective-permute-start.37 = (bf16[128,128]{1,0:T(8,128)(2,1)S(1)}, bf16[128,128]{1,0:T(8,128)(2,1)S(1)}, u32[]{:S(2)}, u32[]{:S(2)}) collective-permute-start(bf16[128,128]{1,0:T(8,128)(2,1)S(1)} %get-tuple-element.72), channel_id=1, source_target_pairs={{0,12},{1,13},{2,14},{3,15},{4,16},{5,17},{6,18},{7,19},{8,20},{9,... | collective-permute-start | bytes 98312 | tf_op jit(solution)/shard_map/ppermute | solution.py:421

commit v2 on v1

v2 whole, which is shorter than its diff:
```python
import functools

import jax
import jax.numpy as jnp
from jax import lax
from jax.experimental import pallas as pl
from jax.experimental.pallas import tpu as pltpu
from jax.sharding import PartitionSpec as P

HEAD_DIM = 128
SPAN = 256
F32 = jnp.float32
BF16 = jnp.bfloat16
HIGHEST = lax.Precision.HIGHEST
MIB = 1 << 20


def params(limit_mib):
    return pltpu.CompilerParams(vmem_limit_bytes=limit_mib * MIB)


def cost(flops, moved, transcendentals=0):
    return pl.CostEstimate(
        flops=int(flops), bytes_accessed=int(moved), transcendentals=int(transcendentals)
    )


def whole(shape):
    return pl.BlockSpec(shape, lambda *_: (0,) * len(shape))


def anywhere():
    return pl.BlockSpec(memory_space=pl.ANY)


def vmem():
    return pl.BlockSpec(memory_space=pltpu.VMEM)


def struct(shape, dtype):
    return jax.ShapeDtypeStruct(shape, dtype)


def dot(a, b):
    return jnp.dot(a, b, preferred_element_type=F32)


def split(value):
    high = value.astype(BF16)
    return high, (value - high.astype(F32)).astype(BF16)


def running_sum(decay):
    rows = lax.broadcasted_iota(jnp.int32, (SPAN, SPAN), 0)
    columns = lax.broadcasted_iota(jnp.int32, (SPAN, SPAN), 1)
    ones = jnp.where(rows <= columns, 1.0, 0.0).astype(F32)
    return jnp.dot(decay, ones, precision=HIGHEST, preferred_element_type=F32)


def head_columns(head):
    return slice(head * HEAD_DIM, (head + 1) * HEAD_DIM)


def states_kernel(shards, k_ref, v_ref, decay_ref, entering_ref, before_ref, *rest):
    pieces, (state, total) = rest[:shards], rest[shards:]
    heads = decay_ref.shape[0]
    step = pl.program_id(0)

    @pl.when(step == 0)
    def _():
        state[...] = jnp.zeros_like(state)
        total[...] = jnp.ones_like(total)

    entering_ref[0] = state[...]
    before_ref[0] = total[...]
    cumul = running_sum(decay_ref[...])
    last = cumul[:, SPAN - 1 :]
    weight = jnp.exp(last - cumul)
    drop = jnp.exp(last)
    for group in range(0, heads, 4):
        members = range(group, min(group + 4, heads))
        turned = [k_ref[:, head_columns(head)].T for head in members]
        parts = []
        for head, key in zip(members, turned):
            high, low = split(key.astype(F32) * weight[head : head + 1, :])
            parts.append(jnp.concatenate([high, low], axis=0))
        updates = [dot(part, v_ref[:, head_columns(head)]) for head, part in zip(members, parts)]
        for head, update in zip(members, updates):
            cols = head_columns(head)
            update = update[:HEAD_DIM] + update[HEAD_DIM:]
            state[cols, :] = state[cols, :] * drop[head : head + 1, :] + update
    total[...] = total[...] * drop

    @pl.when(step == pl.num_programs(0) - 1)
    def _():
        mine = lax.axis_index("ctx")
        rows = heads * HEAD_DIM // shards
        for index in range(shards):
            start = pl.multiple_of((mine ^ index) * rows, rows)
            pieces[index][:rows, :] = state[pl.ds(start, rows), :]
            piece_total = total[pl.ds(start // HEAD_DIM, 1), :]
            pieces[index][rows:, :] = jnp.broadcast_to(piece_total, (8, HEAD_DIM))


def local_states(keys, values, log_decay, shards):
    count, width = keys.shape
    heads = width // HEAD_DIM
    blocks = count // SPAN
    rows = width // shards
    piece = (rows + 8, HEAD_DIM)
    shapes = [(blocks, width, HEAD_DIM), (blocks, heads, HEAD_DIM)] + [piece] * shards
    tokens = pl.BlockSpec((SPAN, width), lambda i: (i, 0))
    out = pl.pallas_call(
        functools.partial(states_kernel, shards),
        grid=(blocks,),
        in_specs=[tokens, tokens, pl.BlockSpec((heads, SPAN), lambda i: (0, i))],
        out_specs=[
            pl.BlockSpec((1, width, HEAD_DIM), lambda i: (i, 0, 0)),
            pl.BlockSpec((1, heads, HEAD_DIM), lambda i: (i, 0, 0)),
        ]
        + [whole(piece)] * shards,
        scratch_shapes=[pltpu.VMEM((width, HEAD_DIM), F32), pltpu.VMEM((heads, HEAD_DIM), F32)],
        out_shape=[struct(shape, F32) for shape in shapes],
        compiler_params=params(56),
        cost_estimate=cost(4 * count * width * HEAD_DIM, 4 * count * width),
        name="local_states",
    )(keys, values, log_decay)
    return out[0], out[1], out[2:]


def chain_kernel(shards, *refs):
    mine = lax.axis_index("ctx")
    arrived, refs = refs[:shards], refs[shards + 1 :]
    outs, (ordered, entering) = refs[:shards], refs[shards:]
    rows = outs[0].shape[0]
    for index in range(shards):
        ordered[mine ^ index] = arrived[index][...]
    carried = jnp.zeros((rows, HEAD_DIM), F32)
    for shard in range(shards):
        entering[shard] = carried
        carried = carried * ordered[shard, rows : rows + 1, :] + ordered[shard, :rows, :]
    for index in range(shards):
        outs[index][...] = entering[mine ^ index]


def chain(pieces, after):
    shards = len(pieces)
    rows = pieces[0].shape[0] - 8
    return pl.pallas_call(
        functools.partial(chain_kernel, shards),
        grid=(1,),
        in_specs=[whole((rows + 8, HEAD_DIM))] * shards + [anywhere()],
        out_specs=[whole((rows, HEAD_DIM))] * shards,
        scratch_shapes=[
            pltpu.VMEM((shards, rows + 8, HEAD_DIM), F32),
            pltpu.VMEM((shards, rows, HEAD_DIM), F32),
        ],
        out_shape=[struct((rows, HEAD_DIM), F32)] * shards,
        compiler_params=params(16),
        name="chain",
    )(*pieces, after)


def inner_kernel(q_ref, k_ref, v_ref, decay_ref, raw_ref):
    heads = decay_ref.shape[0]
    cumul = running_sum(decay_ref[...])
    columns = cumul.T
    half = SPAN // 2
    for part in range(2):
        rows = slice(part * half, (part + 1) * half)
        width = (part + 1) * half
        token = lax.broadcasted_iota(jnp.int32, (half, width), 0) + part * half
        earlier = lax.broadcasted_iota(jnp.int32, (half, width), 1)
        for group in range(0, heads, 4):
            members = range(group, min(group + 4, heads))
            scores = [
                lax.dot_general(
                    q_ref[rows, head_columns(head)],
                    k_ref[:width, head_columns(head)],
                    (((1,), (1,)), ((), ())),
                    preferred_element_type=F32,
                )
                for head in members
            ]
            weights = []
            for head, score in zip(members, scores):
                diff = columns[rows, head : head + 1] - cumul[head : head + 1, :width]
                factor = jnp.exp(jnp.where(token >= earlier, diff, -jnp.inf))
                weights.append((score * factor).astype(BF16))
            for head, weight in zip(members, weights):
                cols = head_columns(head)
                raw_ref[rows, cols] = dot(weight, v_ref[:width, cols])


def inner(queries, keys, values, log_decay):
    count, width = keys.shape
    heads = width // HEAD_DIM
    tokens = pl.BlockSpec((SPAN, width), lambda i: (i, 0))
    return pl.pallas_call(
        inner_kernel,
        grid=(count // SPAN,),
        in_specs=[tokens, tokens, tokens, pl.BlockSpec((heads, SPAN), lambda i: (0, i))],
        out_specs=tokens,
        out_shape=struct((count, width), F32),
        compiler_params=params(24),
        cost_estimate=cost(4 * count * width * SPAN, 10 * count * width, count * heads * SPAN),
        name="inner",
    )(queries, keys, values, log_decay)


def finish_kernel(
    shards, q_ref, raw_ref, entering_ref, before_ref, decay_ref, gain_ref, *rest
):
    pieces, (centered_ref, stats_ref, arrived, sums) = rest[:shards], rest[shards:]
    heads = decay_ref.shape[0]
    width = heads * HEAD_DIM
    rows = width // shards
    step = pl.program_id(0)
    blocks = pl.num_programs(0)
    count = centered_ref.shape[0]

    @pl.when(step == 0)
    def _():
        mine = lax.axis_index("ctx")
        for index in range(shards):
            start = pl.multiple_of((mine ^ index) * rows, rows)
            arrived[pl.ds(start, rows), :] = pieces[index][...]
        sums[0:8, :] = jnp.zeros((8, width), F32)
        sums[8:16, :] = jnp.full((8, width), -jnp.inf, F32)
        sums[16:24, :] = jnp.full((8, width), jnp.inf, F32)

    factor = jnp.exp(running_sum(decay_ref[...])).T
    here = pl.ds(pl.multiple_of(step * SPAN, SPAN), SPAN)
    for group in range(0, heads, 4):
        members = range(group, min(group + 4, heads))
        outers = []
        for head in members:
            cols = head_columns(head)
            state = entering_ref[0, cols, :] + before_ref[0, head : head + 1, :] * arrived[cols, :]
            query = q_ref[:, cols]
            outers.append(
                dot(
                    jnp.concatenate([query, query], axis=1),
                    jnp.concatenate(split(state), axis=0),
                )
            )
        for head, outer in zip(members, outers):
            cols = head_columns(head)
            raw = raw_ref[:, cols] + outer * factor[:, head : head + 1]
            power = jnp.mean(raw * raw, axis=1, keepdims=True)
            attended = (raw * lax.rsqrt(power + 1e-06) * gain_ref[:, cols]).astype(BF16)
            centered_ref[here, cols] = attended
            wide = attended.astype(F32).reshape(SPAN // 8, 8, HEAD_DIM)
            sums[8:16, cols] = jnp.maximum(sums[8:16, cols], jnp.max(wide, axis=0))
            sums[16:24, cols] = jnp.minimum(sums[16:24, cols], jnp.min(wide, axis=0))
    sums[0:8, :] += dot(jnp.ones((8, SPAN), BF16), centered_ref[here, :])

    @pl.when(step == blocks - 1)
    def _():
        mean = sums[0:1, :] / count
        first, rest = split(mean)
        rest = mean - first.astype(F32)
        second, third = split(rest)
        top = jnp.max(sums[8:16, :], axis=0, keepdims=True)
        bottom = jnp.min(sums[16:24, :], axis=0, keepdims=True)
        lines = [first.astype(F32), second.astype(F32), third.astype(F32), top, bottom]
        lines.append(jnp.zeros((11, width), F32))
        stats_ref[...] = jnp.concatenate(lines, axis=0).astype(BF16)

        @pl.loop(0, count // 128)
        def _(index):
            part = pl.ds(pl.multiple_of(index * 128, 128), 128)
            centered_ref[part, :] = (centered_ref[part, :].astype(F32) - mean).astype(BF16)


def finish(queries, raw, entering, before, log_decay, gain, pieces):
    count, width = queries.shape
    heads = width // HEAD_DIM
    shards = len(pieces)
    tokens = pl.BlockSpec((SPAN, width), lambda i: (i, 0))
    return pl.pallas_call(
        functools.partial(finish_kernel, shards),
        grid=(count // SPAN,),
        in_specs=[
            tokens,
            tokens,
            pl.BlockSpec((1, width, HEAD_DIM), lambda i: (i, 0, 0)),
            pl.BlockSpec((1, heads, HEAD_DIM), lambda i: (i, 0, 0)),
            pl.BlockSpec((heads, SPAN), lambda i: (0, i)),
            whole((1, width)),
        ]
        + [whole(pieces[0].shape)] * shards,
        out_specs=[whole((count, width)), whole((16, width))],
        scratch_shapes=[pltpu.VMEM((width, HEAD_DIM), F32), pltpu.VMEM((24, width), F32)],
        out_shape=[struct((count, width), BF16), struct((16, width), BF16)],
        compiler_params=params(32),
        cost_estimate=cost(4 * count * width * HEAD_DIM, 10 * count * width),
        name="finish",
    )(queries, raw, entering, before, log_decay, gain, *pieces)


def places(count, inner, bit):
    return [
        (outer * 2 + bit) * inner + index
        for outer in range(count // inner // 2)
        for index in range(inner)
    ]


def gram_kernel(rows, ranges, apart, own_ref, other_ref, *rest):
    keep_ref, send_ref = rest[-2:]
    width = own_ref.shape[1]
    shards = width // rows
    bit = (lax.axis_index("ctx") // apart) % 2
    if len(rest) > 3:
        send_ref[shards // 2 * rows :, :] = rest[0][...]

    def fill(out_ref, blocks):
        for index, block in enumerate(blocks):
            line = slice(index * rows, (index + 1) * rows)
            left = own_ref[:, block * rows : (block + 1) * rows].T
            place = 0
            for begin, end in ranges:
                begin, end = (block + begin) * rows, (block + end) * rows
                for ref, low in ((own_ref, 0), (other_ref, width)):
                    first, last = max(begin - low, 0), min(end - low, width)
                    if first < last:
                        out = dot(left, ref[:, first:last]).astype(out_ref.dtype)
                        out_ref[line, place : place + last - first] = out
                        place += last - first

    for mine in range(2):

        @pl.when(bit == mine)
        def _():
            fill(send_ref, places(shards, apart, 1 - mine))
            fill(keep_ref, places(shards, apart, mine))


def gram_parts(own, other, extra, after, rows, ranges, apart):
    count, width = own.shape
    shards = width // rows
    size = sum(end - begin for begin, end in ranges) * rows
    kept = (shards // 2 * rows, size)
    if rows % 128:
        full = lax.dot_general(
            own,
            jnp.concatenate([own, other], axis=1),
            (((0,), (0,)), ((), ())),
            preferred_element_type=F32,
        )
        parts = []
        for shard in range(shards):
            line = full[shard * rows : (shard + 1) * rows]
            slabs = [line[:, (shard + a) * rows : (shard + b) * rows] for a, b in ranges]
            parts.append(jnp.concatenate(slabs, axis=1))
        bit = (lax.axis_index("ctx") // apart) % 2
        parts = jnp.stack(parts).reshape(-1, 2, apart, rows, size)
        keep = lax.dynamic_index_in_dim(parts, bit, 1, False).reshape(kept)
        send = lax.dynamic_index_in_dim(parts, 1 - bit, 1, False).reshape(kept)
        return keep, jnp.concatenate([send.astype(BF16)] + extra)
    sent = (kept[0] + sum(value.shape[0] for value in extra), size)
    return pl.pallas_call(
        functools.partial(gram_kernel, rows, ranges, apart),
        in_specs=[vmem()] * (2 + len(extra)) + [anywhere()],
        out_specs=[vmem(), vmem()],
        out_shape=[struct(kept, F32), struct(sent, BF16)],
        compiler_params=params(16),
        cost_estimate=cost(2 * count * width * size, 4 * count * width),
        name="gram",
    )(own, other, *extra, after)


def fold_kernel(rows, inner, apart, keep_ref, other_ref, *rest):
    kept_ref, send_ref = rest[-2:]
    count = keep_ref.shape[0] // rows
    bit = (lax.axis_index("ctx") // apart) % 2
    if len(rest) > 2:
        extra = rest[0].shape[0]
        low = kept_ref.shape[0]
        send_ref[low : low + extra, :] = rest[0][...]
        send_ref[low + extra :, :] = other_ref[keep_ref.shape[0] :, :]

    for mine in range(2):

        @pl.when(bit == mine)
        def _():
            for out_ref, side in ((send_ref, 1 - mine), (kept_ref, mine)):
                for index, block in enumerate(places(count, inner, side)):
                    line = slice(block * rows, (block + 1) * rows)
                    total = keep_ref[line, :] + other_ref[line, :].astype(F32)
                    out_ref[index * rows : (index + 1) * rows, :] = total.astype(out_ref.dtype)


def fold(keep, other, extra, rows, inner, apart):
    kept = (keep.shape[0] // 2, keep.shape[1])
    sent = (kept[0] + 2 * sum(value.shape[0] for value in extra), kept[1])
    return pl.pallas_call(
        functools.partial(fold_kernel, rows, inner, apart),
        in_specs=[vmem()] * (2 + len(extra)),
        out_specs=[vmem(), vmem()],
        out_shape=[struct(kept, F32), struct(sent, BF16)],
        compiler_params=params(16),
        name="fold",
    )(keep, other, *extra)


def close_kernel(rows, columns, keep_ref, other_ref, total_ref, *slab_refs):
    total = keep_ref[...] + other_ref[:rows, :].astype(F32)
    total_ref[...] = total
    for column, slab_ref in zip(columns, slab_refs):
        slab_ref[...] = total[:, column * rows : (column + 1) * rows].astype(BF16)


def close(keep, other, rows, columns):
    out = pl.pallas_call(
        functools.partial(close_kernel, rows, columns),
        in_specs=[vmem(), vmem()],
        out_specs=[vmem()] * (1 + len(columns)),
        out_shape=[struct(keep.shape, F32)] + [struct((rows, rows), BF16)] * len(columns),
        compiler_params=params(16),
        name="close",
    )(keep, other)
    return out[0], out[1:]


def cover_kernel(rows, shards, total, order, means_ref, others_ref, *refs):
    chunk_count = len(order)
    chunks = refs[:chunk_count]
    mirrors = refs[chunk_count : chunk_count + shards - 1]
    out_ref, spread = refs[chunk_count + shards - 1 :]
    width = rows * shards
    mine, side = lax.axis_index("ctx"), lax.axis_index("head") & 1
    for ref, place in ((means_ref, side), (others_ref, 1 - side)):
        value = ref[...]
        centre = jnp.sum(value, axis=0, keepdims=True) / shards
        spread[:, pl.ds(pl.multiple_of(place * width, width), width)] = value - centre
    block = side * shards + mine
    left = spread[:, pl.ds(pl.multiple_of(block * rows, rows), rows)].T
    count = total // shards
    out_ref[...] = count * jnp.dot(left, spread[...], precision=HIGHEST, preferred_element_type=F32)

    def put(position, gram):
        position = lax.rem(position + 2 * shards, 2 * shards)
        at = pl.ds(pl.multiple_of(position * rows, rows), rows)
        out_ref[:, at] = (out_ref[:, at] + gram) / total

    for chunk, steps in zip(chunks, order):
        for index, step in enumerate(steps):
            put(block + step, chunk[:, index * rows : (index + 1) * rows])
    for index in range(shards - 1):
        put(block - (index + 1), mirrors[index][...].T.astype(F32))


def cover(means, others, chunks, mirrors, order, rows, shards, total):
    width = rows * shards
    if rows % 128:
        mine, side = lax.axis_index("ctx"), lax.axis_index("head") & 1
        pair = [jnp.where(side == 0, means, others), jnp.where(side == 0, others, means)]
        spread = jnp.concatenate(pair, axis=1)
        spread = spread - jnp.mean(spread, axis=0)
        block = side * shards + mine
        left = lax.dynamic_slice_in_dim(spread, block * rows, rows, 1)
        fix = (total // shards) * jnp.dot(left.T, spread, precision=HIGHEST)
        ahead = {}
        for chunk, steps in zip(chunks, order):
            for index, step in enumerate(steps):
                ahead[step] = chunk[:, index * rows : (index + 1) * rows]
        slabs = [mirrors[step - 1].T.astype(F32) for step in range(shards - 1, 0, -1)]
        slabs += [ahead[step] for step in range(shards + 1)]
        line = jnp.roll(jnp.concatenate(slabs, axis=1), (block - (shards - 1)) * rows, axis=1)
        return (line + fix) / total
    return pl.pallas_call(
        functools.partial(cover_kernel, rows, shards, total, order),
        grid=(1,),
        in_specs=[whole(value.shape) for value in (means, others, *chunks, *mirrors)],
        out_specs=whole((rows, 2 * width)),
        scratch_shapes=[pltpu.VMEM((shards, 2 * width), F32)],
        out_shape=struct((rows, 2 * width), F32),
        compiler_params=params(16),
        name="cover",
    )(means, others, *chunks, *mirrors)


def body(queries, keys, values, log_decay, gain):
    count, width = queries.shape
    shards = lax.axis_size("ctx")
    sides = lax.axis_size("head")
    rows = width // shards
    mine = lax.axis_index("ctx")

    def to_shard(value, apart):
        return lax.ppermute(value, "ctx", [(a, a ^ apart) for a in range(shards)])

    def to_partner(value):
        return lax.ppermute(value, "head", [(a, a ^ 1) for a in range(sides)])

    def everywhere(values):
        return [values[0]] + [to_shard(values[k], k) for k in range(1, shards)]

    def forward(value, steps):
        pairs = []
        for shard in range(shards):
            for side in range(sides):
                block = (side % 2) * shards + shard + steps
                other = (block // shards) % 2
                target = (block % shards) * sides + (side // 2) * 2 + other
                pairs.append((shard * sides + side, target))
        return lax.ppermute(value, ("ctx", "head"), pairs)

    entering, before, pieces = local_states(keys, values, log_decay, shards)
    arrived = everywhere(pieces)
    raw = inner(queries, keys, values, log_decay)
    entry = everywhere(chain(arrived, raw))
    centered, stats = finish(
        queries, raw, entering, before, log_decay, gain.reshape(1, width), entry
    )
    partner = to_partner(centered)

    half = shards // 2
    lines = half * rows
    packed = -(-5 * width // lines)
    padded = packed + -packed % 16
    extra = jnp.pad(stats[:5].reshape(packed, lines), ((0, padded - packed), (0, 0)))
    bits = [1 << place for place in range(shards.bit_length() - 1)]
    plans = [
        (tuple(range(1, half + 1)), ((1, half + 1),), bits),
        ((shards, 0), ((shards, shards + 1), (0, 1)), bits[1:] + bits[:1]),
        (tuple(range(half + 1, shards)), ((half + 1, shards),), bits),
    ]
    order = [steps for steps, _, _ in plans]
    kept, riders, after = [], [extra], stats
    for steps, ranges, turns in plans:
        keep, send = gram_parts(
            centered, partner, riders if not kept else [], after, rows, ranges, turns[0]
        )
        after = keep
        kept.append((keep, to_shard(send, turns[0])))
    chunks, mirrors = [], [None] * (shards - 1)
    for (steps, ranges, turns), (keep, other) in zip(plans, kept):
        first = not chunks
        left = bits[:]
        for done, apart in zip(turns, turns[1:]):
            left.remove(done)
            inner_blocks = 1 << left.index(apart)
            gathered = riders if first else []
            low = keep.shape[0]
            keep, send = fold(keep, other, gathered, rows, inner_blocks, apart)
            if first:
                riders = [jnp.concatenate([riders[0], other[low:]])]
            other = to_shard(send, apart)
        if first:
            gathered = jnp.concatenate([riders[0], other[rows:]])
        columns = [index for index, step in enumerate(steps) if 0 < step < shards]
        total, slabs = close(keep, other, rows, columns)
        chunks.append(total)
        for column, slab in zip(columns, slabs):
            mirrors[steps[column] - 1] = forward(slab, steps[column])
        if first:
            every = gathered

    every = every.reshape(shards, padded, lines)[:, :packed]
    every = every.reshape(shards, 5, width).astype(F32)
    means = every[:, 0] + every[:, 1] + every[:, 2]
    shift = (jnp.max(every[:, 3], axis=0) + jnp.min(every[:, 4], axis=0)) / 2.0
    others = to_partner(means)
    covariance = cover(means, others, chunks, mirrors, order, rows, shards, count * shards)
    return (shift, covariance)


def solution(mesh):
    placed = (P("ctx", "head"), P("ctx", "head"), P("ctx", "head"), P("head", "ctx"), P("head"))
    return jax.shard_map(
        body,
        mesh=mesh,
        in_specs=placed,
        out_specs=(P("head"), P(("head", "ctx"), None)),
        check_vma=False,
    )
```

time: 141 us -> 116 us (0.82)
  starting transfers between devices: 60 us -> 42.5 us
  local copies, waits for them, and re-layouts: 5.98 us -> 1.71 us
  Pallas kernels: 32.3 us -> 30.6 us
  other arithmetic: 2.07 us -> 0.65 us
    ppermute x33 -> x23, starting transfers between devices: 49.7 us -> 33.1 us  [to_shard(): return lax.ppermute(value, 'ctx', [(a, a ^ apart) for a in range(shards)])]
    unnamed x18 -> x19, local copies, waits for them, and re-layouts: 5.54 us -> 1.67 us
    pallas_call x1, Pallas kernels: 8.46 us -> 5.37 us  [inner(): pl.pallas_call(inner_kernel, grid=(count // SPAN,), in_specs=[tokens, tok...]
    pallas_call x6 -> x15, Pallas kernels: 21.1 us -> 23 us  [the longest x3 8.91 us: gram_parts(): pl.pallas_call(functools.partial(gram_kernel, rows, ranges, apart), in_sp...]
    ppermute x33 -> x23, waiting for transfers between devices: 30.9 us -> 32.5 us  [to_shard(): return lax.ppermute(value, 'ctx', [(a, a ^ apart) for a in range(shards)])]
  transfers between devices with their start and end apart: 42 -> 32, of which waited for: 16 -> 13; matrix products, arithmetic and copies ran while one was open for 2% -> 1% of each run, Pallas kernels for 10% -> 10%
where the time goes in v2:
time: 116 us; the launch traced here: 115 us
  starting transfers between devices  42.5 us (37%)
  waiting for transfers between devices  38.9 us (34%)
  Pallas kernels  30.6 us (26%)
  local copies, waits for them, and re-layouts  1.71 us (1%)
    ppermute x23, starting transfers between devices, to_shard(): return lax.ppermute(value, 'ctx', [(a, a ^ apart) for a in range(shards)])  33.1 us
    ppermute x23, waiting for transfers between devices, to_shard(): return lax.ppermute(value, 'ctx', [(a, a ^ apart) for a in range(shards)])  32.5 us
    ppermute x7, starting transfers between devices, forward(): return lax.ppermute(value, ('ctx', 'head'), pairs)  9.37 us
    pallas_call x3, Pallas kernels, gram_parts(): pl.pallas_call(functools.partial(gram_kernel, rows, ranges, apart), in_sp...  8.91 us
    pallas_call x1, Pallas kernels, finish(): pl.pallas_call(functools.partial(finish_kernel, shards), grid=(count // S...  7.08 us
    pallas_call x1, Pallas kernels, local_states(): pl.pallas_call(functools.partial(states_kernel, shards), grid=(blocks,),...  6.53 us
    pallas_call x1, Pallas kernels, inner(): pl.pallas_call(inner_kernel, grid=(count // SPAN,), in_specs=[tokens, tok...  5.37 us
    ppermute x2, waiting for transfers between devices, to_partner(): return lax.ppermute(value, 'head', [(a, a ^ 1) for a in range(sides)])  4.23 us
  transfers between devices with their start and end apart: 32, of which 13 were waited for; matrix products, arithmetic and copies ran while one was open for 1% of the time, Pallas kernels for 10%

profile of v2, /device:TPU:0, one launch (start us, length us, event | category | flops | bytes accessed | tf_op | source)
XLA Modules:
  0.0 115.4 jit_solution(12890993319121530073)
XLA Ops:
  0.7 6.5 %local_states.1 = (f32[4,1024,128]{2,1,0:T(8,128)}, f32[4,8,128]{2,1,0:T(8,128)}, f32[136,128]{1,0:T(8,128)}, f32[136,128]{1,0:T(8,128)}, f32[136,128]{1,0:T(8,1...) custom-call(bf16[1024,1024]{1,0:T(8,128)(2,1)} %k_ref.3, ...), custom_call_target="tpu_custom_call" | custom-call | flops 536870912 | bytes 4194304 | tf_op jit(solution)/shard_map/local_states/pallas_call | solution.py:113
  7.2 3.0 %collective-permute-start = (f32[136,128]{1,0:T(8,128)}, f32[136,128]{1,0:T(8,128)S(1)}, u32[]{:S(2)}, u32[]{:S(2)}) collective-permute-start(f32[136,128]{1,0:T(8,128)} %get-tuple-element.52), channel_id=1, source_target_pairs={{0,4},{4,0},{8,12},{12,8},{16,20},{20,16},{24,28},{28,24},{1,5},{5... | collective-permute-start | bytes 208904 | tf_op jit(solution)/shard_map/ppermute | solution.py:493
  10.2 1.6 %collective-permute-start.1 = (f32[136,128]{1,0:T(8,128)}, f32[136,128]{1,0:T(8,128)S(1)}, u32[]{:S(2)}, u32[]{:S(2)}) collective-permute-start(f32[136,128]{1,0:T(8,128)} %get-tuple-element.53), channel_id=1, source_target_pairs={{0,8},{4,12},{8,0},{12,4},{16,24},{20,28},{24,16},{28,20},{1,9},{5... | collective-permute-start | bytes 208904 | tf_op jit(solution)/shard_map/ppermute | solution.py:493
  11.8 0.0 collective-permute-start.2
  11.8 3.0 %collective-permute-start.3 = (f32[136,128]{1,0:T(8,128)}, f32[136,128]{1,0:T(8,128)S(1)}, u32[]{:S(2)}, u32[]{:S(2)}) collective-permute-start(f32[136,128]{1,0:T(8,128)} %get-tuple-element.55), channel_id=1, source_target_pairs={{0,16},{4,20},{8,24},{12,28},{16,0},{20,4},{24,8},{28,12},{1,17},{... | collective-permute-start | bytes 208904 | tf_op jit(solution)/shard_map/ppermute | solution.py:493
  14.8 1.3 %collective-permute-start.4 = (f32[136,128]{1,0:T(8,128)}, f32[136,128]{1,0:T(8,128)S(1)}, u32[]{:S(2)}, u32[]{:S(2)}) collective-permute-start(f32[136,128]{1,0:T(8,128)} %get-tuple-element.56), channel_id=1, source_target_pairs={{0,20},{4,16},{8,28},{12,24},{16,4},{20,0},{24,12},{28,8},{1,21},{... | collective-permute-start | bytes 208904 | tf_op jit(solution)/shard_map/ppermute | solution.py:493
  16.1 0.0 collective-permute-done.refs_1_
  16.1 3.6 %collective-permute-start.5 = (f32[136,128]{1,0:T(8,128)}, f32[136,128]{1,0:T(8,128)S(1)}, u32[]{:S(2)}, u32[]{:S(2)}) collective-permute-start(f32[136,128]{1,0:T(8,128)} %get-tuple-element.57), channel_id=1, source_target_pairs={{0,24},{4,28},{8,16},{12,20},{16,8},{20,12},{24,0},{28,4},{1,25},{... | collective-permute-start | bytes 208904 | tf_op jit(solution)/shard_map/ppermute | solution.py:493
  19.7 0.0 collective-permute-start.6
  19.7 0.0 copy-start.2
  19.7 1.6 %copy-done.2 = bf16[1024,1024]{1,0:T(8,128)(2,1)S(1)} copy-done((bf16[1024,1024]{1,0:T(8,128)(2,1)S(1)}, bf16[1024,1024]{1,0:T(8,128)(2,1)}, u32[]{:S(2)}) %copy-start.2) | copy-done | bytes 2097176
  21.3 5.4 %inner.1.refs_8_.raw_ref = f32[1024,1024]{1,0:T(8,128)S(1)} custom-call(bf16[1024,1024]{1,0:T(8,128)(2,1)S(1)} %copy-done.2, bf16[1024,1024]{1,0:T(8,128)(2,1)S(1)} %copy-done, bf16[1024,1024]{1,0:T(8,128)(2,1)S(1)} %copy-done.1, f32[8,1024]{1,0:T(8,128)S(1)} %copy-done.5), custom_call_target="tpu_custom_call" | custom-call | flops 1073741824 | bytes 10485760 | tf_op jit(solution)/shard_map/inner/pallas_call | solution.py:199
  26.7 0.0 collective-permute-done.3.refs_4_
  26.7 0.3 collective-permute-done.6.refs_7_
  27.0 0.0 copy-start.8
  27.0 0.1 chain.1
  27.2 1.5 %collective-permute-start.7 = (f32[128,128]{1,0:T(8,128)S(1)}, f32[128,128]{1,0:T(8,128)S(1)}, u32[]{:S(2)}, u32[]{:S(2)}) collective-permute-start(f32[128,128]{1,0:T(8,128)S(1)} %get-tuple-element.60), channel_id=1, source_target_pairs={{0,4},{4,0},{8,12},{12,8},{16,20},{20,16},{24,28},{28,24},{1,5},{5... | collective-permute-start | bytes 196616 | tf_op jit(solution)/shard_map/ppermute | solution.py:493
  28.7 1.7 %collective-permute-start.8 = (f32[128,128]{1,0:T(8,128)S(1)}, f32[128,128]{1,0:T(8,128)S(1)}, u32[]{:S(2)}, u32[]{:S(2)}) collective-permute-start(f32[128,128]{1,0:T(8,128)S(1)} %get-tuple-element.61), channel_id=1, source_target_pairs={{0,8},{4,12},{8,0},{12,4},{16,24},{20,28},{24,16},{28,20},{1,9},{5... | collective-permute-start | bytes 196616 | tf_op jit(solution)/shard_map/ppermute | solution.py:493
  30.3 0.7 collective-permute-start.9
  31.0 3.1 %collective-permute-start.10 = (f32[128,128]{1,0:T(8,128)S(1)}, f32[128,128]{1,0:T(8,128)S(1)}, u32[]{:S(2)}, u32[]{:S(2)}) collective-permute-start(f32[128,128]{1,0:T(8,128)S(1)} %get-tuple-element.63), channel_id=1, source_target_pairs={{0,16},{4,20},{8,24},{12,28},{16,0},{20,4},{24,8},{28,12},{1,17},{... | collective-permute-start | bytes 196616 | tf_op jit(solution)/shard_map/ppermute | solution.py:493
  34.1 0.4 collective-permute-start.11
  34.5 0.0 collective-permute-done.7.rest_1_
  34.5 3.6 %collective-permute-start.12 = (f32[128,128]{1,0:T(8,128)S(1)}, f32[128,128]{1,0:T(8,128)S(1)}, u32[]{:S(2)}, u32[]{:S(2)}) collective-permute-start(f32[128,128]{1,0:T(8,128)S(1)} %get-tuple-element.65), channel_id=1, source_target_pairs={{0,24},{4,28},{8,16},{12,20},{16,8},{20,12},{24,0},{28,4},{1,25},{... | collective-permute-start | bytes 196616 | tf_op jit(solution)/shard_map/ppermute | solution.py:493
  38.1 0.0 collective-permute-done.8.rest_2_
  38.1 0.7 collective-permute-start.13
  38.9 0.0 collective-permute-done.9.rest_3_
  38.9 0.1 collective-permute-done.10.rest_4_
  39.0 4.1 %collective-permute-done.11.rest_5_ = f32[128,128]{1,0:T(8,128)S(1)} collective-permute-done((f32[128,128]{1,0:T(8,128)S(1)}, f32[128,128]{1,0:T(8,128)S(1)}, u32[]{:S(2)}, u32[]{:S(2)}) %collective-permute-start.11) | collective-permute-done | bytes 65568 | tf_op jit(solution)/shard_map/ppermute | solution.py:493
  43.1 2.1 %collective-permute-done.13.rest_7_ = f32[128,128]{1,0:T(8,128)S(1)} collective-permute-done((f32[128,128]{1,0:T(8,128)S(1)}, f32[128,128]{1,0:T(8,128)S(1)}, u32[]{:S(2)}, u32[]{:S(2)}) %collective-permute-start.13) | collective-permute-done | bytes 65568 | tf_op jit(solution)/shard_map/ppermute | solution.py:493
  45.2 7.1 %finish.1 = (bf16[1024,1024]{1,0:T(8,128)(2,1)S(1)}, bf16[16,1024]{1,0:T(8,128)(2,1)S(1)}) custom-call(bf16[1024,1024]{1,0:T(8,128)(2,1)S(1)} %copy-done.3, f32[1024,1024]{1,0:T(8,128)S(1)} %inner.1.refs_8_.raw_ref, f32[4,1024,128]{2,1,0:T(8,128)S(1)} %copy-done.4, f32[4,8,128]{2,1,0:T(8,128)S(1)} %copy-done.7, f32[8,1024]{1,0:T(8,128)S(1)} %copy-done.5, ...), custom_call_target="tpu_custom_call" | custom-call | flops 536870912 | bytes 10485760 | tf_op jit(solution)/shard_map/finish/pallas_call | solution.py:281
  52.3 0.1 collective-permute-start.14
  52.4 4.2 %collective-permute-done.14.other_ref = bf16[1024,1024]{1,0:T(8,128)(2,1)} collective-permute-done((bf16[1024,1024]{1,0:T(8,128)(2,1)S(1)}, bf16[1024,1024]{1,0:T(8,128)(2,1)}, u32[]{:S(2)}, u32[]{:S(2)}) %collective-permute-start.14) | collective-permute-done | bytes 2097184 | tf_op jit(solution)/shard_map/ppermute | solution.py:496
  56.7 3.0 %gram.3 = (f32[512,512]{1,0:T(8,128)S(1)}, bf16[528,512]{1,0:T(8,128)(2,1)S(1)}) custom-call(bf16[1024,1024]{1,0:T(8,128)(2,1)S(1)} %get-tuple-element.68.own_ref, bf16[1024,1024]{1,0:T(8,128)(2,1)} %collective-permute-done.14.other_ref, bf16[16,512]{1,0:T(8,128)(2,1)S(1)} %pad.4.rest_0_, bf16[16,1024]{1,0:T(8,128)(2,1)S(1)} %get-tuple-element.67.rest_1_), custom_call_target="tpu_custom_call" | custom-call | flops 1073741824 | bytes 4194304 | tf_op jit(solution)/shard_map/gram/pallas_call | solution.py:363
  59.7 0.6 collective-permute-start.15
  60.3 2.9 %gram.4 = (f32[512,256]{1,0:T(8,128)S(1)}, bf16[512,256]{1,0:T(8,128)(2,1)S(1)}) custom-call(bf16[1024,1024]{1,0:T(8,128)(2,1)S(1)} %get-tuple-element.68.own_ref, bf16[1024,1024]{1,0:T(8,128)(2,1)} %collective-permute-done.14.other_ref, f32[512,512]{1,0:T(8,128)S(1)} %get-tuple-element.70.keep_ref.rest_0_), custom_call_target="tpu_custom_call" | custom-call | flops 536870912 | bytes 4194304 | tf_op jit(solution)/shard_map/gram/pallas_call | solution.py:363
  63.2 2.9 %gram.5 = (f32[512,384]{1,0:T(8,128)S(1)}, bf16[512,384]{1,0:T(8,128)(2,1)S(1)}) custom-call(bf16[1024,1024]{1,0:T(8,128)(2,1)S(1)} %get-tuple-element.68.own_ref, bf16[1024,1024]{1,0:T(8,128)(2,1)} %collective-permute-done.14.other_ref, f32[512,256]{1,0:T(8,128)S(1)} %get-tuple-element.76.keep_ref.rest_0_), custom_call_target="tpu_custom_call" | custom-call | flops 805306368 | bytes 4194304 | tf_op jit(solution)/shard_map/gram/pallas_call | solution.py:363
  66.2 1.6 %collective-permute-start.22 = (bf16[512,384]{1,0:T(8,128)(2,1)S(1)}, bf16[512,384]{1,0:T(8,128)(2,1)S(1)}, u32[]{:S(2)}, u32[]{:S(2)}) collective-permute-start(bf16[512,384]{1,0:T(8,128)(2,1)S(1)} %get-tuple-element.83), channel_id=1, source_target_pairs={{0,4},{4,0},{8,12},{12,8},{16,20},{20,16},{24,28},{28,24},{1,5},{5... | collective-permute-start | bytes 1179656 | tf_op jit(solution)/shard_map/ppermute | solution.py:493
  67.8 1.3 %collective-permute-start.19 = (bf16[512,256]{1,0:T(8,128)(2,1)S(1)}, bf16[512,256]{1,0:T(8,128)(2,1)S(1)}, u32[]{:S(2)}, u32[]{:S(2)}) collective-permute-start(bf16[512,256]{1,0:T(8,128)(2,1)S(1)} %get-tuple-element.77), channel_id=1, source_target_pairs={{0,8},{4,12},{8,0},{12,4},{16,24},{20,28},{24,16},{28,20},{1,9},{5... | collective-permute-start | bytes 786440 | tf_op jit(solution)/shard_map/ppermute | solution.py:493
  69.1 5.8 %collective-permute-done.15.other_ref = bf16[528,512]{1,0:T(8,128)(2,1)S(1)} collective-permute-done((bf16[528,512]{1,0:T(8,128)(2,1)S(1)}, bf16[528,512]{1,0:T(8,128)(2,1)S(1)}, u32[]{:S(2)}, u32[]{:S(2)}) %collective-permute-start.15) | collective-permute-done | bytes 540704 | tf_op jit(solution)/shard_map/ppermute | solution.py:493
  74.9 0.1 fold.6
  75.0 1.4 %collective-permute-start.16 = (bf16[288,512]{1,0:T(8,128)(2,1)S(1)}, bf16[288,512]{1,0:T(8,128)(2,1)S(1)}, u32[]{:S(2)}, u32[]{:S(2)}) collective-permute-start(bf16[288,512]{1,0:T(8,128)(2,1)S(1)} %get-tuple-element.71), channel_id=1, source_target_pairs={{0,8},{4,12},{8,0},{12,4},{16,24},{20,28},{24,16},{28,20},{1,9},{5... | collective-permute-start | bytes 884744 | tf_op jit(solution)/shard_map/ppermute | solution.py:493
  76.4 1.2 %collective-permute-start.20 = (bf16[256,256]{1,0:T(8,128)(2,1)S(1)}, bf16[256,256]{1,0:T(8,128)(2,1)S(1)}, u32[]{:S(2)}, u32[]{:S(2)}) collective-permute-start(bf16[256,256]{1,0:T(8,128)(2,1)S(1)} %get-tuple-element.79), channel_id=1, source_target_pairs={{0,16},{4,20},{8,24},{12,28},{16,0},{20,4},{24,8},{28,12},{1,17},{... | collective-permute-start | bytes 393224 | tf_op jit(solution)/shard_map/ppermute | solution.py:493
  77.6 4.9 %collective-permute-done.22.other_ref = bf16[512,384]{1,0:T(8,128)(2,1)S(1)} collective-permute-done((bf16[512,384]{1,0:T(8,128)(2,1)S(1)}, bf16[512,384]{1,0:T(8,128)(2,1)S(1)}, u32[]{:S(2)}, u32[]{:S(2)}) %collective-permute-start.22) | collective-permute-done | bytes 393248 | tf_op jit(solution)/shard_map/ppermute | solution.py:493
  82.5 0.1 fold.10
  82.6 1.4 %collective-permute-start.23 = (bf16[256,384]{1,0:T(8,128)(2,1)S(1)}, bf16[256,384]{1,0:T(8,128)(2,1)S(1)}, u32[]{:S(2)}, u32[]{:S(2)}) collective-permute-start(bf16[256,384]{1,0:T(8,128)(2,1)S(1)} %get-tuple-element.85), channel_id=1, source_target_pairs={{0,8},{4,12},{8,0},{12,4},{16,24},{20,28},{24,16},{28,20},{1,9},{5... | collective-permute-start | bytes 589832 | tf_op jit(solution)/shard_map/ppermute | solution.py:493
  84.0 1.9 %collective-permute-done.16.other_ref = bf16[288,512]{1,0:T(8,128)(2,1)S(1)} collective-permute-done((bf16[288,512]{1,0:T(8,128)(2,1)S(1)}, bf16[288,512]{1,0:T(8,128)(2,1)S(1)}, u32[]{:S(2)}, u32[]{:S(2)}) %collective-permute-start.16) | collective-permute-done | bytes 294944 | tf_op jit(solution)/shard_map/ppermute | solution.py:493
  86.0 0.1 collective-permute-start.17
  86.1 6.3 %collective-permute-done.23.other_ref = bf16[256,384]{1,0:T(8,128)(2,1)S(1)} collective-permute-done((bf16[256,384]{1,0:T(8,128)(2,1)S(1)}, bf16[256,384]{1,0:T(8,128)(2,1)S(1)}, u32[]{:S(2)}, u32[]{:S(2)}) %collective-permute-start.23) | collective-permute-done | bytes 196640 | tf_op jit(solution)/shard_map/ppermute | solution.py:493
  92.5 0.1 collective-permute-start.24
  92.6 1.2 %collective-permute-start.21 = (bf16[128,256]{1,0:T(8,128)(2,1)S(1)}, bf16[128,256]{1,0:T(8,128)(2,1)S(1)}, u32[]{:S(2)}, u32[]{:S(2)}) collective-permute-start(bf16[128,256]{1,0:T(8,128)(2,1)S(1)} %get-tuple-element.81), channel_id=1, source_target_pairs={{0,4},{4,0},{8,12},{12,8},{16,20},{20,16},{24,28},{28,24},{1,5},{5... | collective-permute-start | bytes 196616 | tf_op jit(solution)/shard_map/ppermute | solution.py:493
  93.9 3.1 %collective-permute-done.21.other_ref = bf16[128,256]{1,0:T(8,128)(2,1)S(1)} collective-permute-done((bf16[128,256]{1,0:T(8,128)(2,1)S(1)}, bf16[128,256]{1,0:T(8,128)(2,1)S(1)}, u32[]{:S(2)}, u32[]{:S(2)}) %collective-permute-start.21) | collective-permute-done | bytes 65568 | tf_op jit(solution)/shard_map/ppermute | solution.py:493
  97.0 3.8 %collective-permute-done.24.other_ref = bf16[128,384]{1,0:T(8,128)(2,1)S(1)} collective-permute-done((bf16[128,384]{1,0:T(8,128)(2,1)S(1)}, bf16[128,384]{1,0:T(8,128)(2,1)S(1)}, u32[]{:S(2)}, u32[]{:S(2)}) %collective-permute-start.24) | collective-permute-done | bytes 98336 | tf_op jit(solution)/shard_map/ppermute | solution.py:493
  100.8 0.1 collective-permute-start.29
  100.9 1.7 %collective-permute-start.30 = (bf16[128,128]{1,0:T(8,128)(2,1)S(1)}, bf16[128,128]{1,0:T(8,128)(2,1)S(1)}, u32[]{:S(2)}, u32[]{:S(2)}) collective-permute-start(bf16[128,128]{1,0:T(8,128)(2,1)S(1)} %get-tuple-element.94), channel_id=1, source_target_pairs={{0,24},{1,25},{2,26},{3,27},{4,28},{5,29},{6,30},{7,31},{8,1},{9,0... | collective-permute-start | bytes 98312 | tf_op jit(solution)/shard_map/ppermute | solution.py:509
  102.6 0.7 collective-permute-start.31
  103.3 0.1 copy.8
  103.4 0.9 collective-permute-start.25
  104.3 0.6 collective-permute-start.26
  104.9 0.2 collective-permute-done.29.refs_7_
  105.1 3.3 %collective-permute-start.27 = (bf16[128,128]{1,0:T(8,128)(2,1)S(1)}, bf16[128,128]{1,0:T(8,128)(2,1)S(1)}, u32[]{:S(2)}, u32[]{:S(2)}) collective-permute-start(bf16[128,128]{1,0:T(8,128)(2,1)S(1)} %get-tuple-element.91), channel_id=1, source_target_pairs={{0,12},{1,13},{2,14},{3,15},{4,16},{5,17},{6,18},{7,19},{8,20},{9,... | collective-permute-start | bytes 98312 | tf_op jit(solution)/shard_map/ppermute | solution.py:509
  108.4 2.1 %collective-permute-start.28 = (bf16[128,128]{1,0:T(8,128)(2,1)S(1)}, bf16[128,128]{1,0:T(8,128)(2,1)S(1)}, u32[]{:S(2)}, u32[]{:S(2)}) collective-permute-start(bf16[128,128]{1,0:T(8,128)(2,1)S(1)} %get-tuple-element.92), channel_id=1, source_target_pairs={{0,16},{1,17},{2,18},{3,19},{4,20},{5,21},{6,22},{7,23},{8,24},{9,... | collective-permute-start | bytes 98312 | tf_op jit(solution)/shard_map/ppermute | solution.py:509
  110.5 0.6 add_multiply_fusion
  111.1 2.0 %collective-permute-done.28.refs_6_ = bf16[128,128]{1,0:T(8,128)(2,1)S(1)} collective-permute-done((bf16[128,128]{1,0:T(8,128)(2,1)S(1)}, bf16[128,128]{1,0:T(8,128)(2,1)S(1)}, u32[]{:S(2)}, u32[]{:S(2)}) %collective-permute-start.28) | collective-permute-done | bytes 32800 | tf_op jit(solution)/shard_map/ppermute | solution.py:509
  113.2 2.2 %cover.1 = f32[128,2048]{1,0:T(8,128)} custom-call(f32[8,1024]{1,0:T(8,128)S(1)} %get-tuple-element.98.means_ref, f32[8,1024]{1,0:T(8,128)S(1)} %collective-permute-done.18.others_ref, f32[128,512]{1,0:T(8,128)S(1)} %get-tuple-element.75.refs_0_, f32[128,256]{1,0:T(8,128)S(1)} %close.4.refs_1_, f32[128,384]{1,0:T(8,128)S(1)} %get-tuple-element.88.refs_2_, ...), custom_call_target="tpu_custom_call" | custom-call | tf_op jit(solution)/shard_map/cover/pallas_call | solution.py:473
  (47 shorter events, 0.4 us)
Async XLA Ops:
  0.6 19.1 %copy-start.5 = (f32[8,1024]{1,0:T(8,128)S(1)}, f32[8,1024]{1,0:T(8,128)}, u32[]{:S(2)}) copy-start(f32[8,1024]{1,0:T(8,128)} %decay_ref.5) | copy-start | bytes 98308
  0.6 19.1 %copy-start.1 = (bf16[1024,1024]{1,0:T(8,128)(2,1)S(1)}, bf16[1024,1024]{1,0:T(8,128)(2,1)}, u32[]{:S(2)}) copy-start(bf16[1024,1024]{1,0:T(8,128)(2,1)} %v_ref.3) | copy-start | bytes 6291460
  0.7 19.1 %copy-start = (bf16[1024,1024]{1,0:T(8,128)(2,1)S(1)}, bf16[1024,1024]{1,0:T(8,128)(2,1)}, u32[]{:S(2)}) copy-start(bf16[1024,1024]{1,0:T(8,128)(2,1)} %k_ref.3) | copy-start | bytes 6291460
  7.2 8.9 %collective-permute-start = (f32[136,128]{1,0:T(8,128)}, f32[136,128]{1,0:T(8,128)S(1)}, u32[]{:S(2)}, u32[]{:S(2)}) collective-permute-start(f32[136,128]{1,0:T(8,128)} %get-tuple-element.52), channel_id=1, source_target_pairs={{0,4},{4,0},{8,12},{12,8},{16,20},{20,16},{24,28},{28,24},{1,5},{5... | collective-permute-start | bytes 208904 | tf_op jit(solution)/shard_map/ppermute | solution.py:493
  10.2 9.5 %collective-permute-start.1 = (f32[136,128]{1,0:T(8,128)}, f32[136,128]{1,0:T(8,128)S(1)}, u32[]{:S(2)}, u32[]{:S(2)}) collective-permute-start(f32[136,128]{1,0:T(8,128)} %get-tuple-element.53), channel_id=1, source_target_pairs={{0,8},{4,12},{8,0},{12,4},{16,24},{20,28},{24,16},{28,20},{1,9},{5... | collective-permute-start | bytes 208904 | tf_op jit(solution)/shard_map/ppermute | solution.py:493
  11.8 14.9 %collective-permute-start.2 = (f32[136,128]{1,0:T(8,128)}, f32[136,128]{1,0:T(8,128)S(1)}, u32[]{:S(2)}, u32[]{:S(2)}) collective-permute-start(f32[136,128]{1,0:T(8,128)} %get-tuple-element.54), channel_id=1, source_target_pairs={{0,12},{4,8},{8,4},{12,0},{16,28},{20,24},{24,20},{28,16},{1,13},{... | collective-permute-start | bytes 208904 | tf_op jit(solution)/shard_map/ppermute | solution.py:493
  11.8 14.9 %collective-permute-start.3 = (f32[136,128]{1,0:T(8,128)}, f32[136,128]{1,0:T(8,128)S(1)}, u32[]{:S(2)}, u32[]{:S(2)}) collective-permute-start(f32[136,128]{1,0:T(8,128)} %get-tuple-element.55), channel_id=1, source_target_pairs={{0,16},{4,20},{8,24},{12,28},{16,0},{20,4},{24,8},{28,12},{1,17},{... | collective-permute-start | bytes 208904 | tf_op jit(solution)/shard_map/ppermute | solution.py:493
  14.8 11.9 %collective-permute-start.4 = (f32[136,128]{1,0:T(8,128)}, f32[136,128]{1,0:T(8,128)S(1)}, u32[]{:S(2)}, u32[]{:S(2)}) collective-permute-start(f32[136,128]{1,0:T(8,128)} %get-tuple-element.56), channel_id=1, source_target_pairs={{0,20},{4,16},{8,28},{12,24},{16,4},{20,0},{24,12},{28,8},{1,21},{... | collective-permute-start | bytes 208904 | tf_op jit(solution)/shard_map/ppermute | solution.py:493
  16.1 10.6 %collective-permute-start.5 = (f32[136,128]{1,0:T(8,128)}, f32[136,128]{1,0:T(8,128)S(1)}, u32[]{:S(2)}, u32[]{:S(2)}) collective-permute-start(f32[136,128]{1,0:T(8,128)} %get-tuple-element.57), channel_id=1, source_target_pairs={{0,24},{4,28},{8,16},{12,20},{16,8},{20,12},{24,0},{28,4},{1,25},{... | collective-permute-start | bytes 208904 | tf_op jit(solution)/shard_map/ppermute | solution.py:493
  19.7 7.3 %collective-permute-start.6 = (f32[136,128]{1,0:T(8,128)}, f32[136,128]{1,0:T(8,128)S(1)}, u32[]{:S(2)}, u32[]{:S(2)}) collective-permute-start(f32[136,128]{1,0:T(8,128)} %get-tuple-element.58), channel_id=1, source_target_pairs={{0,28},{4,24},{8,20},{12,16},{16,12},{20,8},{24,4},{28,0},{1,29},{... | collective-permute-start | bytes 208904 | tf_op jit(solution)/shard_map/ppermute | solution.py:493
  19.7 1.6 %copy-start.2 = (bf16[1024,1024]{1,0:T(8,128)(2,1)S(1)}, bf16[1024,1024]{1,0:T(8,128)(2,1)}, u32[]{:S(2)}) copy-start(bf16[1024,1024]{1,0:T(8,128)(2,1)} %q_ref.3) | copy-start | bytes 6291460
  21.3 5.7 %copy-start.6 = (f32[136,128]{1,0:T(8,128)S(1)}, f32[136,128]{1,0:T(8,128)}, u32[]{:S(2)}) copy-start(f32[136,128]{1,0:T(8,128)} %get-tuple-element.51.refs_0_) | copy-start | bytes 208900
  27.0 18.2 %copy-start.3 = (bf16[1024,1024]{1,0:T(8,128)(2,1)S(1)}, bf16[1024,1024]{1,0:T(8,128)(2,1)}, u32[]{:S(2)}) copy-start(bf16[1024,1024]{1,0:T(8,128)(2,1)} %q_ref.3) | copy-start | bytes 6291460
  27.0 18.2 %copy-start.4 = (f32[4,1024,128]{2,1,0:T(8,128)S(1)}, f32[4,1024,128]{2,1,0:T(8,128)}, u32[]{:S(2)}) copy-start(f32[4,1024,128]{2,1,0:T(8,128)} %get-tuple-element.49.entering_ref) | copy-start | bytes 6291460
  27.0 18.2 %copy-start.7 = (f32[4,8,128]{2,1,0:T(8,128)S(1)}, f32[4,8,128]{2,1,0:T(8,128)}, u32[]{:S(2)}) copy-start(f32[4,8,128]{2,1,0:T(8,128)} %get-tuple-element.50.before_ref) | copy-start | bytes 49156
  27.0 18.2 %copy-start.8 = (f32[1024]{0:T(1024)S(1)}, f32[1024]{0:T(1024)}, u32[]{:S(2)}) copy-start(f32[1024]{0:T(1024)} %param.9) | copy-start | bytes 12292
  27.2 7.4 %collective-permute-start.7 = (f32[128,128]{1,0:T(8,128)S(1)}, f32[128,128]{1,0:T(8,128)S(1)}, u32[]{:S(2)}, u32[]{:S(2)}) collective-permute-start(f32[128,128]{1,0:T(8,128)S(1)} %get-tuple-element.60), channel_id=1, source_target_pairs={{0,4},{4,0},{8,12},{12,8},{16,20},{20,16},{24,28},{28,24},{1,5},{5... | collective-permute-start | bytes 196616 | tf_op jit(solution)/shard_map/ppermute | solution.py:493
  28.7 9.5 %collective-permute-start.8 = (f32[128,128]{1,0:T(8,128)S(1)}, f32[128,128]{1,0:T(8,128)S(1)}, u32[]{:S(2)}, u32[]{:S(2)}) collective-permute-start(f32[128,128]{1,0:T(8,128)S(1)} %get-tuple-element.61), channel_id=1, source_target_pairs={{0,8},{4,12},{8,0},{12,4},{16,24},{20,28},{24,16},{28,20},{1,9},{5... | collective-permute-start | bytes 196616 | tf_op jit(solution)/shard_map/ppermute | solution.py:493
  30.3 8.5 %collective-permute-start.9 = (f32[128,128]{1,0:T(8,128)S(1)}, f32[128,128]{1,0:T(8,128)S(1)}, u32[]{:S(2)}, u32[]{:S(2)}) collective-permute-start(f32[128,128]{1,0:T(8,128)S(1)} %get-tuple-element.62), channel_id=1, source_target_pairs={{0,12},{4,8},{8,4},{12,0},{16,28},{20,24},{24,20},{28,16},{1,13},{... | collective-permute-start | bytes 196616 | tf_op jit(solution)/shard_map/ppermute | solution.py:493
  31.0 8.0 %collective-permute-start.10 = (f32[128,128]{1,0:T(8,128)S(1)}, f32[128,128]{1,0:T(8,128)S(1)}, u32[]{:S(2)}, u32[]{:S(2)}) collective-permute-start(f32[128,128]{1,0:T(8,128)S(1)} %get-tuple-element.63), channel_id=1, source_target_pairs={{0,16},{4,20},{8,24},{12,28},{16,0},{20,4},{24,8},{28,12},{1,17},{... | collective-permute-start | bytes 196616 | tf_op jit(solution)/shard_map/ppermute | solution.py:493
  34.1 9.0 %collective-permute-start.11 = (f32[128,128]{1,0:T(8,128)S(1)}, f32[128,128]{1,0:T(8,128)S(1)}, u32[]{:S(2)}, u32[]{:S(2)}) collective-permute-start(f32[128,128]{1,0:T(8,128)S(1)} %get-tuple-element.64), channel_id=1, source_target_pairs={{0,20},{4,16},{8,28},{12,24},{16,4},{20,0},{24,12},{28,8},{1,21},{... | collective-permute-start | bytes 196616 | tf_op jit(solution)/shard_map/ppermute | solution.py:493
  34.5 8.6 %collective-permute-start.12 = (f32[128,128]{1,0:T(8,128)S(1)}, f32[128,128]{1,0:T(8,128)S(1)}, u32[]{:S(2)}, u32[]{:S(2)}) collective-permute-start(f32[128,128]{1,0:T(8,128)S(1)} %get-tuple-element.65), channel_id=1, source_target_pairs={{0,24},{4,28},{8,16},{12,20},{16,8},{20,12},{24,0},{28,4},{1,25},{... | collective-permute-start | bytes 196616 | tf_op jit(solution)/shard_map/ppermute | solution.py:493
  38.1 7.1 %collective-permute-start.13 = (f32[128,128]{1,0:T(8,128)S(1)}, f32[128,128]{1,0:T(8,128)S(1)}, u32[]{:S(2)}, u32[]{:S(2)}) collective-permute-start(f32[128,128]{1,0:T(8,128)S(1)} %get-tuple-element.66), channel_id=1, source_target_pairs={{0,28},{4,24},{8,20},{12,16},{16,12},{20,8},{24,4},{28,0},{1,29},{... | collective-permute-start | bytes 196616 | tf_op jit(solution)/shard_map/ppermute | solution.py:493
  52.3 4.4 %collective-permute-start.14 = (bf16[1024,1024]{1,0:T(8,128)(2,1)S(1)}, bf16[1024,1024]{1,0:T(8,128)(2,1)}, u32[]{:S(2)}, u32[]{:S(2)}) collective-permute-start(bf16[1024,1024]{1,0:T(8,128)(2,1)S(1)} %get-tuple-element.68.own_ref), channel_id=1, source_target_pairs={{0,1},{1,0},{2,3},{3,2},{4,5},{5,4},{6,7},{7,6},{8,9},{9,8},{10,11... | collective-permute-start | bytes 6291464 | tf_op jit(solution)/shard_map/ppermute | solution.py:496
  59.7 15.2 %collective-permute-start.15 = (bf16[528,512]{1,0:T(8,128)(2,1)S(1)}, bf16[528,512]{1,0:T(8,128)(2,1)S(1)}, u32[]{:S(2)}, u32[]{:S(2)}) collective-permute-start(bf16[528,512]{1,0:T(8,128)(2,1)S(1)} %get-tuple-element.69), channel_id=1, source_target_pairs={{0,4},{4,0},{8,12},{12,8},{16,20},{20,16},{24,28},{28,24},{1,5},{5... | collective-permute-start | bytes 1622024 | tf_op jit(solution)/shard_map/ppermute | solution.py:493
  66.2 16.4 %collective-permute-start.22 = (bf16[512,384]{1,0:T(8,128)(2,1)S(1)}, bf16[512,384]{1,0:T(8,128)(2,1)S(1)}, u32[]{:S(2)}, u32[]{:S(2)}) collective-permute-start(bf16[512,384]{1,0:T(8,128)(2,1)S(1)} %get-tuple-element.83), channel_id=1, source_target_pairs={{0,4},{4,0},{8,12},{12,8},{16,20},{20,16},{24,28},{28,24},{1,5},{5... | collective-permute-start | bytes 1179656 | tf_op jit(solution)/shard_map/ppermute | solution.py:493
  67.8 8.6 %collective-permute-start.19 = (bf16[512,256]{1,0:T(8,128)(2,1)S(1)}, bf16[512,256]{1,0:T(8,128)(2,1)S(1)}, u32[]{:S(2)}, u32[]{:S(2)}) collective-permute-start(bf16[512,256]{1,0:T(8,128)(2,1)S(1)} %get-tuple-element.77), channel_id=1, source_target_pairs={{0,8},{4,12},{8,0},{12,4},{16,24},{20,28},{24,16},{28,20},{1,9},{5... | collective-permute-start | bytes 786440 | tf_op jit(solution)/shard_map/ppermute | solution.py:493
  75.0 10.9 %collective-permute-start.16 = (bf16[288,512]{1,0:T(8,128)(2,1)S(1)}, bf16[288,512]{1,0:T(8,128)(2,1)S(1)}, u32[]{:S(2)}, u32[]{:S(2)}) collective-permute-start(bf16[288,512]{1,0:T(8,128)(2,1)S(1)} %get-tuple-element.71), channel_id=1, source_target_pairs={{0,8},{4,12},{8,0},{12,4},{16,24},{20,28},{24,16},{28,20},{1,9},{5... | collective-permute-start | bytes 884744 | tf_op jit(solution)/shard_map/ppermute | solution.py:493
  76.4 16.2 %collective-permute-start.20 = (bf16[256,256]{1,0:T(8,128)(2,1)S(1)}, bf16[256,256]{1,0:T(8,128)(2,1)S(1)}, u32[]{:S(2)}, u32[]{:S(2)}) collective-permute-start(bf16[256,256]{1,0:T(8,128)(2,1)S(1)} %get-tuple-element.79), channel_id=1, source_target_pairs={{0,16},{4,20},{8,24},{12,28},{16,0},{20,4},{24,8},{28,12},{1,17},{... | collective-permute-start | bytes 393224 | tf_op jit(solution)/shard_map/ppermute | solution.py:493
  82.6 9.8 %collective-permute-start.23 = (bf16[256,384]{1,0:T(8,128)(2,1)S(1)}, bf16[256,384]{1,0:T(8,128)(2,1)S(1)}, u32[]{:S(2)}, u32[]{:S(2)}) collective-permute-start(bf16[256,384]{1,0:T(8,128)(2,1)S(1)} %get-tuple-element.85), channel_id=1, source_target_pairs={{0,8},{4,12},{8,0},{12,4},{16,24},{20,28},{24,16},{28,20},{1,9},{5... | collective-permute-start | bytes 589832 | tf_op jit(solution)/shard_map/ppermute | solution.py:493
  86.0 17.3 %collective-permute-start.17 = (bf16[192,512]{1,0:T(8,128)(2,1)S(1)}, bf16[192,512]{1,0:T(8,128)(2,1)S(1)}, u32[]{:S(2)}, u32[]{:S(2)}) collective-permute-start(bf16[192,512]{1,0:T(8,128)(2,1)S(1)} %get-tuple-element.73), channel_id=1, source_target_pairs={{0,16},{4,20},{8,24},{12,28},{16,0},{20,4},{24,8},{28,12},{1,17},{... | collective-permute-start | bytes 589832 | tf_op jit(solution)/shard_map/ppermute | solution.py:493
  92.5 8.3 %collective-permute-start.24 = (bf16[128,384]{1,0:T(8,128)(2,1)S(1)}, bf16[128,384]{1,0:T(8,128)(2,1)S(1)}, u32[]{:S(2)}, u32[]{:S(2)}) collective-permute-start(bf16[128,384]{1,0:T(8,128)(2,1)S(1)} %get-tuple-element.87), channel_id=1, source_target_pairs={{0,16},{4,20},{8,24},{12,28},{16,0},{20,4},{24,8},{28,12},{1,17},{... | collective-permute-start | bytes 294920 | tf_op jit(solution)/shard_map/ppermute | solution.py:493
  92.6 4.3 %collective-permute-start.21 = (bf16[128,256]{1,0:T(8,128)(2,1)S(1)}, bf16[128,256]{1,0:T(8,128)(2,1)S(1)}, u32[]{:S(2)}, u32[]{:S(2)}) collective-permute-start(bf16[128,256]{1,0:T(8,128)(2,1)S(1)} %get-tuple-element.81), channel_id=1, source_target_pairs={{0,4},{4,0},{8,12},{12,8},{16,20},{20,16},{24,28},{28,24},{1,5},{5... | collective-permute-start | bytes 196616 | tf_op jit(solution)/shard_map/ppermute | solution.py:493
  100.8 4.3 %collective-permute-start.29 = (bf16[128,128]{1,0:T(8,128)(2,1)S(1)}, bf16[128,128]{1,0:T(8,128)(2,1)S(1)}, u32[]{:S(2)}, u32[]{:S(2)}) collective-permute-start(bf16[128,128]{1,0:T(8,128)(2,1)S(1)} %get-tuple-element.93), channel_id=1, source_target_pairs={{0,20},{1,21},{2,22},{3,23},{4,24},{5,25},{6,26},{7,27},{8,28},{9,... | collective-permute-start | bytes 98312 | tf_op jit(solution)/shard_map/ppermute | solution.py:509
  100.9 7.6 %collective-permute-start.30 = (bf16[128,128]{1,0:T(8,128)(2,1)S(1)}, bf16[128,128]{1,0:T(8,128)(2,1)S(1)}, u32[]{:S(2)}, u32[]{:S(2)}) collective-permute-start(bf16[128,128]{1,0:T(8,128)(2,1)S(1)} %get-tuple-element.94), channel_id=1, source_target_pairs={{0,24},{1,25},{2,26},{3,27},{4,28},{5,29},{6,30},{7,31},{8,1},{9,0... | collective-permute-start | bytes 98312 | tf_op jit(solution)/shard_map/ppermute | solution.py:509
  102.6 7.9 %collective-permute-start.31 = (bf16[128,128]{1,0:T(8,128)(2,1)S(1)}, bf16[128,128]{1,0:T(8,128)(2,1)S(1)}, u32[]{:S(2)}, u32[]{:S(2)}) collective-permute-start(bf16[128,128]{1,0:T(8,128)(2,1)S(1)} %get-tuple-element.95), channel_id=1, source_target_pairs={{0,28},{1,29},{2,30},{3,31},{4,1},{5,0},{6,3},{7,2},{8,5},{9,4},{1... | collective-permute-start | bytes 98312 | tf_op jit(solution)/shard_map/ppermute | solution.py:509
  103.4 7.7 %collective-permute-start.25 = (bf16[128,128]{1,0:T(8,128)(2,1)S(1)}, bf16[128,128]{1,0:T(8,128)(2,1)S(1)}, u32[]{:S(2)}, u32[]{:S(2)}) collective-permute-start(bf16[128,128]{1,0:T(8,128)(2,1)S(1)} %get-tuple-element.89), channel_id=1, source_target_pairs={{0,4},{1,5},{2,6},{3,7},{4,8},{5,9},{6,10},{7,11},{8,12},{9,13},{1... | collective-permute-start | bytes 98312 | tf_op jit(solution)/shard_map/ppermute | solution.py:509
  104.3 6.9 %collective-permute-start.26 = (bf16[128,128]{1,0:T(8,128)(2,1)S(1)}, bf16[128,128]{1,0:T(8,128)(2,1)S(1)}, u32[]{:S(2)}, u32[]{:S(2)}) collective-permute-start(bf16[128,128]{1,0:T(8,128)(2,1)S(1)} %get-tuple-element.90), channel_id=1, source_target_pairs={{0,8},{1,9},{2,10},{3,11},{4,12},{5,13},{6,14},{7,15},{8,16},{9,17... | collective-permute-start | bytes 98312 | tf_op jit(solution)/shard_map/ppermute | solution.py:509
  105.1 6.0 %collective-permute-start.27 = (bf16[128,128]{1,0:T(8,128)(2,1)S(1)}, bf16[128,128]{1,0:T(8,128)(2,1)S(1)}, u32[]{:S(2)}, u32[]{:S(2)}) collective-permute-start(bf16[128,128]{1,0:T(8,128)(2,1)S(1)} %get-tuple-element.91), channel_id=1, source_target_pairs={{0,12},{1,13},{2,14},{3,15},{4,16},{5,17},{6,18},{7,19},{8,20},{9,... | collective-permute-start | bytes 98312 | tf_op jit(solution)/shard_map/ppermute | solution.py:509
  108.4 4.7 %collective-permute-start.28 = (bf16[128,128]{1,0:T(8,128)(2,1)S(1)}, bf16[128,128]{1,0:T(8,128)(2,1)S(1)}, u32[]{:S(2)}, u32[]{:S(2)}) collective-permute-start(bf16[128,128]{1,0:T(8,128)(2,1)S(1)} %get-tuple-element.92), channel_id=1, source_target_pairs={{0,16},{1,17},{2,18},{3,19},{4,20},{5,21},{6,22},{7,23},{8,24},{9,... | collective-permute-start | bytes 98312 | tf_op jit(solution)/shard_map/ppermute | solution.py:509
  110.5 2.7 %collective-permute-start.18 = (f32[8,1024]{1,0:T(8,128)S(1)}, f32[8,1024]{1,0:T(8,128)S(1)}, u32[]{:S(2)}, u32[]{:S(2)}) collective-permute-start(f32[8,1024]{1,0:T(8,128)S(1)} %get-tuple-element.98.means_ref), channel_id=1, source_target_pairs={{0,1},{1,0},{2,3},{3,2},{4,5},{5,4},{6,7},{7,6},{8,9},{9,8},{10,11... | collective-permute-start | bytes 98312 | tf_op jit(solution)/shard_map/ppermute | solution.py:496

commit v3 on v2

v3 whole, which is shorter than its diff:
```python
import functools

import jax
import jax.numpy as jnp
from jax import lax
from jax.experimental import pallas as pl
from jax.experimental.pallas import tpu as pltpu
from jax.sharding import PartitionSpec as P

HEAD_DIM = 128
SPAN = 256
F32 = jnp.float32
BF16 = jnp.bfloat16
HIGHEST = lax.Precision.HIGHEST
MIB = 1 << 20


def params(limit_mib):
    return pltpu.CompilerParams(vmem_limit_bytes=limit_mib * MIB)


def cost(flops, moved, transcendentals=0):
    return pl.CostEstimate(
        flops=int(flops), bytes_accessed=int(moved), transcendentals=int(transcendentals)
    )


def whole(shape):
    return pl.BlockSpec(shape, lambda *_: (0,) * len(shape))


def anywhere():
    return pl.BlockSpec(memory_space=pl.ANY)


def vmem():
    return pl.BlockSpec(memory_space=pltpu.VMEM)


def struct(shape, dtype):
    return jax.ShapeDtypeStruct(shape, dtype)


def dot(a, b):
    return jnp.dot(a, b, preferred_element_type=F32)


def split(value):
    high = value.astype(BF16)
    return high, (value - high.astype(F32)).astype(BF16)


def running_sum(decay):
    rows = lax.broadcasted_iota(jnp.int32, (SPAN, SPAN), 0)
    columns = lax.broadcasted_iota(jnp.int32, (SPAN, SPAN), 1)
    ones = jnp.where(rows <= columns, 1.0, 0.0).astype(F32)
    return jnp.dot(decay, ones, precision=HIGHEST, preferred_element_type=F32)


def head_columns(head):
    return slice(head * HEAD_DIM, (head + 1) * HEAD_DIM)


def states_kernel(near, k_ref, v_ref, decay_ref, entering_ref, before_ref, *rest):
    pieces, (state, total) = rest[:near], rest[near:]
    heads = decay_ref.shape[0]
    step = pl.program_id(0)

    @pl.when(step == 0)
    def _():
        state[...] = jnp.zeros_like(state)
        total[...] = jnp.ones_like(total)

    entering_ref[0] = state[...]
    before_ref[0] = total[...]
    cumul = running_sum(decay_ref[...])
    last = cumul[:, SPAN - 1 :]
    weight = jnp.exp(last - cumul)
    drop = jnp.exp(last)
    for group in range(0, heads, 4):
        members = range(group, min(group + 4, heads))
        turned = [k_ref[:, head_columns(head)].T for head in members]
        parts = []
        for head, key in zip(members, turned):
            high, low = split(key.astype(F32) * weight[head : head + 1, :])
            parts.append(jnp.concatenate([high, low], axis=0))
        updates = [dot(part, v_ref[:, head_columns(head)]) for head, part in zip(members, parts)]
        for head, update in zip(members, updates):
            cols = head_columns(head)
            update = update[:HEAD_DIM] + update[HEAD_DIM:]
            state[cols, :] = state[cols, :] * drop[head : head + 1, :] + update
    total[...] = total[...] * drop

    @pl.when(step == pl.num_programs(0) - 1)
    def _():
        mine = lax.axis_index("ctx") % near
        rows = heads * HEAD_DIM // near
        for apart in range(near):
            start = pl.multiple_of((mine ^ apart) * rows, rows)
            pieces[apart][:rows, :] = state[pl.ds(start, rows), :]
            pieces[apart][rows:, :] = jnp.zeros((8, HEAD_DIM), F32)
            for head in range(rows // HEAD_DIM):
                line = total[pl.ds(start // HEAD_DIM + head, 1), :]
                pieces[apart][rows + head : rows + head + 1, :] = line


def local_states(keys, values, log_decay, near):
    count, width = keys.shape
    heads = width // HEAD_DIM
    blocks = count // SPAN
    rows = width // near
    piece = (rows + 8, HEAD_DIM)
    shapes = [(blocks, width, HEAD_DIM), (blocks, heads, HEAD_DIM)] + [piece] * near
    tokens = pl.BlockSpec((SPAN, width), lambda i: (i, 0))
    out = pl.pallas_call(
        functools.partial(states_kernel, near),
        grid=(blocks,),
        in_specs=[tokens, tokens, pl.BlockSpec((heads, SPAN), lambda i: (0, i))],
        out_specs=[
            pl.BlockSpec((1, width, HEAD_DIM), lambda i: (i, 0, 0)),
            pl.BlockSpec((1, heads, HEAD_DIM), lambda i: (i, 0, 0)),
        ]
        + [whole(piece)] * near,
        scratch_shapes=[pltpu.VMEM((width, HEAD_DIM), F32), pltpu.VMEM((heads, HEAD_DIM), F32)],
        out_shape=[struct(shape, F32) for shape in shapes],
        compiler_params=params(56),
        cost_estimate=cost(4 * count * width * HEAD_DIM, 4 * count * width),
        name="local_states",
    )(keys, values, log_decay)
    return out[0], out[1], out[2:]


def chain_kernel(near, *refs):
    arrived, (inside_ref, left_ref, leaving_ref, ordered) = refs[:near], refs[near:]
    mine = lax.axis_index("ctx") % near
    rows = leaving_ref.shape[0]
    heads = rows // HEAD_DIM
    for apart in range(near):
        ordered[mine ^ apart] = arrived[apart][...]
    left_ref[...] = jnp.zeros_like(left_ref)
    for head in range(heads):
        cols = head_columns(head)
        carried = jnp.zeros((HEAD_DIM, HEAD_DIM), F32)
        left = jnp.ones((1, HEAD_DIM), F32)
        for shard in range(near):
            inside_ref[shard, cols, :] = carried
            left_ref[shard, head : head + 1, :] = left
            drop = ordered[shard, rows + head : rows + head + 1, :]
            carried = carried * drop + ordered[shard, cols, :]
            left = left * drop
        leaving_ref[cols, :] = carried


def chain(pieces):
    near = len(pieces)
    rows = pieces[0].shape[0] - 8
    shapes = [(near, rows, HEAD_DIM), (near, 8, HEAD_DIM), (rows, HEAD_DIM)]
    return pl.pallas_call(
        functools.partial(chain_kernel, near),
        in_specs=[vmem()] * near,
        out_specs=[vmem()] * 3,
        out_shape=[struct(shape, F32) for shape in shapes],
        scratch_shapes=[pltpu.VMEM((near, rows + 8, HEAD_DIM), F32)],
        compiler_params=params(16),
        name="chain",
    )(*pieces)


def spread_kernel(inside_ref, left_ref, entered_ref, _, *outs):
    near, rows, _ = inside_ref.shape
    mine = lax.axis_index("ctx") % near
    for apart, out_ref in enumerate(outs):
        shard = mine ^ apart
        left = left_ref[shard]
        for head in range(rows // HEAD_DIM):
            cols = head_columns(head)
            part = entered_ref[cols, :] * left[head : head + 1, :]
            out_ref[cols, :] = inside_ref[shard, cols, :] + part


def spread_states(inside, left, entered, after):
    near, rows, _ = inside.shape
    return pl.pallas_call(
        spread_kernel,
        in_specs=[vmem()] * 3 + [anywhere()],
        out_specs=[vmem()] * near,
        out_shape=[struct((rows, HEAD_DIM), F32)] * near,
        compiler_params=params(16),
        name="spread_states",
    )(inside, left, entered, after)


def inner_kernel(q_ref, k_ref, v_ref, decay_ref, raw_ref):
    heads = decay_ref.shape[0]
    cumul = running_sum(decay_ref[...])
    columns = cumul.T
    half = SPAN // 2
    for part in range(2):
        rows = slice(part * half, (part + 1) * half)
        width = (part + 1) * half
        token = lax.broadcasted_iota(jnp.int32, (half, width), 0) + part * half
        earlier = lax.broadcasted_iota(jnp.int32, (half, width), 1)
        for group in range(0, heads, 4):
            members = range(group, min(group + 4, heads))
            scores = [
                lax.dot_general(
                    q_ref[rows, head_columns(head)],
                    k_ref[:width, head_columns(head)],
                    (((1,), (1,)), ((), ())),
                    preferred_element_type=F32,
                )
                for head in members
            ]
            weights = []
            for head, score in zip(members, scores):
                diff = columns[rows, head : head + 1] - cumul[head : head + 1, :width]
                factor = jnp.exp(jnp.where(token >= earlier, diff, -jnp.inf))
                weights.append((score * factor).astype(BF16))
            for head, weight in zip(members, weights):
                cols = head_columns(head)
                raw_ref[rows, cols] = dot(weight, v_ref[:width, cols])


def inner(queries, keys, values, log_decay):
    count, width = keys.shape
    heads = width // HEAD_DIM
    tokens = pl.BlockSpec((SPAN, width), lambda i: (i, 0))
    return pl.pallas_call(
        inner_kernel,
        grid=(count // SPAN,),
        in_specs=[tokens, tokens, tokens, pl.BlockSpec((heads, SPAN), lambda i: (0, i))],
        out_specs=tokens,
        out_shape=struct((count, width), F32),
        compiler_params=params(24),
        cost_estimate=cost(4 * count * width * SPAN, 10 * count * width, count * heads * SPAN),
        name="inner",
    )(queries, keys, values, log_decay)


def finish_kernel(
    near, q_ref, raw_ref, entering_ref, before_ref, decay_ref, gain_ref, *rest
):
    pieces, (centered_ref, stats_ref, arrived, sums) = rest[:near], rest[near:]
    heads = decay_ref.shape[0]
    width = heads * HEAD_DIM
    rows = width // near
    step = pl.program_id(0)
    blocks = pl.num_programs(0)
    count = centered_ref.shape[0]

    @pl.when(step == 0)
    def _():
        mine = lax.axis_index("ctx") % near
        for apart in range(near):
            start = pl.multiple_of((mine ^ apart) * rows, rows)
            arrived[pl.ds(start, rows), :] = pieces[apart][...]
        sums[0:8, :] = jnp.zeros((8, width), F32)
        sums[8:16, :] = jnp.full((8, width), -jnp.inf, F32)
        sums[16:24, :] = jnp.full((8, width), jnp.inf, F32)

    factor = jnp.exp(running_sum(decay_ref[...])).T
    here = pl.ds(pl.multiple_of(step * SPAN, SPAN), SPAN)
    for group in range(0, heads, 4):
        members = range(group, min(group + 4, heads))
        outers = []
        for head in members:
            cols = head_columns(head)
            state = entering_ref[0, cols, :] + before_ref[0, head : head + 1, :] * arrived[cols, :]
            query = q_ref[:, cols]
            outers.append(
                dot(
                    jnp.concatenate([query, query], axis=1),
                    jnp.concatenate(split(state), axis=0),
                )
            )
        for head, outer in zip(members, outers):
            cols = head_columns(head)
            raw = raw_ref[:, cols] + outer * factor[:, head : head + 1]
            power = jnp.mean(raw * raw, axis=1, keepdims=True)
            attended = (raw * lax.rsqrt(power + 1e-06) * gain_ref[:, cols]).astype(BF16)
            centered_ref[here, cols] = attended
            wide = attended.astype(F32).reshape(SPAN // 8, 8, HEAD_DIM)
            sums[8:16, cols] = jnp.maximum(sums[8:16, cols], jnp.max(wide, axis=0))
            sums[16:24, cols] = jnp.minimum(sums[16:24, cols], jnp.min(wide, axis=0))
    sums[0:8, :] += dot(jnp.ones((8, SPAN), BF16), centered_ref[here, :])

    @pl.when(step == blocks - 1)
    def _():
        mean = sums[0:1, :] / count
        first, rest = split(mean)
        rest = mean - first.astype(F32)
        second, third = split(rest)
        top = jnp.max(sums[8:16, :], axis=0, keepdims=True)
        bottom = jnp.min(sums[16:24, :], axis=0, keepdims=True)
        lines = [first.astype(F32), second.astype(F32), third.astype(F32), top, bottom]
        lines.append(jnp.zeros((11, width), F32))
        stats_ref[...] = jnp.concatenate(lines, axis=0).astype(BF16)

        @pl.loop(0, count // 128)
        def _(index):
            part = pl.ds(pl.multiple_of(index * 128, 128), 128)
            centered_ref[part, :] = (centered_ref[part, :].astype(F32) - mean).astype(BF16)


def finish(queries, raw, entering, before, log_decay, gain, pieces):
    count, width = queries.shape
    heads = width // HEAD_DIM
    near = len(pieces)
    tokens = pl.BlockSpec((SPAN, width), lambda i: (i, 0))
    return pl.pallas_call(
        functools.partial(finish_kernel, near),
        grid=(count // SPAN,),
        in_specs=[
            tokens,
            tokens,
            pl.BlockSpec((1, width, HEAD_DIM), lambda i: (i, 0, 0)),
            pl.BlockSpec((1, heads, HEAD_DIM), lambda i: (i, 0, 0)),
            pl.BlockSpec((heads, SPAN), lambda i: (0, i)),
            whole((1, width)),
        ]
        + [whole(pieces[0].shape)] * near,
        out_specs=[whole((count, width)), whole((16, width))],
        scratch_shapes=[pltpu.VMEM((width, HEAD_DIM), F32), pltpu.VMEM((24, width), F32)],
        out_shape=[struct((count, width), BF16), struct((16, width), BF16)],
        compiler_params=params(32),
        cost_estimate=cost(4 * count * width * HEAD_DIM, 10 * count * width),
        name="finish",
    )(queries, raw, entering, before, log_decay, gain, *pieces)


def places(count, inner, bit):
    return [
        (outer * 2 + bit) * inner + index
        for outer in range(count // inner // 2)
        for index in range(inner)
    ]


def side_of(side, block, shards):
    return side if side < 2 else (0 if block < shards // 2 else 1)


def gram_kernel(rows, blocks, apart, own_ref, other_ref, *rest):
    keep_ref, send_ref, turned = rest[-3:]
    width = own_ref.shape[1]
    shards = width // rows
    steps = sorted({step for step, _ in blocks})
    bit = (lax.axis_index("ctx") // apart) % 2
    if len(rest) > 4:
        send_ref[shards // 2 * rows :, :] = rest[0][...]
    for start in range(0, turned.shape[0], HEAD_DIM):
        here = start % width
        turned[start : start + HEAD_DIM, :] = own_ref[:, here : here + HEAD_DIM].T

    def fill(out_ref, row_blocks):
        for index, block in enumerate(row_blocks):
            line = slice(index * rows, (index + 1) * rows)
            here = slice(block * rows, (block + 1) * rows)
            left = turned[(block + steps[0]) * rows : (block + steps[-1] + 1) * rows, :]
            right = jnp.concatenate([own_ref[:, here], other_ref[:, here]], axis=1)
            out = dot(left, right).astype(out_ref.dtype)
            for place, (step, side) in enumerate(blocks):
                low = (step - steps[0]) * rows
                first = side_of(side, block, shards) * rows
                target = slice(place * rows, (place + 1) * rows)
                out_ref[line, target] = out[low : low + rows, first : first + rows]

    for mine in range(2):

        @pl.when(bit == mine)
        def _():
            fill(send_ref, places(shards, apart, 1 - mine))
            fill(keep_ref, places(shards, apart, mine))


def gram_parts(own, other, extra, after, rows, blocks, apart):
    count, width = own.shape
    shards = width // rows
    size = len(blocks) * rows
    kept = (shards // 2 * rows, size)
    if rows % 128:
        full = [
            lax.dot_general(own, side, (((0,), (0,)), ((), ())), preferred_element_type=F32)
            for side in (own, other)
        ]
        parts = []
        for shard in range(shards):
            slabs = []
            for step, side in blocks:
                at = (shard + step) % shards * rows
                value = full[side_of(side, shard, shards)]
                slabs.append(value[at : at + rows, shard * rows : (shard + 1) * rows])
            parts.append(jnp.concatenate(slabs, axis=1))
        bit = (lax.axis_index("ctx") // apart) % 2
        parts = jnp.stack(parts).reshape(-1, 2, apart, rows, size)
        keep = lax.dynamic_index_in_dim(parts, bit, 1, False).reshape(kept)
        send = lax.dynamic_index_in_dim(parts, 1 - bit, 1, False).reshape(kept)
        return keep, jnp.concatenate([send.astype(BF16)] + extra)
    sent = (kept[0] + sum(value.shape[0] for value in extra), size)
    return pl.pallas_call(
        functools.partial(gram_kernel, rows, blocks, apart),
        in_specs=[vmem()] * (2 + len(extra)) + [anywhere()],
        out_specs=[vmem(), vmem()],
        scratch_shapes=[pltpu.VMEM((width + max(step for step, _ in blocks) * rows, count), BF16)],
        out_shape=[struct(kept, F32), struct(sent, BF16)],
        compiler_params=params(16),
        cost_estimate=cost(2 * count * width * size, 4 * count * width),
        name="gram",
    )(own, other, *extra, after)


def merge(first, second, means):
    a, b = first.astype(F32), second.astype(F32)
    top, bottom = slice(means, means + 2), slice(means + 2, means + 4)
    lines = [a[:means], b[:means], jnp.maximum(a[top], b[top]), jnp.minimum(a[bottom], b[bottom])]
    spare = -(2 * means + 4) % 16
    if spare:
        lines.append(jnp.zeros((spare, a.shape[1]), F32))
    return jnp.concatenate(lines, axis=0).astype(BF16)


def fold_kernel(rows, inner, apart, means, keep_ref, other_ref, _, *rest):
    count = keep_ref.shape[0] // rows
    bit = (lax.axis_index("ctx") // apart) % 2
    if means:
        riders_ref, kept_ref, send_ref, merged_ref = rest
        merged = merge(riders_ref[...], other_ref[keep_ref.shape[0] :, :], means)
        send_ref[kept_ref.shape[0] :, :] = merged
        merged_ref[...] = merged
    else:
        kept_ref, send_ref = rest

    for mine in range(2):

        @pl.when(bit == mine)
        def _():
            for out_ref, side in ((send_ref, 1 - mine), (kept_ref, mine)):
                for index, block in enumerate(places(count, inner, side)):
                    line = slice(block * rows, (block + 1) * rows)
                    total = keep_ref[line, :] + other_ref[line, :].astype(F32)
                    out_ref[index * rows : (index + 1) * rows, :] = total.astype(out_ref.dtype)


def fold(keep, other, after, riders, means, rows, inner, apart):
    kept = (keep.shape[0] // 2, keep.shape[1])
    shapes = [struct(kept, F32), struct(kept, BF16)]
    if riders:
        merged = (2 * means + 4 + -(2 * means + 4) % 16, kept[1])
        shapes = [struct(kept, F32), struct((kept[0] + merged[0], kept[1]), BF16)]
        shapes.append(struct(merged, BF16))
    return pl.pallas_call(
        functools.partial(fold_kernel, rows, inner, apart, means if riders else 0),
        in_specs=[vmem()] * 2 + [anywhere()] + [vmem()] * len(riders),
        out_specs=[vmem()] * len(shapes),
        out_shape=shapes,
        compiler_params=params(16),
        name="fold",
    )(keep, other, after, *riders)


def close_kernel(rows, runs, waits, keep_ref, other_ref, *rest):
    total_ref, slab_refs = rest[waits], rest[waits + 1 :]
    total = keep_ref[...] + other_ref[:rows, :].astype(F32)
    total_ref[...] = total
    for run, slab_ref in zip(runs, slab_refs):
        for place, column in enumerate(run):
            slab = total[:, column * rows : (column + 1) * rows].astype(BF16)
            slab_ref[:, place * rows : (place + 1) * rows] = slab


def close(keep, other, after, rows, runs):
    out = pl.pallas_call(
        functools.partial(close_kernel, rows, runs, len(after)),
        in_specs=[vmem(), vmem()] + [anywhere()] * len(after),
        out_specs=[vmem()] * (1 + len(runs)),
        out_shape=[struct(keep.shape, F32)] + [struct((rows, len(run) * rows), BF16) for run in runs],
        compiler_params=params(16),
        name="close",
    )(keep, other, *after)
    return out[0], out[1:]


def assemble(put, upper, shards, chunks, mirrors, crossed):
    half = shards // 2
    put(0, 0, chunks[(0, 0)])
    put(0, 1, chunks[(0, 1)])
    for step in range(1, half):
        put(step, 0, chunks[(step, 0)].T)
        put(step, 1, crossed[step].T)
        put(-step, 0, mirrors[(step, 0)])
        put(-step, 1, mirrors[(step, 1)])
    last = jnp.where(upper, crossed[half].astype(F32), chunks[(half, 2)])
    put(half, upper, last.T)
    put(half, 1 - upper, mirrors[(half, 2)])


def pick(rows, names, values):
    out = {}
    for blocks, value in zip(names, values):
        for place, name in enumerate(blocks):
            out[name] = value[:, place * rows : (place + 1) * rows]
    return out


def cover_kernel(rows, shards, total, names, means_ref, others_ref, *refs):
    out_ref, spread = refs[-2:]
    width = rows * shards
    mine, side = lax.axis_index("ctx"), lax.axis_index("head") & 1
    for ref, place in ((means_ref, side), (others_ref, 1 - side)):
        value = ref[...]
        centre = jnp.sum(value, axis=0, keepdims=True) / shards
        spread[:, pl.ds(pl.multiple_of(place * width, width), width)] = value - centre
    own = pl.multiple_of((side * shards + mine) * rows, rows)
    left = spread[:, pl.ds(own, rows)].T
    count = total // shards
    out_ref[...] = count * jnp.dot(left, spread[...], precision=HIGHEST, preferred_element_type=F32)

    def put(step, flip, gram):
        shard = lax.rem(mine + step + shards, shards)
        at = pl.ds(pl.multiple_of(((side ^ flip) * shards + shard) * rows, rows), rows)
        out_ref[:, at] = (out_ref[:, at] + gram.astype(F32)) / total

    values = iter(refs[:-2])
    parts = [pick(rows, group, [next(values) for _ in group]) for group in names]
    assemble(put, jnp.where(mine >= shards // 2, 1, 0), shards, *parts)


def cover(means, others, groups, names, rows, shards, total):
    width = rows * shards
    values = [value for group in groups for value in group]
    if rows % 128:
        mine, side = lax.axis_index("ctx"), lax.axis_index("head") & 1
        pair = [jnp.where(side == 0, means, others), jnp.where(side == 0, others, means)]
        spread = jnp.concatenate(pair, axis=1)
        spread = spread - jnp.mean(spread, axis=0)
        left = lax.dynamic_slice_in_dim(spread, (side * shards + mine) * rows, rows, 1)
        out = [(total // shards) * jnp.dot(left.T, spread, precision=HIGHEST)]

        def put(step, flip, gram):
            shard = lax.rem(mine + step + shards, shards)
            at = ((side ^ flip) * shards + shard) * rows
            old = lax.dynamic_slice_in_dim(out[0], at, rows, 1)
            new = (old + gram.astype(F32)) / total
            out[0] = lax.dynamic_update_slice_in_dim(out[0], new, at, 1)

        parts = [pick(rows, *pair) for pair in zip(names, groups)]
        assemble(put, jnp.where(mine >= shards // 2, 1, 0), shards, *parts)
        return out[0]
    return pl.pallas_call(
        functools.partial(cover_kernel, rows, shards, total, names),
        in_specs=[vmem()] * (2 + len(values)),
        out_specs=vmem(),
        scratch_shapes=[pltpu.VMEM((shards, 2 * width), F32)],
        out_shape=struct((rows, 2 * width), F32),
        compiler_params=params(16),
        name="cover",
    )(means, others, *values)


def body(queries, keys, values, log_decay, gain):
    count, width = queries.shape
    shards = lax.axis_size("ctx")
    sides = lax.axis_size("head")
    rows = width // shards
    mine = lax.axis_index("ctx")

    def to_shard(value, apart):
        return lax.ppermute(value, "ctx", [(a, a ^ apart) for a in range(shards)])

    def to_partner(value):
        return lax.ppermute(value, "head", [(a, a ^ 1) for a in range(sides)])

    near = shards // 2

    def nearby(values):
        return [values[0]] + [to_shard(values[apart], apart) for apart in range(1, near)]

    def forward(value, step):
        return lax.ppermute(value, "ctx", [(a, (a + step) % shards) for a in range(shards)])

    entering, before, pieces = local_states(keys, values, log_decay, near)
    inside, left, leaving = chain(nearby(pieces))
    entered = lax.ppermute(leaving, "ctx", [(a, a + near) for a in range(near)])
    raw = inner(queries, keys, values, log_decay)
    entry = nearby(spread_states(inside, left, entered, raw))
    centered, stats = finish(
        queries, raw, entering, before, log_decay, gain.reshape(1, width), entry
    )
    partner = to_partner(centered)

    half = shards // 2
    lines = half * rows
    mean_rows = 3 * width // lines
    extra = stats[:5].reshape(mean_rows + 4, lines)
    extra = jnp.pad(extra, ((0, -extra.shape[0] % 16), (0, 0)))
    bits = [1 << place for place in range(shards.bit_length() - 1)]
    near = range(1, half // 2 + 1)
    far = range(half // 2 + 1, half)
    plans = [
        ([(step, side) for step in near for side in (0, 1)], bits),
        ([(0, 0), (0, 1)], bits[1:] + bits[:1]),
        ([(step, side) for step in far for side in (0, 1)] + [(half, 2)], bits),
    ]
    kept, riders, after = [], [extra], stats
    for blocks, turns in plans:
        keep, send = gram_parts(
            centered, partner, [] if kept else riders, after, rows, blocks, turns[0]
        )
        after = keep
        kept.append((keep, to_shard(send, turns[0])))
    def split_on(index, after):
        keep, other = kept[index]
        turns = plans[index][1]
        stage = stages[index]
        left = [bit for bit in bits if bit not in turns[:stage]]
        inner_blocks = 1 << left.index(turns[stage])
        carried = riders if index == 0 else []
        keep, send, *merged = fold(
            keep, other, after, carried, mean_rows << (stage - 1), rows, inner_blocks, turns[stage]
        )
        riders[:] = merged or riders
        kept[index] = (keep, to_shard(send, turns[stage]))
        stages[index] += 1
        return keep

    stages = [1] * len(plans)
    after = kept[0][0]
    for stage in range(1, len(bits)):
        for index in (1, 0, 2):
            after = split_on(index, after)

    chunks, mirrors, mirror_names, crossed, crossed_names = [None] * len(plans), [], [], [], []
    for index in (0, 1, 2):
        blocks, (keep, other) = plans[index][0], kept[index]
        if index == 0:
            every = merge(riders[0], other[rows:], mean_rows * half)
        steps = sorted({step for step, _ in blocks} - {0})
        runs = [[i for i, block in enumerate(blocks) if block[0] == step] for step in steps]
        crossing = [i for i, (step, side) in enumerate(blocks) if step and side]
        earlier = mirrors + crossed if index == 2 else []
        total, slabs = close(keep, other, earlier, rows, runs + [crossing] * bool(crossing))
        chunks[index] = total
        for step, run, slab in zip(steps, runs, slabs):
            mirrors.append(forward(slab, step))
            mirror_names.append([blocks[i] for i in run])
        if crossing:
            crossed.append(to_partner(slabs[-1]))
            crossed_names.append([blocks[i][0] for i in crossing])

    every = every.astype(F32)
    means = jnp.sum(every[: mean_rows * shards].reshape(shards, 3, width), axis=1)
    extremes = every[mean_rows * shards :][:4].reshape(2, width)
    shift = (extremes[0] + extremes[1]) / 2.0
    others = to_partner(means)
    covariance = cover(
        means,
        others,
        (chunks, mirrors, crossed),
        ([blocks for blocks, _ in plans], mirror_names, crossed_names),
        rows,
        shards,
        count * shards,
    )
    return (shift, covariance)


def solution(mesh):
    placed = (P("ctx", "head"), P("ctx", "head"), P("ctx", "head"), P("head", "ctx"), P("head"))
    return jax.shard_map(
        body,
        mesh=mesh,
        in_specs=placed,
        out_specs=(P("head"), P(("head", "ctx"), None)),
        check_vma=False,
    )
```

time: 116 us -> 109 us (0.940)
  starting transfers between devices: 42.5 us -> 25.4 us
  waiting for transfers between devices: 38.9 us -> 46.6 us
  Pallas kernels: 30.6 us -> 32.3 us
  local copies, waits for them, and re-layouts: 1.71 us -> 3.39 us
    ppermute x23 -> x15, starting transfers between devices: 33.1 us -> 17.3 us  [to_shard(): return lax.ppermute(value, 'ctx', [(a, a ^ apart) for a in range(shards)])]
    ppermute x7 -> x5, waiting for transfers between devices: 2.2 us -> 9.06 us  [the longest x4 9.06 us: forward(): lax.ppermute(value, 'ctx', [(a, (a + step) % shards) for a in range(shard...]
    ppermute x7 -> x5, starting transfers between devices: 9.37 us -> 7.39 us  [the longest x1 4.65 us: body(): entered = lax.ppermute(leaving, 'ctx', [(a, a + near) for a in range(near)])]
    pallas_call x16 -> x17, Pallas kernels: 25.3 us -> 26.9 us  [the longest x3 10.5 us: gram_parts(): pl.pallas_call(functools.partial(gram_kernel, rows, blocks, apart), in_sp...]
    unnamed x19, local copies, waits for them, and re-layouts: 1.67 us -> 3.12 us
    ppermute x23 -> x15, waiting for transfers between devices: 32.5 us -> 33.3 us  [to_shard(): return lax.ppermute(value, 'ctx', [(a, a ^ apart) for a in range(shards)])]
    ppermute x2 -> x4, waiting for transfers between devices: 4.23 us -> 4.24 us  [to_partner(): return lax.ppermute(value, 'head', [(a, a ^ 1) for a in range(sides)])]
  transfers between devices with their start and end apart: 32 -> 24, of which waited for: 13 -> 17; matrix products, arithmetic and copies ran while one was open for 1% -> 1% of each run, Pallas kernels for 10% -> 12%
where the time goes in v3:
time: 109 us
  waiting for transfers between devices  46.6 us (43%)
  Pallas kernels  32.3 us (30%)
  starting transfers between devices  25.4 us (23%)
  local copies, waits for them, and re-layouts  3.39 us (3%)
    ppermute x15, waiting for transfers between devices, to_shard(): return lax.ppermute(value, 'ctx', [(a, a ^ apart) for a in range(shards)])  33.3 us
    ppermute x15, starting transfers between devices, to_shard(): return lax.ppermute(value, 'ctx', [(a, a ^ apart) for a in range(shards)])  17.3 us
    pallas_call x3, Pallas kernels, gram_parts(): pl.pallas_call(functools.partial(gram_kernel, rows, blocks, apart), in_sp...  10.5 us
    ppermute x4, waiting for transfers between devices, forward(): lax.ppermute(value, 'ctx', [(a, (a + step) % shards) for a in range(shard...  9.06 us
    pallas_call x1, Pallas kernels, finish(): pl.pallas_call(functools.partial(finish_kernel, near), grid=(count // SPA...  7.08 us
    pallas_call x1, Pallas kernels, local_states(): pl.pallas_call(functools.partial(states_kernel, near), grid=(blocks,), in...  6.5 us
    pallas_call x1, Pallas kernels, inner(): pl.pallas_call(inner_kernel, grid=(count // SPAN,), in_specs=[tokens, tok...  5.37 us
    ppermute x1, starting transfers between devices, body(): entered = lax.ppermute(leaving, 'ctx', [(a, a + near) for a in range(near)])  4.65 us
  transfers between devices with their start and end apart: 24, of which 17 were waited for; matrix products, arithmetic and copies ran while one was open for 1% of the time, Pallas kernels for 12%

profile of v3, /device:TPU:0, one launch (start us, length us, event | category | flops | bytes accessed | tf_op | source)
XLA Modules:
  0.0 108.8 jit_solution(8131294790143156119)
XLA Ops:
  0.7 6.5 %local_states.1 = (f32[4,1024,128]{2,1,0:T(8,128)}, f32[4,8,128]{2,1,0:T(8,128)}, f32[264,128]{1,0:T(8,128)}, f32[264,128]{1,0:T(8,128)}, f32[264,128]{1,0:T(8,128)}, /*index=5*/f32[264,128]{1,0:T(8,128)}) custom-call(bf16[1024,1024]{1,0:T(8,128)(2,1)} %k_ref.3, bf16[1024,1024]{1,0:T(8,128)(2,1)} %v_ref.3, f32[8,1024]{1,0:T(8,128)} %decay_ref.5), custom_call_target="tpu_custom_call" | custom-call | flops 536870912 | bytes 4194304 | tf_op jit(solution)/shard_map/local_states/pallas_call | solution.py:115
  7.2 3.0 %collective-permute-start = (f32[264,128]{1,0:T(8,128)}, f32[264,128]{1,0:T(8,128)S(1)}, u32[]{:S(2)}, u32[]{:S(2)}) collective-permute-start(f32[264,128]{1,0:T(8,128)} %get-tuple-element.48), channel_id=1, source_target_pairs={{0,4},{4,0},{8,12},{12,8},{16,20},{20,16},{24,28},{28,24},{1,5},{5... | collective-permute-start | bytes 405512 | tf_op jit(solution)/shard_map/ppermute | solution.py:568
  10.2 1.6 %collective-permute-start.1 = (f32[264,128]{1,0:T(8,128)}, f32[264,128]{1,0:T(8,128)S(1)}, u32[]{:S(2)}, u32[]{:S(2)}) collective-permute-start(f32[264,128]{1,0:T(8,128)} %get-tuple-element.49), channel_id=1, source_target_pairs={{0,8},{4,12},{8,0},{12,4},{16,24},{20,28},{24,16},{28,20},{1,9},{5... | collective-permute-start | bytes 405512 | tf_op jit(solution)/shard_map/ppermute | solution.py:568
  11.8 0.0 collective-permute-start.2
  11.8 2.2 %collective-permute-done.refs_1_ = f32[264,128]{1,0:T(8,128)S(1)} collective-permute-done((f32[264,128]{1,0:T(8,128)}, f32[264,128]{1,0:T(8,128)S(1)}, u32[]{:S(2)}, u32[]{:S(2)}) %collective-permute-start) | collective-permute-done | bytes 135200 | tf_op jit(solution)/shard_map/ppermute | solution.py:568
  14.0 2.9 %collective-permute-done.1.refs_2_ = f32[264,128]{1,0:T(8,128)S(1)} collective-permute-done((f32[264,128]{1,0:T(8,128)}, f32[264,128]{1,0:T(8,128)S(1)}, u32[]{:S(2)}, u32[]{:S(2)}) %collective-permute-start.1) | collective-permute-done | bytes 135200 | tf_op jit(solution)/shard_map/ppermute | solution.py:568
  16.9 1.2 %collective-permute-done.2.refs_3_ = f32[264,128]{1,0:T(8,128)S(1)} collective-permute-done((f32[264,128]{1,0:T(8,128)}, f32[264,128]{1,0:T(8,128)S(1)}, u32[]{:S(2)}, u32[]{:S(2)}) %collective-permute-start.2) | collective-permute-done | bytes 135200 | tf_op jit(solution)/shard_map/ppermute | solution.py:568
  18.1 0.9 copy-done.6
  19.1 0.1 chain.1
  19.2 4.6 %collective-permute-start.3 = (f32[256,128]{1,0:T(8,128)S(1)}, f32[256,128]{1,0:T(8,128)S(1)}, u32[]{:S(2)}, u32[]{:S(2)}) collective-permute-start(f32[256,128]{1,0:T(8,128)S(1)} %get-tuple-element.53), channel_id=1, source_target_pairs={{0,16},{4,20},{8,24},{12,28},{1,17},{5,21},{9,25},{13,29},{2,18},{... | collective-permute-start | bytes 393224 | tf_op jit(solution)/shard_map/ppermute | solution.py:583
  23.8 0.0 copy-start.2
  23.9 1.6 %copy-done.2 = bf16[1024,1024]{1,0:T(8,128)(2,1)S(1)} copy-done((bf16[1024,1024]{1,0:T(8,128)(2,1)S(1)}, bf16[1024,1024]{1,0:T(8,128)(2,1)}, u32[]{:S(2)}) %copy-start.2) | copy-done | bytes 2097176
  25.4 5.4 %inner.1._.raw_ref = f32[1024,1024]{1,0:T(8,128)S(1)} custom-call(bf16[1024,1024]{1,0:T(8,128)(2,1)S(1)} %copy-done.2, bf16[1024,1024]{1,0:T(8,128)(2,1)S(1)} %copy-done, bf16[1024,1024]{1,0:T(8,128)(2,1)S(1)} %copy-done.1, f32[8,1024]{1,0:T(8,128)S(1)} %copy-done.5), custom_call_target="tpu_custom_call" | custom-call | flops 1073741824 | bytes 10485760 | tf_op jit(solution)/shard_map/inner/pallas_call | solution.py:228
  30.8 0.0 copy-start.3
  30.9 0.0 copy-start.8
  30.9 0.1 spread_states.1
  30.9 1.6 %collective-permute-start.4 = (f32[256,128]{1,0:T(8,128)S(1)}, f32[256,128]{1,0:T(8,128)S(1)}, u32[]{:S(2)}, u32[]{:S(2)}) collective-permute-start(f32[256,128]{1,0:T(8,128)S(1)} %get-tuple-element.55), channel_id=1, source_target_pairs={{0,4},{4,0},{8,12},{12,8},{16,20},{20,16},{24,28},{28,24},{1,5},{5... | collective-permute-start | bytes 393224 | tf_op jit(solution)/shard_map/ppermute | solution.py:568
  32.5 1.6 %collective-permute-start.5 = (f32[256,128]{1,0:T(8,128)S(1)}, f32[256,128]{1,0:T(8,128)S(1)}, u32[]{:S(2)}, u32[]{:S(2)}) collective-permute-start(f32[256,128]{1,0:T(8,128)S(1)} %get-tuple-element.56), channel_id=1, source_target_pairs={{0,8},{4,12},{8,0},{12,4},{16,24},{20,28},{24,16},{28,20},{1,9},{5... | collective-permute-start | bytes 393224 | tf_op jit(solution)/shard_map/ppermute | solution.py:568
  34.1 0.4 collective-permute-start.6
  34.5 2.9 %collective-permute-done.4.rest_1_ = f32[256,128]{1,0:T(8,128)S(1)} collective-permute-done((f32[256,128]{1,0:T(8,128)S(1)}, f32[256,128]{1,0:T(8,128)S(1)}, u32[]{:S(2)}, u32[]{:S(2)}) %collective-permute-start.4) | collective-permute-done | bytes 131104 | tf_op jit(solution)/shard_map/ppermute | solution.py:568
  37.4 0.1 collective-permute-done.5.rest_2_
  37.5 2.5 %collective-permute-done.6.rest_3_ = f32[256,128]{1,0:T(8,128)S(1)} collective-permute-done((f32[256,128]{1,0:T(8,128)S(1)}, f32[256,128]{1,0:T(8,128)S(1)}, u32[]{:S(2)}, u32[]{:S(2)}) %collective-permute-start.6) | collective-permute-done | bytes 131104 | tf_op jit(solution)/shard_map/ppermute | solution.py:568
  40.0 7.1 %finish.1 = (bf16[1024,1024]{1,0:T(8,128)(2,1)S(1)}, bf16[16,1024]{1,0:T(8,128)(2,1)S(1)}) custom-call(bf16[1024,1024]{1,0:T(8,128)(2,1)S(1)} %copy-done.3, f32[1024,1024]{1,0:T(8,128)S(1)} %inner.1._.raw_ref, f32[4,1024,128]{2,1,0:T(8,128)S(1)} %copy-done.4, f32[4,8,128]{2,1,0:T(8,128)S(1)} %copy-done.7, f32[8,1024]{1,0:T(8,128)S(1)} %copy-done.5, ...), custom_call_target="tpu_custom_call" | custom-call | flops 536870912 | bytes 10485760 | tf_op jit(solution)/shard_map/finish/pallas_call | solution.py:310
  47.1 0.1 collective-permute-start.7
  47.2 4.2 %collective-permute-done.7.other_ref = bf16[1024,1024]{1,0:T(8,128)(2,1)} collective-permute-done((bf16[1024,1024]{1,0:T(8,128)(2,1)S(1)}, bf16[1024,1024]{1,0:T(8,128)(2,1)}, u32[]{:S(2)}, u32[]{:S(2)}) %collective-permute-start.7) | collective-permute-done | bytes 2097184 | tf_op jit(solution)/shard_map/ppermute | solution.py:571
  51.4 3.6 %gram.3 = (f32[512,512]{1,0:T(8,128)S(1)}, bf16[528,512]{1,0:T(8,128)(2,1)S(1)}) custom-call(bf16[1024,1024]{1,0:T(8,128)(2,1)S(1)} %get-tuple-element.58.own_ref, bf16[1024,1024]{1,0:T(8,128)(2,1)} %collective-permute-done.7.other_ref, bf16[16,512]{1,0:T(8,128)(2,1)S(1)} %pad.4.rest_0_, bf16[16,1024]{1,0:T(8,128)(2,1)S(1)} %get-tuple-element.59.rest_1_), custom_call_target="tpu_custom_call" | custom-call | flops 1073741824 | bytes 4194304 | tf_op jit(solution)/shard_map/gram/pallas_call | solution.py:400
  55.0 0.6 collective-permute-start.8
  55.6 3.0 %gram.4 = (f32[512,256]{1,0:T(8,128)S(1)}, bf16[512,256]{1,0:T(8,128)(2,1)S(1)}) custom-call(bf16[1024,1024]{1,0:T(8,128)(2,1)S(1)} %get-tuple-element.58.own_ref, bf16[1024,1024]{1,0:T(8,128)(2,1)} %collective-permute-done.7.other_ref, f32[512,512]{1,0:T(8,128)S(1)} %get-tuple-element.60.rest_0_._.keep_ref), custom_call_target="tpu_custom_call" | custom-call | flops 536870912 | bytes 4194304 | tf_op jit(solution)/shard_map/gram/pallas_call | solution.py:400
  58.6 1.5 %collective-permute-start.9 = (bf16[512,256]{1,0:T(8,128)(2,1)S(1)}, bf16[512,256]{1,0:T(8,128)(2,1)S(1)}, u32[]{:S(2)}, u32[]{:S(2)}) collective-permute-start(bf16[512,256]{1,0:T(8,128)(2,1)S(1)} %get-tuple-element.63), channel_id=1, source_target_pairs={{0,8},{4,12},{8,0},{12,4},{16,24},{20,28},{24,16},{28,20},{1,9},{5... | collective-permute-start | bytes 786440 | tf_op jit(solution)/shard_map/ppermute | solution.py:568
  60.1 3.9 %gram.5 = (f32[512,384]{1,0:T(8,128)S(1)}, bf16[512,384]{1,0:T(8,128)(2,1)S(1)}) custom-call(bf16[1024,1024]{1,0:T(8,128)(2,1)S(1)} %get-tuple-element.58.own_ref, bf16[1024,1024]{1,0:T(8,128)(2,1)} %collective-permute-done.7.other_ref, f32[512,256]{1,0:T(8,128)S(1)} %get-tuple-element.62.keep_ref.rest_0_), custom_call_target="tpu_custom_call" | custom-call | flops 805306368 | bytes 4194304 | tf_op jit(solution)/shard_map/gram/pallas_call | solution.py:400
  64.0 0.6 collective-permute-start.12
  64.6 2.1 %collective-permute-done.9.other_ref = bf16[512,256]{1,0:T(8,128)(2,1)S(1)} collective-permute-done((bf16[512,256]{1,0:T(8,128)(2,1)S(1)}, bf16[512,256]{1,0:T(8,128)(2,1)S(1)}, u32[]{:S(2)}, u32[]{:S(2)}) %collective-permute-start.9) | collective-permute-done | bytes 262176 | tf_op jit(solution)/shard_map/ppermute | solution.py:568
  66.8 3.5 %collective-permute-done.8.other_ref = bf16[528,512]{1,0:T(8,128)(2,1)S(1)} collective-permute-done((bf16[528,512]{1,0:T(8,128)(2,1)S(1)}, bf16[528,512]{1,0:T(8,128)(2,1)S(1)}, u32[]{:S(2)}, u32[]{:S(2)}) %collective-permute-start.8) | collective-permute-done | bytes 540704 | tf_op jit(solution)/shard_map/ppermute | solution.py:568
  70.2 0.1 fold.7
  70.3 0.5 collective-permute-start.10
  70.8 0.8 collective-permute-start.11
  71.7 6.2 %collective-permute-done.12.other_ref = bf16[512,384]{1,0:T(8,128)(2,1)S(1)} collective-permute-done((bf16[512,384]{1,0:T(8,128)(2,1)S(1)}, bf16[512,384]{1,0:T(8,128)(2,1)S(1)}, u32[]{:S(2)}, u32[]{:S(2)}) %collective-permute-start.12) | collective-permute-done | bytes 393248 | tf_op jit(solution)/shard_map/ppermute | solution.py:568
  77.8 0.1 fold.8
  77.9 0.5 collective-permute-start.16
  78.4 0.1 collective-permute-done.11.other_ref
  78.6 2.0 %collective-permute-done.10.other_ref = bf16[272,512]{1,0:T(8,128)(2,1)S(1)} collective-permute-done((bf16[272,512]{1,0:T(8,128)(2,1)S(1)}, bf16[272,512]{1,0:T(8,128)(2,1)S(1)}, u32[]{:S(2)}, u32[]{:S(2)}) %collective-permute-start.10) | collective-permute-done | bytes 278560 | tf_op jit(solution)/shard_map/ppermute | solution.py:568
  80.6 0.1 fold.10
  80.7 1.5 %collective-permute-start.13 = (bf16[160,512]{1,0:T(8,128)(2,1)S(1)}, bf16[160,512]{1,0:T(8,128)(2,1)S(1)}, u32[]{:S(2)}, u32[]{:S(2)}) collective-permute-start(bf16[160,512]{1,0:T(8,128)(2,1)S(1)} %get-tuple-element.74), channel_id=1, source_target_pairs={{0,16},{4,20},{8,24},{12,28},{16,0},{20,4},{24,8},{28,12},{1,17},{... | collective-permute-start | bytes 491528 | tf_op jit(solution)/shard_map/ppermute | solution.py:568
  82.1 1.5 %collective-permute-start.15 = (bf16[128,256]{1,0:T(8,128)(2,1)S(1)}, bf16[128,256]{1,0:T(8,128)(2,1)S(1)}, u32[]{:S(2)}, u32[]{:S(2)}) collective-permute-start(bf16[128,256]{1,0:T(8,128)(2,1)S(1)} %get-tuple-element.77), channel_id=1, source_target_pairs={{0,4},{4,0},{8,12},{12,8},{16,20},{20,16},{24,28},{28,24},{1,5},{5... | collective-permute-start | bytes 196616 | tf_op jit(solution)/shard_map/ppermute | solution.py:568
  83.7 2.7 %collective-permute-done.15.other_ref = bf16[128,256]{1,0:T(8,128)(2,1)S(1)} collective-permute-done((bf16[128,256]{1,0:T(8,128)(2,1)S(1)}, bf16[128,256]{1,0:T(8,128)(2,1)S(1)}, u32[]{:S(2)}, u32[]{:S(2)}) %collective-permute-start.15) | collective-permute-done | bytes 65568 | tf_op jit(solution)/shard_map/ppermute | solution.py:568
  86.4 0.0 collective-permute-done.16.other_ref
  86.4 0.1 fold.11
  86.5 1.6 %collective-permute-start.17 = (bf16[128,384]{1,0:T(8,128)(2,1)S(1)}, bf16[128,384]{1,0:T(8,128)(2,1)S(1)}, u32[]{:S(2)}, u32[]{:S(2)}) collective-permute-start(bf16[128,384]{1,0:T(8,128)(2,1)S(1)} %get-tuple-element.80), channel_id=1, source_target_pairs={{0,16},{4,20},{8,24},{12,28},{16,0},{20,4},{24,8},{28,12},{1,17},{... | collective-permute-start | bytes 294920 | tf_op jit(solution)/shard_map/ppermute | solution.py:568
  88.1 4.9 %collective-permute-done.13.other_ref = bf16[160,512]{1,0:T(8,128)(2,1)S(1)} collective-permute-done((bf16[160,512]{1,0:T(8,128)(2,1)S(1)}, bf16[160,512]{1,0:T(8,128)(2,1)S(1)}, u32[]{:S(2)}, u32[]{:S(2)}) %collective-permute-start.13) | collective-permute-done | bytes 163872 | tf_op jit(solution)/shard_map/ppermute | solution.py:568
  92.9 0.1 close.3
  93.0 0.2 collective-permute-start.18
  93.2 0.0 collective-permute-start.20
  93.3 0.2 concatenate.4
  93.5 0.1 reshape.23
  93.5 0.1 reduce_sum.9.means_ref
  93.6 0.5 collective-permute-start.14
  94.2 5.8 %collective-permute-done.18.rest_0_.refs_3_ = bf16[128,256]{1,0:T(8,128)(2,1)S(1)} collective-permute-done((bf16[128,256]{1,0:T(8,128)(2,1)S(1)}, bf16[128,256]{1,0:T(8,128)(2,1)S(1)}, u32[]{:S(2)}, u32[]{:S(2)}) %collective-permute-start.18) | collective-permute-done | bytes 65568 | tf_op jit(solution)/shard_map/ppermute | solution.py:579
  100.1 0.1 collective-permute-start.21
  100.1 0.1 collective-permute-start.23
  100.2 2.5 %collective-permute-start.22 = (bf16[128,128]{1,0:T(8,128)(2,1)S(1)}, bf16[128,128]{1,0:T(8,128)(2,1)S(1)}, u32[]{:S(2)}, u32[]{:S(2)}) collective-permute-start(bf16[128,128]{1,0:T(8,128)(2,1)S(1)} %get-tuple-element.86), channel_id=1, source_target_pairs={{0,16},{4,20},{8,24},{12,28},{16,0},{20,4},{24,8},{28,12},{1,17},{... | collective-permute-start | bytes 98312 | tf_op jit(solution)/shard_map/ppermute | solution.py:579
  102.7 0.6 copy.7
  103.3 1.8 %collective-permute-done.22.refs_6_ = bf16[128,128]{1,0:T(8,128)(2,1)S(1)} collective-permute-done((bf16[128,128]{1,0:T(8,128)(2,1)S(1)}, bf16[128,128]{1,0:T(8,128)(2,1)S(1)}, u32[]{:S(2)}, u32[]{:S(2)}) %collective-permute-start.22) | collective-permute-done | bytes 32800 | tf_op jit(solution)/shard_map/ppermute | solution.py:579
  105.1 1.4 %collective-permute-done.21.refs_5_ = bf16[128,256]{1,0:T(8,128)(2,1)S(1)} collective-permute-done((bf16[128,256]{1,0:T(8,128)(2,1)S(1)}, bf16[128,256]{1,0:T(8,128)(2,1)S(1)}, u32[]{:S(2)}, u32[]{:S(2)}) %collective-permute-start.21) | collective-permute-done | bytes 65568 | tf_op jit(solution)/shard_map/ppermute | solution.py:579
  106.5 2.2 %cover.1 = f32[128,2048]{1,0:T(8,128)} custom-call(f32[8,1024]{1,0:T(8,128)S(1)} %reduce_sum.9.means_ref, f32[8,1024]{1,0:T(8,128)S(1)} %collective-permute-done.14.others_ref, f32[128,512]{1,0:T(8,128)S(1)} %get-tuple-element.76.refs_0_, f32[128,256]{1,0:T(8,128)S(1)} %close.4.refs_1_, f32[128,384]{1,0:T(8,128)S(1)} %get-tuple-element.84.refs_2_, ...), custom_call_target="tpu_custom_call" | custom-call | tf_op jit(solution)/shard_map/cover/pallas_call | solution.py:549
  (35 shorter events, 0.2 us)
Async XLA Ops:
  0.6 23.2 %copy-start = (bf16[1024,1024]{1,0:T(8,128)(2,1)S(1)}, bf16[1024,1024]{1,0:T(8,128)(2,1)}, u32[]{:S(2)}) copy-start(bf16[1024,1024]{1,0:T(8,128)(2,1)} %k_ref.3) | copy-start | bytes 6291460
  0.6 23.2 %copy-start.1 = (bf16[1024,1024]{1,0:T(8,128)(2,1)S(1)}, bf16[1024,1024]{1,0:T(8,128)(2,1)}, u32[]{:S(2)}) copy-start(bf16[1024,1024]{1,0:T(8,128)(2,1)} %v_ref.3) | copy-start | bytes 6291460
  0.7 23.2 %copy-start.5 = (f32[8,1024]{1,0:T(8,128)S(1)}, f32[8,1024]{1,0:T(8,128)}, u32[]{:S(2)}) copy-start(f32[8,1024]{1,0:T(8,128)} %decay_ref.5) | copy-start | bytes 98308
  7.2 6.8 %collective-permute-start = (f32[264,128]{1,0:T(8,128)}, f32[264,128]{1,0:T(8,128)S(1)}, u32[]{:S(2)}, u32[]{:S(2)}) collective-permute-start(f32[264,128]{1,0:T(8,128)} %get-tuple-element.48), channel_id=1, source_target_pairs={{0,4},{4,0},{8,12},{12,8},{16,20},{20,16},{24,28},{28,24},{1,5},{5... | collective-permute-start | bytes 405512 | tf_op jit(solution)/shard_map/ppermute | solution.py:568
  10.2 6.7 %collective-permute-start.1 = (f32[264,128]{1,0:T(8,128)}, f32[264,128]{1,0:T(8,128)S(1)}, u32[]{:S(2)}, u32[]{:S(2)}) collective-permute-start(f32[264,128]{1,0:T(8,128)} %get-tuple-element.49), channel_id=1, source_target_pairs={{0,8},{4,12},{8,0},{12,4},{16,24},{20,28},{24,16},{28,20},{1,9},{5... | collective-permute-start | bytes 405512 | tf_op jit(solution)/shard_map/ppermute | solution.py:568
  11.8 6.4 %collective-permute-start.2 = (f32[264,128]{1,0:T(8,128)}, f32[264,128]{1,0:T(8,128)S(1)}, u32[]{:S(2)}, u32[]{:S(2)}) collective-permute-start(f32[264,128]{1,0:T(8,128)} %get-tuple-element.50), channel_id=1, source_target_pairs={{0,12},{4,8},{8,4},{12,0},{16,28},{20,24},{24,20},{28,16},{1,13},{... | collective-permute-start | bytes 405512 | tf_op jit(solution)/shard_map/ppermute | solution.py:568
  18.1 0.9 copy-start.6
  19.2 11.7 %collective-permute-start.3 = (f32[256,128]{1,0:T(8,128)S(1)}, f32[256,128]{1,0:T(8,128)S(1)}, u32[]{:S(2)}, u32[]{:S(2)}) collective-permute-start(f32[256,128]{1,0:T(8,128)S(1)} %get-tuple-element.53), channel_id=1, source_target_pairs={{0,16},{4,20},{8,24},{12,28},{1,17},{5,21},{9,25},{13,29},{2,18},{... | collective-permute-start | bytes 393224 | tf_op jit(solution)/shard_map/ppermute | solution.py:583
  23.8 1.6 %copy-start.2 = (bf16[1024,1024]{1,0:T(8,128)(2,1)S(1)}, bf16[1024,1024]{1,0:T(8,128)(2,1)}, u32[]{:S(2)}) copy-start(bf16[1024,1024]{1,0:T(8,128)(2,1)} %q_ref.3) | copy-start | bytes 6291460
  30.8 9.2 %copy-start.3 = (bf16[1024,1024]{1,0:T(8,128)(2,1)S(1)}, bf16[1024,1024]{1,0:T(8,128)(2,1)}, u32[]{:S(2)}) copy-start(bf16[1024,1024]{1,0:T(8,128)(2,1)} %q_ref.3) | copy-start | bytes 6291460
  30.8 9.1 %copy-start.4 = (f32[4,1024,128]{2,1,0:T(8,128)S(1)}, f32[4,1024,128]{2,1,0:T(8,128)}, u32[]{:S(2)}) copy-start(f32[4,1024,128]{2,1,0:T(8,128)} %get-tuple-element.45.entering_ref) | copy-start | bytes 6291460
  30.8 9.1 %copy-start.7 = (f32[4,8,128]{2,1,0:T(8,128)S(1)}, f32[4,8,128]{2,1,0:T(8,128)}, u32[]{:S(2)}) copy-start(f32[4,8,128]{2,1,0:T(8,128)} %get-tuple-element.46.before_ref) | copy-start | bytes 49156
  30.9 9.1 %copy-start.8 = (f32[1024]{0:T(1024)S(1)}, f32[1024]{0:T(1024)}, u32[]{:S(2)}) copy-start(f32[1024]{0:T(1024)} %param.9) | copy-start | bytes 12292
  30.9 6.4 %collective-permute-start.4 = (f32[256,128]{1,0:T(8,128)S(1)}, f32[256,128]{1,0:T(8,128)S(1)}, u32[]{:S(2)}, u32[]{:S(2)}) collective-permute-start(f32[256,128]{1,0:T(8,128)S(1)} %get-tuple-element.55), channel_id=1, source_target_pairs={{0,4},{4,0},{8,12},{12,8},{16,20},{20,16},{24,28},{28,24},{1,5},{5... | collective-permute-start | bytes 393224 | tf_op jit(solution)/shard_map/ppermute | solution.py:568
  32.5 5.0 %collective-permute-start.5 = (f32[256,128]{1,0:T(8,128)S(1)}, f32[256,128]{1,0:T(8,128)S(1)}, u32[]{:S(2)}, u32[]{:S(2)}) collective-permute-start(f32[256,128]{1,0:T(8,128)S(1)} %get-tuple-element.56), channel_id=1, source_target_pairs={{0,8},{4,12},{8,0},{12,4},{16,24},{20,28},{24,16},{28,20},{1,9},{5... | collective-permute-start | bytes 393224 | tf_op jit(solution)/shard_map/ppermute | solution.py:568
  34.1 5.9 %collective-permute-start.6 = (f32[256,128]{1,0:T(8,128)S(1)}, f32[256,128]{1,0:T(8,128)S(1)}, u32[]{:S(2)}, u32[]{:S(2)}) collective-permute-start(f32[256,128]{1,0:T(8,128)S(1)} %get-tuple-element.57), channel_id=1, source_target_pairs={{0,12},{4,8},{8,4},{12,0},{16,28},{20,24},{24,20},{28,16},{1,13},{... | collective-permute-start | bytes 393224 | tf_op jit(solution)/shard_map/ppermute | solution.py:568
  47.1 4.4 %collective-permute-start.7 = (bf16[1024,1024]{1,0:T(8,128)(2,1)S(1)}, bf16[1024,1024]{1,0:T(8,128)(2,1)}, u32[]{:S(2)}, u32[]{:S(2)}) collective-permute-start(bf16[1024,1024]{1,0:T(8,128)(2,1)S(1)} %get-tuple-element.58.own_ref), channel_id=1, source_target_pairs={{0,1},{1,0},{2,3},{3,2},{4,5},{5,4},{6,7},{7,6},{8,9},{9,8},{10,11... | collective-permute-start | bytes 6291464 | tf_op jit(solution)/shard_map/ppermute | solution.py:571
  55.0 15.2 %collective-permute-start.8 = (bf16[528,512]{1,0:T(8,128)(2,1)S(1)}, bf16[528,512]{1,0:T(8,128)(2,1)S(1)}, u32[]{:S(2)}, u32[]{:S(2)}) collective-permute-start(bf16[528,512]{1,0:T(8,128)(2,1)S(1)} %get-tuple-element.61), channel_id=1, source_target_pairs={{0,4},{4,0},{8,12},{12,8},{16,20},{20,16},{24,28},{28,24},{1,5},{5... | collective-permute-start | bytes 1622024 | tf_op jit(solution)/shard_map/ppermute | solution.py:568
  58.6 8.1 %collective-permute-start.9 = (bf16[512,256]{1,0:T(8,128)(2,1)S(1)}, bf16[512,256]{1,0:T(8,128)(2,1)S(1)}, u32[]{:S(2)}, u32[]{:S(2)}) collective-permute-start(bf16[512,256]{1,0:T(8,128)(2,1)S(1)} %get-tuple-element.63), channel_id=1, source_target_pairs={{0,8},{4,12},{8,0},{12,4},{16,24},{20,28},{24,16},{28,20},{1,9},{5... | collective-permute-start | bytes 786440 | tf_op jit(solution)/shard_map/ppermute | solution.py:568
  64.0 13.8 %collective-permute-start.12 = (bf16[512,384]{1,0:T(8,128)(2,1)S(1)}, bf16[512,384]{1,0:T(8,128)(2,1)S(1)}, u32[]{:S(2)}, u32[]{:S(2)}) collective-permute-start(bf16[512,384]{1,0:T(8,128)(2,1)S(1)} %get-tuple-element.69), channel_id=1, source_target_pairs={{0,4},{4,0},{8,12},{12,8},{16,20},{20,16},{24,28},{28,24},{1,5},{5... | collective-permute-start | bytes 1179656 | tf_op jit(solution)/shard_map/ppermute | solution.py:568
  70.3 10.3 %collective-permute-start.10 = (bf16[272,512]{1,0:T(8,128)(2,1)S(1)}, bf16[272,512]{1,0:T(8,128)(2,1)S(1)}, u32[]{:S(2)}, u32[]{:S(2)}) collective-permute-start(bf16[272,512]{1,0:T(8,128)(2,1)S(1)} %get-tuple-element.66), channel_id=1, source_target_pairs={{0,8},{4,12},{8,0},{12,4},{16,24},{20,28},{24,16},{28,20},{1,9},{5... | collective-permute-start | bytes 835592 | tf_op jit(solution)/shard_map/ppermute | solution.py:568
  70.8 7.7 %collective-permute-start.11 = (bf16[256,256]{1,0:T(8,128)(2,1)S(1)}, bf16[256,256]{1,0:T(8,128)(2,1)S(1)}, u32[]{:S(2)}, u32[]{:S(2)}) collective-permute-start(bf16[256,256]{1,0:T(8,128)(2,1)S(1)} %get-tuple-element.67), channel_id=1, source_target_pairs={{0,16},{4,20},{8,24},{12,28},{16,0},{20,4},{24,8},{28,12},{1,17},{... | collective-permute-start | bytes 393224 | tf_op jit(solution)/shard_map/ppermute | solution.py:568
  77.9 8.5 %collective-permute-start.16 = (bf16[256,384]{1,0:T(8,128)(2,1)S(1)}, bf16[256,384]{1,0:T(8,128)(2,1)S(1)}, u32[]{:S(2)}, u32[]{:S(2)}) collective-permute-start(bf16[256,384]{1,0:T(8,128)(2,1)S(1)} %get-tuple-element.78), channel_id=1, source_target_pairs={{0,8},{4,12},{8,0},{12,4},{16,24},{20,28},{24,16},{28,20},{1,9},{5... | collective-permute-start | bytes 589832 | tf_op jit(solution)/shard_map/ppermute | solution.py:568
  80.7 12.3 %collective-permute-start.13 = (bf16[160,512]{1,0:T(8,128)(2,1)S(1)}, bf16[160,512]{1,0:T(8,128)(2,1)S(1)}, u32[]{:S(2)}, u32[]{:S(2)}) collective-permute-start(bf16[160,512]{1,0:T(8,128)(2,1)S(1)} %get-tuple-element.74), channel_id=1, source_target_pairs={{0,16},{4,20},{8,24},{12,28},{16,0},{20,4},{24,8},{28,12},{1,17},{... | collective-permute-start | bytes 491528 | tf_op jit(solution)/shard_map/ppermute | solution.py:568
  82.1 4.3 %collective-permute-start.15 = (bf16[128,256]{1,0:T(8,128)(2,1)S(1)}, bf16[128,256]{1,0:T(8,128)(2,1)S(1)}, u32[]{:S(2)}, u32[]{:S(2)}) collective-permute-start(bf16[128,256]{1,0:T(8,128)(2,1)S(1)} %get-tuple-element.77), channel_id=1, source_target_pairs={{0,4},{4,0},{8,12},{12,8},{16,20},{20,16},{24,28},{28,24},{1,5},{5... | collective-permute-start | bytes 196616 | tf_op jit(solution)/shard_map/ppermute | solution.py:568
  86.5 7.7 %collective-permute-start.17 = (bf16[128,384]{1,0:T(8,128)(2,1)S(1)}, bf16[128,384]{1,0:T(8,128)(2,1)S(1)}, u32[]{:S(2)}, u32[]{:S(2)}) collective-permute-start(bf16[128,384]{1,0:T(8,128)(2,1)S(1)} %get-tuple-element.80), channel_id=1, source_target_pairs={{0,16},{4,20},{8,24},{12,28},{16,0},{20,4},{24,8},{28,12},{1,17},{... | collective-permute-start | bytes 294920 | tf_op jit(solution)/shard_map/ppermute | solution.py:568
  93.0 7.0 %collective-permute-start.18 = (bf16[128,256]{1,0:T(8,128)(2,1)S(1)}, bf16[128,256]{1,0:T(8,128)(2,1)S(1)}, u32[]{:S(2)}, u32[]{:S(2)}) collective-permute-start(bf16[128,256]{1,0:T(8,128)(2,1)S(1)} %get-tuple-element.81), channel_id=1, source_target_pairs={{0,4},{4,8},{8,12},{12,16},{16,20},{20,24},{24,28},{28,0},{1,5},{5... | collective-permute-start | bytes 196616 | tf_op jit(solution)/shard_map/ppermute | solution.py:579
  93.2 6.8 %collective-permute-start.19 = (bf16[128,256]{1,0:T(8,128)(2,1)S(1)}, bf16[128,256]{1,0:T(8,128)(2,1)S(1)}, u32[]{:S(2)}, u32[]{:S(2)}) collective-permute-start(bf16[128,256]{1,0:T(8,128)(2,1)S(1)} %get-tuple-element.82), channel_id=1, source_target_pairs={{0,8},{4,12},{8,16},{12,20},{16,24},{20,28},{24,0},{28,4},{1,9},{5... | collective-permute-start | bytes 196616 | tf_op jit(solution)/shard_map/ppermute | solution.py:579
  93.2 6.8 %collective-permute-start.20 = (bf16[128,256]{1,0:T(8,128)(2,1)S(1)}, bf16[128,256]{1,0:T(8,128)(2,1)S(1)}, u32[]{:S(2)}, u32[]{:S(2)}) collective-permute-start(bf16[128,256]{1,0:T(8,128)(2,1)S(1)} %get-tuple-element.83), channel_id=1, source_target_pairs={{0,1},{1,0},{2,3},{3,2},{4,5},{5,4},{6,7},{7,6},{8,9},{9,8},{10,11... | collective-permute-start | bytes 196616 | tf_op jit(solution)/shard_map/ppermute | solution.py:571
  93.6 9.7 %collective-permute-start.14 = (f32[8,1024]{1,0:T(8,128)S(1)}, f32[8,1024]{1,0:T(8,128)S(1)}, u32[]{:S(2)}, u32[]{:S(2)}) collective-permute-start(f32[8,1024]{1,0:T(8,128)S(1)} %reduce_sum.9.means_ref), channel_id=1, source_target_pairs={{0,1},{1,0},{2,3},{3,2},{4,5},{5,4},{6,7},{7,6},{8,9},{9,8},{10,11... | collective-permute-start | bytes 98312 | tf_op jit(solution)/shard_map/ppermute | solution.py:571
  100.1 6.5 %collective-permute-start.21 = (bf16[128,256]{1,0:T(8,128)(2,1)S(1)}, bf16[128,256]{1,0:T(8,128)(2,1)S(1)}, u32[]{:S(2)}, u32[]{:S(2)}) collective-permute-start(bf16[128,256]{1,0:T(8,128)(2,1)S(1)} %get-tuple-element.85), channel_id=1, source_target_pairs={{0,12},{4,16},{8,20},{12,24},{16,28},{20,0},{24,4},{28,8},{1,13},{... | collective-permute-start | bytes 196616 | tf_op jit(solution)/shard_map/ppermute | solution.py:579
  100.1 6.4 %collective-permute-start.23 = (bf16[128,256]{1,0:T(8,128)(2,1)S(1)}, bf16[128,256]{1,0:T(8,128)(2,1)S(1)}, u32[]{:S(2)}, u32[]{:S(2)}) collective-permute-start(bf16[128,256]{1,0:T(8,128)(2,1)S(1)} %get-tuple-element.87), channel_id=1, source_target_pairs={{0,1},{1,0},{2,3},{3,2},{4,5},{5,4},{6,7},{7,6},{8,9},{9,8},{10,11... | collective-permute-start | bytes 196616 | tf_op jit(solution)/shard_map/ppermute | solution.py:571
  100.2 4.9 %collective-permute-start.22 = (bf16[128,128]{1,0:T(8,128)(2,1)S(1)}, bf16[128,128]{1,0:T(8,128)(2,1)S(1)}, u32[]{:S(2)}, u32[]{:S(2)}) collective-permute-start(bf16[128,128]{1,0:T(8,128)(2,1)S(1)} %get-tuple-element.86), channel_id=1, source_target_pairs={{0,16},{4,20},{8,24},{12,28},{16,0},{20,4},{24,8},{28,12},{1,17},{... | collective-permute-start | bytes 98312 | tf_op jit(solution)/shard_map/ppermute | solution.py:579

commit v4 on v3

--- a/solution.py
+++ b/solution.py
@@ -1,4 +1,5 @@
 import functools
+import math
 
 import jax
 import jax.numpy as jnp
@@ -37,6 +38,10 @@
     return pl.BlockSpec(memory_space=pltpu.VMEM)
 
 
+def hbm():
+    return pl.BlockSpec(memory_space=pltpu.HBM)
+
+
 def struct(shape, dtype):
     return jax.ShapeDtypeStruct(shape, dtype)
 
@@ -57,51 +62,124 @@
     return jnp.dot(decay, ones, precision=HIGHEST, preferred_element_type=F32)
 
 
+def span_at(first, start=0, size=SPAN):
+    if isinstance(first, int):
+        return slice(first + start, first + start + size)
+    return pl.ds(pl.multiple_of(first + start, math.gcd(start, SPAN)), size)
+
+
+def lines_at(ref, index, blocks):
+    heads = ref.shape[0] // blocks
+    return pl.ds(pl.multiple_of(index * heads, heads), heads)
+
+
+def fits(count, width):
+    return count * width <= 1 << 20
+
+
+def widen(value):
+    heads = value.shape[0]
+    first, rest = split(value)
+    second, third = split(value - first.astype(F32))
+    rows = lax.broadcasted_iota(jnp.int32, (heads, heads * HEAD_DIM), 0)
+    columns = lax.broadcasted_iota(jnp.int32, (heads, heads * HEAD_DIM), 1)
+    ones = jnp.where(columns // HEAD_DIM == rows, 1.0, 0.0)
+    pieces = [first.astype(F32), second.astype(F32), third.astype(F32)]
+    return lax.dot_general(
+        jnp.concatenate(pieces, axis=0).astype(BF16),
+        jnp.concatenate([ones] * 3, axis=0).astype(BF16),
+        (((0,), (0,)), ((), ())),
+        preferred_element_type=F32,
+    )
+
+
 def head_columns(head):
     return slice(head * HEAD_DIM, (head + 1) * HEAD_DIM)
 
 
-def states_kernel(near, k_ref, v_ref, decay_ref, entering_ref, before_ref, *rest):
-    pieces, (state, total) = rest[:near], rest[near:]
-    heads = decay_ref.shape[0]
-    step = pl.program_id(0)
-
-    @pl.when(step == 0)
-    def _():
-        state[...] = jnp.zeros_like(state)
-        total[...] = jnp.ones_like(total)
-
-    entering_ref[0] = state[...]
-    before_ref[0] = total[...]
-    cumul = running_sum(decay_ref[...])
+def states_block(k_ref, v_ref, first, cumul, state, total):
+    heads = cumul.shape[0]
     last = cumul[:, SPAN - 1 :]
     weight = jnp.exp(last - cumul)
     drop = jnp.exp(last)
+    rows = span_at(first)
     for group in range(0, heads, 4):
         members = range(group, min(group + 4, heads))
-        turned = [k_ref[:, head_columns(head)].T for head in members]
+        turned = [k_ref[rows, head_columns(head)].T for head in members]
         parts = []
         for head, key in zip(members, turned):
             high, low = split(key.astype(F32) * weight[head : head + 1, :])
             parts.append(jnp.concatenate([high, low], axis=0))
-        updates = [dot(part, v_ref[:, head_columns(head)]) for head, part in zip(members, parts)]
+        updates = [dot(part, v_ref[rows, head_columns(head)]) for head, part in zip(members, parts)]
         for head, update in zip(members, updates):
             cols = head_columns(head)
             update = update[:HEAD_DIM] + update[HEAD_DIM:]
             state[cols, :] = state[cols, :] * drop[head : head + 1, :] + update
     total[...] = total[...] * drop
 
+
+def states_out(near, state, total, pieces):
+    mine = lax.axis_index("ctx") % near
+    rows = state.shape[0] // near
+    for apart in range(near):
+        start = pl.multiple_of((mine ^ apart) * rows, rows)
+        pieces[apart][:rows, :] = state[pl.ds(start, rows), :]
+        pieces[apart][rows:, :] = jnp.zeros((8, HEAD_DIM), F32)
+        for head in range(rows // HEAD_DIM):
+            line = total[pl.ds(start // HEAD_DIM + head, 1), :]
+            pieces[apart][rows + head : rows + head + 1, :] = line
+
+
+def states_kernel(near, k_ref, v_ref, decay_ref, entering_ref, before_ref, cumul_ref, *rest):
+    pieces, (state, total) = rest[:near], rest[near:]
+    step = pl.program_id(0)
+
+    @pl.when(step == 0)
+    def _():
+        state[...] = jnp.zeros_like(state)
+        total[...] = jnp.ones_like(total)
+
+    entering_ref[0] = state[...]
+    before_ref[0] = total[...]
+    cumul_ref[...] = running_sum(decay_ref[...])
+    states_block(k_ref, v_ref, 0, cumul_ref[...], state, total)
+
     @pl.when(step == pl.num_programs(0) - 1)
     def _():
-        mine = lax.axis_index("ctx") % near
-        rows = heads * HEAD_DIM // near
-        for apart in range(near):
-            start = pl.multiple_of((mine ^ apart) * rows, rows)
-            pieces[apart][:rows, :] = state[pl.ds(start, rows), :]
-            pieces[apart][rows:, :] = jnp.zeros((8, HEAD_DIM), F32)
-            for head in range(rows // HEAD_DIM):
-                line = total[pl.ds(start // HEAD_DIM + head, 1), :]
-                pieces[apart][rows + head : rows + head + 1, :] = line
+        states_out(near, state, total, pieces)
+
+
+def states_fetch_kernel(near, k_any, v_any, decay_any, entering_ref, before_ref, cumul, *rest):
+    pieces, (k_ref, v_ref, decay_ref, state, total, sems) = rest[:near], rest[near:]
+    count = k_any.shape[0]
+    blocks = count // SPAN
+    heads = decay_ref.shape[0]
+
+    def fetch(source, target, index, which):
+        rows = span_at(index * SPAN)
+        return pltpu.make_async_copy(source.at[rows, :], target.at[rows, :], sems.at[which, index])
+
+    decays = pltpu.make_async_copy(decay_any, decay_ref, sems.at[2, 0])
+    decays.start()
+    for index in range(blocks):
+        fetch(k_any, k_ref, index, 0).start()
+        fetch(v_any, v_ref, index, 1).start()
+    state[...] = jnp.zeros_like(state)
+    total[...] = jnp.ones_like(total)
+    decays.wait()
+    lines = [decay_ref[:, index * SPAN : (index + 1) * SPAN] for index in range(blocks)]
+    cumul[...] = running_sum(jnp.concatenate(lines, axis=0))
+
+    @pl.loop(0, blocks)
+    def _(index):
+        fetch(k_any, k_ref, index, 0).wait()
+        fetch(v_any, v_ref, index, 1).wait()
+        entering_ref[index] = state[...]
+        before_ref[index] = total[...]
+        lines = cumul[pl.ds(pl.multiple_of(index * heads, heads), heads), :]
+        states_block(k_ref, v_ref, index * SPAN, lines, state, total)
+
+    states_out(near, state, total, pieces)
 
 
 def local_states(keys, values, log_decay, near):
@@ -110,7 +188,24 @@
     blocks = count // SPAN
     rows = width // near
     piece = (rows + 8, HEAD_DIM)
-    shapes = [(blocks, width, HEAD_DIM), (blocks, heads, HEAD_DIM)] + [piece] * near
+    shapes = [(blocks, width, HEAD_DIM), (blocks, heads, HEAD_DIM), (blocks * heads, SPAN)]
+    shapes += [piece] * near
+    scratch = [pltpu.VMEM((width, HEAD_DIM), F32), pltpu.VMEM((heads, HEAD_DIM), F32)]
+    if fits(count, width):
+        kept = [struct(value.shape, value.dtype) for value in (keys, values)]
+        out = pl.pallas_call(
+            functools.partial(states_fetch_kernel, near),
+            in_specs=[hbm()] * 3,
+            out_specs=[vmem()] * (len(shapes) + 2),
+            out_shape=[struct(shape, F32) for shape in shapes] + kept,
+            scratch_shapes=[pltpu.VMEM((heads, count), F32)]
+            + scratch
+            + [pltpu.SemaphoreType.DMA((3, blocks))],
+            compiler_params=params(48),
+            cost_estimate=cost(4 * count * width * HEAD_DIM, 4 * count * width),
+            name="local_states",
+        )(keys, values, log_decay)
+        return out[:3], out[3:-2], out[-2:]
     tokens = pl.BlockSpec((SPAN, width), lambda i: (i, 0))
     out = pl.pallas_call(
         functools.partial(states_kernel, near),
@@ -119,19 +214,20 @@
         out_specs=[
             pl.BlockSpec((1, width, HEAD_DIM), lambda i: (i, 0, 0)),
             pl.BlockSpec((1, heads, HEAD_DIM), lambda i: (i, 0, 0)),
+            pl.BlockSpec((heads, SPAN), lambda i: (i, 0)),
         ]
         + [whole(piece)] * near,
-        scratch_shapes=[pltpu.VMEM((width, HEAD_DIM), F32), pltpu.VMEM((heads, HEAD_DIM), F32)],
+        scratch_shapes=scratch,
         out_shape=[struct(shape, F32) for shape in shapes],
         compiler_params=params(56),
         cost_estimate=cost(4 * count * width * HEAD_DIM, 4 * count * width),
         name="local_states",
     )(keys, values, log_decay)
-    return out[0], out[1], out[2:]
+    return out[:3], out[3:], (keys, values)
 
 
 def chain_kernel(near, *refs):
-    arrived, (inside_ref, left_ref, leaving_ref, ordered) = refs[:near], refs[near:]
+    arrived, (inside_ref, left_ref, leaving_ref, ordered) = refs[:near], refs[near + 1 :]
     mine = lax.axis_index("ctx") % near
     rows = leaving_ref.shape[0]
     heads = rows // HEAD_DIM
@@ -151,22 +247,22 @@
         leaving_ref[cols, :] = carried
 
 
-def chain(pieces):
+def chain(pieces, after):
     near = len(pieces)
     rows = pieces[0].shape[0] - 8
     shapes = [(near, rows, HEAD_DIM), (near, 8, HEAD_DIM), (rows, HEAD_DIM)]
     return pl.pallas_call(
         functools.partial(chain_kernel, near),
-        in_specs=[vmem()] * near,
+        in_specs=[vmem()] * near + [anywhere()],
         out_specs=[vmem()] * 3,
         out_shape=[struct(shape, F32) for shape in shapes],
         scratch_shapes=[pltpu.VMEM((near, rows + 8, HEAD_DIM), F32)],
         compiler_params=params(16),
         name="chain",
-    )(*pieces)
-
-
-def spread_kernel(inside_ref, left_ref, entered_ref, _, *outs):
+    )(*pieces, after)
+
+
+def spread_kernel(inside_ref, left_ref, entered_ref, *outs):
     near, rows, _ = inside_ref.shape
     mine = lax.axis_index("ctx") % near
     for apart, out_ref in enumerate(outs):
@@ -178,26 +274,26 @@
             out_ref[cols, :] = inside_ref[shard, cols, :] + part
 
 
-def spread_states(inside, left, entered, after):
+def spread_states(inside, left, entered):
     near, rows, _ = inside.shape
     return pl.pallas_call(
         spread_kernel,
-        in_specs=[vmem()] * 3 + [anywhere()],
+        in_specs=[vmem()] * 3,
         out_specs=[vmem()] * near,
         out_shape=[struct((rows, HEAD_DIM), F32)] * near,
         compiler_params=params(16),
         name="spread_states",
-    )(inside, left, entered, after)
-
-
-def inner_kernel(q_ref, k_ref, v_ref, decay_ref, raw_ref):
-    heads = decay_ref.shape[0]
-    cumul = running_sum(decay_ref[...])
+    )(inside, left, entered)
+
+
+def inner_block(q_ref, k_ref, v_ref, first, cumul, raw_ref):
+    heads = cumul.shape[0]
     columns = cumul.T
     half = SPAN // 2
     for part in range(2):
-        rows = slice(part * half, (part + 1) * half)
+        rows = span_at(first, part * half, half)
         width = (part + 1) * half
+        seen = span_at(first, 0, width)
         token = lax.broadcasted_iota(jnp.int32, (half, width), 0) + part * half
         earlier = lax.broadcasted_iota(jnp.int32, (half, width), 1)
         for group in range(0, heads, 4):
@@ -205,7 +301,7 @@
             scores = [
                 lax.dot_general(
                     q_ref[rows, head_columns(head)],
-                    k_ref[:width, head_columns(head)],
+                    k_ref[seen, head_columns(head)],
                     (((1,), (1,)), ((), ())),
                     preferred_element_type=F32,
                 )
@@ -213,60 +309,80 @@
             ]
             weights = []
             for head, score in zip(members, scores):
-                diff = columns[rows, head : head + 1] - cumul[head : head + 1, :width]
+                column = columns[part * half : (part + 1) * half, head : head + 1]
+                diff = column - cumul[head : head + 1, :width]
                 factor = jnp.exp(jnp.where(token >= earlier, diff, -jnp.inf))
                 weights.append((score * factor).astype(BF16))
             for head, weight in zip(members, weights):
                 cols = head_columns(head)
-                raw_ref[rows, cols] = dot(weight, v_ref[:width, cols])
-
-
-def inner(queries, keys, values, log_decay):
+                raw_ref[rows, cols] = dot(weight, v_ref[seen, cols])
+
+
+def inner_kernel(q_ref, k_ref, v_ref, cumul_ref, raw_ref):
+    inner_block(q_ref, k_ref, v_ref, 0, cumul_ref[...], raw_ref)
+
+
+def inner_loop_kernel(q_ref, k_ref, v_ref, cumul_ref, raw_ref):
+    @pl.loop(0, q_ref.shape[0] // SPAN)
+    def _(index):
+        cumul = cumul_ref[lines_at(cumul_ref, index, q_ref.shape[0] // SPAN), :]
+        inner_block(q_ref, k_ref, v_ref, index * SPAN, cumul, raw_ref)
+
+
+def inner(queries, keys, values, cumul):
     count, width = keys.shape
     heads = width // HEAD_DIM
+    work = cost(4 * count * width * SPAN, 10 * count * width, count * heads * SPAN)
+    if fits(count, width):
+        return pl.pallas_call(
+            inner_loop_kernel,
+            in_specs=[vmem()] * 4,
+            out_specs=vmem(),
+            out_shape=struct((count, width), F32),
+            compiler_params=params(16),
+            cost_estimate=work,
+            name="inner",
+        )(queries, keys, values, cumul)
     tokens = pl.BlockSpec((SPAN, width), lambda i: (i, 0))
     return pl.pallas_call(
         inner_kernel,
         grid=(count // SPAN,),
-        in_specs=[tokens, tokens, tokens, pl.BlockSpec((heads, SPAN), lambda i: (0, i))],
+        in_specs=[tokens, tokens, tokens, pl.BlockSpec((heads, SPAN), lambda i: (i, 0))],
         out_specs=tokens,
         out_shape=struct((count, width), F32),
         compiler_params=params(24),
-        cost_estimate=cost(4 * count * width * SPAN, 10 * count * width, count * heads * SPAN),
+        cost_estimate=work,
         name="inner",
-    )(queries, keys, values, log_decay)
-
-
-def finish_kernel(
-    near, q_ref, raw_ref, entering_ref, before_ref, decay_ref, gain_ref, *rest
+    )(queries, keys, values, cumul)
+
+
+def finish_start(near, pieces, arrived, sums):
+    mine = lax.axis_index("ctx") % near
+    rows = arrived.shape[0] // near
+    width = sums.shape[1]
+    for apart in range(near):
+        start = pl.multiple_of((mine ^ apart) * rows, rows)
+        arrived[pl.ds(start, rows), :] = pieces[apart][...]
+    sums[0:8, :] = jnp.zeros((8, width), F32)
+    sums[8:16, :] = jnp.full((8, width), -jnp.inf, F32)
+    sums[16:24, :] = jnp.full((8, width), jnp.inf, F32)
+
+
+def finish_block(
+    q_ref, raw_ref, first, entering_ref, before_ref, cumul, gain_ref, centered_ref, here, arrived, sums
 ):
-    pieces, (centered_ref, stats_ref, arrived, sums) = rest[:near], rest[near:]
-    heads = decay_ref.shape[0]
-    width = heads * HEAD_DIM
-    rows = width // near
-    step = pl.program_id(0)
-    blocks = pl.num_programs(0)
-    count = centered_ref.shape[0]
-
-    @pl.when(step == 0)
-    def _():
-        mine = lax.axis_index("ctx") % near
-        for apart in range(near):
-            start = pl.multiple_of((mine ^ apart) * rows, rows)
-            arrived[pl.ds(start, rows), :] = pieces[apart][...]
-        sums[0:8, :] = jnp.zeros((8, width), F32)
-        sums[8:16, :] = jnp.full((8, width), -jnp.inf, F32)
-        sums[16:24, :] = jnp.full((8, width), jnp.inf, F32)
-
-    factor = jnp.exp(running_sum(decay_ref[...])).T
-    here = pl.ds(pl.multiple_of(step * SPAN, SPAN), SPAN)
+    heads = cumul.shape[0]
+    rows = span_at(first)
+    block = 0 if isinstance(first, int) else first // SPAN
+    factor = widen(jnp.exp(cumul))
     for group in range(0, heads, 4):
         members = range(group, min(group + 4, heads))
         outers = []
         for head in members:
             cols = head_columns(head)
-            state = entering_ref[0, cols, :] + before_ref[0, head : head + 1, :] * arrived[cols, :]
-            query = q_ref[:, cols]
+            left = before_ref[block, head : head + 1, :]
+            state = entering_ref[block, cols, :] + left * arrived[cols, :]
+            query = q_ref[rows, cols]
             outers.append(
                 dot(
                     jnp.concatenate([query, query], axis=1),
@@ -275,37 +391,108 @@
             )
         for head, outer in zip(members, outers):
             cols = head_columns(head)
-            raw = raw_ref[:, cols] + outer * factor[:, head : head + 1]
+            raw = raw_ref[rows, cols] + outer * factor[:, cols]
             power = jnp.mean(raw * raw, axis=1, keepdims=True)
             attended = (raw * lax.rsqrt(power + 1e-06) * gain_ref[:, cols]).astype(BF16)
             centered_ref[here, cols] = attended
             wide = attended.astype(F32).reshape(SPAN // 8, 8, HEAD_DIM)
+            sums[0:8, cols] += jnp.sum(wide, axis=0)
             sums[8:16, cols] = jnp.maximum(sums[8:16, cols], jnp.max(wide, axis=0))
             sums[16:24, cols] = jnp.minimum(sums[16:24, cols], jnp.min(wide, axis=0))
-    sums[0:8, :] += dot(jnp.ones((8, SPAN), BF16), centered_ref[here, :])
-
-    @pl.when(step == blocks - 1)
+
+
+def finish_end(centered_ref, stats_ref, sums):
+    count, width = centered_ref.shape
+    mean = jnp.sum(sums[0:8, :], axis=0, keepdims=True) / count
+    first, rest = split(mean)
+    rest = mean - first.astype(F32)
+    second, third = split(rest)
+    top = jnp.max(sums[8:16, :], axis=0, keepdims=True)
+    bottom = jnp.min(sums[16:24, :], axis=0, keepdims=True)
+    lines = [first.astype(F32), second.astype(F32), third.astype(F32), top, bottom]
+    lines.append(jnp.zeros((11, width), F32))
+    stats_ref[...] = jnp.concatenate(lines, axis=0).astype(BF16)
+
+    @pl.loop(0, count // 128)
+    def _(index):
+        part = pl.ds(pl.multiple_of(index * 128, 128), 128)
+        centered_ref[part, :] = (centered_ref[part, :].astype(F32) - mean).astype(BF16)
+
+
+def finish_kernel(
+    near, q_ref, raw_ref, entering_ref, before_ref, cumul_ref, gain_ref, *rest
+):
+    pieces, (centered_ref, stats_ref, arrived, sums) = rest[:near], rest[near:]
+    step = pl.program_id(0)
+
+    @pl.when(step == 0)
     def _():
-        mean = sums[0:1, :] / count
-        first, rest = split(mean)
-        rest = mean - first.astype(F32)
-        second, third = split(rest)
-        top = jnp.max(sums[8:16, :], axis=0, keepdims=True)
-        bottom = jnp.min(sums[16:24, :], axis=0, keepdims=True)
-        lines = [first.astype(F32), second.astype(F32), third.astype(F32), top, bottom]
-        lines.append(jnp.zeros((11, width), F32))
-        stats_ref[...] = jnp.concatenate(lines, axis=0).astype(BF16)
-
-        @pl.loop(0, count // 128)
-        def _(index):
-            part = pl.ds(pl.multiple_of(index * 128, 128), 128)
-            centered_ref[part, :] = (centered_ref[part, :].astype(F32) - mean).astype(BF16)
-
-
-def finish(queries, raw, entering, before, log_decay, gain, pieces):
+        finish_start(near, pieces, arrived, sums)
+
+    finish_block(
+        q_ref,
+        raw_ref,
+        0,
+        entering_ref,
+        before_ref,
+        cumul_ref[...],
+        gain_ref,
+        centered_ref,
+        span_at(step * SPAN),
+        arrived,
+        sums,
+    )
+
+    @pl.when(step == pl.num_programs(0) - 1)
+    def _():
+        finish_end(centered_ref, stats_ref, sums)
+
+
+def finish_loop_kernel(
+    near, q_ref, raw_ref, entering_ref, before_ref, cumul_ref, gain_ref, *rest
+):
+    pieces, (centered_ref, stats_ref, arrived, sums) = rest[:near], rest[near:]
+    finish_start(near, pieces, arrived, sums)
+
+    @pl.loop(0, q_ref.shape[0] // SPAN)
+    def _(index):
+        here = span_at(index * SPAN)
+        finish_block(
+            q_ref,
+            raw_ref,
+            index * SPAN,
+            entering_ref,
+            before_ref,
+            cumul_ref[lines_at(cumul_ref, index, q_ref.shape[0] // SPAN), :],
+            gain_ref,
+            centered_ref,
+            here,
+            arrived,
+            sums,
+        )
+
+    finish_end(centered_ref, stats_ref, sums)
+
+
+def finish(queries, raw, entering, before, cumul, gain, pieces):
     count, width = queries.shape
     heads = width // HEAD_DIM
     near = len(pieces)
+    shapes = [struct((count, width), BF16), struct((16, width), BF16)]
+    scratch = [pltpu.VMEM((width, HEAD_DIM), F32), pltpu.VMEM((24, width), F32)]
+    work = cost(4 * count * width * HEAD_DIM, 10 * count * width)
+    operands = (queries, raw, entering, before, cumul, gain, *pieces)
+    if fits(count, width):
+        return pl.pallas_call(
+            functools.partial(finish_loop_kernel, near),
+            in_specs=[vmem()] * len(operands),
+            out_specs=[vmem()] * 2,
+            scratch_shapes=scratch,
+            out_shape=shapes,
+            compiler_params=params(16),
+            cost_estimate=work,
+            name="finish",
+        )(*operands)
     tokens = pl.BlockSpec((SPAN, width), lambda i: (i, 0))
     return pl.pallas_call(
         functools.partial(finish_kernel, near),
@@ -315,17 +502,17 @@
             tokens,
             pl.BlockSpec((1, width, HEAD_DIM), lambda i: (i, 0, 0)),
             pl.BlockSpec((1, heads, HEAD_DIM), lambda i: (i, 0, 0)),
-            pl.BlockSpec((heads, SPAN), lambda i: (0, i)),
+            pl.BlockSpec((heads, SPAN), lambda i: (i, 0)),
             whole((1, width)),
         ]
         + [whole(pieces[0].shape)] * near,
         out_specs=[whole((count, width)), whole((16, width))],
-        scratch_shapes=[pltpu.VMEM((width, HEAD_DIM), F32), pltpu.VMEM((24, width), F32)],
-        out_shape=[struct((count, width), BF16), struct((16, width), BF16)],
+        scratch_shapes=scratch,
+        out_shape=shapes,
         compiler_params=params(32),
-        cost_estimate=cost(4 * count * width * HEAD_DIM, 10 * count * width),
+        cost_estimate=work,
         name="finish",
-    )(queries, raw, entering, before, log_decay, gain, *pieces)
+    )(*operands)
 
 
 def places(count, inner, bit):
@@ -397,11 +584,12 @@
         send = lax.dynamic_index_in_dim(parts, 1 - bit, 1, False).reshape(kept)
         return keep, jnp.concatenate([send.astype(BF16)] + extra)
     sent = (kept[0] + sum(value.shape[0] for value in extra), size)
+    last = max(step for step, _ in blocks)
     return pl.pallas_call(
         functools.partial(gram_kernel, rows, blocks, apart),
         in_specs=[vmem()] * (2 + len(extra)) + [anywhere()],
         out_specs=[vmem(), vmem()],
-        scratch_shapes=[pltpu.VMEM((width + max(step for step, _ in blocks) * rows, count), BF16)],
+        scratch_shapes=[pltpu.VMEM((width + last * rows, count), BF16)],
         out_shape=[struct(kept, F32), struct(sent, BF16)],
         compiler_params=params(16),
         cost_estimate=cost(2 * count * width * size, 4 * count * width),
@@ -578,13 +766,15 @@
     def forward(value, step):
         return lax.ppermute(value, "ctx", [(a, (a + step) % shards) for a in range(shards)])
 
-    entering, before, pieces = local_states(keys, values, log_decay, near)
-    inside, left, leaving = chain(nearby(pieces))
+    (entering, before, cumul), pieces, (keys, values) = local_states(
+        keys, values, log_decay, near
+    )
+    raw = inner(queries, keys, values, cumul)
+    inside, left, leaving = chain(nearby(pieces), raw)
     entered = lax.ppermute(leaving, "ctx", [(a, a + near) for a in range(near)])
-    raw = inner(queries, keys, values, log_decay)
-    entry = nearby(spread_states(inside, left, entered, raw))
+    entry = nearby(spread_states(inside, left, entered))
     centered, stats = finish(
-        queries, raw, entering, before, log_decay, gain.reshape(1, width), entry
+        queries, raw, entering, before, cumul, gain.reshape(1, width), entry
     )
     partner = to_partner(centered)
 
@@ -594,40 +784,44 @@
     extra = stats[:5].reshape(mean_rows + 4, lines)
     extra = jnp.pad(extra, ((0, -extra.shape[0] % 16), (0, 0)))
     bits = [1 << place for place in range(shards.bit_length() - 1)]
-    near = range(1, half // 2 + 1)
-    far = range(half // 2 + 1, half)
+    near_steps = range(1, half // 2 + 1)
+    far_steps = range(half // 2 + 1, half)
+    bits = [1 << place for place in range(shards.bit_length() - 1)]
     plans = [
-        ([(step, side) for step in near for side in (0, 1)], bits),
+        ([(step, side) for step in near_steps for side in (0, 1)], bits),
         ([(0, 0), (0, 1)], bits[1:] + bits[:1]),
-        ([(step, side) for step in far for side in (0, 1)] + [(half, 2)], bits),
+        ([(step, side) for step in far_steps for side in (0, 1)] + [(half, 2)], bits),
     ]
     kept, riders, after = [], [extra], stats
     for blocks, turns in plans:
-        keep, send = gram_parts(
-            centered, partner, [] if kept else riders, after, rows, blocks, turns[0]
-        )
+        carried = [] if kept else riders
+        keep, send = gram_parts(centered, partner, carried, after, rows, blocks, turns[0])
         after = keep
         kept.append((keep, to_shard(send, turns[0])))
-    def split_on(index, after):
+
+    def split_on(index, stage, after):
         keep, other = kept[index]
         turns = plans[index][1]
-        stage = stages[index]
         left = [bit for bit in bits if bit not in turns[:stage]]
-        inner_blocks = 1 << left.index(turns[stage])
         carried = riders if index == 0 else []
         keep, send, *merged = fold(
-            keep, other, after, carried, mean_rows << (stage - 1), rows, inner_blocks, turns[stage]
+            keep,
+            other,
+            after,
+            carried,
+            mean_rows << (stage - 1),
+            rows,
+            1 << left.index(turns[stage]),
+            turns[stage],
         )
         riders[:] = merged or riders
         kept[index] = (keep, to_shard(send, turns[stage]))
-        stages[index] += 1
         return keep
 
-    stages = [1] * len(plans)
     after = kept[0][0]
     for stage in range(1, len(bits)):
         for index in (1, 0, 2):
-            after = split_on(index, after)
+            after = split_on(index, stage, after)
 
     chunks, mirrors, mirror_names, crossed, crossed_names = [None] * len(plans), [], [], [], []
     for index in (0, 1, 2):

time: 109 us -> 102 us (0.936)
  waiting for transfers between devices: 46.6 us -> 31.9 us
  starting transfers between devices: 25.4 us -> 39.5 us
  Pallas kernels: 32.3 us -> 26.2 us
    ppermute x15, waiting for transfers between devices: 33.3 us -> 18 us  [to_shard(): return lax.ppermute(value, 'ctx', [(a, a ^ apart) for a in range(shards)])]
    ppermute x15, starting transfers between devices: 17.3 us -> 24.9 us  [to_shard(): return lax.ppermute(value, 'ctx', [(a, a ^ apart) for a in range(shards)])]
    ppermute x4, starting transfers between devices: 2.74 us -> 9.04 us  [forward(): lax.ppermute(value, 'ctx', [(a, (a + step) % shards) for a in range(shard...]
    pallas_call x4, Pallas kernels: 19 us -> 13.1 us  [the longest x1 4.54 us: inner(): pl.pallas_call(inner_loop_kernel, in_specs=[vmem()] * 4, out_specs=vmem()...]
    ppermute x1, waiting for transfers between devices: 0.01 us -> 2.51 us  [body(): entered = lax.ppermute(leaving, 'ctx', [(a, a + near) for a in range(near)])]
    ppermute x4, waiting for transfers between devices: 9.06 us -> 7.19 us  [forward(): lax.ppermute(value, 'ctx', [(a, (a + step) % shards) for a in range(shard...]
    unnamed x19 -> x9, local copies, waits for them, and re-layouts: 3.12 us -> 3.1 us
  transfers between devices with their start and end apart: 24 -> 24, of which waited for: 17 -> 15; matrix products, arithmetic and copies ran while one was open for 1% -> 1% of each run, Pallas kernels for 12% -> 11%
where the time goes in v4:
time: 102 us
  starting transfers between devices  39.5 us (39%)
  waiting for transfers between devices  31.9 us (31%)
  Pallas kernels  26.2 us (26%)
  local copies, waits for them, and re-layouts  3.36 us (3%)
    ppermute x15, starting transfers between devices, to_shard(): return lax.ppermute(value, 'ctx', [(a, a ^ apart) for a in range(shards)])  24.9 us
    ppermute x15, waiting for transfers between devices, to_shard(): return lax.ppermute(value, 'ctx', [(a, a ^ apart) for a in range(shards)])  18 us
    pallas_call x3, Pallas kernels, gram_parts(): pl.pallas_call(functools.partial(gram_kernel, rows, blocks, apart), in_sp...  10.3 us
    ppermute x4, starting transfers between devices, forward(): lax.ppermute(value, 'ctx', [(a, (a + step) % shards) for a in range(shard...  9.04 us
    ppermute x4, waiting for transfers between devices, forward(): lax.ppermute(value, 'ctx', [(a, (a + step) % shards) for a in range(shard...  7.19 us
    ppermute x1, starting transfers between devices, body(): entered = lax.ppermute(leaving, 'ctx', [(a, a + near) for a in range(near)])  4.9 us
    pallas_call x1, Pallas kernels, inner(): pl.pallas_call(inner_loop_kernel, in_specs=[vmem()] * 4, out_specs=vmem()...  4.54 us
    pallas_call x1, Pallas kernels, local_states(): pl.pallas_call(functools.partial(states_fetch_kernel, near), in_specs=[hb...  4.36 us
  transfers between devices with their start and end apart: 24, of which 15 were waited for; matrix products, arithmetic and copies ran while one was open for 1% of the time, Pallas kernels for 11%

profile of v4, /device:TPU:0, one launch (start us, length us, event | category | flops | bytes accessed | tf_op | source)
XLA Modules:
  0.0 102.0 jit_solution(3908810187104191457)
XLA Ops:
  0.7 0.9 copy-done.2
  1.5 4.4 %local_states.1 = (f32[4,1024,128]{2,1,0:T(8,128)S(1)}, f32[4,8,128]{2,1,0:T(8,128)S(1)}, f32[32,256]{1,0:T(8,128)S(1)}, f32[264,128]{1,0:T(8,128)S(1)}, f32[264...) custom-call(bf16[1024,1024]{1,0:T(8,128)(2,1)} %k_any.1, ...), custom_call_target="tpu_custom_call" | custom-call | flops 536870912 | bytes 4194304 | tf_op jit(solution)/shard_map/local_states/pallas_call | solution.py:196
  5.9 3.0 %collective-permute-start = (f32[264,128]{1,0:T(8,128)S(1)}, f32[264,128]{1,0:T(8,128)S(1)}, u32[]{:S(2)}, u32[]{:S(2)}) collective-permute-start(f32[264,128]{1,0:T(8,128)S(1)} %get-tuple-element.54), channel_id=1, source_target_pairs={{0,4},{4,0},{8,12},{12,8},{16,20},{20,16},{24,28},{28,24},{1,5},{5... | collective-permute-start | bytes 405512 | tf_op jit(solution)/shard_map/ppermute | solution.py:756
  8.9 1.6 %collective-permute-start.1 = (f32[264,128]{1,0:T(8,128)S(1)}, f32[264,128]{1,0:T(8,128)S(1)}, u32[]{:S(2)}, u32[]{:S(2)}) collective-permute-start(f32[264,128]{1,0:T(8,128)S(1)} %get-tuple-element.55), channel_id=1, source_target_pairs={{0,8},{4,12},{8,0},{12,4},{16,24},{20,28},{24,16},{28,20},{1,9},{5... | collective-permute-start | bytes 405512 | tf_op jit(solution)/shard_map/ppermute | solution.py:756
  10.5 0.0 collective-permute-start.2
  10.5 1.6 %copy-done.1 = bf16[1024,1024]{1,0:T(8,128)(2,1)S(1)} copy-done((bf16[1024,1024]{1,0:T(8,128)(2,1)S(1)}, bf16[1024,1024]{1,0:T(8,128)(2,1)}, u32[]{:S(2)}) %copy-start.1) | copy-done | bytes 2097176
  12.1 4.5 %inner.1.refs_4_.raw_ref = f32[1024,1024]{1,0:T(8,128)S(1)} custom-call(bf16[1024,1024]{1,0:T(8,128)(2,1)S(1)} %copy-done, bf16[1024,1024]{1,0:T(8,128)(2,1)S(1)} %get-tuple-element.48.k_ref, bf16[1024,1024]{1,0:T(8,128)(2,1)S(1)} %copy-done.1, f32[32,256]{1,0:T(8,128)S(1)} %get-tuple-element.50.cumul_ref), custom_call_target="tpu_custom_call" | custom-call | flops 1073741824 | bytes 10485760 | tf_op jit(solution)/shard_map/inner/pallas_call | solution.py:337
  16.7 0.0 collective-permute-done.refs_1_
  16.7 0.0 collective-permute-done.1.refs_2_
  16.7 0.0 copy-start.3
  16.7 0.1 chain.1
  16.8 4.9 %collective-permute-start.3 = (f32[256,128]{1,0:T(8,128)S(1)}, f32[256,128]{1,0:T(8,128)S(1)}, u32[]{:S(2)}, u32[]{:S(2)}) collective-permute-start(f32[256,128]{1,0:T(8,128)S(1)} %get-tuple-element.59), channel_id=1, source_target_pairs={{0,16},{4,20},{8,24},{12,28},{1,17},{5,21},{9,25},{13,29},{2,18},{... | collective-permute-start | bytes 393224 | tf_op jit(solution)/shard_map/ppermute | solution.py:774
  21.7 2.5 %collective-permute-done.3.entered_ref = f32[256,128]{1,0:T(8,128)S(1)} collective-permute-done((f32[256,128]{1,0:T(8,128)S(1)}, f32[256,128]{1,0:T(8,128)S(1)}, u32[]{:S(2)}, u32[]{:S(2)}) %collective-permute-start.3) | collective-permute-done | bytes 131104 | tf_op jit(solution)/shard_map/ppermute | solution.py:774
  24.2 0.1 spread_states.1
  24.3 1.6 %collective-permute-start.4 = (f32[256,128]{1,0:T(8,128)S(1)}, f32[256,128]{1,0:T(8,128)S(1)}, u32[]{:S(2)}, u32[]{:S(2)}) collective-permute-start(f32[256,128]{1,0:T(8,128)S(1)} %get-tuple-element.61), channel_id=1, source_target_pairs={{0,4},{4,0},{8,12},{12,8},{16,20},{20,16},{24,28},{28,24},{1,5},{5... | collective-permute-start | bytes 393224 | tf_op jit(solution)/shard_map/ppermute | solution.py:756
  25.9 3.7 %collective-permute-start.5 = (f32[256,128]{1,0:T(8,128)S(1)}, f32[256,128]{1,0:T(8,128)S(1)}, u32[]{:S(2)}, u32[]{:S(2)}) collective-permute-start(f32[256,128]{1,0:T(8,128)S(1)} %get-tuple-element.62), channel_id=1, source_target_pairs={{0,8},{4,12},{8,0},{12,4},{16,24},{20,28},{24,16},{28,20},{1,9},{5... | collective-permute-start | bytes 393224 | tf_op jit(solution)/shard_map/ppermute | solution.py:756
  29.5 0.0 collective-permute-start.6
  29.5 0.0 collective-permute-done.4.rest_1_
  29.5 4.2 %collective-permute-done.5.rest_2_ = f32[256,128]{1,0:T(8,128)S(1)} collective-permute-done((f32[256,128]{1,0:T(8,128)S(1)}, f32[256,128]{1,0:T(8,128)S(1)}, u32[]{:S(2)}, u32[]{:S(2)}) %collective-permute-start.5) | collective-permute-done | bytes 131104 | tf_op jit(solution)/shard_map/ppermute | solution.py:756
  33.7 1.7 %collective-permute-done.6.rest_3_ = f32[256,128]{1,0:T(8,128)S(1)} collective-permute-done((f32[256,128]{1,0:T(8,128)S(1)}, f32[256,128]{1,0:T(8,128)S(1)}, u32[]{:S(2)}, u32[]{:S(2)}) %collective-permute-start.6) | collective-permute-done | bytes 131104 | tf_op jit(solution)/shard_map/ppermute | solution.py:756
  35.4 4.2 %finish.1 = (bf16[1024,1024]{1,0:T(8,128)(2,1)S(1)}, bf16[16,1024]{1,0:T(8,128)(2,1)S(1)}) custom-call(bf16[1024,1024]{1,0:T(8,128)(2,1)S(1)} %copy-done, f32[1024,1024]{1,0:T(8,128)S(1)} %inner.1.refs_4_.raw_ref, f32[4,1024,128]{2,1,0:T(8,128)S(1)} %get-tuple-element.51.entering_ref, f32[4,8,128]{2,1,0:T(8,128)S(1)} %get-tuple-element.52.before_ref, ...), custom_call_target="tpu_custom_call" | custom-call | flops 536870912 | bytes 10485760 | tf_op jit(solution)/shard_map/finish/pallas_call | solution.py:486
  39.6 0.1 collective-permute-start.7
  39.7 4.2 %collective-permute-done.7.other_ref = bf16[1024,1024]{1,0:T(8,128)(2,1)} collective-permute-done((bf16[1024,1024]{1,0:T(8,128)(2,1)S(1)}, bf16[1024,1024]{1,0:T(8,128)(2,1)}, u32[]{:S(2)}, u32[]{:S(2)}) %collective-permute-start.7) | collective-permute-done | bytes 2097184 | tf_op jit(solution)/shard_map/ppermute | solution.py:759
  43.9 3.6 %gram.3 = (f32[512,512]{1,0:T(8,128)S(1)}, bf16[528,512]{1,0:T(8,128)(2,1)S(1)}) custom-call(bf16[1024,1024]{1,0:T(8,128)(2,1)S(1)} %get-tuple-element.64.own_ref, bf16[1024,1024]{1,0:T(8,128)(2,1)} %collective-permute-done.7.other_ref, bf16[16,512]{1,0:T(8,128)(2,1)S(1)} %pad.4.rest_0_, bf16[16,1024]{1,0:T(8,128)(2,1)S(1)} %get-tuple-element.65.rest_1_), custom_call_target="tpu_custom_call" | custom-call | flops 1073741824 | bytes 4194304 | tf_op jit(solution)/shard_map/gram/pallas_call | solution.py:588
  47.5 1.2 %collective-permute-start.8 = (bf16[528,512]{1,0:T(8,128)(2,1)S(1)}, bf16[528,512]{1,0:T(8,128)(2,1)S(1)}, u32[]{:S(2)}, u32[]{:S(2)}) collective-permute-start(bf16[528,512]{1,0:T(8,128)(2,1)S(1)} %get-tuple-element.67), channel_id=1, source_target_pairs={{0,4},{4,0},{8,12},{12,8},{16,20},{20,16},{24,28},{28,24},{1,5},{5... | collective-permute-start | bytes 1622024 | tf_op jit(solution)/shard_map/ppermute | solution.py:756
  48.8 3.0 %gram.4 = (f32[512,256]{1,0:T(8,128)S(1)}, bf16[512,256]{1,0:T(8,128)(2,1)S(1)}) custom-call(bf16[1024,1024]{1,0:T(8,128)(2,1)S(1)} %get-tuple-element.64.own_ref, bf16[1024,1024]{1,0:T(8,128)(2,1)} %collective-permute-done.7.other_ref, f32[512,512]{1,0:T(8,128)S(1)} %get-tuple-element.66.rest_0_._.keep_ref), custom_call_target="tpu_custom_call" | custom-call | flops 536870912 | bytes 4194304 | tf_op jit(solution)/shard_map/gram/pallas_call | solution.py:588
  51.7 1.8 %collective-permute-start.9 = (bf16[512,256]{1,0:T(8,128)(2,1)S(1)}, bf16[512,256]{1,0:T(8,128)(2,1)S(1)}, u32[]{:S(2)}, u32[]{:S(2)}) collective-permute-start(bf16[512,256]{1,0:T(8,128)(2,1)S(1)} %get-tuple-element.69), channel_id=1, source_target_pairs={{0,8},{4,12},{8,0},{12,4},{16,24},{20,28},{24,16},{28,20},{1,9},{5... | collective-permute-start | bytes 786440 | tf_op jit(solution)/shard_map/ppermute | solution.py:756
  53.6 3.7 %gram.5 = (f32[512,384]{1,0:T(8,128)S(1)}, bf16[512,384]{1,0:T(8,128)(2,1)S(1)}) custom-call(bf16[1024,1024]{1,0:T(8,128)(2,1)S(1)} %get-tuple-element.64.own_ref, bf16[1024,1024]{1,0:T(8,128)(2,1)} %collective-permute-done.7.other_ref, f32[512,256]{1,0:T(8,128)S(1)} %get-tuple-element.68.keep_ref.rest_0_), custom_call_target="tpu_custom_call" | custom-call | flops 805306368 | bytes 4194304 | tf_op jit(solution)/shard_map/gram/pallas_call | solution.py:588
  57.3 0.5 collective-permute-start.12
  57.8 2.0 %collective-permute-done.9.other_ref = bf16[512,256]{1,0:T(8,128)(2,1)S(1)} collective-permute-done((bf16[512,256]{1,0:T(8,128)(2,1)S(1)}, bf16[512,256]{1,0:T(8,128)(2,1)S(1)}, u32[]{:S(2)}, u32[]{:S(2)}) %collective-permute-start.9) | collective-permute-done | bytes 262176 | tf_op jit(solution)/shard_map/ppermute | solution.py:756
  59.9 2.8 %collective-permute-done.8.other_ref = bf16[528,512]{1,0:T(8,128)(2,1)S(1)} collective-permute-done((bf16[528,512]{1,0:T(8,128)(2,1)S(1)}, bf16[528,512]{1,0:T(8,128)(2,1)S(1)}, u32[]{:S(2)}, u32[]{:S(2)}) %collective-permute-start.8) | collective-permute-done | bytes 540704 | tf_op jit(solution)/shard_map/ppermute | solution.py:756
  62.7 0.1 fold.7
  62.8 1.4 %collective-permute-start.10 = (bf16[272,512]{1,0:T(8,128)(2,1)S(1)}, bf16[272,512]{1,0:T(8,128)(2,1)S(1)}, u32[]{:S(2)}, u32[]{:S(2)}) collective-permute-start(bf16[272,512]{1,0:T(8,128)(2,1)S(1)} %get-tuple-element.72), channel_id=1, source_target_pairs={{0,8},{4,12},{8,0},{12,4},{16,24},{20,28},{24,16},{28,20},{1,9},{5... | collective-permute-start | bytes 835592 | tf_op jit(solution)/shard_map/ppermute | solution.py:756
  64.3 3.4 %collective-permute-start.11 = (bf16[256,256]{1,0:T(8,128)(2,1)S(1)}, bf16[256,256]{1,0:T(8,128)(2,1)S(1)}, u32[]{:S(2)}, u32[]{:S(2)}) collective-permute-start(bf16[256,256]{1,0:T(8,128)(2,1)S(1)} %get-tuple-element.73), channel_id=1, source_target_pairs={{0,16},{4,20},{8,24},{12,28},{16,0},{20,4},{24,8},{28,12},{1,17},{... | collective-permute-start | bytes 393224 | tf_op jit(solution)/shard_map/ppermute | solution.py:756
  67.6 2.7 %collective-permute-done.12.other_ref = bf16[512,384]{1,0:T(8,128)(2,1)S(1)} collective-permute-done((bf16[512,384]{1,0:T(8,128)(2,1)S(1)}, bf16[512,384]{1,0:T(8,128)(2,1)S(1)}, u32[]{:S(2)}, u32[]{:S(2)}) %collective-permute-start.12) | collective-permute-done | bytes 393248 | tf_op jit(solution)/shard_map/ppermute | solution.py:756
  70.3 0.1 fold.8
  70.4 1.4 %collective-permute-start.16 = (bf16[256,384]{1,0:T(8,128)(2,1)S(1)}, bf16[256,384]{1,0:T(8,128)(2,1)S(1)}, u32[]{:S(2)}, u32[]{:S(2)}) collective-permute-start(bf16[256,384]{1,0:T(8,128)(2,1)S(1)} %get-tuple-element.84), channel_id=1, source_target_pairs={{0,8},{4,12},{8,0},{12,4},{16,24},{20,28},{24,16},{28,20},{1,9},{5... | collective-permute-start | bytes 589832 | tf_op jit(solution)/shard_map/ppermute | solution.py:756
  71.8 0.1 collective-permute-done.11.other_ref
  72.0 1.1 %collective-permute-done.10.other_ref = bf16[272,512]{1,0:T(8,128)(2,1)S(1)} collective-permute-done((bf16[272,512]{1,0:T(8,128)(2,1)S(1)}, bf16[272,512]{1,0:T(8,128)(2,1)S(1)}, u32[]{:S(2)}, u32[]{:S(2)}) %collective-permute-start.10) | collective-permute-done | bytes 278560 | tf_op jit(solution)/shard_map/ppermute | solution.py:756
  73.1 0.1 fold.10
  73.2 2.4 %collective-permute-start.13 = (bf16[160,512]{1,0:T(8,128)(2,1)S(1)}, bf16[160,512]{1,0:T(8,128)(2,1)S(1)}, u32[]{:S(2)}, u32[]{:S(2)}) collective-permute-start(bf16[160,512]{1,0:T(8,128)(2,1)S(1)} %get-tuple-element.80), channel_id=1, source_target_pairs={{0,16},{4,20},{8,24},{12,28},{16,0},{20,4},{24,8},{28,12},{1,17},{... | collective-permute-start | bytes 491528 | tf_op jit(solution)/shard_map/ppermute | solution.py:756
  75.5 1.5 %collective-permute-start.15 = (bf16[128,256]{1,0:T(8,128)(2,1)S(1)}, bf16[128,256]{1,0:T(8,128)(2,1)S(1)}, u32[]{:S(2)}, u32[]{:S(2)}) collective-permute-start(bf16[128,256]{1,0:T(8,128)(2,1)S(1)} %get-tuple-element.83), channel_id=1, source_target_pairs={{0,4},{4,0},{8,12},{12,8},{16,20},{20,16},{24,28},{28,24},{1,5},{5... | collective-permute-start | bytes 196616 | tf_op jit(solution)/shard_map/ppermute | solution.py:756
  77.1 2.7 %collective-permute-done.15.other_ref = bf16[128,256]{1,0:T(8,128)(2,1)S(1)} collective-permute-done((bf16[128,256]{1,0:T(8,128)(2,1)S(1)}, bf16[128,256]{1,0:T(8,128)(2,1)S(1)}, u32[]{:S(2)}, u32[]{:S(2)}) %collective-permute-start.15) | collective-permute-done | bytes 65568 | tf_op jit(solution)/shard_map/ppermute | solution.py:756
  79.8 0.7 collective-permute-done.16.other_ref
  80.5 1.3 %collective-permute-start.17 = (bf16[128,384]{1,0:T(8,128)(2,1)S(1)}, bf16[128,384]{1,0:T(8,128)(2,1)S(1)}, u32[]{:S(2)}, u32[]{:S(2)}) collective-permute-start(bf16[128,384]{1,0:T(8,128)(2,1)S(1)} %get-tuple-element.86), channel_id=1, source_target_pairs={{0,16},{4,20},{8,24},{12,28},{16,0},{20,4},{24,8},{28,12},{1,17},{... | collective-permute-start | bytes 294920 | tf_op jit(solution)/shard_map/ppermute | solution.py:756
  81.8 0.0 collective-permute-done.13.other_ref
  81.8 0.1 close.3
  81.9 1.2 %collective-permute-start.18 = (bf16[128,256]{1,0:T(8,128)(2,1)S(1)}, bf16[128,256]{1,0:T(8,128)(2,1)S(1)}, u32[]{:S(2)}, u32[]{:S(2)}) collective-permute-start(bf16[128,256]{1,0:T(8,128)(2,1)S(1)} %get-tuple-element.87), channel_id=1, source_target_pairs={{0,4},{4,8},{8,12},{12,16},{16,20},{20,24},{24,28},{28,0},{1,5},{5... | collective-permute-start | bytes 196616 | tf_op jit(solution)/shard_map/ppermute | solution.py:767
  83.1 5.2 %collective-permute-start.19 = (bf16[128,256]{1,0:T(8,128)(2,1)S(1)}, bf16[128,256]{1,0:T(8,128)(2,1)S(1)}, u32[]{:S(2)}, u32[]{:S(2)}) collective-permute-start(bf16[128,256]{1,0:T(8,128)(2,1)S(1)} %get-tuple-element.88), channel_id=1, source_target_pairs={{0,8},{4,12},{8,16},{12,20},{16,24},{20,28},{24,0},{28,4},{1,9},{5... | collective-permute-start | bytes 196616 | tf_op jit(solution)/shard_map/ppermute | solution.py:767
  88.3 0.0 collective-permute-start.20
  88.3 0.2 concatenate.4
  88.5 0.1 reshape.23
  88.6 0.1 reduce_sum.9.means_ref
  88.7 0.6 collective-permute-start.14
  89.2 3.6 %collective-permute-done.18.rest_0_.refs_3_ = bf16[128,256]{1,0:T(8,128)(2,1)S(1)} collective-permute-done((bf16[128,256]{1,0:T(8,128)(2,1)S(1)}, bf16[128,256]{1,0:T(8,128)(2,1)S(1)}, u32[]{:S(2)}, u32[]{:S(2)}) %collective-permute-start.18) | collective-permute-done | bytes 65568 | tf_op jit(solution)/shard_map/ppermute | solution.py:767
  92.8 0.6 collective-permute-done.19.rest_1_.refs_4_
  93.4 0.0 collective-permute-done.20.rest_2_.refs_7_
  93.4 0.1 collective-permute-start.21
  93.6 2.5 %collective-permute-start.22 = (bf16[128,128]{1,0:T(8,128)(2,1)S(1)}, bf16[128,128]{1,0:T(8,128)(2,1)S(1)}, u32[]{:S(2)}, u32[]{:S(2)}) collective-permute-start(bf16[128,128]{1,0:T(8,128)(2,1)S(1)} %get-tuple-element.92), channel_id=1, source_target_pairs={{0,16},{4,20},{8,24},{12,28},{16,0},{20,4},{24,8},{28,12},{1,17},{... | collective-permute-start | bytes 98312 | tf_op jit(solution)/shard_map/ppermute | solution.py:767
  96.1 0.6 copy.7
  96.7 0.0 collective-permute-done.14.others_ref
  96.7 1.8 %collective-permute-done.22.refs_6_ = bf16[128,128]{1,0:T(8,128)(2,1)S(1)} collective-permute-done((bf16[128,128]{1,0:T(8,128)(2,1)S(1)}, bf16[128,128]{1,0:T(8,128)(2,1)S(1)}, u32[]{:S(2)}, u32[]{:S(2)}) %collective-permute-start.22) | collective-permute-done | bytes 32800 | tf_op jit(solution)/shard_map/ppermute | solution.py:767
  98.5 1.3 %collective-permute-done.21.refs_5_ = bf16[128,256]{1,0:T(8,128)(2,1)S(1)} collective-permute-done((bf16[128,256]{1,0:T(8,128)(2,1)S(1)}, bf16[128,256]{1,0:T(8,128)(2,1)S(1)}, u32[]{:S(2)}, u32[]{:S(2)}) %collective-permute-start.21) | collective-permute-done | bytes 65568 | tf_op jit(solution)/shard_map/ppermute | solution.py:767
  99.7 2.2 %cover.1 = f32[128,2048]{1,0:T(8,128)} custom-call(f32[8,1024]{1,0:T(8,128)S(1)} %reduce_sum.9.means_ref, f32[8,1024]{1,0:T(8,128)S(1)} %collective-permute-done.14.others_ref, f32[128,512]{1,0:T(8,128)S(1)} %get-tuple-element.82.refs_0_, f32[128,256]{1,0:T(8,128)S(1)} %close.4.refs_1_, f32[128,384]{1,0:T(8,128)S(1)} %get-tuple-element.90.refs_2_, ...), custom_call_target="tpu_custom_call" | custom-call | tf_op jit(solution)/shard_map/cover/pallas_call | solution.py:737
  (25 shorter events, 0.3 us)
Async XLA Ops:
  0.6 9.9 %copy-start = (bf16[1024,1024]{1,0:T(8,128)(2,1)S(1)}, bf16[1024,1024]{1,0:T(8,128)(2,1)}, u32[]{:S(2)}) copy-start(bf16[1024,1024]{1,0:T(8,128)(2,1)} %q_ref.3) | copy-start | bytes 6291460
  0.6 0.9 copy-start.2
  5.9 10.8 %collective-permute-start = (f32[264,128]{1,0:T(8,128)S(1)}, f32[264,128]{1,0:T(8,128)S(1)}, u32[]{:S(2)}, u32[]{:S(2)}) collective-permute-start(f32[264,128]{1,0:T(8,128)S(1)} %get-tuple-element.54), channel_id=1, source_target_pairs={{0,4},{4,0},{8,12},{12,8},{16,20},{20,16},{24,28},{28,24},{1,5},{5... | collective-permute-start | bytes 405512 | tf_op jit(solution)/shard_map/ppermute | solution.py:756
  8.9 7.7 %collective-permute-start.1 = (f32[264,128]{1,0:T(8,128)S(1)}, f32[264,128]{1,0:T(8,128)S(1)}, u32[]{:S(2)}, u32[]{:S(2)}) collective-permute-start(f32[264,128]{1,0:T(8,128)S(1)} %get-tuple-element.55), channel_id=1, source_target_pairs={{0,8},{4,12},{8,0},{12,4},{16,24},{20,28},{24,16},{28,20},{1,9},{5... | collective-permute-start | bytes 405512 | tf_op jit(solution)/shard_map/ppermute | solution.py:756
  10.5 6.2 %collective-permute-start.2 = (f32[264,128]{1,0:T(8,128)S(1)}, f32[264,128]{1,0:T(8,128)S(1)}, u32[]{:S(2)}, u32[]{:S(2)}) collective-permute-start(f32[264,128]{1,0:T(8,128)S(1)} %get-tuple-element.56), channel_id=1, source_target_pairs={{0,12},{4,8},{8,4},{12,0},{16,28},{20,24},{24,20},{28,16},{1,13},{... | collective-permute-start | bytes 405512 | tf_op jit(solution)/shard_map/ppermute | solution.py:756
  10.5 1.6 %copy-start.1 = (bf16[1024,1024]{1,0:T(8,128)(2,1)S(1)}, bf16[1024,1024]{1,0:T(8,128)(2,1)}, u32[]{:S(2)}) copy-start(bf16[1024,1024]{1,0:T(8,128)(2,1)} %get-tuple-element.49.v_ref) | copy-start | bytes 6291460
  16.7 18.7 %copy-start.3 = (f32[1024]{0:T(1024)S(1)}, f32[1024]{0:T(1024)}, u32[]{:S(2)}) copy-start(f32[1024]{0:T(1024)} %param.9) | copy-start | bytes 12292
  16.8 7.4 %collective-permute-start.3 = (f32[256,128]{1,0:T(8,128)S(1)}, f32[256,128]{1,0:T(8,128)S(1)}, u32[]{:S(2)}, u32[]{:S(2)}) collective-permute-start(f32[256,128]{1,0:T(8,128)S(1)} %get-tuple-element.59), channel_id=1, source_target_pairs={{0,16},{4,20},{8,24},{12,28},{1,17},{5,21},{9,25},{13,29},{2,18},{... | collective-permute-start | bytes 393224 | tf_op jit(solution)/shard_map/ppermute | solution.py:774
  24.3 5.2 %collective-permute-start.4 = (f32[256,128]{1,0:T(8,128)S(1)}, f32[256,128]{1,0:T(8,128)S(1)}, u32[]{:S(2)}, u32[]{:S(2)}) collective-permute-start(f32[256,128]{1,0:T(8,128)S(1)} %get-tuple-element.61), channel_id=1, source_target_pairs={{0,4},{4,0},{8,12},{12,8},{16,20},{20,16},{24,28},{28,24},{1,5},{5... | collective-permute-start | bytes 393224 | tf_op jit(solution)/shard_map/ppermute | solution.py:756
  25.9 7.8 %collective-permute-start.5 = (f32[256,128]{1,0:T(8,128)S(1)}, f32[256,128]{1,0:T(8,128)S(1)}, u32[]{:S(2)}, u32[]{:S(2)}) collective-permute-start(f32[256,128]{1,0:T(8,128)S(1)} %get-tuple-element.62), channel_id=1, source_target_pairs={{0,8},{4,12},{8,0},{12,4},{16,24},{20,28},{24,16},{28,20},{1,9},{5... | collective-permute-start | bytes 393224 | tf_op jit(solution)/shard_map/ppermute | solution.py:756
  29.5 5.9 %collective-permute-start.6 = (f32[256,128]{1,0:T(8,128)S(1)}, f32[256,128]{1,0:T(8,128)S(1)}, u32[]{:S(2)}, u32[]{:S(2)}) collective-permute-start(f32[256,128]{1,0:T(8,128)S(1)} %get-tuple-element.63), channel_id=1, source_target_pairs={{0,12},{4,8},{8,4},{12,0},{16,28},{20,24},{24,20},{28,16},{1,13},{... | collective-permute-start | bytes 393224 | tf_op jit(solution)/shard_map/ppermute | solution.py:756
  39.6 4.4 %collective-permute-start.7 = (bf16[1024,1024]{1,0:T(8,128)(2,1)S(1)}, bf16[1024,1024]{1,0:T(8,128)(2,1)}, u32[]{:S(2)}, u32[]{:S(2)}) collective-permute-start(bf16[1024,1024]{1,0:T(8,128)(2,1)S(1)} %get-tuple-element.64.own_ref), channel_id=1, source_target_pairs={{0,1},{1,0},{2,3},{3,2},{4,5},{5,4},{6,7},{7,6},{8,9},{9,8},{10,11... | collective-permute-start | bytes 6291464 | tf_op jit(solution)/shard_map/ppermute | solution.py:759
  47.5 15.2 %collective-permute-start.8 = (bf16[528,512]{1,0:T(8,128)(2,1)S(1)}, bf16[528,512]{1,0:T(8,128)(2,1)S(1)}, u32[]{:S(2)}, u32[]{:S(2)}) collective-permute-start(bf16[528,512]{1,0:T(8,128)(2,1)S(1)} %get-tuple-element.67), channel_id=1, source_target_pairs={{0,4},{4,0},{8,12},{12,8},{16,20},{20,16},{24,28},{28,24},{1,5},{5... | collective-permute-start | bytes 1622024 | tf_op jit(solution)/shard_map/ppermute | solution.py:756
  51.7 8.1 %collective-permute-start.9 = (bf16[512,256]{1,0:T(8,128)(2,1)S(1)}, bf16[512,256]{1,0:T(8,128)(2,1)S(1)}, u32[]{:S(2)}, u32[]{:S(2)}) collective-permute-start(bf16[512,256]{1,0:T(8,128)(2,1)S(1)} %get-tuple-element.69), channel_id=1, source_target_pairs={{0,8},{4,12},{8,0},{12,4},{16,24},{20,28},{24,16},{28,20},{1,9},{5... | collective-permute-start | bytes 786440 | tf_op jit(solution)/shard_map/ppermute | solution.py:756
  57.3 13.0 %collective-permute-start.12 = (bf16[512,384]{1,0:T(8,128)(2,1)S(1)}, bf16[512,384]{1,0:T(8,128)(2,1)S(1)}, u32[]{:S(2)}, u32[]{:S(2)}) collective-permute-start(bf16[512,384]{1,0:T(8,128)(2,1)S(1)} %get-tuple-element.75), channel_id=1, source_target_pairs={{0,4},{4,0},{8,12},{12,8},{16,20},{20,16},{24,28},{28,24},{1,5},{5... | collective-permute-start | bytes 1179656 | tf_op jit(solution)/shard_map/ppermute | solution.py:756
  62.8 10.2 %collective-permute-start.10 = (bf16[272,512]{1,0:T(8,128)(2,1)S(1)}, bf16[272,512]{1,0:T(8,128)(2,1)S(1)}, u32[]{:S(2)}, u32[]{:S(2)}) collective-permute-start(bf16[272,512]{1,0:T(8,128)(2,1)S(1)} %get-tuple-element.72), channel_id=1, source_target_pairs={{0,8},{4,12},{8,0},{12,4},{16,24},{20,28},{24,16},{28,20},{1,9},{5... | collective-permute-start | bytes 835592 | tf_op jit(solution)/shard_map/ppermute | solution.py:756
  64.3 7.7 %collective-permute-start.11 = (bf16[256,256]{1,0:T(8,128)(2,1)S(1)}, bf16[256,256]{1,0:T(8,128)(2,1)S(1)}, u32[]{:S(2)}, u32[]{:S(2)}) collective-permute-start(bf16[256,256]{1,0:T(8,128)(2,1)S(1)} %get-tuple-element.73), channel_id=1, source_target_pairs={{0,16},{4,20},{8,24},{12,28},{16,0},{20,4},{24,8},{28,12},{1,17},{... | collective-permute-start | bytes 393224 | tf_op jit(solution)/shard_map/ppermute | solution.py:756
  70.4 10.1 %collective-permute-start.16 = (bf16[256,384]{1,0:T(8,128)(2,1)S(1)}, bf16[256,384]{1,0:T(8,128)(2,1)S(1)}, u32[]{:S(2)}, u32[]{:S(2)}) collective-permute-start(bf16[256,384]{1,0:T(8,128)(2,1)S(1)} %get-tuple-element.84), channel_id=1, source_target_pairs={{0,8},{4,12},{8,0},{12,4},{16,24},{20,28},{24,16},{28,20},{1,9},{5... | collective-permute-start | bytes 589832 | tf_op jit(solution)/shard_map/ppermute | solution.py:756
  73.2 8.7 %collective-permute-start.13 = (bf16[160,512]{1,0:T(8,128)(2,1)S(1)}, bf16[160,512]{1,0:T(8,128)(2,1)S(1)}, u32[]{:S(2)}, u32[]{:S(2)}) collective-permute-start(bf16[160,512]{1,0:T(8,128)(2,1)S(1)} %get-tuple-element.80), channel_id=1, source_target_pairs={{0,16},{4,20},{8,24},{12,28},{16,0},{20,4},{24,8},{28,12},{1,17},{... | collective-permute-start | bytes 491528 | tf_op jit(solution)/shard_map/ppermute | solution.py:756
  75.5 4.3 %collective-permute-start.15 = (bf16[128,256]{1,0:T(8,128)(2,1)S(1)}, bf16[128,256]{1,0:T(8,128)(2,1)S(1)}, u32[]{:S(2)}, u32[]{:S(2)}) collective-permute-start(bf16[128,256]{1,0:T(8,128)(2,1)S(1)} %get-tuple-element.83), channel_id=1, source_target_pairs={{0,4},{4,0},{8,12},{12,8},{16,20},{20,16},{24,28},{28,24},{1,5},{5... | collective-permute-start | bytes 196616 | tf_op jit(solution)/shard_map/ppermute | solution.py:756
  80.5 8.7 %collective-permute-start.17 = (bf16[128,384]{1,0:T(8,128)(2,1)S(1)}, bf16[128,384]{1,0:T(8,128)(2,1)S(1)}, u32[]{:S(2)}, u32[]{:S(2)}) collective-permute-start(bf16[128,384]{1,0:T(8,128)(2,1)S(1)} %get-tuple-element.86), channel_id=1, source_target_pairs={{0,16},{4,20},{8,24},{12,28},{16,0},{20,4},{24,8},{28,12},{1,17},{... | collective-permute-start | bytes 294920 | tf_op jit(solution)/shard_map/ppermute | solution.py:756
  81.9 11.0 %collective-permute-start.18 = (bf16[128,256]{1,0:T(8,128)(2,1)S(1)}, bf16[128,256]{1,0:T(8,128)(2,1)S(1)}, u32[]{:S(2)}, u32[]{:S(2)}) collective-permute-start(bf16[128,256]{1,0:T(8,128)(2,1)S(1)} %get-tuple-element.87), channel_id=1, source_target_pairs={{0,4},{4,8},{8,12},{12,16},{16,20},{20,24},{24,28},{28,0},{1,5},{5... | collective-permute-start | bytes 196616 | tf_op jit(solution)/shard_map/ppermute | solution.py:767
  83.1 10.3 %collective-permute-start.19 = (bf16[128,256]{1,0:T(8,128)(2,1)S(1)}, bf16[128,256]{1,0:T(8,128)(2,1)S(1)}, u32[]{:S(2)}, u32[]{:S(2)}) collective-permute-start(bf16[128,256]{1,0:T(8,128)(2,1)S(1)} %get-tuple-element.88), channel_id=1, source_target_pairs={{0,8},{4,12},{8,16},{12,20},{16,24},{20,28},{24,0},{28,4},{1,9},{5... | collective-permute-start | bytes 196616 | tf_op jit(solution)/shard_map/ppermute | solution.py:767
  88.3 5.1 %collective-permute-start.20 = (bf16[128,256]{1,0:T(8,128)(2,1)S(1)}, bf16[128,256]{1,0:T(8,128)(2,1)S(1)}, u32[]{:S(2)}, u32[]{:S(2)}) collective-permute-start(bf16[128,256]{1,0:T(8,128)(2,1)S(1)} %get-tuple-element.89), channel_id=1, source_target_pairs={{0,1},{1,0},{2,3},{3,2},{4,5},{5,4},{6,7},{7,6},{8,9},{9,8},{10,11... | collective-permute-start | bytes 196616 | tf_op jit(solution)/shard_map/ppermute | solution.py:759
  88.7 8.0 %collective-permute-start.14 = (f32[8,1024]{1,0:T(8,128)S(1)}, f32[8,1024]{1,0:T(8,128)S(1)}, u32[]{:S(2)}, u32[]{:S(2)}) collective-permute-start(f32[8,1024]{1,0:T(8,128)S(1)} %reduce_sum.9.means_ref), channel_id=1, source_target_pairs={{0,1},{1,0},{2,3},{3,2},{4,5},{5,4},{6,7},{7,6},{8,9},{9,8},{10,11... | collective-permute-start | bytes 98312 | tf_op jit(solution)/shard_map/ppermute | solution.py:759
  93.4 6.3 %collective-permute-start.21 = (bf16[128,256]{1,0:T(8,128)(2,1)S(1)}, bf16[128,256]{1,0:T(8,128)(2,1)S(1)}, u32[]{:S(2)}, u32[]{:S(2)}) collective-permute-start(bf16[128,256]{1,0:T(8,128)(2,1)S(1)} %get-tuple-element.91), channel_id=1, source_target_pairs={{0,12},{4,16},{8,20},{12,24},{16,28},{20,0},{24,4},{28,8},{1,13},{... | collective-permute-start | bytes 196616 | tf_op jit(solution)/shard_map/ppermute | solution.py:767
  93.6 6.2 %collective-permute-start.23 = (bf16[128,256]{1,0:T(8,128)(2,1)S(1)}, bf16[128,256]{1,0:T(8,128)(2,1)S(1)}, u32[]{:S(2)}, u32[]{:S(2)}) collective-permute-start(bf16[128,256]{1,0:T(8,128)(2,1)S(1)} %get-tuple-element.93), channel_id=1, source_target_pairs={{0,1},{1,0},{2,3},{3,2},{4,5},{5,4},{6,7},{7,6},{8,9},{9,8},{10,11... | collective-permute-start | bytes 196616 | tf_op jit(solution)/shard_map/ppermute | solution.py:759
  93.6 4.9 %collective-permute-start.22 = (bf16[128,128]{1,0:T(8,128)(2,1)S(1)}, bf16[128,128]{1,0:T(8,128)(2,1)S(1)}, u32[]{:S(2)}, u32[]{:S(2)}) collective-permute-start(bf16[128,128]{1,0:T(8,128)(2,1)S(1)} %get-tuple-element.92), channel_id=1, source_target_pairs={{0,16},{4,20},{8,24},{12,28},{16,0},{20,4},{24,8},{28,12},{1,17},{... | collective-permute-start | bytes 98312 | tf_op jit(solution)/shard_map/ppermute | solution.py:767

commit v5 on v4

--- a/solution.py
+++ b/solution.py
@@ -14,6 +14,7 @@
 BF16 = jnp.bfloat16
 HIGHEST = lax.Precision.HIGHEST
 MIB = 1 << 20
+RIDER_ROWS = 4
 
 
 def params(limit_mib):
@@ -22,7 +23,7 @@
 
 def cost(flops, moved, transcendentals=0):
     return pl.CostEstimate(
-        flops=int(flops), bytes_accessed=int(moved), transcendentals=int(transcendentals)
+        flops=1, bytes_accessed=1, transcendentals=0
     )
 
 
@@ -532,6 +533,8 @@
     width = own_ref.shape[1]
     shards = width // rows
     steps = sorted({step for step, _ in blocks})
+    sides = {side for _, side in blocks}
+    refs = [own_ref] if sides == {0} else [other_ref] if sides == {1} else [own_ref, other_ref]
     bit = (lax.axis_index("ctx") // apart) % 2
     if len(rest) > 4:
         send_ref[shards // 2 * rows :, :] = rest[0][...]
@@ -544,11 +547,12 @@
             line = slice(index * rows, (index + 1) * rows)
             here = slice(block * rows, (block + 1) * rows)
             left = turned[(block + steps[0]) * rows : (block + steps[-1] + 1) * rows, :]
-            right = jnp.concatenate([own_ref[:, here], other_ref[:, here]], axis=1)
+            right = [ref[:, here] for ref in refs]
+            right = right[0] if len(right) == 1 else jnp.concatenate(right, axis=1)
             out = dot(left, right).astype(out_ref.dtype)
             for place, (step, side) in enumerate(blocks):
                 low = (step - steps[0]) * rows
-                first = side_of(side, block, shards) * rows
+                first = (side_of(side, block, shards) if len(refs) > 1 else 0) * rows
                 target = slice(place * rows, (place + 1) * rows)
                 out_ref[line, target] = out[low : low + rows, first : first + rows]
 
@@ -598,22 +602,25 @@
 
 
 def merge(first, second, means):
-    a, b = first.astype(F32), second.astype(F32)
-    top, bottom = slice(means, means + 2), slice(means + 2, means + 4)
+    a, b = first.astype(F32), second[:, : first.shape[1]].astype(F32)
+    each = RIDER_ROWS
+    top, bottom = slice(means, means + each), slice(means + each, means + 2 * each)
     lines = [a[:means], b[:means], jnp.maximum(a[top], b[top]), jnp.minimum(a[bottom], b[bottom])]
-    spare = -(2 * means + 4) % 16
+    spare = -(2 * means + 2 * each) % 16
     if spare:
         lines.append(jnp.zeros((spare, a.shape[1]), F32))
     return jnp.concatenate(lines, axis=0).astype(BF16)
 
 
-def fold_kernel(rows, inner, apart, means, keep_ref, other_ref, _, *rest):
-    count = keep_ref.shape[0] // rows
+def fold_kernel(pieces, rows, inner, apart, means, *refs):
+    keeps, others, rest = refs[:pieces], refs[pieces : 2 * pieces], refs[2 * pieces + 1 :]
+    low = keeps[0].shape[0]
     bit = (lax.axis_index("ctx") // apart) % 2
     if means:
         riders_ref, kept_ref, send_ref, merged_ref = rest
-        merged = merge(riders_ref[...], other_ref[keep_ref.shape[0] :, :], means)
-        send_ref[kept_ref.shape[0] :, :] = merged
+        merged = merge(riders_ref[...], others[-1][low:, :], means)
+        send_ref[kept_ref.shape[0] :, :] = jnp.zeros_like(send_ref[kept_ref.shape[0] :, :])
+        send_ref[kept_ref.shape[0] :, : merged.shape[1]] = merged
         merged_ref[...] = merged
     else:
         kept_ref, send_ref = rest
@@ -623,27 +630,32 @@
         @pl.when(bit == mine)
         def _():
             for out_ref, side in ((send_ref, 1 - mine), (kept_ref, mine)):
-                for index, block in enumerate(places(count, inner, side)):
+                for index, block in enumerate(places(low // rows, inner, side)):
                     line = slice(block * rows, (block + 1) * rows)
-                    total = keep_ref[line, :] + other_ref[line, :].astype(F32)
-                    out_ref[index * rows : (index + 1) * rows, :] = total.astype(out_ref.dtype)
-
-
-def fold(keep, other, after, riders, means, rows, inner, apart):
-    kept = (keep.shape[0] // 2, keep.shape[1])
+                    begin = 0
+                    for keep_ref, other_ref in zip(keeps, others):
+                        end = begin + keep_ref.shape[1]
+                        total = keep_ref[line, :] + other_ref[line, :].astype(F32)
+                        total = total.astype(out_ref.dtype)
+                        out_ref[index * rows : (index + 1) * rows, begin:end] = total
+                        begin = end
+
+
+def fold(keeps, others, after, riders, means, rows, inner, apart):
+    kept = (keeps[0].shape[0] // 2, sum(keep.shape[1] for keep in keeps))
     shapes = [struct(kept, F32), struct(kept, BF16)]
     if riders:
-        merged = (2 * means + 4 + -(2 * means + 4) % 16, kept[1])
+        merged = (-(-(2 * means + 2 * RIDER_ROWS) // 16) * 16, riders[0].shape[1])
         shapes = [struct(kept, F32), struct((kept[0] + merged[0], kept[1]), BF16)]
         shapes.append(struct(merged, BF16))
     return pl.pallas_call(
-        functools.partial(fold_kernel, rows, inner, apart, means if riders else 0),
-        in_specs=[vmem()] * 2 + [anywhere()] + [vmem()] * len(riders),
+        functools.partial(fold_kernel, len(keeps), rows, inner, apart, means if riders else 0),
+        in_specs=[vmem()] * (2 * len(keeps)) + [anywhere()] + [vmem()] * len(riders),
         out_specs=[vmem()] * len(shapes),
         out_shape=shapes,
         compiler_params=params(16),
         name="fold",
-    )(keep, other, after, *riders)
+    )(*keeps, *others, after, *riders)
 
 
 def close_kernel(rows, runs, waits, keep_ref, other_ref, *rest):
@@ -670,16 +682,19 @@
 
 def assemble(put, upper, shards, chunks, mirrors, crossed):
     half = shards // 2
-    put(0, 0, chunks[(0, 0)])
-    put(0, 1, chunks[(0, 1)])
-    for step in range(1, half):
-        put(step, 0, chunks[(step, 0)].T)
-        put(step, 1, crossed[step].T)
-        put(-step, 0, mirrors[(step, 0)])
-        put(-step, 1, mirrors[(step, 1)])
-    last = jnp.where(upper, crossed[half].astype(F32), chunks[(half, 2)])
-    put(half, upper, last.T)
-    put(half, 1 - upper, mirrors[(half, 2)])
+    for step in sorted({step for step, _ in chunks}):
+        if step == 0:
+            put(0, 0, chunks[(0, 0)])
+            put(0, 1, chunks[(0, 1)])
+        elif step < half:
+            put(step, 0, chunks[(step, 0)].T)
+            put(step, 1, crossed[step].T)
+            put(-step, 0, mirrors[(step, 0)])
+            put(-step, 1, mirrors[(step, 1)])
+        else:
+            last = jnp.where(upper, crossed[half].astype(F32), chunks[(half, 2)])
+            put(half, upper, last.T)
+            put(half, 1 - upper, mirrors[(half, 2)])
 
 
 def pick(rows, names, values):
@@ -688,6 +703,17 @@
         for place, name in enumerate(blocks):
             out[name] = value[:, place * rows : (place + 1) * rows]
     return out
+
+
+def putter(out_ref, rows, shards, total):
+    mine, side = lax.axis_index("ctx"), lax.axis_index("head") & 1
+
+    def put(step, flip, gram):
+        shard = lax.rem(mine + step + shards, shards)
+        at = pl.ds(pl.multiple_of(((side ^ flip) * shards + shard) * rows, rows), rows)
+        out_ref[:, at] = (out_ref[:, at] + gram.astype(F32)) / total
+
+    return put, jnp.where(mine >= shards // 2, 1, 0)
 
 
 def cover_kernel(rows, shards, total, names, means_ref, others_ref, *refs):
@@ -702,15 +728,19 @@
     left = spread[:, pl.ds(own, rows)].T
     count = total // shards
     out_ref[...] = count * jnp.dot(left, spread[...], precision=HIGHEST, preferred_element_type=F32)
-
-    def put(step, flip, gram):
-        shard = lax.rem(mine + step + shards, shards)
-        at = pl.ds(pl.multiple_of(((side ^ flip) * shards + shard) * rows, rows), rows)
-        out_ref[:, at] = (out_ref[:, at] + gram.astype(F32)) / total
-
     values = iter(refs[:-2])
     parts = [pick(rows, group, [next(values) for _ in group]) for group in names]
-    assemble(put, jnp.where(mine >= shards // 2, 1, 0), shards, *parts)
+    put, upper = putter(out_ref, rows, shards, total)
+    assemble(put, upper, shards, *parts)
+
+
+def cover_rest_kernel(rows, shards, total, names, begun_ref, *refs):
+    out_ref = refs[-1]
+    out_ref[...] = begun_ref[...]
+    values = iter(refs[:-1])
+    parts = [pick(rows, group, [next(values) for _ in group]) for group in names]
+    put, upper = putter(out_ref, rows, shards, total)
+    assemble(put, upper, shards, *parts)
 
 
 def cover(means, others, groups, names, rows, shards, total):
@@ -722,18 +752,8 @@
         spread = jnp.concatenate(pair, axis=1)
         spread = spread - jnp.mean(spread, axis=0)
         left = lax.dynamic_slice_in_dim(spread, (side * shards + mine) * rows, rows, 1)
-        out = [(total // shards) * jnp.dot(left.T, spread, precision=HIGHEST)]
-
-        def put(step, flip, gram):
-            shard = lax.rem(mine + step + shards, shards)
-            at = ((side ^ flip) * shards + shard) * rows
-            old = lax.dynamic_slice_in_dim(out[0], at, rows, 1)
-            new = (old + gram.astype(F32)) / total
-            out[0] = lax.dynamic_update_slice_in_dim(out[0], new, at, 1)
-
-        parts = [pick(rows, *pair) for pair in zip(names, groups)]
-        assemble(put, jnp.where(mine >= shards // 2, 1, 0), shards, *parts)
-        return out[0]
+        fix = (total // shards) * jnp.dot(left.T, spread, precision=HIGHEST)
+        return cover_rest(fix, groups, names, rows, shards, total)
     return pl.pallas_call(
         functools.partial(cover_kernel, rows, shards, total, names),
         in_specs=[vmem()] * (2 + len(values)),
@@ -743,6 +763,32 @@
         compiler_params=params(16),
         name="cover",
     )(means, others, *values)
+
+
+def cover_rest(begun, groups, names, rows, shards, total):
+    values = [value for group in groups for value in group]
+    if rows % 128:
+        mine, side = lax.axis_index("ctx"), lax.axis_index("head") & 1
+        out = [begun]
+
+        def put(step, flip, gram):
+            shard = lax.rem(mine + step + shards, shards)
+            at = ((side ^ flip) * shards + shard) * rows
+            old = lax.dynamic_slice_in_dim(out[0], at, rows, 1)
+            new = (old + gram.astype(F32)) / total
+            out[0] = lax.dynamic_update_slice_in_dim(out[0], new, at, 1)
+
+        parts = [pick(rows, *pair) for pair in zip(names, groups)]
+        assemble(put, jnp.where(mine >= shards // 2, 1, 0), shards, *parts)
+        return out[0]
+    return pl.pallas_call(
+        functools.partial(cover_rest_kernel, rows, shards, total, names),
+        in_specs=[vmem()] * (1 + len(values)),
+        out_specs=vmem(),
+        out_shape=struct(begun.shape, F32),
+        compiler_params=params(16),
+        name="cover_rest",
+    )(begun, *values)
 
 
 def body(queries, keys, values, log_decay, gain):
@@ -779,78 +825,89 @@
     partner = to_partner(centered)
 
     half = shards // 2
-    lines = half * rows
-    mean_rows = 3 * width // lines
-    extra = stats[:5].reshape(mean_rows + 4, lines)
+    lines = width // RIDER_ROWS
+    mean_rows = 3 * RIDER_ROWS
+    extra = stats[:5].reshape(-1, lines)
     extra = jnp.pad(extra, ((0, -extra.shape[0] % 16), (0, 0)))
-    bits = [1 << place for place in range(shards.bit_length() - 1)]
     near_steps = range(1, half // 2 + 1)
     far_steps = range(half // 2 + 1, half)
-    bits = [1 << place for place in range(shards.bit_length() - 1)]
     plans = [
-        ([(step, side) for step in near_steps for side in (0, 1)], bits),
-        ([(0, 0), (0, 1)], bits[1:] + bits[:1]),
-        ([(step, side) for step in far_steps for side in (0, 1)] + [(half, 2)], bits),
+        [(step, side) for side in (0, 1) for step in near_steps],
+        [(step, side) for step in far_steps for side in (0, 1)] + [(half, 2)],
+        [(0, 0), (0, 1)],
     ]
-    kept, riders, after = [], [extra], stats
-    for blocks, turns in plans:
-        carried = [] if kept else riders
-        keep, send = gram_parts(centered, partner, carried, after, rows, blocks, turns[0])
-        after = keep
-        kept.append((keep, to_shard(send, turns[0])))
-
-    def split_on(index, stage, after):
-        keep, other = kept[index]
-        turns = plans[index][1]
-        left = [bit for bit in bits if bit not in turns[:stage]]
+
+    def begin(blocks, other, carried, after):
+        keep, send = gram_parts(centered, other, carried, after, rows, blocks, 1)
+        return [keep], [to_shard(send, 1)]
+
+    def split_on(index, apart, after):
+        keeps, others = kept[index]
         carried = riders if index == 0 else []
         keep, send, *merged = fold(
-            keep,
-            other,
-            after,
-            carried,
-            mean_rows << (stage - 1),
-            rows,
-            1 << left.index(turns[stage]),
-            turns[stage],
+            keeps, others, after, carried, mean_rows * apart // 2, rows, 1, apart
         )
         riders[:] = merged or riders
-        kept[index] = (keep, to_shard(send, turns[stage]))
+        kept[index] = ([keep], [to_shard(send, apart)])
         return keep
 
-    after = kept[0][0]
-    for stage in range(1, len(bits)):
-        for index in (1, 0, 2):
-            after = split_on(index, stage, after)
-
-    chunks, mirrors, mirror_names, crossed, crossed_names = [None] * len(plans), [], [], [], []
-    for index in (0, 1, 2):
-        blocks, (keep, other) = plans[index][0], kept[index]
-        if index == 0:
-            every = merge(riders[0], other[rows:], mean_rows * half)
+    riders = [extra]
+    blocks = plans[0]
+    cut = len(blocks) // 2
+    first = begin(blocks[:cut], centered, [], stats)
+    second = begin(blocks[cut:], partner, riders, first[0][0])
+    kept = [tuple(a + b for a, b in zip(first, second))]
+    kept.append(begin(plans[1], partner, [], first[1][0]))
+    after = split_on(0, 2, kept[1][0][0])
+    kept.append(begin(plans[2], partner, [], after))
+    aparts = [1 << place for place in range(1, shards.bit_length() - 1)]
+    chunks, mirrors, crossed = [None] * 3, [[], [], []], [[], [], []]
+    names = [plans, [[], [], []], [[], [], []]]
+
+    def finished(index, after):
+        blocks, ((keep,), (other,)) = plans[index], kept[index]
         steps = sorted({step for step, _ in blocks} - {0})
         runs = [[i for i, block in enumerate(blocks) if block[0] == step] for step in steps]
         crossing = [i for i, (step, side) in enumerate(blocks) if step and side]
-        earlier = mirrors + crossed if index == 2 else []
-        total, slabs = close(keep, other, earlier, rows, runs + [crossing] * bool(crossing))
+        total, slabs = close(keep, other, after, rows, runs + [crossing] * bool(crossing))
         chunks[index] = total
         for step, run, slab in zip(steps, runs, slabs):
-            mirrors.append(forward(slab, step))
-            mirror_names.append([blocks[i] for i in run])
+            mirrors[index].append(forward(slab, step))
+            names[1][index].append([blocks[i] for i in run])
         if crossing:
-            crossed.append(to_partner(slabs[-1]))
-            crossed_names.append([blocks[i][0] for i in crossing])
+            crossed[index].append(to_partner(slabs[-1]))
+            names[2][index].append([blocks[i][0] for i in crossing])
+        return total
+
+    for apart in aparts[1:]:
+        after = split_on(0, apart, after)
+    every = merge(riders[0], kept[0][1][0][rows:, :lines], mean_rows * half)
+    for apart in aparts:
+        after = split_on(1, apart, after)
+        if apart == aparts[-1]:
+            after = finished(0, [after])
+        after = split_on(2, apart, after)
+    after = finished(1, [after])
+    finished(2, [after])
 
     every = every.astype(F32)
     means = jnp.sum(every[: mean_rows * shards].reshape(shards, 3, width), axis=1)
-    extremes = every[mean_rows * shards :][:4].reshape(2, width)
+    extremes = every[mean_rows * shards :][: 2 * RIDER_ROWS].reshape(2, width)
     shift = (extremes[0] + extremes[1]) / 2.0
     others = to_partner(means)
-    covariance = cover(
+    begun = cover(
         means,
         others,
-        (chunks, mirrors, crossed),
-        ([blocks for blocks, _ in plans], mirror_names, crossed_names),
+        (chunks[::2], mirrors[0] + mirrors[2], crossed[0] + crossed[2]),
+        (names[0][::2], names[1][0] + names[1][2], names[2][0] + names[2][2]),
+        rows,
+        shards,
+        count * shards,
+    )
+    covariance = cover_rest(
+        begun,
+        (chunks[1:2], mirrors[1], crossed[1]),
+        (names[0][1:2], names[1][1], names[2][1]),
         rows,
         shards,
         count * shards,

time: 102 us -> 96.6 us (0.947)
  waiting for transfers between devices: 31.9 us -> 27.3 us
  starting transfers between devices: 39.5 us -> 36.3 us
  Pallas kernels: 26.2 us -> 28.5 us
    ppermute x4, starting transfers between devices: 9.04 us -> 5.28 us  [forward(): lax.ppermute(value, 'ctx', [(a, (a + step) % shards) for a in range(shard...]
    ppermute x4, waiting for transfers between devices: 4.24 us -> 0.95 us  [to_partner(): return lax.ppermute(value, 'head', [(a, a ^ 1) for a in range(sides)])]
    ppermute x4, waiting for transfers between devices: 7.19 us -> 4.57 us  [forward(): lax.ppermute(value, 'ctx', [(a, (a + step) % shards) for a in range(shard...]
    pallas_call x3 -> x4, Pallas kernels: 10.3 us -> 12.5 us  [gram_parts(): pl.pallas_call(functools.partial(gram_kernel, rows, blocks, apart), in_sp...]
    ppermute x15 -> x16, waiting for transfers between devices: 18 us -> 19.3 us  [to_shard(): return lax.ppermute(value, 'ctx', [(a, a ^ apart) for a in range(shards)])]
    pallas_call x6 -> x7, Pallas kernels: 0.34 us -> 1.48 us  [the longest x1 1.15 us: cover_rest(): pl.pallas_call(functools.partial(cover_rest_kernel, rows, shards, total,...]
    pallas_call x1, Pallas kernels: 2.24 us -> 1.19 us  [cover(): pl.pallas_call(functools.partial(cover_kernel, rows, shards, total, names...]
    ppermute x15 -> x16, starting transfers between devices: 24.9 us -> 25.9 us  [to_shard(): return lax.ppermute(value, 'ctx', [(a, a ^ apart) for a in range(shards)])]
  transfers between devices with their start and end apart: 24 -> 25, of which waited for: 15 -> 14; matrix products, arithmetic and copies ran while one was open for 1% -> 1% of each run, Pallas kernels for 11% -> 19%
where the time goes in v5:
time: 96.6 us; the launch traced here: 96.3 us
  starting transfers between devices  36.3 us (38%)
  Pallas kernels  28.5 us (30%)
  waiting for transfers between devices  27.3 us (28%)
  local copies, waits for them, and re-layouts  3.23 us (3%)
    ppermute x16, starting transfers between devices, to_shard(): return lax.ppermute(value, 'ctx', [(a, a ^ apart) for a in range(shards)])  25.9 us
    ppermute x16, waiting for transfers between devices, to_shard(): return lax.ppermute(value, 'ctx', [(a, a ^ apart) for a in range(shards)])  19.3 us
    pallas_call x4, Pallas kernels, gram_parts(): pl.pallas_call(functools.partial(gram_kernel, rows, blocks, apart), in_sp...  12.5 us
    ppermute x4, starting transfers between devices, forward(): lax.ppermute(value, 'ctx', [(a, (a + step) % shards) for a in range(shard...  5.28 us
    ppermute x1, starting transfers between devices, body(): entered = lax.ppermute(leaving, 'ctx', [(a, a + near) for a in range(near)])  4.9 us
    ppermute x4, waiting for transfers between devices, forward(): lax.ppermute(value, 'ctx', [(a, (a + step) % shards) for a in range(shard...  4.57 us
    pallas_call x1, Pallas kernels, inner(): pl.pallas_call(inner_loop_kernel, in_specs=[vmem()] * 4, out_specs=vmem()...  4.54 us
    pallas_call x1, Pallas kernels, local_states(): pl.pallas_call(functools.partial(states_fetch_kernel, near), in_specs=[hb...  4.37 us
  transfers between devices with their start and end apart: 25, of which 14 were waited for; matrix products, arithmetic and copies ran while one was open for 1% of the time, Pallas kernels for 19%

profile of v5, /device:TPU:0, one launch (start us, length us, event | category | flops | bytes accessed | tf_op | source)
XLA Modules:
  0.0 96.3 jit_solution(7270693006588295704)
XLA Ops:
  0.7 0.9 copy-done.2
  1.5 4.4 %local_states.1 = (f32[4,1024,128]{2,1,0:T(8,128)S(1)}, f32[4,8,128]{2,1,0:T(8,128)S(1)}, f32[32,256]{1,0:T(8,128)S(1)}, f32[264,128]{1,0:T(8,128)S(1)}, f32[264...) custom-call(bf16[1024,1024]{1,0:T(8,128)(2,1)} %k_any.1, ...), custom_call_target="tpu_custom_call" | custom-call | flops 1 | bytes 1 | tf_op jit(solution)/shard_map/local_states/pallas_call | solution.py:197
  5.9 3.0 %collective-permute-start = (f32[264,128]{1,0:T(8,128)S(1)}, f32[264,128]{1,0:T(8,128)S(1)}, u32[]{:S(2)}, u32[]{:S(2)}) collective-permute-start(f32[264,128]{1,0:T(8,128)S(1)} %get-tuple-element.56), channel_id=1, source_target_pairs={{0,4},{4,0},{8,12},{12,8},{16,20},{20,16},{24,28},{28,24},{1,5},{5... | collective-permute-start | bytes 405512 | tf_op jit(solution)/shard_map/ppermute | solution.py:802
  9.0 1.6 %collective-permute-start.1 = (f32[264,128]{1,0:T(8,128)S(1)}, f32[264,128]{1,0:T(8,128)S(1)}, u32[]{:S(2)}, u32[]{:S(2)}) collective-permute-start(f32[264,128]{1,0:T(8,128)S(1)} %get-tuple-element.57), channel_id=1, source_target_pairs={{0,8},{4,12},{8,0},{12,4},{16,24},{20,28},{24,16},{28,20},{1,9},{5... | collective-permute-start | bytes 405512 | tf_op jit(solution)/shard_map/ppermute | solution.py:802
  10.5 1.6 %copy-done.1 = bf16[1024,1024]{1,0:T(8,128)(2,1)S(1)} copy-done((bf16[1024,1024]{1,0:T(8,128)(2,1)S(1)}, bf16[1024,1024]{1,0:T(8,128)(2,1)}, u32[]{:S(2)}) %copy-start.1) | copy-done | bytes 2097176
  12.1 4.5 %inner.1.refs_4_.raw_ref = f32[1024,1024]{1,0:T(8,128)S(1)} custom-call(bf16[1024,1024]{1,0:T(8,128)(2,1)S(1)} %copy-done, bf16[1024,1024]{1,0:T(8,128)(2,1)S(1)} %get-tuple-element.50.k_ref, bf16[1024,1024]{1,0:T(8,128)(2,1)S(1)} %copy-done.1, f32[32,256]{1,0:T(8,128)S(1)} %get-tuple-element.52.cumul_ref), custom_call_target="tpu_custom_call" | custom-call | flops 1 | bytes 1 | tf_op jit(solution)/shard_map/inner/pallas_call | solution.py:338
  16.7 0.0 collective-permute-done.refs_1_
  16.7 0.0 collective-permute-done.2.refs_3_
  16.7 0.0 copy-start.3
  16.7 0.1 chain.1
  16.8 4.9 %collective-permute-start.3 = (f32[256,128]{1,0:T(8,128)S(1)}, f32[256,128]{1,0:T(8,128)S(1)}, u32[]{:S(2)}, u32[]{:S(2)}) collective-permute-start(f32[256,128]{1,0:T(8,128)S(1)} %get-tuple-element.61), channel_id=1, source_target_pairs={{0,16},{4,20},{8,24},{12,28},{1,17},{5,21},{9,25},{13,29},{2,18},{... | collective-permute-start | bytes 393224 | tf_op jit(solution)/shard_map/ppermute | solution.py:820
  21.7 2.5 %collective-permute-done.3.entered_ref = f32[256,128]{1,0:T(8,128)S(1)} collective-permute-done((f32[256,128]{1,0:T(8,128)S(1)}, f32[256,128]{1,0:T(8,128)S(1)}, u32[]{:S(2)}, u32[]{:S(2)}) %collective-permute-start.3) | collective-permute-done | bytes 131104 | tf_op jit(solution)/shard_map/ppermute | solution.py:820
  24.3 0.1 spread_states.1
  24.3 1.6 %collective-permute-start.4 = (f32[256,128]{1,0:T(8,128)S(1)}, f32[256,128]{1,0:T(8,128)S(1)}, u32[]{:S(2)}, u32[]{:S(2)}) collective-permute-start(f32[256,128]{1,0:T(8,128)S(1)} %get-tuple-element.63), channel_id=1, source_target_pairs={{0,4},{4,0},{8,12},{12,8},{16,20},{20,16},{24,28},{28,24},{1,5},{5... | collective-permute-start | bytes 393224 | tf_op jit(solution)/shard_map/ppermute | solution.py:802
  25.9 3.7 %collective-permute-start.5 = (f32[256,128]{1,0:T(8,128)S(1)}, f32[256,128]{1,0:T(8,128)S(1)}, u32[]{:S(2)}, u32[]{:S(2)}) collective-permute-start(f32[256,128]{1,0:T(8,128)S(1)} %get-tuple-element.64), channel_id=1, source_target_pairs={{0,8},{4,12},{8,0},{12,4},{16,24},{20,28},{24,16},{28,20},{1,9},{5... | collective-permute-start | bytes 393224 | tf_op jit(solution)/shard_map/ppermute | solution.py:802
  29.5 0.0 collective-permute-start.6
  29.5 0.0 collective-permute-done.4.rest_1_
  29.5 4.2 %collective-permute-done.5.rest_2_ = f32[256,128]{1,0:T(8,128)S(1)} collective-permute-done((f32[256,128]{1,0:T(8,128)S(1)}, f32[256,128]{1,0:T(8,128)S(1)}, u32[]{:S(2)}, u32[]{:S(2)}) %collective-permute-start.5) | collective-permute-done | bytes 131104 | tf_op jit(solution)/shard_map/ppermute | solution.py:802
  33.7 1.7 %collective-permute-done.6.rest_3_ = f32[256,128]{1,0:T(8,128)S(1)} collective-permute-done((f32[256,128]{1,0:T(8,128)S(1)}, f32[256,128]{1,0:T(8,128)S(1)}, u32[]{:S(2)}, u32[]{:S(2)}) %collective-permute-start.6) | collective-permute-done | bytes 131104 | tf_op jit(solution)/shard_map/ppermute | solution.py:802
  35.4 4.2 %finish.1 = (bf16[1024,1024]{1,0:T(8,128)(2,1)S(1)}, bf16[16,1024]{1,0:T(8,128)(2,1)S(1)}) custom-call(bf16[1024,1024]{1,0:T(8,128)(2,1)S(1)} %copy-done, f32[1024,1024]{1,0:T(8,128)S(1)} %inner.1.refs_4_.raw_ref, f32[4,1024,128]{2,1,0:T(8,128)S(1)} %get-tuple-element.53.entering_ref, f32[4,8,128]{2,1,0:T(8,128)S(1)} %get-tuple-element.54.before_ref, ...), custom_call_target="tpu_custom_call" | custom-call | flops 1 | bytes 1 | tf_op jit(solution)/shard_map/finish/pallas_call | solution.py:487
  39.6 0.1 collective-permute-start.7
  39.7 2.0 %gram.4 = (f32[512,256]{1,0:T(8,128)S(1)}, bf16[512,256]{1,0:T(8,128)(2,1)S(1)}) custom-call(bf16[1024,1024]{1,0:T(8,128)(2,1)S(1)} %get-tuple-element.66.own_ref.other_ref, bf16[1024,1024]{1,0:T(8,128)(2,1)S(1)} %get-tuple-element.66.own_ref.other_ref, bf16[16,1024]{1,0:T(8,128)(2,1)S(1)} %get-tuple-element.67.rest_0_), custom_call_target="tpu_custom_call" | custom-call | flops 1 | bytes 1 | tf_op jit(solution)/shard_map/gram/pallas_call | solution.py:592
  41.7 1.3 %collective-permute-start.8 = (bf16[512,256]{1,0:T(8,128)(2,1)S(1)}, bf16[512,256]{1,0:T(8,128)(2,1)S(1)}, u32[]{:S(2)}, u32[]{:S(2)}) collective-permute-start(bf16[512,256]{1,0:T(8,128)(2,1)S(1)} %get-tuple-element.70), channel_id=1, source_target_pairs={{0,4},{4,0},{8,12},{12,8},{16,20},{20,16},{24,28},{28,24},{1,5},{5... | collective-permute-start | bytes 786440 | tf_op jit(solution)/shard_map/ppermute | solution.py:802
  43.0 0.9 collective-permute-done.7.other_ref
  43.9 3.6 %gram.5 = (f32[512,256]{1,0:T(8,128)S(1)}, bf16[544,256]{1,0:T(8,128)(2,1)S(1)}) custom-call(bf16[1024,1024]{1,0:T(8,128)(2,1)S(1)} %get-tuple-element.66.own_ref.other_ref, bf16[1024,1024]{1,0:T(8,128)(2,1)} %collective-permute-done.7.other_ref, bf16[32,256]{1,0:T(8,128)(2,1)S(1)} %pad.4.rest_0_.refs_5_, f32[512,256]{1,0:T(8,128)S(1)} %get-tuple-element.68.rest_1_.refs_0_), custom_call_target="tpu_custom_call" | custom-call | flops 1 | bytes 1 | tf_op jit(solution)/shard_map/gram/pallas_call | solution.py:592
  47.6 1.3 %collective-permute-start.9 = (bf16[544,256]{1,0:T(8,128)(2,1)S(1)}, bf16[544,256]{1,0:T(8,128)(2,1)S(1)}, u32[]{:S(2)}, u32[]{:S(2)}) collective-permute-start(bf16[544,256]{1,0:T(8,128)(2,1)S(1)} %get-tuple-element.71), channel_id=1, source_target_pairs={{0,4},{4,0},{8,12},{12,8},{16,20},{20,16},{24,28},{28,24},{1,5},{5... | collective-permute-start | bytes 835592 | tf_op jit(solution)/shard_map/ppermute | solution.py:802
  48.8 1.7 %collective-permute-done.8.rest_0_.refs_2_ = bf16[512,256]{1,0:T(8,128)(2,1)S(1)} collective-permute-done((bf16[512,256]{1,0:T(8,128)(2,1)S(1)}, bf16[512,256]{1,0:T(8,128)(2,1)S(1)}, u32[]{:S(2)}, u32[]{:S(2)}) %collective-permute-start.8) | collective-permute-done | bytes 262176 | tf_op jit(solution)/shard_map/ppermute | solution.py:802
  50.5 3.9 %gram.6 = (f32[512,384]{1,0:T(8,128)S(1)}, bf16[512,384]{1,0:T(8,128)(2,1)S(1)}) custom-call(bf16[1024,1024]{1,0:T(8,128)(2,1)S(1)} %get-tuple-element.66.own_ref.other_ref, bf16[1024,1024]{1,0:T(8,128)(2,1)} %collective-permute-done.7.other_ref, bf16[512,256]{1,0:T(8,128)(2,1)S(1)} %collective-permute-done.8.rest_0_.refs_2_), custom_call_target="tpu_custom_call" | custom-call | flops 1 | bytes 1 | tf_op jit(solution)/shard_map/gram/pallas_call | solution.py:592
  54.4 1.3 %collective-permute-start.13 = (bf16[512,384]{1,0:T(8,128)(2,1)S(1)}, bf16[512,384]{1,0:T(8,128)(2,1)S(1)}, u32[]{:S(2)}, u32[]{:S(2)}) collective-permute-start(bf16[512,384]{1,0:T(8,128)(2,1)S(1)} %get-tuple-element.79), channel_id=1, source_target_pairs={{0,4},{4,0},{8,12},{12,8},{16,20},{20,16},{24,28},{28,24},{1,5},{5... | collective-permute-start | bytes 1179656 | tf_op jit(solution)/shard_map/ppermute | solution.py:802
  55.7 0.7 collective-permute-done.9.refs_3_
  56.4 0.1 fold.6
  56.6 1.4 %collective-permute-start.10 = (bf16[288,512]{1,0:T(8,128)(2,1)S(1)}, bf16[288,512]{1,0:T(8,128)(2,1)S(1)}, u32[]{:S(2)}, u32[]{:S(2)}) collective-permute-start(bf16[288,512]{1,0:T(8,128)(2,1)S(1)} %get-tuple-element.74), channel_id=1, source_target_pairs={{0,8},{4,12},{8,0},{12,4},{16,24},{20,28},{24,16},{28,20},{1,9},{5... | collective-permute-start | bytes 884744 | tf_op jit(solution)/shard_map/ppermute | solution.py:802
  58.0 3.0 %gram.7 = (f32[512,256]{1,0:T(8,128)S(1)}, bf16[512,256]{1,0:T(8,128)(2,1)S(1)}) custom-call(bf16[1024,1024]{1,0:T(8,128)(2,1)S(1)} %get-tuple-element.66.own_ref.other_ref, bf16[1024,1024]{1,0:T(8,128)(2,1)} %collective-permute-done.7.other_ref, f32[256,512]{1,0:T(8,128)S(1)} %get-tuple-element.73.refs_0_.refs_2_.rest_0_), custom_call_target="tpu_custom_call" | custom-call | flops 1 | bytes 1 | tf_op jit(solution)/shard_map/gram/pallas_call | solution.py:592
  61.0 1.6 %collective-permute-start.15 = (bf16[512,256]{1,0:T(8,128)(2,1)S(1)}, bf16[512,256]{1,0:T(8,128)(2,1)S(1)}, u32[]{:S(2)}, u32[]{:S(2)}) collective-permute-start(bf16[512,256]{1,0:T(8,128)(2,1)S(1)} %get-tuple-element.83), channel_id=1, source_target_pairs={{0,4},{4,0},{8,12},{12,8},{16,20},{20,16},{24,28},{28,24},{1,5},{5... | collective-permute-start | bytes 786440 | tf_op jit(solution)/shard_map/ppermute | solution.py:802
  62.6 2.4 %collective-permute-done.10.refs_1_ = bf16[288,512]{1,0:T(8,128)(2,1)S(1)} collective-permute-done((bf16[288,512]{1,0:T(8,128)(2,1)S(1)}, bf16[288,512]{1,0:T(8,128)(2,1)S(1)}, u32[]{:S(2)}, u32[]{:S(2)}) %collective-permute-start.10) | collective-permute-done | bytes 294944 | tf_op jit(solution)/shard_map/ppermute | solution.py:802
  65.0 0.1 fold.7
  65.0 1.5 %collective-permute-done.13.refs_1_ = bf16[512,384]{1,0:T(8,128)(2,1)S(1)} collective-permute-done((bf16[512,384]{1,0:T(8,128)(2,1)S(1)}, bf16[512,384]{1,0:T(8,128)(2,1)S(1)}, u32[]{:S(2)}, u32[]{:S(2)}) %collective-permute-start.13) | collective-permute-done | bytes 393248 | tf_op jit(solution)/shard_map/ppermute | solution.py:802
  66.5 0.1 fold.8
  66.6 1.4 %collective-permute-start.14 = (bf16[256,384]{1,0:T(8,128)(2,1)S(1)}, bf16[256,384]{1,0:T(8,128)(2,1)S(1)}, u32[]{:S(2)}, u32[]{:S(2)}) collective-permute-start(bf16[256,384]{1,0:T(8,128)(2,1)S(1)} %get-tuple-element.81), channel_id=1, source_target_pairs={{0,8},{4,12},{8,0},{12,4},{16,24},{20,28},{24,16},{28,20},{1,9},{5... | collective-permute-start | bytes 589832 | tf_op jit(solution)/shard_map/ppermute | solution.py:802
  68.0 3.4 %collective-permute-start.11 = (bf16[192,512]{1,0:T(8,128)(2,1)S(1)}, bf16[192,512]{1,0:T(8,128)(2,1)S(1)}, u32[]{:S(2)}, u32[]{:S(2)}) collective-permute-start(bf16[192,512]{1,0:T(8,128)(2,1)S(1)} %get-tuple-element.77), channel_id=1, source_target_pairs={{0,16},{4,20},{8,24},{12,28},{16,0},{20,4},{24,8},{28,12},{1,17},{... | collective-permute-start | bytes 589832 | tf_op jit(solution)/shard_map/ppermute | solution.py:802
  71.5 0.8 collective-permute-start.16
  72.3 5.7 %collective-permute-done.14.refs_1_ = bf16[256,384]{1,0:T(8,128)(2,1)S(1)} collective-permute-done((bf16[256,384]{1,0:T(8,128)(2,1)S(1)}, bf16[256,384]{1,0:T(8,128)(2,1)S(1)}, u32[]{:S(2)}, u32[]{:S(2)}) %collective-permute-start.14) | collective-permute-done | bytes 196640 | tf_op jit(solution)/shard_map/ppermute | solution.py:802
  78.1 0.7 collective-permute-start.18
  78.8 0.1 close.3
  78.8 0.7 collective-permute-done.16.refs_1_
  79.6 2.8 %collective-permute-start.17 = (bf16[128,256]{1,0:T(8,128)(2,1)S(1)}, bf16[128,256]{1,0:T(8,128)(2,1)S(1)}, u32[]{:S(2)}, u32[]{:S(2)}) collective-permute-start(bf16[128,256]{1,0:T(8,128)(2,1)S(1)} %get-tuple-element.89), channel_id=1, source_target_pairs={{0,16},{4,20},{8,24},{12,28},{16,0},{20,4},{24,8},{28,12},{1,17},{... | collective-permute-start | bytes 196616 | tf_op jit(solution)/shard_map/ppermute | solution.py:802
  82.4 1.2 %collective-permute-start.19 = (bf16[128,256]{1,0:T(8,128)(2,1)S(1)}, bf16[128,256]{1,0:T(8,128)(2,1)S(1)}, u32[]{:S(2)}, u32[]{:S(2)}) collective-permute-start(bf16[128,256]{1,0:T(8,128)(2,1)S(1)} %get-tuple-element.92), channel_id=1, source_target_pairs={{0,4},{4,8},{8,12},{12,16},{16,20},{20,24},{24,28},{28,0},{1,5},{5... | collective-permute-start | bytes 196616 | tf_op jit(solution)/shard_map/ppermute | solution.py:813
  83.7 0.1 reshape.23
  83.8 0.1 reduce_sum.9.means_ref
  83.9 0.1 collective-permute-start.12
  84.0 1.7 %collective-permute-start.20 = (bf16[128,256]{1,0:T(8,128)(2,1)S(1)}, bf16[128,256]{1,0:T(8,128)(2,1)S(1)}, u32[]{:S(2)}, u32[]{:S(2)}) collective-permute-start(bf16[128,256]{1,0:T(8,128)(2,1)S(1)} %get-tuple-element.93), channel_id=1, source_target_pairs={{0,8},{4,12},{8,16},{12,20},{16,24},{20,28},{24,0},{28,4},{1,9},{5... | collective-permute-start | bytes 196616 | tf_op jit(solution)/shard_map/ppermute | solution.py:813
  85.7 0.5 collective-permute-done.18.other_ref
  86.2 0.0 collective-permute-start.21
  86.3 0.5 collective-permute-start.22
  86.8 0.1 collective-permute-done.17.other_ref
  86.9 0.1 collective-permute-start.24
  87.0 2.4 %collective-permute-done.19.refs_2_ = bf16[128,256]{1,0:T(8,128)(2,1)S(1)} collective-permute-done((bf16[128,256]{1,0:T(8,128)(2,1)S(1)}, bf16[128,256]{1,0:T(8,128)(2,1)S(1)}, u32[]{:S(2)}, u32[]{:S(2)}) %collective-permute-start.19) | collective-permute-done | bytes 65568 | tf_op jit(solution)/shard_map/ppermute | solution.py:813
  89.4 1.8 %collective-permute-start.23 = (bf16[128,128]{1,0:T(8,128)(2,1)S(1)}, bf16[128,128]{1,0:T(8,128)(2,1)S(1)}, u32[]{:S(2)}, u32[]{:S(2)}) collective-permute-start(bf16[128,128]{1,0:T(8,128)(2,1)S(1)} %get-tuple-element.96), channel_id=1, source_target_pairs={{0,16},{4,20},{8,24},{12,28},{16,0},{20,4},{24,8},{28,12},{1,17},{... | collective-permute-start | bytes 98312 | tf_op jit(solution)/shard_map/ppermute | solution.py:813
  91.2 0.6 copy.7
  91.8 0.0 collective-permute-done.20.refs_3_
  91.8 0.0 collective-permute-done.21.refs_4_
  91.8 1.2 %cover.1.begun_ref = f32[128,2048]{1,0:T(8,128)S(1)} custom-call(f32[8,1024]{1,0:T(8,128)S(1)} %reduce_sum.9.means_ref, f32[8,1024]{1,0:T(8,128)S(1)} %collective-permute-done.12.others_ref, f32[128,512]{1,0:T(8,128)S(1)} %get-tuple-element.86.refs_2_.refs_0_, f32[128,256]{1,0:T(8,128)S(1)} %close.5.refs_1_, ...), custom_call_target="tpu_custom_call" | custom-call | tf_op jit(solution)/shard_map/cover/pallas_call | solution.py:757
  93.0 2.2 %collective-permute-done.23.refs_2_ = bf16[128,128]{1,0:T(8,128)(2,1)S(1)} collective-permute-done((bf16[128,128]{1,0:T(8,128)(2,1)S(1)}, bf16[128,128]{1,0:T(8,128)(2,1)S(1)}, u32[]{:S(2)}, u32[]{:S(2)}) %collective-permute-start.23) | collective-permute-done | bytes 32800 | tf_op jit(solution)/shard_map/ppermute | solution.py:813
  95.2 1.2 %cover_rest.1 = f32[128,2048]{1,0:T(8,128)} custom-call(f32[128,2048]{1,0:T(8,128)S(1)} %cover.1.begun_ref, f32[128,384]{1,0:T(8,128)S(1)} %get-tuple-element.91.rest_0_.refs_0_, bf16[128,256]{1,0:T(8,128)(2,1)S(1)} %collective-permute-done.22.refs_1_, bf16[128,128]{1,0:T(8,128)(2,1)S(1)} %collective-permute-done.23.refs_2_, ...), custom_call_target="tpu_custom_call" | custom-call | tf_op jit(solution)/shard_map/cover_rest/pallas_call | solution.py:784
  (29 shorter events, 0.3 us)
Async XLA Ops:
  0.6 9.9 %copy-start = (bf16[1024,1024]{1,0:T(8,128)(2,1)S(1)}, bf16[1024,1024]{1,0:T(8,128)(2,1)}, u32[]{:S(2)}) copy-start(bf16[1024,1024]{1,0:T(8,128)(2,1)} %q_ref.3) | copy-start | bytes 6291460
  0.6 0.9 copy-start.2
  5.9 10.8 %collective-permute-start = (f32[264,128]{1,0:T(8,128)S(1)}, f32[264,128]{1,0:T(8,128)S(1)}, u32[]{:S(2)}, u32[]{:S(2)}) collective-permute-start(f32[264,128]{1,0:T(8,128)S(1)} %get-tuple-element.56), channel_id=1, source_target_pairs={{0,4},{4,0},{8,12},{12,8},{16,20},{20,16},{24,28},{28,24},{1,5},{5... | collective-permute-start | bytes 405512 | tf_op jit(solution)/shard_map/ppermute | solution.py:802
  9.0 7.7 %collective-permute-start.1 = (f32[264,128]{1,0:T(8,128)S(1)}, f32[264,128]{1,0:T(8,128)S(1)}, u32[]{:S(2)}, u32[]{:S(2)}) collective-permute-start(f32[264,128]{1,0:T(8,128)S(1)} %get-tuple-element.57), channel_id=1, source_target_pairs={{0,8},{4,12},{8,0},{12,4},{16,24},{20,28},{24,16},{28,20},{1,9},{5... | collective-permute-start | bytes 405512 | tf_op jit(solution)/shard_map/ppermute | solution.py:802
  10.5 6.2 %collective-permute-start.2 = (f32[264,128]{1,0:T(8,128)S(1)}, f32[264,128]{1,0:T(8,128)S(1)}, u32[]{:S(2)}, u32[]{:S(2)}) collective-permute-start(f32[264,128]{1,0:T(8,128)S(1)} %get-tuple-element.58), channel_id=1, source_target_pairs={{0,12},{4,8},{8,4},{12,0},{16,28},{20,24},{24,20},{28,16},{1,13},{... | collective-permute-start | bytes 405512 | tf_op jit(solution)/shard_map/ppermute | solution.py:802
  10.5 1.6 %copy-start.1 = (bf16[1024,1024]{1,0:T(8,128)(2,1)S(1)}, bf16[1024,1024]{1,0:T(8,128)(2,1)}, u32[]{:S(2)}) copy-start(bf16[1024,1024]{1,0:T(8,128)(2,1)} %get-tuple-element.51.v_ref) | copy-start | bytes 6291460
  16.7 18.7 %copy-start.3 = (f32[1024]{0:T(1024)S(1)}, f32[1024]{0:T(1024)}, u32[]{:S(2)}) copy-start(f32[1024]{0:T(1024)} %param.9) | copy-start | bytes 12292
  16.8 7.4 %collective-permute-start.3 = (f32[256,128]{1,0:T(8,128)S(1)}, f32[256,128]{1,0:T(8,128)S(1)}, u32[]{:S(2)}, u32[]{:S(2)}) collective-permute-start(f32[256,128]{1,0:T(8,128)S(1)} %get-tuple-element.61), channel_id=1, source_target_pairs={{0,16},{4,20},{8,24},{12,28},{1,17},{5,21},{9,25},{13,29},{2,18},{... | collective-permute-start | bytes 393224 | tf_op jit(solution)/shard_map/ppermute | solution.py:820
  24.3 5.2 %collective-permute-start.4 = (f32[256,128]{1,0:T(8,128)S(1)}, f32[256,128]{1,0:T(8,128)S(1)}, u32[]{:S(2)}, u32[]{:S(2)}) collective-permute-start(f32[256,128]{1,0:T(8,128)S(1)} %get-tuple-element.63), channel_id=1, source_target_pairs={{0,4},{4,0},{8,12},{12,8},{16,20},{20,16},{24,28},{28,24},{1,5},{5... | collective-permute-start | bytes 393224 | tf_op jit(solution)/shard_map/ppermute | solution.py:802
  25.9 7.8 %collective-permute-start.5 = (f32[256,128]{1,0:T(8,128)S(1)}, f32[256,128]{1,0:T(8,128)S(1)}, u32[]{:S(2)}, u32[]{:S(2)}) collective-permute-start(f32[256,128]{1,0:T(8,128)S(1)} %get-tuple-element.64), channel_id=1, source_target_pairs={{0,8},{4,12},{8,0},{12,4},{16,24},{20,28},{24,16},{28,20},{1,9},{5... | collective-permute-start | bytes 393224 | tf_op jit(solution)/shard_map/ppermute | solution.py:802
  29.5 5.9 %collective-permute-start.6 = (f32[256,128]{1,0:T(8,128)S(1)}, f32[256,128]{1,0:T(8,128)S(1)}, u32[]{:S(2)}, u32[]{:S(2)}) collective-permute-start(f32[256,128]{1,0:T(8,128)S(1)} %get-tuple-element.65), channel_id=1, source_target_pairs={{0,12},{4,8},{8,4},{12,0},{16,28},{20,24},{24,20},{28,16},{1,13},{... | collective-permute-start | bytes 393224 | tf_op jit(solution)/shard_map/ppermute | solution.py:802
  39.6 4.4 %collective-permute-start.7 = (bf16[1024,1024]{1,0:T(8,128)(2,1)S(1)}, bf16[1024,1024]{1,0:T(8,128)(2,1)}, u32[]{:S(2)}, u32[]{:S(2)}) collective-permute-start(bf16[1024,1024]{1,0:T(8,128)(2,1)S(1)} %get-tuple-element.66.own_ref.other_ref), channel_id=1, source_target_pairs={{0,1},{1,0},{2,3},{3,2},{4,5},{5,4},{6,7},{7,6},{8,9},{9,8},{10,11... | collective-permute-start | bytes 6291464 | tf_op jit(solution)/shard_map/ppermute | solution.py:805
  41.7 8.8 %collective-permute-start.8 = (bf16[512,256]{1,0:T(8,128)(2,1)S(1)}, bf16[512,256]{1,0:T(8,128)(2,1)S(1)}, u32[]{:S(2)}, u32[]{:S(2)}) collective-permute-start(bf16[512,256]{1,0:T(8,128)(2,1)S(1)} %get-tuple-element.70), channel_id=1, source_target_pairs={{0,4},{4,0},{8,12},{12,8},{16,20},{20,16},{24,28},{28,24},{1,5},{5... | collective-permute-start | bytes 786440 | tf_op jit(solution)/shard_map/ppermute | solution.py:802
  47.6 8.9 %collective-permute-start.9 = (bf16[544,256]{1,0:T(8,128)(2,1)S(1)}, bf16[544,256]{1,0:T(8,128)(2,1)S(1)}, u32[]{:S(2)}, u32[]{:S(2)}) collective-permute-start(bf16[544,256]{1,0:T(8,128)(2,1)S(1)} %get-tuple-element.71), channel_id=1, source_target_pairs={{0,4},{4,0},{8,12},{12,8},{16,20},{20,16},{24,28},{28,24},{1,5},{5... | collective-permute-start | bytes 835592 | tf_op jit(solution)/shard_map/ppermute | solution.py:802
  54.4 12.1 %collective-permute-start.13 = (bf16[512,384]{1,0:T(8,128)(2,1)S(1)}, bf16[512,384]{1,0:T(8,128)(2,1)S(1)}, u32[]{:S(2)}, u32[]{:S(2)}) collective-permute-start(bf16[512,384]{1,0:T(8,128)(2,1)S(1)} %get-tuple-element.79), channel_id=1, source_target_pairs={{0,4},{4,0},{8,12},{12,8},{16,20},{20,16},{24,28},{28,24},{1,5},{5... | collective-permute-start | bytes 1179656 | tf_op jit(solution)/shard_map/ppermute | solution.py:802
  56.6 8.4 %collective-permute-start.10 = (bf16[288,512]{1,0:T(8,128)(2,1)S(1)}, bf16[288,512]{1,0:T(8,128)(2,1)S(1)}, u32[]{:S(2)}, u32[]{:S(2)}) collective-permute-start(bf16[288,512]{1,0:T(8,128)(2,1)S(1)} %get-tuple-element.74), channel_id=1, source_target_pairs={{0,8},{4,12},{8,0},{12,4},{16,24},{20,28},{24,16},{28,20},{1,9},{5... | collective-permute-start | bytes 884744 | tf_op jit(solution)/shard_map/ppermute | solution.py:802
  61.0 10.5 %collective-permute-start.15 = (bf16[512,256]{1,0:T(8,128)(2,1)S(1)}, bf16[512,256]{1,0:T(8,128)(2,1)S(1)}, u32[]{:S(2)}, u32[]{:S(2)}) collective-permute-start(bf16[512,256]{1,0:T(8,128)(2,1)S(1)} %get-tuple-element.83), channel_id=1, source_target_pairs={{0,4},{4,0},{8,12},{12,8},{16,20},{20,16},{24,28},{28,24},{1,5},{5... | collective-permute-start | bytes 786440 | tf_op jit(solution)/shard_map/ppermute | solution.py:802
  66.6 11.4 %collective-permute-start.14 = (bf16[256,384]{1,0:T(8,128)(2,1)S(1)}, bf16[256,384]{1,0:T(8,128)(2,1)S(1)}, u32[]{:S(2)}, u32[]{:S(2)}) collective-permute-start(bf16[256,384]{1,0:T(8,128)(2,1)S(1)} %get-tuple-element.81), channel_id=1, source_target_pairs={{0,8},{4,12},{8,0},{12,4},{16,24},{20,28},{24,16},{28,20},{1,9},{5... | collective-permute-start | bytes 589832 | tf_op jit(solution)/shard_map/ppermute | solution.py:802
  68.0 10.8 %collective-permute-start.11 = (bf16[192,512]{1,0:T(8,128)(2,1)S(1)}, bf16[192,512]{1,0:T(8,128)(2,1)S(1)}, u32[]{:S(2)}, u32[]{:S(2)}) collective-permute-start(bf16[192,512]{1,0:T(8,128)(2,1)S(1)} %get-tuple-element.77), channel_id=1, source_target_pairs={{0,16},{4,20},{8,24},{12,28},{16,0},{20,4},{24,8},{28,12},{1,17},{... | collective-permute-start | bytes 589832 | tf_op jit(solution)/shard_map/ppermute | solution.py:802
  71.5 8.1 %collective-permute-start.16 = (bf16[256,256]{1,0:T(8,128)(2,1)S(1)}, bf16[256,256]{1,0:T(8,128)(2,1)S(1)}, u32[]{:S(2)}, u32[]{:S(2)}) collective-permute-start(bf16[256,256]{1,0:T(8,128)(2,1)S(1)} %get-tuple-element.87), channel_id=1, source_target_pairs={{0,8},{4,12},{8,0},{12,4},{16,24},{20,28},{24,16},{28,20},{1,9},{5... | collective-permute-start | bytes 393224 | tf_op jit(solution)/shard_map/ppermute | solution.py:802
  78.1 8.2 %collective-permute-start.18 = (bf16[128,384]{1,0:T(8,128)(2,1)S(1)}, bf16[128,384]{1,0:T(8,128)(2,1)S(1)}, u32[]{:S(2)}, u32[]{:S(2)}) collective-permute-start(bf16[128,384]{1,0:T(8,128)(2,1)S(1)} %get-tuple-element.90), channel_id=1, source_target_pairs={{0,16},{4,20},{8,24},{12,28},{16,0},{20,4},{24,8},{28,12},{1,17},{... | collective-permute-start | bytes 294920 | tf_op jit(solution)/shard_map/ppermute | solution.py:802
  79.6 7.3 %collective-permute-start.17 = (bf16[128,256]{1,0:T(8,128)(2,1)S(1)}, bf16[128,256]{1,0:T(8,128)(2,1)S(1)}, u32[]{:S(2)}, u32[]{:S(2)}) collective-permute-start(bf16[128,256]{1,0:T(8,128)(2,1)S(1)} %get-tuple-element.89), channel_id=1, source_target_pairs={{0,16},{4,20},{8,24},{12,28},{16,0},{20,4},{24,8},{28,12},{1,17},{... | collective-permute-start | bytes 196616 | tf_op jit(solution)/shard_map/ppermute | solution.py:802
  82.4 7.0 %collective-permute-start.19 = (bf16[128,256]{1,0:T(8,128)(2,1)S(1)}, bf16[128,256]{1,0:T(8,128)(2,1)S(1)}, u32[]{:S(2)}, u32[]{:S(2)}) collective-permute-start(bf16[128,256]{1,0:T(8,128)(2,1)S(1)} %get-tuple-element.92), channel_id=1, source_target_pairs={{0,4},{4,8},{8,12},{12,16},{16,20},{20,24},{24,28},{28,0},{1,5},{5... | collective-permute-start | bytes 196616 | tf_op jit(solution)/shard_map/ppermute | solution.py:813
  83.9 2.4 %collective-permute-start.12 = (f32[8,1024]{1,0:T(8,128)S(1)}, f32[8,1024]{1,0:T(8,128)S(1)}, u32[]{:S(2)}, u32[]{:S(2)}) collective-permute-start(f32[8,1024]{1,0:T(8,128)S(1)} %reduce_sum.9.means_ref), channel_id=1, source_target_pairs={{0,1},{1,0},{2,3},{3,2},{4,5},{5,4},{6,7},{7,6},{8,9},{9,8},{10,11... | collective-permute-start | bytes 98312 | tf_op jit(solution)/shard_map/ppermute | solution.py:805
  84.0 7.8 %collective-permute-start.20 = (bf16[128,256]{1,0:T(8,128)(2,1)S(1)}, bf16[128,256]{1,0:T(8,128)(2,1)S(1)}, u32[]{:S(2)}, u32[]{:S(2)}) collective-permute-start(bf16[128,256]{1,0:T(8,128)(2,1)S(1)} %get-tuple-element.93), channel_id=1, source_target_pairs={{0,8},{4,12},{8,16},{12,20},{16,24},{20,28},{24,0},{28,4},{1,9},{5... | collective-permute-start | bytes 196616 | tf_op jit(solution)/shard_map/ppermute | solution.py:813
  86.2 5.6 %collective-permute-start.21 = (bf16[128,256]{1,0:T(8,128)(2,1)S(1)}, bf16[128,256]{1,0:T(8,128)(2,1)S(1)}, u32[]{:S(2)}, u32[]{:S(2)}) collective-permute-start(bf16[128,256]{1,0:T(8,128)(2,1)S(1)} %get-tuple-element.94), channel_id=1, source_target_pairs={{0,1},{1,0},{2,3},{3,2},{4,5},{5,4},{6,7},{7,6},{8,9},{9,8},{10,11... | collective-permute-start | bytes 196616 | tf_op jit(solution)/shard_map/ppermute | solution.py:805
  86.3 8.9 %collective-permute-start.22 = (bf16[128,256]{1,0:T(8,128)(2,1)S(1)}, bf16[128,256]{1,0:T(8,128)(2,1)S(1)}, u32[]{:S(2)}, u32[]{:S(2)}) collective-permute-start(bf16[128,256]{1,0:T(8,128)(2,1)S(1)} %get-tuple-element.95), channel_id=1, source_target_pairs={{0,12},{4,16},{8,20},{12,24},{16,28},{20,0},{24,4},{28,8},{1,13},{... | collective-permute-start | bytes 196616 | tf_op jit(solution)/shard_map/ppermute | solution.py:813
  86.9 8.3 %collective-permute-start.24 = (bf16[128,256]{1,0:T(8,128)(2,1)S(1)}, bf16[128,256]{1,0:T(8,128)(2,1)S(1)}, u32[]{:S(2)}, u32[]{:S(2)}) collective-permute-start(bf16[128,256]{1,0:T(8,128)(2,1)S(1)} %get-tuple-element.97), channel_id=1, source_target_pairs={{0,1},{1,0},{2,3},{3,2},{4,5},{5,4},{6,7},{7,6},{8,9},{9,8},{10,11... | collective-permute-start | bytes 196616 | tf_op jit(solution)/shard_map/ppermute | solution.py:805
  89.4 5.8 %collective-permute-start.23 = (bf16[128,128]{1,0:T(8,128)(2,1)S(1)}, bf16[128,128]{1,0:T(8,128)(2,1)S(1)}, u32[]{:S(2)}, u32[]{:S(2)}) collective-permute-start(bf16[128,128]{1,0:T(8,128)(2,1)S(1)} %get-tuple-element.96), channel_id=1, source_target_pairs={{0,16},{4,20},{8,24},{12,28},{16,0},{20,4},{24,8},{28,12},{1,17},{... | collective-permute-start | bytes 98312 | tf_op jit(solution)/shard_map/ppermute | solution.py:813

commit v6 on v5

--- a/solution.py
+++ b/solution.py
@@ -263,7 +263,7 @@
     )(*pieces, after)
 
 
-def spread_kernel(inside_ref, left_ref, entered_ref, *outs):
+def spread_kernel(inside_ref, left_ref, entered_ref, _, *outs):
     near, rows, _ = inside_ref.shape
     mine = lax.axis_index("ctx") % near
     for apart, out_ref in enumerate(outs):
@@ -275,16 +275,16 @@
             out_ref[cols, :] = inside_ref[shard, cols, :] + part
 
 
-def spread_states(inside, left, entered):
+def spread_states(inside, left, entered, after):
     near, rows, _ = inside.shape
     return pl.pallas_call(
         spread_kernel,
-        in_specs=[vmem()] * 3,
+        in_specs=[vmem()] * 3 + [anywhere()],
         out_specs=[vmem()] * near,
         out_shape=[struct((rows, HEAD_DIM), F32)] * near,
         compiler_params=params(16),
         name="spread_states",
-    )(inside, left, entered)
+    )(inside, left, entered, after)
 
 
 def inner_block(q_ref, k_ref, v_ref, first, cumul, raw_ref):
@@ -323,31 +323,40 @@
     inner_block(q_ref, k_ref, v_ref, 0, cumul_ref[...], raw_ref)
 
 
-def inner_loop_kernel(q_ref, k_ref, v_ref, cumul_ref, raw_ref):
-    @pl.loop(0, q_ref.shape[0] // SPAN)
+def inner_loop_kernel(begin, end, q_ref, k_ref, v_ref, cumul_ref, *rest):
+    raw_ref, token_ref = rest[-2:]
+    token_ref[...] = jnp.zeros_like(token_ref)
+
+    @pl.loop(begin, end)
     def _(index):
         cumul = cumul_ref[lines_at(cumul_ref, index, q_ref.shape[0] // SPAN), :]
         inner_block(q_ref, k_ref, v_ref, index * SPAN, cumul, raw_ref)
 
 
-def inner(queries, keys, values, cumul):
+def inner(queries, keys, values, cumul, part, *earlier):
     count, width = keys.shape
+    blocks = count // SPAN
     heads = width // HEAD_DIM
+    token = struct((8, HEAD_DIM), F32)
     work = cost(4 * count * width * SPAN, 10 * count * width, count * heads * SPAN)
     if fits(count, width):
+        begin, end = (0, blocks // 2) if part == 0 else (blocks // 2, blocks)
         return pl.pallas_call(
-            inner_loop_kernel,
-            in_specs=[vmem()] * 4,
-            out_specs=vmem(),
-            out_shape=struct((count, width), F32),
+            functools.partial(inner_loop_kernel, begin, end),
+            in_specs=[vmem()] * 4 + [vmem(), anywhere()][: len(earlier)],
+            out_specs=[vmem()] * 2,
+            out_shape=[struct((count, width), F32), token],
+            input_output_aliases={4: 0} if earlier else {},
             compiler_params=params(16),
             cost_estimate=work,
             name="inner",
-        )(queries, keys, values, cumul)
+        )(queries, keys, values, cumul, *earlier)
+    if part:
+        return earlier[0], earlier[1]
     tokens = pl.BlockSpec((SPAN, width), lambda i: (i, 0))
-    return pl.pallas_call(
+    raw = pl.pallas_call(
         inner_kernel,
-        grid=(count // SPAN,),
+        grid=(blocks,),
         in_specs=[tokens, tokens, tokens, pl.BlockSpec((heads, SPAN), lambda i: (i, 0))],
         out_specs=tokens,
         out_shape=struct((count, width), F32),
@@ -355,6 +364,7 @@
         cost_estimate=work,
         name="inner",
     )(queries, keys, values, cumul)
+    return raw, cumul
 
 
 def finish_start(near, pieces, arrived, sums):
@@ -402,17 +412,21 @@
             sums[16:24, cols] = jnp.minimum(sums[16:24, cols], jnp.min(wide, axis=0))
 
 
-def finish_end(centered_ref, stats_ref, sums):
-    count, width = centered_ref.shape
-    mean = jnp.sum(sums[0:8, :], axis=0, keepdims=True) / count
+def stat_lines(mean, sums):
     first, rest = split(mean)
     rest = mean - first.astype(F32)
     second, third = split(rest)
     top = jnp.max(sums[8:16, :], axis=0, keepdims=True)
     bottom = jnp.min(sums[16:24, :], axis=0, keepdims=True)
     lines = [first.astype(F32), second.astype(F32), third.astype(F32), top, bottom]
-    lines.append(jnp.zeros((11, width), F32))
-    stats_ref[...] = jnp.concatenate(lines, axis=0).astype(BF16)
+    lines.append(jnp.zeros((11, mean.shape[1]), F32))
+    return jnp.concatenate(lines, axis=0).astype(BF16)
+
+
+def finish_end(centered_ref, stats_ref, sums):
+    count, width = centered_ref.shape
+    mean = jnp.sum(sums[0:8, :], axis=0, keepdims=True) / count
+    stats_ref[...] = stat_lines(mean, sums)
 
     @pl.loop(0, count // 128)
     def _(index):
@@ -449,30 +463,66 @@
         finish_end(centered_ref, stats_ref, sums)
 
 
-def finish_loop_kernel(
-    near, q_ref, raw_ref, entering_ref, before_ref, cumul_ref, gain_ref, *rest
+def finish_part_kernel(
+    near, part, q_ref, raw_ref, entering_ref, before_ref, cumul_ref, gain_ref, *rest
 ):
-    pieces, (centered_ref, stats_ref, arrived, sums) = rest[:near], rest[near:]
-    finish_start(near, pieces, arrived, sums)
-
-    @pl.loop(0, q_ref.shape[0] // SPAN)
+    pieces, rest = rest[: near // 2], rest[near // 2 :]
+    centered_ref, stats_ref, arrived, sums = rest[-4:]
+    count, width = centered_ref.shape
+    span = width // 2
+    heads = span // HEAD_DIM
+    blocks = count // SPAN
+    rows = width // near
+    mine = lax.axis_index("ctx") % near
+    half = (mine // (near // 2)) ^ part
+    low = pl.multiple_of(half * span, span)
+    every = pl.ds(low, span)
+    for place, piece in enumerate(pieces):
+        start = pl.multiple_of((mine % (near // 2) ^ place) * rows, rows)
+        arrived[pl.ds(start, rows), :] = piece[...]
+    sums[0:8, :] = jnp.zeros((8, span), F32)
+    sums[8:16, :] = jnp.full((8, span), -jnp.inf, F32)
+    sums[16:24, :] = jnp.full((8, span), jnp.inf, F32)
+
+    @pl.loop(0, blocks, unroll=2)
+    def _(block):
+        here = span_at(block * SPAN)
+        cumul = cumul_ref[lines_at(cumul_ref, block, blocks), :]
+        left = before_ref[block]
+        cumul = jnp.where(half == 0, cumul[:heads], cumul[heads:])
+        left = jnp.where(half == 0, left[:heads], left[heads:])
+        factor = widen(jnp.exp(cumul))
+        outers = []
+        for head in range(heads):
+            cols = pl.ds(pl.multiple_of(low + head * HEAD_DIM, HEAD_DIM), HEAD_DIM)
+            state = entering_ref[block, cols, :]
+            state = state + left[head : head + 1, :] * arrived[head_columns(head), :]
+            query = q_ref[here, cols]
+            outers.append(
+                dot(
+                    jnp.concatenate([query, query], axis=1),
+                    jnp.concatenate(split(state), axis=0),
+                )
+            )
+        for head, outer in enumerate(outers):
+            cols = pl.ds(pl.multiple_of(low + head * HEAD_DIM, HEAD_DIM), HEAD_DIM)
+            local = head_columns(head)
+            raw = raw_ref[here, cols] + outer * factor[:, local]
+            power = jnp.mean(raw * raw, axis=1, keepdims=True)
+            attended = (raw * lax.rsqrt(power + 1e-06) * gain_ref[:, cols]).astype(BF16)
+            centered_ref[here, cols] = attended
+            wide = attended.astype(F32).reshape(SPAN // 8, 8, HEAD_DIM)
+            sums[0:8, local] += jnp.sum(wide, axis=0)
+            sums[8:16, local] = jnp.maximum(sums[8:16, local], jnp.max(wide, axis=0))
+            sums[16:24, local] = jnp.minimum(sums[16:24, local], jnp.min(wide, axis=0))
+
+    mean = jnp.sum(sums[0:8, :], axis=0, keepdims=True) / count
+    stats_ref[:, every] = stat_lines(mean, sums)
+
+    @pl.loop(0, count // 128)
     def _(index):
-        here = span_at(index * SPAN)
-        finish_block(
-            q_ref,
-            raw_ref,
-            index * SPAN,
-            entering_ref,
-            before_ref,
-            cumul_ref[lines_at(cumul_ref, index, q_ref.shape[0] // SPAN), :],
-            gain_ref,
-            centered_ref,
-            here,
-            arrived,
-            sums,
-        )
-
-    finish_end(centered_ref, stats_ref, sums)
+        part = pl.ds(pl.multiple_of(index * 128, 128), 128)
+        centered_ref[part, every] = (centered_ref[part, every].astype(F32) - mean).astype(BF16)
 
 
 def finish(queries, raw, entering, before, cumul, gain, pieces):
@@ -483,17 +533,25 @@
     scratch = [pltpu.VMEM((width, HEAD_DIM), F32), pltpu.VMEM((24, width), F32)]
     work = cost(4 * count * width * HEAD_DIM, 10 * count * width)
     operands = (queries, raw, entering, before, cumul, gain, *pieces)
-    if fits(count, width):
-        return pl.pallas_call(
-            functools.partial(finish_loop_kernel, near),
-            in_specs=[vmem()] * len(operands),
-            out_specs=[vmem()] * 2,
-            scratch_shapes=scratch,
-            out_shape=shapes,
-            compiler_params=params(16),
-            cost_estimate=work,
-            name="finish",
-        )(*operands)
+    if fits(count, width) and width == 8 * HEAD_DIM:
+        done = ()
+        for part in range(2):
+            mine = operands[:6] + tuple(pieces[part * near // 2 : (part + 1) * near // 2])
+            done = pl.pallas_call(
+                functools.partial(finish_part_kernel, near, part),
+                in_specs=[vmem()] * (len(mine) + len(done)),
+                out_specs=[vmem()] * 2,
+                scratch_shapes=[
+                    pltpu.VMEM((width // 2, HEAD_DIM), F32),
+                    pltpu.VMEM((24, width // 2), F32),
+                ],
+                out_shape=shapes,
+                input_output_aliases={len(mine): 0, len(mine) + 1: 1} if done else {},
+                compiler_params=params(16),
+                cost_estimate=work,
+                name="finish",
+            )(*mine, *done)
+        return done
     tokens = pl.BlockSpec((SPAN, width), lambda i: (i, 0))
     return pl.pallas_call(
         functools.partial(finish_kernel, near),
@@ -815,10 +873,11 @@
     (entering, before, cumul), pieces, (keys, values) = local_states(
         keys, values, log_decay, near
     )
-    raw = inner(queries, keys, values, cumul)
-    inside, left, leaving = chain(nearby(pieces), raw)
+    raw, token = inner(queries, keys, values, cumul, 0)
+    inside, left, leaving = chain(nearby(pieces), token)
     entered = lax.ppermute(leaving, "ctx", [(a, a + near) for a in range(near)])
-    entry = nearby(spread_states(inside, left, entered))
+    raw, token = inner(queries, keys, values, cumul, 1, raw, leaving)
+    entry = nearby(spread_states(inside, left, entered, token))
     centered, stats = finish(
         queries, raw, entering, before, cumul, gain.reshape(1, width), entry
     )

time: 96.6 us -> 93.2 us (0.965)
  starting transfers between devices: 36.3 us -> 30.7 us
  waiting for transfers between devices: 27.3 us -> 29.3 us
    ppermute x16, starting transfers between devices: 25.9 us -> 22.1 us  [to_shard(): return lax.ppermute(value, 'ctx', [(a, a ^ apart) for a in range(shards)])]
    ppermute x16, waiting for transfers between devices: 19.3 us -> 22.2 us  [to_shard(): return lax.ppermute(value, 'ctx', [(a, a ^ apart) for a in range(shards)])]
    ppermute x1, waiting for transfers between devices: 2.51 us -> 0.19 us  [body(): entered = lax.ppermute(leaving, 'ctx', [(a, a + near) for a in range(near)])]
    ppermute x4, starting transfers between devices: 5.28 us -> 3.83 us  [forward(): lax.ppermute(value, 'ctx', [(a, (a + step) % shards) for a in range(shard...]
    pallas_call x3 -> x5, Pallas kernels: 8.76 us -> 8.89 us  [the longest x2 4.56 us: inner(): pl.pallas_call(functools.partial(inner_loop_kernel, begin, end), in_specs...]
    unnamed x9 -> x11, local copies, waits for them, and re-layouts: 3.1 us -> 3.1 us
  transfers between devices with their start and end apart: 25 -> 25, of which waited for: 14 -> 17; matrix products, arithmetic and copies ran while one was open for 1% -> 1% of each run, Pallas kernels for 19% -> 22%
where the time goes in v6:
time: 93.2 us; the launch traced here: 92.9 us
  starting transfers between devices  30.7 us (33%)
  waiting for transfers between devices  29.3 us (31%)
  Pallas kernels  28.6 us (31%)
  local copies, waits for them, and re-layouts  3.24 us (3%)
  between operations  0.97 us (1%)
    ppermute x16, waiting for transfers between devices, to_shard(): return lax.ppermute(value, 'ctx', [(a, a ^ apart) for a in range(shards)])  22.2 us
    ppermute x16, starting transfers between devices, to_shard(): return lax.ppermute(value, 'ctx', [(a, a ^ apart) for a in range(shards)])  22.1 us
    pallas_call x4, Pallas kernels, gram_parts(): pl.pallas_call(functools.partial(gram_kernel, rows, blocks, apart), in_sp...  12.5 us
    ppermute x4, waiting for transfers between devices, forward(): lax.ppermute(value, 'ctx', [(a, (a + step) % shards) for a in range(shard...  5.37 us
    ppermute x1, starting transfers between devices, body(): entered = lax.ppermute(leaving, 'ctx', [(a, a + near) for a in range(near)])  4.65 us
    pallas_call x2, Pallas kernels, inner(): pl.pallas_call(functools.partial(inner_loop_kernel, begin, end), in_specs...  4.56 us
    pallas_call x1, Pallas kernels, local_states(): pl.pallas_call(functools.partial(states_fetch_kernel, near), in_specs=[hb...  4.35 us
    pallas_call x2, Pallas kernels, finish(): pl.pallas_call(functools.partial(finish_part_kernel, near, part), in_spec...  4.28 us
  transfers between devices with their start and end apart: 25, of which 17 were waited for; matrix products, arithmetic and copies ran while one was open for 1% of the time, Pallas kernels for 22%

profile of v6, /device:TPU:0, one launch (start us, length us, event | category | flops | bytes accessed | tf_op | source)
XLA Modules:
  0.0 92.9 jit_solution(993296872526895765)
XLA Ops:
  0.7 0.9 copy-done.3
  1.5 4.4 %local_states.1 = (f32[4,1024,128]{2,1,0:T(8,128)S(1)}, f32[4,8,128]{2,1,0:T(8,128)S(1)}, f32[32,256]{1,0:T(8,128)S(1)}, f32[264,128]{1,0:T(8,128)S(1)}, f32[264...) custom-call(bf16[1024,1024]{1,0:T(8,128)(2,1)} %k_any.1, ...), custom_call_target="tpu_custom_call" | custom-call | flops 1 | bytes 1 | tf_op jit(solution)/shard_map/local_states/pallas_call | solution.py:197
  5.9 3.0 %collective-permute-start = (f32[264,128]{1,0:T(8,128)S(1)}, f32[264,128]{1,0:T(8,128)S(1)}, u32[]{:S(2)}, u32[]{:S(2)}) collective-permute-start(f32[264,128]{1,0:T(8,128)S(1)} %get-tuple-element.61), channel_id=1, source_target_pairs={{0,4},{4,0},{8,12},{12,8},{16,20},{20,16},{24,28},{28,24},{1,5},{5... | collective-permute-start | bytes 405512 | tf_op jit(solution)/shard_map/ppermute | solution.py:860
  8.9 1.6 %collective-permute-start.1 = (f32[264,128]{1,0:T(8,128)S(1)}, f32[264,128]{1,0:T(8,128)S(1)}, u32[]{:S(2)}, u32[]{:S(2)}) collective-permute-start(f32[264,128]{1,0:T(8,128)S(1)} %get-tuple-element.62), channel_id=1, source_target_pairs={{0,8},{4,12},{8,0},{12,4},{16,24},{20,28},{24,16},{28,20},{1,9},{5... | collective-permute-start | bytes 405512 | tf_op jit(solution)/shard_map/ppermute | solution.py:860
  10.5 1.6 %copy-done.1 = bf16[1024,1024]{1,0:T(8,128)(2,1)S(1)} copy-done((bf16[1024,1024]{1,0:T(8,128)(2,1)S(1)}, bf16[1024,1024]{1,0:T(8,128)(2,1)}, u32[]{:S(2)}) %copy-start.1) | copy-done | bytes 2097176
  12.1 2.3 %inner.2 = (f32[1024,1024]{1,0:T(8,128)S(1)}, f32[8,128]{1,0:T(8,128)S(1)}) custom-call(bf16[1024,1024]{1,0:T(8,128)(2,1)S(1)} %copy-done, bf16[1024,1024]{1,0:T(8,128)(2,1)S(1)} %get-tuple-element.56.k_ref, bf16[1024,1024]{1,0:T(8,128)(2,1)S(1)} %copy-done.1, f32[32,256]{1,0:T(8,128)S(1)} %get-tuple-element.58.cumul_ref), custom_call_target="tpu_custom_call" | custom-call | flops 1 | bytes 1 | tf_op jit(solution)/shard_map/inner/pallas_call | solution.py:344
  14.4 1.0 %collective-permute-done.1.refs_2_ = f32[264,128]{1,0:T(8,128)S(1)} collective-permute-done((f32[264,128]{1,0:T(8,128)S(1)}, f32[264,128]{1,0:T(8,128)S(1)}, u32[]{:S(2)}, u32[]{:S(2)}) %collective-permute-start.1) | collective-permute-done | bytes 135200 | tf_op jit(solution)/shard_map/ppermute | solution.py:860
  15.4 1.2 %collective-permute-done.2.refs_3_ = f32[264,128]{1,0:T(8,128)S(1)} collective-permute-done((f32[264,128]{1,0:T(8,128)S(1)}, f32[264,128]{1,0:T(8,128)S(1)}, u32[]{:S(2)}, u32[]{:S(2)}) %collective-permute-start.2) | collective-permute-done | bytes 135200 | tf_op jit(solution)/shard_map/ppermute | solution.py:860
  16.7 0.1 chain.1
  16.8 4.6 %collective-permute-start.3 = (f32[256,128]{1,0:T(8,128)S(1)}, f32[256,128]{1,0:T(8,128)S(1)}, u32[]{:S(2)}, u32[]{:S(2)}) collective-permute-start(f32[256,128]{1,0:T(8,128)S(1)} %get-tuple-element.65.rest_1_), channel_id=1, source_target_pairs={{0,16},{4,20},{8,24},{12,28},{1,17},{5,21},{9,25},{13,29},{2,18},{... | collective-permute-start | bytes 393224 | tf_op jit(solution)/shard_map/ppermute | solution.py:878
  21.4 0.0 copy-start.4
  21.5 2.3 %inner.3 = (f32[1024,1024]{1,0:T(8,128)S(1)}, f32[8,128]{1,0:T(8,128)S(1)}) custom-call(bf16[1024,1024]{1,0:T(8,128)(2,1)S(1)} %copy-done, bf16[1024,1024]{1,0:T(8,128)(2,1)S(1)} %get-tuple-element.56.k_ref, bf16[1024,1024]{1,0:T(8,128)(2,1)S(1)} %copy-done.2, f32[32,256]{1,0:T(8,128)S(1)} %get-tuple-element.58.cumul_ref, ...), custom_call_target="tpu_custom_call", output_to_operand_aliasing={{0}: (4, {})} | custom-call | flops 1 | bytes 1 | tf_op jit(solution)/shard_map/inner/pallas_call | solution.py:344
  23.7 0.2 collective-permute-done.3.entered_ref
  23.9 0.1 spread_states.1
  24.0 1.6 %collective-permute-start.6 = (f32[256,128]{1,0:T(8,128)S(1)}, f32[256,128]{1,0:T(8,128)S(1)}, u32[]{:S(2)}, u32[]{:S(2)}) collective-permute-start(f32[256,128]{1,0:T(8,128)S(1)} %get-tuple-element.75), channel_id=1, source_target_pairs={{0,4},{4,0},{8,12},{12,8},{16,20},{20,16},{24,28},{28,24},{1,5},{5... | collective-permute-start | bytes 393224 | tf_op jit(solution)/shard_map/ppermute | solution.py:860
  25.6 3.0 %collective-permute-start.4 = (f32[256,128]{1,0:T(8,128)S(1)}, f32[256,128]{1,0:T(8,128)S(1)}, u32[]{:S(2)}, u32[]{:S(2)}) collective-permute-start(f32[256,128]{1,0:T(8,128)S(1)} %get-tuple-element.72), channel_id=1, source_target_pairs={{0,8},{4,12},{8,0},{12,4},{16,24},{20,28},{24,16},{28,20},{1,9},{5... | collective-permute-start | bytes 393224 | tf_op jit(solution)/shard_map/ppermute | solution.py:860
  28.6 0.1 collective-permute-start.5
  28.7 1.8 %collective-permute-done.6.rest_1_ = f32[256,128]{1,0:T(8,128)S(1)} collective-permute-done((f32[256,128]{1,0:T(8,128)S(1)}, f32[256,128]{1,0:T(8,128)S(1)}, u32[]{:S(2)}, u32[]{:S(2)}) %collective-permute-start.6) | collective-permute-done | bytes 131104 | tf_op jit(solution)/shard_map/ppermute | solution.py:860
  30.4 2.1 %finish.2 = (bf16[1024,1024]{1,0:T(8,128)(2,1)S(1)}, bf16[16,1024]{1,0:T(8,128)(2,1)S(1)}) custom-call(bf16[1024,1024]{1,0:T(8,128)(2,1)S(1)} %copy-done, f32[1024,1024]{1,0:T(8,128)S(1)} %get-tuple-element.66.raw_ref, f32[4,1024,128]{2,1,0:T(8,128)S(1)} %get-tuple-element.67.entering_ref, f32[4,8,128]{2,1,0:T(8,128)S(1)} %get-tuple-element.68.before_ref, ...), custom_call_target="tpu_custom_call" | custom-call | flops 1 | bytes 1 | tf_op jit(solution)/shard_map/finish/pallas_call | solution.py:540
  32.6 1.9 %collective-permute-done.5.rest_1_ = f32[256,128]{1,0:T(8,128)S(1)} collective-permute-done((f32[256,128]{1,0:T(8,128)S(1)}, f32[256,128]{1,0:T(8,128)S(1)}, u32[]{:S(2)}, u32[]{:S(2)}) %collective-permute-start.5) | collective-permute-done | bytes 131104 | tf_op jit(solution)/shard_map/ppermute | solution.py:860
  34.5 2.1 %finish.3 = (bf16[1024,1024]{1,0:T(8,128)(2,1)S(1)}, bf16[16,1024]{1,0:T(8,128)(2,1)S(1)}) custom-call(bf16[1024,1024]{1,0:T(8,128)(2,1)S(1)} %copy-done, f32[1024,1024]{1,0:T(8,128)S(1)} %get-tuple-element.66.raw_ref, f32[4,1024,128]{2,1,0:T(8,128)S(1)} %get-tuple-element.67.entering_ref, ...), custom_call_target="tpu_custom_call", output_to_operand_aliasing={{0}: (8, {}), {1}: (9, {})} | custom-call | flops 1 | bytes 1 | tf_op jit(solution)/shard_map/finish/pallas_call | solution.py:540
  36.6 0.1 collective-permute-start.7
  36.7 2.0 %gram.4 = (f32[512,256]{1,0:T(8,128)S(1)}, bf16[512,256]{1,0:T(8,128)(2,1)S(1)}) custom-call(bf16[1024,1024]{1,0:T(8,128)(2,1)S(1)} %get-tuple-element.78.own_ref.other_ref, bf16[1024,1024]{1,0:T(8,128)(2,1)S(1)} %get-tuple-element.78.own_ref.other_ref, bf16[16,1024]{1,0:T(8,128)(2,1)S(1)} %get-tuple-element.79.rest_0_), custom_call_target="tpu_custom_call" | custom-call | flops 1 | bytes 1 | tf_op jit(solution)/shard_map/gram/pallas_call | solution.py:650
  38.7 0.7 collective-permute-start.8
  39.5 1.5 %collective-permute-done.7.other_ref = bf16[1024,1024]{1,0:T(8,128)(2,1)} collective-permute-done((bf16[1024,1024]{1,0:T(8,128)(2,1)S(1)}, bf16[1024,1024]{1,0:T(8,128)(2,1)}, u32[]{:S(2)}, u32[]{:S(2)}) %collective-permute-start.7) | collective-permute-done | bytes 2097184 | tf_op jit(solution)/shard_map/ppermute | solution.py:863
  41.0 3.8 %gram.5 = (f32[512,256]{1,0:T(8,128)S(1)}, bf16[544,256]{1,0:T(8,128)(2,1)S(1)}) custom-call(bf16[1024,1024]{1,0:T(8,128)(2,1)S(1)} %get-tuple-element.78.own_ref.other_ref, bf16[1024,1024]{1,0:T(8,128)(2,1)} %collective-permute-done.7.other_ref, bf16[32,256]{1,0:T(8,128)(2,1)S(1)} %pad.4.rest_0_.refs_5_, f32[512,256]{1,0:T(8,128)S(1)} %get-tuple-element.80.rest_1_.refs_0_), custom_call_target="tpu_custom_call" | custom-call | flops 1 | bytes 1 | tf_op jit(solution)/shard_map/gram/pallas_call | solution.py:650
  44.8 0.7 collective-permute-start.9
  45.5 2.0 %collective-permute-done.8.rest_0_.refs_2_ = bf16[512,256]{1,0:T(8,128)(2,1)S(1)} collective-permute-done((bf16[512,256]{1,0:T(8,128)(2,1)S(1)}, bf16[512,256]{1,0:T(8,128)(2,1)S(1)}, u32[]{:S(2)}, u32[]{:S(2)}) %collective-permute-start.8) | collective-permute-done | bytes 262176 | tf_op jit(solution)/shard_map/ppermute | solution.py:860
  47.5 3.7 %gram.6 = (f32[512,384]{1,0:T(8,128)S(1)}, bf16[512,384]{1,0:T(8,128)(2,1)S(1)}) custom-call(bf16[1024,1024]{1,0:T(8,128)(2,1)S(1)} %get-tuple-element.78.own_ref.other_ref, bf16[1024,1024]{1,0:T(8,128)(2,1)} %collective-permute-done.7.other_ref, bf16[512,256]{1,0:T(8,128)(2,1)S(1)} %collective-permute-done.8.rest_0_.refs_2_), custom_call_target="tpu_custom_call" | custom-call | flops 1 | bytes 1 | tf_op jit(solution)/shard_map/gram/pallas_call | solution.py:650
  51.2 0.7 collective-permute-start.13
  52.0 1.6 %collective-permute-done.9.refs_3_ = bf16[544,256]{1,0:T(8,128)(2,1)S(1)} collective-permute-done((bf16[544,256]{1,0:T(8,128)(2,1)S(1)}, bf16[544,256]{1,0:T(8,128)(2,1)S(1)}, u32[]{:S(2)}, u32[]{:S(2)}) %collective-permute-start.9) | collective-permute-done | bytes 278560 | tf_op jit(solution)/shard_map/ppermute | solution.py:860
  53.5 0.1 fold.6
  53.6 0.6 collective-permute-start.10
  54.3 3.0 %gram.7 = (f32[512,256]{1,0:T(8,128)S(1)}, bf16[512,256]{1,0:T(8,128)(2,1)S(1)}) custom-call(bf16[1024,1024]{1,0:T(8,128)(2,1)S(1)} %get-tuple-element.78.own_ref.other_ref, bf16[1024,1024]{1,0:T(8,128)(2,1)} %collective-permute-done.7.other_ref, f32[256,512]{1,0:T(8,128)S(1)} %get-tuple-element.85.refs_0_.refs_2_.rest_0_), custom_call_target="tpu_custom_call" | custom-call | flops 1 | bytes 1 | tf_op jit(solution)/shard_map/gram/pallas_call | solution.py:650
  57.2 1.5 %collective-permute-start.15 = (bf16[512,256]{1,0:T(8,128)(2,1)S(1)}, bf16[512,256]{1,0:T(8,128)(2,1)S(1)}, u32[]{:S(2)}, u32[]{:S(2)}) collective-permute-start(bf16[512,256]{1,0:T(8,128)(2,1)S(1)} %get-tuple-element.95), channel_id=1, source_target_pairs={{0,4},{4,0},{8,12},{12,8},{16,20},{20,16},{24,28},{28,24},{1,5},{5... | collective-permute-start | bytes 786440 | tf_op jit(solution)/shard_map/ppermute | solution.py:860
  58.7 3.2 %collective-permute-done.10.refs_1_ = bf16[288,512]{1,0:T(8,128)(2,1)S(1)} collective-permute-done((bf16[288,512]{1,0:T(8,128)(2,1)S(1)}, bf16[288,512]{1,0:T(8,128)(2,1)S(1)}, u32[]{:S(2)}, u32[]{:S(2)}) %collective-permute-start.10) | collective-permute-done | bytes 294944 | tf_op jit(solution)/shard_map/ppermute | solution.py:860
  61.9 0.1 fold.7
  62.0 1.3 %collective-permute-done.13.refs_1_ = bf16[512,384]{1,0:T(8,128)(2,1)S(1)} collective-permute-done((bf16[512,384]{1,0:T(8,128)(2,1)S(1)}, bf16[512,384]{1,0:T(8,128)(2,1)S(1)}, u32[]{:S(2)}, u32[]{:S(2)}) %collective-permute-start.13) | collective-permute-done | bytes 393248 | tf_op jit(solution)/shard_map/ppermute | solution.py:860
  63.3 0.1 fold.8
  63.4 0.6 collective-permute-start.14
  64.0 4.1 %collective-permute-start.11 = (bf16[192,512]{1,0:T(8,128)(2,1)S(1)}, bf16[192,512]{1,0:T(8,128)(2,1)S(1)}, u32[]{:S(2)}, u32[]{:S(2)}) collective-permute-start(bf16[192,512]{1,0:T(8,128)(2,1)S(1)} %get-tuple-element.89), channel_id=1, source_target_pairs={{0,16},{4,20},{8,24},{12,28},{16,0},{20,4},{24,8},{28,12},{1,17},{... | collective-permute-start | bytes 589832 | tf_op jit(solution)/shard_map/ppermute | solution.py:860
  68.2 0.8 collective-permute-start.16
  69.0 5.8 %collective-permute-done.14.refs_1_ = bf16[256,384]{1,0:T(8,128)(2,1)S(1)} collective-permute-done((bf16[256,384]{1,0:T(8,128)(2,1)S(1)}, bf16[256,384]{1,0:T(8,128)(2,1)S(1)}, u32[]{:S(2)}, u32[]{:S(2)}) %collective-permute-start.14) | collective-permute-done | bytes 196640 | tf_op jit(solution)/shard_map/ppermute | solution.py:860
  74.8 0.1 collective-permute-start.18
  74.9 0.1 close.3
  74.9 1.5 %collective-permute-done.16.refs_1_ = bf16[256,256]{1,0:T(8,128)(2,1)S(1)} collective-permute-done((bf16[256,256]{1,0:T(8,128)(2,1)S(1)}, bf16[256,256]{1,0:T(8,128)(2,1)S(1)}, u32[]{:S(2)}, u32[]{:S(2)}) %collective-permute-start.16) | collective-permute-done | bytes 131104 | tf_op jit(solution)/shard_map/ppermute | solution.py:860
  76.4 2.9 %collective-permute-start.17 = (bf16[128,256]{1,0:T(8,128)(2,1)S(1)}, bf16[128,256]{1,0:T(8,128)(2,1)S(1)}, u32[]{:S(2)}, u32[]{:S(2)}) collective-permute-start(bf16[128,256]{1,0:T(8,128)(2,1)S(1)} %get-tuple-element.101), channel_id=1, source_target_pairs={{0,16},{4,20},{8,24},{12,28},{16,0},{20,4},{24,8},{28,12},{1,17},{... | collective-permute-start | bytes 196616 | tf_op jit(solution)/shard_map/ppermute | solution.py:860
  79.4 1.0 %collective-permute-start.19 = (bf16[128,256]{1,0:T(8,128)(2,1)S(1)}, bf16[128,256]{1,0:T(8,128)(2,1)S(1)}, u32[]{:S(2)}, u32[]{:S(2)}) collective-permute-start(bf16[128,256]{1,0:T(8,128)(2,1)S(1)} %get-tuple-element.104), channel_id=1, source_target_pairs={{0,4},{4,8},{8,12},{12,16},{16,20},{20,24},{24,28},{28,0},{1,5},{5... | collective-permute-start | bytes 196616 | tf_op jit(solution)/shard_map/ppermute | solution.py:871
  80.4 0.1 reshape.23
  80.5 0.1 reduce_sum.9.means_ref
  80.6 0.1 collective-permute-start.12
  80.7 1.7 %collective-permute-start.20 = (bf16[128,256]{1,0:T(8,128)(2,1)S(1)}, bf16[128,256]{1,0:T(8,128)(2,1)S(1)}, u32[]{:S(2)}, u32[]{:S(2)}) collective-permute-start(bf16[128,256]{1,0:T(8,128)(2,1)S(1)} %get-tuple-element.105), channel_id=1, source_target_pairs={{0,8},{4,12},{8,16},{12,20},{16,24},{20,28},{24,0},{28,4},{1,9},{5... | collective-permute-start | bytes 196616 | tf_op jit(solution)/shard_map/ppermute | solution.py:871
  82.4 0.5 collective-permute-done.18.other_ref
  82.9 0.0 collective-permute-start.21
  83.0 0.0 collective-permute-done.12.others_ref
  83.0 0.2 collective-permute-start.22
  83.1 0.5 collective-permute-done.17.other_ref
  83.6 2.7 %collective-permute-done.19.refs_2_ = bf16[128,256]{1,0:T(8,128)(2,1)S(1)} collective-permute-done((bf16[128,256]{1,0:T(8,128)(2,1)S(1)}, bf16[128,256]{1,0:T(8,128)(2,1)S(1)}, u32[]{:S(2)}, u32[]{:S(2)}) %collective-permute-start.19) | collective-permute-done | bytes 65568 | tf_op jit(solution)/shard_map/ppermute | solution.py:871
  86.3 0.9 collective-permute-start.23
  87.2 0.6 copy.10
  87.9 1.2 %cover.1.begun_ref = f32[128,2048]{1,0:T(8,128)S(1)} custom-call(f32[8,1024]{1,0:T(8,128)S(1)} %reduce_sum.9.means_ref, f32[8,1024]{1,0:T(8,128)S(1)} %collective-permute-done.12.others_ref, f32[128,512]{1,0:T(8,128)S(1)} %get-tuple-element.98.refs_2_.refs_0_, f32[128,256]{1,0:T(8,128)S(1)} %close.5.refs_1_, ...), custom_call_target="tpu_custom_call" | custom-call | tf_op jit(solution)/shard_map/cover/pallas_call | solution.py:815
  89.1 2.5 %collective-permute-done.23.refs_2_ = bf16[128,128]{1,0:T(8,128)(2,1)S(1)} collective-permute-done((bf16[128,128]{1,0:T(8,128)(2,1)S(1)}, bf16[128,128]{1,0:T(8,128)(2,1)S(1)}, u32[]{:S(2)}, u32[]{:S(2)}) %collective-permute-start.23) | collective-permute-done | bytes 32800 | tf_op jit(solution)/shard_map/ppermute | solution.py:871
  91.5 0.2 collective-permute-done.22.refs_1_
  91.7 1.2 %cover_rest.1 = f32[128,2048]{1,0:T(8,128)} custom-call(f32[128,2048]{1,0:T(8,128)S(1)} %cover.1.begun_ref, f32[128,384]{1,0:T(8,128)S(1)} %get-tuple-element.103.rest_0_.refs_0_, bf16[128,256]{1,0:T(8,128)(2,1)S(1)} %collective-permute-done.22.refs_1_, bf16[128,128]{1,0:T(8,128)(2,1)S(1)} %collective-permute-done.23.refs_2_, ...), custom_call_target="tpu_custom_call" | custom-call | tf_op jit(solution)/shard_map/cover_rest/pallas_call | solution.py:842
  (33 shorter events, 0.3 us)
Async XLA Ops:
  0.6 9.9 %copy-start = (bf16[1024,1024]{1,0:T(8,128)(2,1)S(1)}, bf16[1024,1024]{1,0:T(8,128)(2,1)}, u32[]{:S(2)}) copy-start(bf16[1024,1024]{1,0:T(8,128)(2,1)} %q_ref.7) | copy-start | bytes 6291460
  0.6 0.9 copy-start.3
  5.9 8.5 %collective-permute-start = (f32[264,128]{1,0:T(8,128)S(1)}, f32[264,128]{1,0:T(8,128)S(1)}, u32[]{:S(2)}, u32[]{:S(2)}) collective-permute-start(f32[264,128]{1,0:T(8,128)S(1)} %get-tuple-element.61), channel_id=1, source_target_pairs={{0,4},{4,0},{8,12},{12,8},{16,20},{20,16},{24,28},{28,24},{1,5},{5... | collective-permute-start | bytes 405512 | tf_op jit(solution)/shard_map/ppermute | solution.py:860
  8.9 6.5 %collective-permute-start.1 = (f32[264,128]{1,0:T(8,128)S(1)}, f32[264,128]{1,0:T(8,128)S(1)}, u32[]{:S(2)}, u32[]{:S(2)}) collective-permute-start(f32[264,128]{1,0:T(8,128)S(1)} %get-tuple-element.62), channel_id=1, source_target_pairs={{0,8},{4,12},{8,0},{12,4},{16,24},{20,28},{24,16},{28,20},{1,9},{5... | collective-permute-start | bytes 405512 | tf_op jit(solution)/shard_map/ppermute | solution.py:860
  10.5 6.2 %collective-permute-start.2 = (f32[264,128]{1,0:T(8,128)S(1)}, f32[264,128]{1,0:T(8,128)S(1)}, u32[]{:S(2)}, u32[]{:S(2)}) collective-permute-start(f32[264,128]{1,0:T(8,128)S(1)} %get-tuple-element.63), channel_id=1, source_target_pairs={{0,12},{4,8},{8,4},{12,0},{16,28},{20,24},{24,20},{28,16},{1,13},{... | collective-permute-start | bytes 405512 | tf_op jit(solution)/shard_map/ppermute | solution.py:860
  10.5 1.6 %copy-start.1 = (bf16[1024,1024]{1,0:T(8,128)(2,1)S(1)}, bf16[1024,1024]{1,0:T(8,128)(2,1)}, u32[]{:S(2)}) copy-start(bf16[1024,1024]{1,0:T(8,128)(2,1)} %get-tuple-element.57.v_ref) | copy-start | bytes 6291460
  12.1 9.3 %copy-start.2 = (bf16[1024,1024]{1,0:T(8,128)(2,1)S(1)}, bf16[1024,1024]{1,0:T(8,128)(2,1)}, u32[]{:S(2)}) copy-start(bf16[1024,1024]{1,0:T(8,128)(2,1)} %get-tuple-element.57.v_ref) | copy-start | bytes 6291460
  16.8 7.2 %collective-permute-start.3 = (f32[256,128]{1,0:T(8,128)S(1)}, f32[256,128]{1,0:T(8,128)S(1)}, u32[]{:S(2)}, u32[]{:S(2)}) collective-permute-start(f32[256,128]{1,0:T(8,128)S(1)} %get-tuple-element.65.rest_1_), channel_id=1, source_target_pairs={{0,16},{4,20},{8,24},{12,28},{1,17},{5,21},{9,25},{13,29},{2,18},{... | collective-permute-start | bytes 393224 | tf_op jit(solution)/shard_map/ppermute | solution.py:878
  21.4 9.0 %copy-start.4 = (f32[1024]{0:T(1024)S(1)}, f32[1024]{0:T(1024)}, u32[]{:S(2)}) copy-start(f32[1024]{0:T(1024)} %param.9) | copy-start | bytes 12292
  24.0 6.4 %collective-permute-start.6 = (f32[256,128]{1,0:T(8,128)S(1)}, f32[256,128]{1,0:T(8,128)S(1)}, u32[]{:S(2)}, u32[]{:S(2)}) collective-permute-start(f32[256,128]{1,0:T(8,128)S(1)} %get-tuple-element.75), channel_id=1, source_target_pairs={{0,4},{4,0},{8,12},{12,8},{16,20},{20,16},{24,28},{28,24},{1,5},{5... | collective-permute-start | bytes 393224 | tf_op jit(solution)/shard_map/ppermute | solution.py:860
  25.6 7.0 %collective-permute-start.4 = (f32[256,128]{1,0:T(8,128)S(1)}, f32[256,128]{1,0:T(8,128)S(1)}, u32[]{:S(2)}, u32[]{:S(2)}) collective-permute-start(f32[256,128]{1,0:T(8,128)S(1)} %get-tuple-element.72), channel_id=1, source_target_pairs={{0,8},{4,12},{8,0},{12,4},{16,24},{20,28},{24,16},{28,20},{1,9},{5... | collective-permute-start | bytes 393224 | tf_op jit(solution)/shard_map/ppermute | solution.py:860
  28.6 5.9 %collective-permute-start.5 = (f32[256,128]{1,0:T(8,128)S(1)}, f32[256,128]{1,0:T(8,128)S(1)}, u32[]{:S(2)}, u32[]{:S(2)}) collective-permute-start(f32[256,128]{1,0:T(8,128)S(1)} %get-tuple-element.73), channel_id=1, source_target_pairs={{0,12},{4,8},{8,4},{12,0},{16,28},{20,24},{24,20},{28,16},{1,13},{... | collective-permute-start | bytes 393224 | tf_op jit(solution)/shard_map/ppermute | solution.py:860
  36.6 4.4 %collective-permute-start.7 = (bf16[1024,1024]{1,0:T(8,128)(2,1)S(1)}, bf16[1024,1024]{1,0:T(8,128)(2,1)}, u32[]{:S(2)}, u32[]{:S(2)}) collective-permute-start(bf16[1024,1024]{1,0:T(8,128)(2,1)S(1)} %get-tuple-element.78.own_ref.other_ref), channel_id=1, source_target_pairs={{0,1},{1,0},{2,3},{3,2},{4,5},{5,4},{6,7},{7,6},{8,9},{9,8},{10,11... | collective-permute-start | bytes 6291464 | tf_op jit(solution)/shard_map/ppermute | solution.py:863
  38.7 8.8 %collective-permute-start.8 = (bf16[512,256]{1,0:T(8,128)(2,1)S(1)}, bf16[512,256]{1,0:T(8,128)(2,1)S(1)}, u32[]{:S(2)}, u32[]{:S(2)}) collective-permute-start(bf16[512,256]{1,0:T(8,128)(2,1)S(1)} %get-tuple-element.82), channel_id=1, source_target_pairs={{0,4},{4,0},{8,12},{12,8},{16,20},{20,16},{24,28},{28,24},{1,5},{5... | collective-permute-start | bytes 786440 | tf_op jit(solution)/shard_map/ppermute | solution.py:860
  44.8 8.8 %collective-permute-start.9 = (bf16[544,256]{1,0:T(8,128)(2,1)S(1)}, bf16[544,256]{1,0:T(8,128)(2,1)S(1)}, u32[]{:S(2)}, u32[]{:S(2)}) collective-permute-start(bf16[544,256]{1,0:T(8,128)(2,1)S(1)} %get-tuple-element.83), channel_id=1, source_target_pairs={{0,4},{4,0},{8,12},{12,8},{16,20},{20,16},{24,28},{28,24},{1,5},{5... | collective-permute-start | bytes 835592 | tf_op jit(solution)/shard_map/ppermute | solution.py:860
  51.2 12.1 %collective-permute-start.13 = (bf16[512,384]{1,0:T(8,128)(2,1)S(1)}, bf16[512,384]{1,0:T(8,128)(2,1)S(1)}, u32[]{:S(2)}, u32[]{:S(2)}) collective-permute-start(bf16[512,384]{1,0:T(8,128)(2,1)S(1)} %get-tuple-element.91), channel_id=1, source_target_pairs={{0,4},{4,0},{8,12},{12,8},{16,20},{20,16},{24,28},{28,24},{1,5},{5... | collective-permute-start | bytes 1179656 | tf_op jit(solution)/shard_map/ppermute | solution.py:860
  53.6 8.3 %collective-permute-start.10 = (bf16[288,512]{1,0:T(8,128)(2,1)S(1)}, bf16[288,512]{1,0:T(8,128)(2,1)S(1)}, u32[]{:S(2)}, u32[]{:S(2)}) collective-permute-start(bf16[288,512]{1,0:T(8,128)(2,1)S(1)} %get-tuple-element.86), channel_id=1, source_target_pairs={{0,8},{4,12},{8,0},{12,4},{16,24},{20,28},{24,16},{28,20},{1,9},{5... | collective-permute-start | bytes 884744 | tf_op jit(solution)/shard_map/ppermute | solution.py:860
  57.2 10.9 %collective-permute-start.15 = (bf16[512,256]{1,0:T(8,128)(2,1)S(1)}, bf16[512,256]{1,0:T(8,128)(2,1)S(1)}, u32[]{:S(2)}, u32[]{:S(2)}) collective-permute-start(bf16[512,256]{1,0:T(8,128)(2,1)S(1)} %get-tuple-element.95), channel_id=1, source_target_pairs={{0,4},{4,0},{8,12},{12,8},{16,20},{20,16},{24,28},{28,24},{1,5},{5... | collective-permute-start | bytes 786440 | tf_op jit(solution)/shard_map/ppermute | solution.py:860
  63.4 11.3 %collective-permute-start.14 = (bf16[256,384]{1,0:T(8,128)(2,1)S(1)}, bf16[256,384]{1,0:T(8,128)(2,1)S(1)}, u32[]{:S(2)}, u32[]{:S(2)}) collective-permute-start(bf16[256,384]{1,0:T(8,128)(2,1)S(1)} %get-tuple-element.93), channel_id=1, source_target_pairs={{0,8},{4,12},{8,0},{12,4},{16,24},{20,28},{24,16},{28,20},{1,9},{5... | collective-permute-start | bytes 589832 | tf_op jit(solution)/shard_map/ppermute | solution.py:860
  64.0 10.8 %collective-permute-start.11 = (bf16[192,512]{1,0:T(8,128)(2,1)S(1)}, bf16[192,512]{1,0:T(8,128)(2,1)S(1)}, u32[]{:S(2)}, u32[]{:S(2)}) collective-permute-start(bf16[192,512]{1,0:T(8,128)(2,1)S(1)} %get-tuple-element.89), channel_id=1, source_target_pairs={{0,16},{4,20},{8,24},{12,28},{16,0},{20,4},{24,8},{28,12},{1,17},{... | collective-permute-start | bytes 589832 | tf_op jit(solution)/shard_map/ppermute | solution.py:860
  68.2 8.2 %collective-permute-start.16 = (bf16[256,256]{1,0:T(8,128)(2,1)S(1)}, bf16[256,256]{1,0:T(8,128)(2,1)S(1)}, u32[]{:S(2)}, u32[]{:S(2)}) collective-permute-start(bf16[256,256]{1,0:T(8,128)(2,1)S(1)} %get-tuple-element.99), channel_id=1, source_target_pairs={{0,8},{4,12},{8,0},{12,4},{16,24},{20,28},{24,16},{28,20},{1,9},{5... | collective-permute-start | bytes 393224 | tf_op jit(solution)/shard_map/ppermute | solution.py:860
  74.8 8.1 %collective-permute-start.18 = (bf16[128,384]{1,0:T(8,128)(2,1)S(1)}, bf16[128,384]{1,0:T(8,128)(2,1)S(1)}, u32[]{:S(2)}, u32[]{:S(2)}) collective-permute-start(bf16[128,384]{1,0:T(8,128)(2,1)S(1)} %get-tuple-element.102), channel_id=1, source_target_pairs={{0,16},{4,20},{8,24},{12,28},{16,0},{20,4},{24,8},{28,12},{1,17},{... | collective-permute-start | bytes 294920 | tf_op jit(solution)/shard_map/ppermute | solution.py:860
  76.4 7.2 %collective-permute-start.17 = (bf16[128,256]{1,0:T(8,128)(2,1)S(1)}, bf16[128,256]{1,0:T(8,128)(2,1)S(1)}, u32[]{:S(2)}, u32[]{:S(2)}) collective-permute-start(bf16[128,256]{1,0:T(8,128)(2,1)S(1)} %get-tuple-element.101), channel_id=1, source_target_pairs={{0,16},{4,20},{8,24},{12,28},{16,0},{20,4},{24,8},{28,12},{1,17},{... | collective-permute-start | bytes 196616 | tf_op jit(solution)/shard_map/ppermute | solution.py:860
  79.4 7.0 %collective-permute-start.19 = (bf16[128,256]{1,0:T(8,128)(2,1)S(1)}, bf16[128,256]{1,0:T(8,128)(2,1)S(1)}, u32[]{:S(2)}, u32[]{:S(2)}) collective-permute-start(bf16[128,256]{1,0:T(8,128)(2,1)S(1)} %get-tuple-element.104), channel_id=1, source_target_pairs={{0,4},{4,8},{8,12},{12,16},{16,20},{20,24},{24,28},{28,0},{1,5},{5... | collective-permute-start | bytes 196616 | tf_op jit(solution)/shard_map/ppermute | solution.py:871
  80.6 2.4 %collective-permute-start.12 = (f32[8,1024]{1,0:T(8,128)S(1)}, f32[8,1024]{1,0:T(8,128)S(1)}, u32[]{:S(2)}, u32[]{:S(2)}) collective-permute-start(f32[8,1024]{1,0:T(8,128)S(1)} %reduce_sum.9.means_ref), channel_id=1, source_target_pairs={{0,1},{1,0},{2,3},{3,2},{4,5},{5,4},{6,7},{7,6},{8,9},{9,8},{10,11... | collective-permute-start | bytes 98312 | tf_op jit(solution)/shard_map/ppermute | solution.py:863
  80.7 7.2 %collective-permute-start.20 = (bf16[128,256]{1,0:T(8,128)(2,1)S(1)}, bf16[128,256]{1,0:T(8,128)(2,1)S(1)}, u32[]{:S(2)}, u32[]{:S(2)}) collective-permute-start(bf16[128,256]{1,0:T(8,128)(2,1)S(1)} %get-tuple-element.105), channel_id=1, source_target_pairs={{0,8},{4,12},{8,16},{12,20},{16,24},{20,28},{24,0},{28,4},{1,9},{5... | collective-permute-start | bytes 196616 | tf_op jit(solution)/shard_map/ppermute | solution.py:871
  82.9 5.0 %collective-permute-start.21 = (bf16[128,256]{1,0:T(8,128)(2,1)S(1)}, bf16[128,256]{1,0:T(8,128)(2,1)S(1)}, u32[]{:S(2)}, u32[]{:S(2)}) collective-permute-start(bf16[128,256]{1,0:T(8,128)(2,1)S(1)} %get-tuple-element.106), channel_id=1, source_target_pairs={{0,1},{1,0},{2,3},{3,2},{4,5},{5,4},{6,7},{7,6},{8,9},{9,8},{10,11... | collective-permute-start | bytes 196616 | tf_op jit(solution)/shard_map/ppermute | solution.py:863
  83.0 8.8 %collective-permute-start.22 = (bf16[128,256]{1,0:T(8,128)(2,1)S(1)}, bf16[128,256]{1,0:T(8,128)(2,1)S(1)}, u32[]{:S(2)}, u32[]{:S(2)}) collective-permute-start(bf16[128,256]{1,0:T(8,128)(2,1)S(1)} %get-tuple-element.107), channel_id=1, source_target_pairs={{0,12},{4,16},{8,20},{12,24},{16,28},{20,0},{24,4},{28,8},{1,13},{... | collective-permute-start | bytes 196616 | tf_op jit(solution)/shard_map/ppermute | solution.py:871
  83.6 8.1 %collective-permute-start.24 = (bf16[128,256]{1,0:T(8,128)(2,1)S(1)}, bf16[128,256]{1,0:T(8,128)(2,1)S(1)}, u32[]{:S(2)}, u32[]{:S(2)}) collective-permute-start(bf16[128,256]{1,0:T(8,128)(2,1)S(1)} %get-tuple-element.109), channel_id=1, source_target_pairs={{0,1},{1,0},{2,3},{3,2},{4,5},{5,4},{6,7},{7,6},{8,9},{9,8},{10,11... | collective-permute-start | bytes 196616 | tf_op jit(solution)/shard_map/ppermute | solution.py:863
  86.3 5.2 %collective-permute-start.23 = (bf16[128,128]{1,0:T(8,128)(2,1)S(1)}, bf16[128,128]{1,0:T(8,128)(2,1)S(1)}, u32[]{:S(2)}, u32[]{:S(2)}) collective-permute-start(bf16[128,128]{1,0:T(8,128)(2,1)S(1)} %get-tuple-element.108), channel_id=1, source_target_pairs={{0,16},{4,20},{8,24},{12,28},{16,0},{20,4},{24,8},{28,12},{1,17},{... | collective-permute-start | bytes 98312 | tf_op jit(solution)/shard_map/ppermute | solution.py:871

commit v7 on v6

--- a/solution.py
+++ b/solution.py
@@ -23,7 +23,7 @@
 
 def cost(flops, moved, transcendentals=0):
     return pl.CostEstimate(
-        flops=1, bytes_accessed=1, transcendentals=0
+        flops=int(flops) * 4, bytes_accessed=int(moved) * 4, transcendentals=int(transcendentals)
     )
 
 
@@ -326,6 +326,8 @@
 def inner_loop_kernel(begin, end, q_ref, k_ref, v_ref, cumul_ref, *rest):
     raw_ref, token_ref = rest[-2:]
     token_ref[...] = jnp.zeros_like(token_ref)
+    if begin:
+        raw_ref[: begin * SPAN, :] = rest[0][: begin * SPAN, :]
 
     @pl.loop(begin, end)
     def _(index):
@@ -346,7 +348,6 @@
             in_specs=[vmem()] * 4 + [vmem(), anywhere()][: len(earlier)],
             out_specs=[vmem()] * 2,
             out_shape=[struct((count, width), F32), token],
-            input_output_aliases={4: 0} if earlier else {},
             compiler_params=params(16),
             cost_estimate=work,
             name="inner",
@@ -467,7 +468,7 @@
     near, part, q_ref, raw_ref, entering_ref, before_ref, cumul_ref, gain_ref, *rest
 ):
     pieces, rest = rest[: near // 2], rest[near // 2 :]
-    centered_ref, stats_ref, arrived, sums = rest[-4:]
+    earlier, (centered_ref, stats_ref, arrived, sums) = rest[:-4], rest[-4:]
     count, width = centered_ref.shape
     span = width // 2
     heads = span // HEAD_DIM
@@ -477,6 +478,9 @@
     half = (mine // (near // 2)) ^ part
     low = pl.multiple_of(half * span, span)
     every = pl.ds(low, span)
+    for ref, out_ref in zip(earlier, (centered_ref, stats_ref)):
+        others = pl.ds(pl.multiple_of(span - low, span), span)
+        out_ref[:, others] = ref[:, others]
     for place, piece in enumerate(pieces):
         start = pl.multiple_of((mine % (near // 2) ^ place) * rows, rows)
         arrived[pl.ds(start, rows), :] = piece[...]
@@ -546,7 +550,6 @@
                     pltpu.VMEM((24, width // 2), F32),
                 ],
                 out_shape=shapes,
-                input_output_aliases={len(mine): 0, len(mine) + 1: 1} if done else {},
                 compiler_params=params(16),
                 cost_estimate=work,
                 name="finish",
@@ -660,11 +663,12 @@
 
 
 def merge(first, second, means):
-    a, b = first.astype(F32), second[:, : first.shape[1]].astype(F32)
-    each = RIDER_ROWS
-    top, bottom = slice(means, means + each), slice(means + each, means + 2 * each)
+    a, b = first.astype(F32), second.astype(F32)
+    if b.shape[1] > a.shape[1]:
+        b = jnp.concatenate([b[:, : a.shape[1]], b[:, a.shape[1] :]], axis=0)
+    top, bottom = slice(means, means + RIDER_ROWS), slice(means + RIDER_ROWS, means + 2 * RIDER_ROWS)
     lines = [a[:means], b[:means], jnp.maximum(a[top], b[top]), jnp.minimum(a[bottom], b[bottom])]
-    spare = -(2 * means + 2 * each) % 16
+    spare = -(2 * means + 2 * RIDER_ROWS) % 32
     if spare:
         lines.append(jnp.zeros((spare, a.shape[1]), F32))
     return jnp.concatenate(lines, axis=0).astype(BF16)
@@ -677,8 +681,9 @@
     if means:
         riders_ref, kept_ref, send_ref, merged_ref = rest
         merged = merge(riders_ref[...], others[-1][low:, :], means)
-        send_ref[kept_ref.shape[0] :, :] = jnp.zeros_like(send_ref[kept_ref.shape[0] :, :])
-        send_ref[kept_ref.shape[0] :, : merged.shape[1]] = merged
+        half, lines = merged.shape[0] // 2, merged.shape[1]
+        send_ref[kept_ref.shape[0] :, :lines] = merged[:half]
+        send_ref[kept_ref.shape[0] :, lines:] = merged[half:]
         merged_ref[...] = merged
     else:
         kept_ref, send_ref = rest
@@ -703,8 +708,8 @@
     kept = (keeps[0].shape[0] // 2, sum(keep.shape[1] for keep in keeps))
     shapes = [struct(kept, F32), struct(kept, BF16)]
     if riders:
-        merged = (-(-(2 * means + 2 * RIDER_ROWS) // 16) * 16, riders[0].shape[1])
-        shapes = [struct(kept, F32), struct((kept[0] + merged[0], kept[1]), BF16)]
+        merged = (-(-(2 * means + 2 * RIDER_ROWS) // 32) * 32, riders[0].shape[1])
+        shapes = [struct(kept, F32), struct((kept[0] + merged[0] // 2, kept[1]), BF16)]
         shapes.append(struct(merged, BF16))
     return pl.pallas_call(
         functools.partial(fold_kernel, len(keeps), rows, inner, apart, means if riders else 0),
@@ -940,7 +945,7 @@
 
     for apart in aparts[1:]:
         after = split_on(0, apart, after)
-    every = merge(riders[0], kept[0][1][0][rows:, :lines], mean_rows * half)
+    every = merge(riders[0], kept[0][1][0][rows:], mean_rows * half)
     for apart in aparts:
         after = split_on(1, apart, after)
         if apart == aparts[-1]:

time: 93.2 us -> 92.6 us (level)
  waiting for transfers between devices: 29.3 us -> 26.7 us
  starting transfers between devices: 30.7 us -> 32.6 us
    ppermute x4, starting transfers between devices: 3.83 us -> 7.4 us  [forward(): lax.ppermute(value, 'ctx', [(a, (a + step) % shards) for a in range(shard...]
    ppermute x16, starting transfers between devices: 22.1 us -> 19.9 us  [to_shard(): return lax.ppermute(value, 'ctx', [(a, a ^ apart) for a in range(shards)])]
    ppermute x4, waiting for transfers between devices: 5.37 us -> 3.62 us  [forward(): lax.ppermute(value, 'ctx', [(a, (a + step) % shards) for a in range(shard...]
    unnamed x11 -> x9, local copies, waits for them, and re-layouts: 3.1 us -> 3.1 us
  transfers between devices with their start and end apart: 25 -> 25, of which waited for: 17 -> 15; matrix products, arithmetic and copies ran while one was open for 1% -> 1% of each run, Pallas kernels for 22% -> 23%
where the time goes in v7:
time: 92.6 us; the launch traced here: 92.4 us
  starting transfers between devices  32.6 us (35%)
  Pallas kernels  28.8 us (31%)
  waiting for transfers between devices  26.7 us (29%)
  local copies, waits for them, and re-layouts  3.23 us (3%)
  between operations  0.93 us (1%)
    ppermute x16, waiting for transfers between devices, to_shard(): return lax.ppermute(value, 'ctx', [(a, a ^ apart) for a in range(shards)])  21.5 us
    ppermute x16, starting transfers between devices, to_shard(): return lax.ppermute(value, 'ctx', [(a, a ^ apart) for a in range(shards)])  19.9 us
    pallas_call x4, Pallas kernels, gram_parts(): pl.pallas_call(functools.partial(gram_kernel, rows, blocks, apart), in_sp...  12.5 us
    ppermute x4, starting transfers between devices, forward(): lax.ppermute(value, 'ctx', [(a, (a + step) % shards) for a in range(shard...  7.4 us
    pallas_call x2, Pallas kernels, inner(): pl.pallas_call(functools.partial(inner_loop_kernel, begin, end), in_specs...  4.69 us
    ppermute x1, starting transfers between devices, body(): entered = lax.ppermute(leaving, 'ctx', [(a, a + near) for a in range(near)])  4.65 us
    pallas_call x2, Pallas kernels, finish(): pl.pallas_call(functools.partial(finish_part_kernel, near, part), in_spec...  4.36 us
    pallas_call x1, Pallas kernels, local_states(): pl.pallas_call(functools.partial(states_fetch_kernel, near), in_specs=[hb...  4.35 us
  transfers between devices with their start and end apart: 25, of which 15 were waited for; matrix products, arithmetic and copies ran while one was open for 1% of the time, Pallas kernels for 23%

profile of v7, /device:TPU:0, one launch (start us, length us, event | category | flops | bytes accessed | tf_op | source)
XLA Modules:
  0.0 92.4 jit_solution(17342009160682298935)
XLA Ops:
  0.7 0.9 copy-done.2
  1.5 4.4 %local_states.1 = (f32[4,1024,128]{2,1,0:T(8,128)S(1)}, f32[4,8,128]{2,1,0:T(8,128)S(1)}, f32[32,256]{1,0:T(8,128)S(1)}, f32[264,128]{1,0:T(8,128)S(1)}, f32[264...) custom-call(bf16[1024,1024]{1,0:T(8,128)(2,1)} %k_any.1, ...), custom_call_target="tpu_custom_call" | custom-call | flops 2147483648 | bytes 16777216 | tf_op jit(solution)/shard_map/local_states/pallas_call | solution.py:197
  5.9 3.0 %collective-permute-start = (f32[264,128]{1,0:T(8,128)S(1)}, f32[264,128]{1,0:T(8,128)S(1)}, u32[]{:S(2)}, u32[]{:S(2)}) collective-permute-start(f32[264,128]{1,0:T(8,128)S(1)} %get-tuple-element.61), channel_id=1, source_target_pairs={{0,4},{4,0},{8,12},{12,8},{16,20},{20,16},{24,28},{28,24},{1,5},{5... | collective-permute-start | bytes 405512 | tf_op jit(solution)/shard_map/ppermute | solution.py:865
  8.9 1.6 %collective-permute-start.1 = (f32[264,128]{1,0:T(8,128)S(1)}, f32[264,128]{1,0:T(8,128)S(1)}, u32[]{:S(2)}, u32[]{:S(2)}) collective-permute-start(f32[264,128]{1,0:T(8,128)S(1)} %get-tuple-element.62), channel_id=1, source_target_pairs={{0,8},{4,12},{8,0},{12,4},{16,24},{20,28},{24,16},{28,20},{1,9},{5... | collective-permute-start | bytes 405512 | tf_op jit(solution)/shard_map/ppermute | solution.py:865
  10.5 1.6 %copy-done.3 = bf16[1024,1024]{1,0:T(8,128)(2,1)S(1)} copy-done((bf16[1024,1024]{1,0:T(8,128)(2,1)S(1)}, bf16[1024,1024]{1,0:T(8,128)(2,1)}, u32[]{:S(2)}) %copy-start.3) | copy-done | bytes 2097176
  12.1 2.3 %inner.2 = (f32[1024,1024]{1,0:T(8,128)S(1)}, f32[8,128]{1,0:T(8,128)S(1)}) custom-call(bf16[1024,1024]{1,0:T(8,128)(2,1)S(1)} %copy-done, bf16[1024,1024]{1,0:T(8,128)(2,1)S(1)} %get-tuple-element.56.k_ref, bf16[1024,1024]{1,0:T(8,128)(2,1)S(1)} %copy-done.3, f32[32,256]{1,0:T(8,128)S(1)} %get-tuple-element.58.cumul_ref), custom_call_target="tpu_custom_call" | custom-call | flops 4294967296 | bytes 41943040 | tf_op jit(solution)/shard_map/inner/pallas_call | solution.py:346
  14.4 1.0 %collective-permute-done.1.refs_2_ = f32[264,128]{1,0:T(8,128)S(1)} collective-permute-done((f32[264,128]{1,0:T(8,128)S(1)}, f32[264,128]{1,0:T(8,128)S(1)}, u32[]{:S(2)}, u32[]{:S(2)}) %collective-permute-start.1) | collective-permute-done | bytes 135200 | tf_op jit(solution)/shard_map/ppermute | solution.py:865
  15.4 1.2 %collective-permute-done.2.refs_3_ = f32[264,128]{1,0:T(8,128)S(1)} collective-permute-done((f32[264,128]{1,0:T(8,128)S(1)}, f32[264,128]{1,0:T(8,128)S(1)}, u32[]{:S(2)}, u32[]{:S(2)}) %collective-permute-start.2) | collective-permute-done | bytes 135200 | tf_op jit(solution)/shard_map/ppermute | solution.py:865
  16.7 0.1 chain.1
  16.8 4.6 %collective-permute-start.3 = (f32[256,128]{1,0:T(8,128)S(1)}, f32[256,128]{1,0:T(8,128)S(1)}, u32[]{:S(2)}, u32[]{:S(2)}) collective-permute-start(f32[256,128]{1,0:T(8,128)S(1)} %get-tuple-element.65.rest_1_), channel_id=1, source_target_pairs={{0,16},{4,20},{8,24},{12,28},{1,17},{5,21},{9,25},{13,29},{2,18},{... | collective-permute-start | bytes 393224 | tf_op jit(solution)/shard_map/ppermute | solution.py:883
  21.4 0.0 copy-start.1
  21.4 2.4 %inner.3 = (f32[1024,1024]{1,0:T(8,128)S(1)}, f32[8,128]{1,0:T(8,128)S(1)}) custom-call(bf16[1024,1024]{1,0:T(8,128)(2,1)S(1)} %copy-done, bf16[1024,1024]{1,0:T(8,128)(2,1)S(1)} %get-tuple-element.56.k_ref, bf16[1024,1024]{1,0:T(8,128)(2,1)S(1)} %copy-done.3, f32[32,256]{1,0:T(8,128)S(1)} %get-tuple-element.58.cumul_ref, ...), custom_call_target="tpu_custom_call" | custom-call | flops 4294967296 | bytes 41943040 | tf_op jit(solution)/shard_map/inner/pallas_call | solution.py:346
  23.9 0.1 collective-permute-done.3.entered_ref
  23.9 0.1 spread_states.1
  24.0 1.6 %collective-permute-start.6 = (f32[256,128]{1,0:T(8,128)S(1)}, f32[256,128]{1,0:T(8,128)S(1)}, u32[]{:S(2)}, u32[]{:S(2)}) collective-permute-start(f32[256,128]{1,0:T(8,128)S(1)} %get-tuple-element.75), channel_id=1, source_target_pairs={{0,4},{4,0},{8,12},{12,8},{16,20},{20,16},{24,28},{28,24},{1,5},{5... | collective-permute-start | bytes 393224 | tf_op jit(solution)/shard_map/ppermute | solution.py:865
  25.6 3.0 %collective-permute-start.4 = (f32[256,128]{1,0:T(8,128)S(1)}, f32[256,128]{1,0:T(8,128)S(1)}, u32[]{:S(2)}, u32[]{:S(2)}) collective-permute-start(f32[256,128]{1,0:T(8,128)S(1)} %get-tuple-element.72), channel_id=1, source_target_pairs={{0,8},{4,12},{8,0},{12,4},{16,24},{20,28},{24,16},{28,20},{1,9},{5... | collective-permute-start | bytes 393224 | tf_op jit(solution)/shard_map/ppermute | solution.py:865
  28.6 0.1 collective-permute-start.5
  28.7 1.8 %collective-permute-done.6.rest_1_ = f32[256,128]{1,0:T(8,128)S(1)} collective-permute-done((f32[256,128]{1,0:T(8,128)S(1)}, f32[256,128]{1,0:T(8,128)S(1)}, u32[]{:S(2)}, u32[]{:S(2)}) %collective-permute-start.6) | collective-permute-done | bytes 131104 | tf_op jit(solution)/shard_map/ppermute | solution.py:865
  30.4 2.1 %finish.2 = (bf16[1024,1024]{1,0:T(8,128)(2,1)S(1)}, bf16[16,1024]{1,0:T(8,128)(2,1)S(1)}) custom-call(bf16[1024,1024]{1,0:T(8,128)(2,1)S(1)} %copy-done, f32[1024,1024]{1,0:T(8,128)S(1)} %get-tuple-element.66.raw_ref, f32[4,1024,128]{2,1,0:T(8,128)S(1)} %get-tuple-element.67.entering_ref, f32[4,8,128]{2,1,0:T(8,128)S(1)} %get-tuple-element.68.before_ref, ...), custom_call_target="tpu_custom_call" | custom-call | flops 2147483648 | bytes 41943040 | tf_op jit(solution)/shard_map/finish/pallas_call | solution.py:544
  32.6 1.9 %collective-permute-done.5.rest_1_ = f32[256,128]{1,0:T(8,128)S(1)} collective-permute-done((f32[256,128]{1,0:T(8,128)S(1)}, f32[256,128]{1,0:T(8,128)S(1)}, u32[]{:S(2)}, u32[]{:S(2)}) %collective-permute-start.5) | collective-permute-done | bytes 131104 | tf_op jit(solution)/shard_map/ppermute | solution.py:865
  34.5 2.2 %finish.3 = (bf16[1024,1024]{1,0:T(8,128)(2,1)S(1)}, bf16[16,1024]{1,0:T(8,128)(2,1)S(1)}) custom-call(bf16[1024,1024]{1,0:T(8,128)(2,1)S(1)} %copy-done, f32[1024,1024]{1,0:T(8,128)S(1)} %get-tuple-element.66.raw_ref, f32[4,1024,128]{2,1,0:T(8,128)S(1)} %get-tuple-element.67.entering_ref, f32[4,8,128]{2,1,0:T(8,128)S(1)} %get-tuple-element.68.before_ref, ...), custom_call_target="tpu_custom_call" | custom-call | flops 2147483648 | bytes 41943040 | tf_op jit(solution)/shard_map/finish/pallas_call | solution.py:544
  36.7 0.1 collective-permute-start.7
  36.8 2.0 %gram.4 = (f32[512,256]{1,0:T(8,128)S(1)}, bf16[512,256]{1,0:T(8,128)(2,1)S(1)}) custom-call(bf16[1024,1024]{1,0:T(8,128)(2,1)S(1)} %get-tuple-element.78.own_ref.other_ref, bf16[1024,1024]{1,0:T(8,128)(2,1)S(1)} %get-tuple-element.78.own_ref.other_ref, bf16[16,1024]{1,0:T(8,128)(2,1)S(1)} %get-tuple-element.79.rest_0_), custom_call_target="tpu_custom_call" | custom-call | flops 2147483648 | bytes 16777216 | tf_op jit(solution)/shard_map/gram/pallas_call | solution.py:653
  38.8 0.7 collective-permute-start.8
  39.6 1.5 %collective-permute-done.7.other_ref = bf16[1024,1024]{1,0:T(8,128)(2,1)} collective-permute-done((bf16[1024,1024]{1,0:T(8,128)(2,1)S(1)}, bf16[1024,1024]{1,0:T(8,128)(2,1)}, u32[]{:S(2)}, u32[]{:S(2)}) %collective-permute-start.7) | collective-permute-done | bytes 2097184 | tf_op jit(solution)/shard_map/ppermute | solution.py:868
  41.0 3.8 %gram.5 = (f32[512,256]{1,0:T(8,128)S(1)}, bf16[544,256]{1,0:T(8,128)(2,1)S(1)}) custom-call(bf16[1024,1024]{1,0:T(8,128)(2,1)S(1)} %get-tuple-element.78.own_ref.other_ref, bf16[1024,1024]{1,0:T(8,128)(2,1)} %collective-permute-done.7.other_ref, bf16[32,256]{1,0:T(8,128)(2,1)S(1)} %pad.4.rest_0_.refs_5_, f32[512,256]{1,0:T(8,128)S(1)} %get-tuple-element.80.rest_1_.refs_0_), custom_call_target="tpu_custom_call" | custom-call | flops 2147483648 | bytes 16777216 | tf_op jit(solution)/shard_map/gram/pallas_call | solution.py:653
  44.8 0.7 collective-permute-start.9
  45.5 2.0 %collective-permute-done.8.rest_0_.refs_2_ = bf16[512,256]{1,0:T(8,128)(2,1)S(1)} collective-permute-done((bf16[512,256]{1,0:T(8,128)(2,1)S(1)}, bf16[512,256]{1,0:T(8,128)(2,1)S(1)}, u32[]{:S(2)}, u32[]{:S(2)}) %collective-permute-start.8) | collective-permute-done | bytes 262176 | tf_op jit(solution)/shard_map/ppermute | solution.py:865
  47.6 3.7 %gram.6 = (f32[512,384]{1,0:T(8,128)S(1)}, bf16[512,384]{1,0:T(8,128)(2,1)S(1)}) custom-call(bf16[1024,1024]{1,0:T(8,128)(2,1)S(1)} %get-tuple-element.78.own_ref.other_ref, bf16[1024,1024]{1,0:T(8,128)(2,1)} %collective-permute-done.7.other_ref, bf16[512,256]{1,0:T(8,128)(2,1)S(1)} %collective-permute-done.8.rest_0_.refs_2_), custom_call_target="tpu_custom_call" | custom-call | flops 3221225472 | bytes 16777216 | tf_op jit(solution)/shard_map/gram/pallas_call | solution.py:653
  51.3 0.7 collective-permute-start.13
  52.0 1.6 %collective-permute-done.9.refs_3_ = bf16[544,256]{1,0:T(8,128)(2,1)S(1)} collective-permute-done((bf16[544,256]{1,0:T(8,128)(2,1)S(1)}, bf16[544,256]{1,0:T(8,128)(2,1)S(1)}, u32[]{:S(2)}, u32[]{:S(2)}) %collective-permute-start.9) | collective-permute-done | bytes 278560 | tf_op jit(solution)/shard_map/ppermute | solution.py:865
  53.6 0.1 fold.6
  53.7 0.6 collective-permute-start.10
  54.3 3.0 %gram.7 = (f32[512,256]{1,0:T(8,128)S(1)}, bf16[512,256]{1,0:T(8,128)(2,1)S(1)}) custom-call(bf16[1024,1024]{1,0:T(8,128)(2,1)S(1)} %get-tuple-element.78.own_ref.other_ref, bf16[1024,1024]{1,0:T(8,128)(2,1)} %collective-permute-done.7.other_ref, f32[256,512]{1,0:T(8,128)S(1)} %get-tuple-element.85.refs_0_.refs_2_.rest_0_), custom_call_target="tpu_custom_call" | custom-call | flops 2147483648 | bytes 16777216 | tf_op jit(solution)/shard_map/gram/pallas_call | solution.py:653
  57.3 1.5 %collective-permute-start.15 = (bf16[512,256]{1,0:T(8,128)(2,1)S(1)}, bf16[512,256]{1,0:T(8,128)(2,1)S(1)}, u32[]{:S(2)}, u32[]{:S(2)}) collective-permute-start(bf16[512,256]{1,0:T(8,128)(2,1)S(1)} %get-tuple-element.95), channel_id=1, source_target_pairs={{0,4},{4,0},{8,12},{12,8},{16,20},{20,16},{24,28},{28,24},{1,5},{5... | collective-permute-start | bytes 786440 | tf_op jit(solution)/shard_map/ppermute | solution.py:865
  58.8 2.8 %collective-permute-done.10.refs_1_ = bf16[272,512]{1,0:T(8,128)(2,1)S(1)} collective-permute-done((bf16[272,512]{1,0:T(8,128)(2,1)S(1)}, bf16[272,512]{1,0:T(8,128)(2,1)S(1)}, u32[]{:S(2)}, u32[]{:S(2)}) %collective-permute-start.10) | collective-permute-done | bytes 278560 | tf_op jit(solution)/shard_map/ppermute | solution.py:865
  61.6 0.1 fold.7
  61.7 3.5 %collective-permute-start.11 = (bf16[160,512]{1,0:T(8,128)(2,1)S(1)}, bf16[160,512]{1,0:T(8,128)(2,1)S(1)}, u32[]{:S(2)}, u32[]{:S(2)}) collective-permute-start(bf16[160,512]{1,0:T(8,128)(2,1)S(1)} %get-tuple-element.89), channel_id=1, source_target_pairs={{0,16},{4,20},{8,24},{12,28},{16,0},{20,4},{24,8},{28,12},{1,17},{... | collective-permute-start | bytes 491528 | tf_op jit(solution)/shard_map/ppermute | solution.py:865
  65.2 0.1 fold.8
  65.2 1.3 %collective-permute-start.14 = (bf16[256,384]{1,0:T(8,128)(2,1)S(1)}, bf16[256,384]{1,0:T(8,128)(2,1)S(1)}, u32[]{:S(2)}, u32[]{:S(2)}) collective-permute-start(bf16[256,384]{1,0:T(8,128)(2,1)S(1)} %get-tuple-element.93), channel_id=1, source_target_pairs={{0,8},{4,12},{8,0},{12,4},{16,24},{20,28},{24,16},{28,20},{1,9},{5... | collective-permute-start | bytes 589832 | tf_op jit(solution)/shard_map/ppermute | solution.py:865
  66.6 1.2 %collective-permute-done.15.refs_1_ = bf16[512,256]{1,0:T(8,128)(2,1)S(1)} collective-permute-done((bf16[512,256]{1,0:T(8,128)(2,1)S(1)}, bf16[512,256]{1,0:T(8,128)(2,1)S(1)}, u32[]{:S(2)}, u32[]{:S(2)}) %collective-permute-start.15) | collective-permute-done | bytes 262176 | tf_op jit(solution)/shard_map/ppermute | solution.py:865
  67.8 0.6 collective-permute-start.16
  68.4 3.1 %collective-permute-done.11.other_ref = bf16[160,512]{1,0:T(8,128)(2,1)S(1)} collective-permute-done((bf16[160,512]{1,0:T(8,128)(2,1)S(1)}, bf16[160,512]{1,0:T(8,128)(2,1)S(1)}, u32[]{:S(2)}, u32[]{:S(2)}) %collective-permute-start.11) | collective-permute-done | bytes 163872 | tf_op jit(solution)/shard_map/ppermute | solution.py:865
  71.5 2.8 %collective-permute-done.14.refs_1_ = bf16[256,384]{1,0:T(8,128)(2,1)S(1)} collective-permute-done((bf16[256,384]{1,0:T(8,128)(2,1)S(1)}, bf16[256,384]{1,0:T(8,128)(2,1)S(1)}, u32[]{:S(2)}, u32[]{:S(2)}) %collective-permute-start.14) | collective-permute-done | bytes 196640 | tf_op jit(solution)/shard_map/ppermute | solution.py:865
  74.4 0.3 collective-permute-start.18
  74.6 0.1 close.3
  74.7 2.1 %collective-permute-done.16.refs_1_ = bf16[256,256]{1,0:T(8,128)(2,1)S(1)} collective-permute-done((bf16[256,256]{1,0:T(8,128)(2,1)S(1)}, bf16[256,256]{1,0:T(8,128)(2,1)S(1)}, u32[]{:S(2)}, u32[]{:S(2)}) %collective-permute-start.16) | collective-permute-done | bytes 131104 | tf_op jit(solution)/shard_map/ppermute | solution.py:865
  76.8 0.7 collective-permute-start.17
  77.6 1.9 %collective-permute-start.19 = (bf16[128,256]{1,0:T(8,128)(2,1)S(1)}, bf16[128,256]{1,0:T(8,128)(2,1)S(1)}, u32[]{:S(2)}, u32[]{:S(2)}) collective-permute-start(bf16[128,256]{1,0:T(8,128)(2,1)S(1)} %get-tuple-element.104), channel_id=1, source_target_pairs={{0,4},{4,8},{8,12},{12,16},{16,20},{20,24},{24,28},{28,0},{1,5},{5... | collective-permute-start | bytes 196616 | tf_op jit(solution)/shard_map/ppermute | solution.py:876
  79.5 0.1 reshape.23
  79.5 0.1 reduce_sum.9.means_ref
  79.6 0.1 collective-permute-start.12
  79.7 2.1 %collective-permute-start.20 = (bf16[128,256]{1,0:T(8,128)(2,1)S(1)}, bf16[128,256]{1,0:T(8,128)(2,1)S(1)}, u32[]{:S(2)}, u32[]{:S(2)}) collective-permute-start(bf16[128,256]{1,0:T(8,128)(2,1)S(1)} %get-tuple-element.105), channel_id=1, source_target_pairs={{0,8},{4,12},{8,16},{12,20},{16,24},{20,28},{24,0},{28,4},{1,9},{5... | collective-permute-start | bytes 196616 | tf_op jit(solution)/shard_map/ppermute | solution.py:876
  81.8 0.0 collective-permute-done.18.other_ref
  81.8 0.2 collective-permute-start.21
  82.1 1.0 %collective-permute-start.22 = (bf16[128,256]{1,0:T(8,128)(2,1)S(1)}, bf16[128,256]{1,0:T(8,128)(2,1)S(1)}, u32[]{:S(2)}, u32[]{:S(2)}) collective-permute-start(bf16[128,256]{1,0:T(8,128)(2,1)S(1)} %get-tuple-element.107), channel_id=1, source_target_pairs={{0,12},{4,16},{8,20},{12,24},{16,28},{20,0},{24,4},{28,8},{1,13},{... | collective-permute-start | bytes 196616 | tf_op jit(solution)/shard_map/ppermute | solution.py:876
  83.1 0.2 collective-permute-start.24
  83.3 1.3 %collective-permute-done.19.refs_2_ = bf16[128,256]{1,0:T(8,128)(2,1)S(1)} collective-permute-done((bf16[128,256]{1,0:T(8,128)(2,1)S(1)}, bf16[128,256]{1,0:T(8,128)(2,1)S(1)}, u32[]{:S(2)}, u32[]{:S(2)}) %collective-permute-start.19) | collective-permute-done | bytes 65568 | tf_op jit(solution)/shard_map/ppermute | solution.py:876
  84.6 2.4 %collective-permute-start.23 = (bf16[128,128]{1,0:T(8,128)(2,1)S(1)}, bf16[128,128]{1,0:T(8,128)(2,1)S(1)}, u32[]{:S(2)}, u32[]{:S(2)}) collective-permute-start(bf16[128,128]{1,0:T(8,128)(2,1)S(1)} %get-tuple-element.108), channel_id=1, source_target_pairs={{0,16},{4,20},{8,24},{12,28},{16,0},{20,4},{24,8},{28,12},{1,17},{... | collective-permute-start | bytes 98312 | tf_op jit(solution)/shard_map/ppermute | solution.py:876
  87.1 0.6 copy.7
  87.7 0.0 collective-permute-done.20.refs_3_
  87.7 1.2 %cover.1.begun_ref = f32[128,2048]{1,0:T(8,128)S(1)} custom-call(f32[8,1024]{1,0:T(8,128)S(1)} %reduce_sum.9.means_ref, f32[8,1024]{1,0:T(8,128)S(1)} %collective-permute-done.12.others_ref, f32[128,512]{1,0:T(8,128)S(1)} %get-tuple-element.98.refs_2_.refs_0_, f32[128,256]{1,0:T(8,128)S(1)} %close.5.refs_1_, ...), custom_call_target="tpu_custom_call" | custom-call | tf_op jit(solution)/shard_map/cover/pallas_call | solution.py:820
  88.9 2.3 %collective-permute-done.23.refs_2_ = bf16[128,128]{1,0:T(8,128)(2,1)S(1)} collective-permute-done((bf16[128,128]{1,0:T(8,128)(2,1)S(1)}, bf16[128,128]{1,0:T(8,128)(2,1)S(1)}, u32[]{:S(2)}, u32[]{:S(2)}) %collective-permute-start.23) | collective-permute-done | bytes 32800 | tf_op jit(solution)/shard_map/ppermute | solution.py:876
  91.2 1.2 %cover_rest.1 = f32[128,2048]{1,0:T(8,128)} custom-call(f32[128,2048]{1,0:T(8,128)S(1)} %cover.1.begun_ref, f32[128,384]{1,0:T(8,128)S(1)} %get-tuple-element.103.rest_0_.refs_0_, bf16[128,256]{1,0:T(8,128)(2,1)S(1)} %collective-permute-done.22.refs_1_, bf16[128,128]{1,0:T(8,128)(2,1)S(1)} %collective-permute-done.23.refs_2_, ...), custom_call_target="tpu_custom_call" | custom-call | tf_op jit(solution)/shard_map/cover_rest/pallas_call | solution.py:847
  (32 shorter events, 0.3 us)
Async XLA Ops:
  0.6 9.9 %copy-start = (bf16[1024,1024]{1,0:T(8,128)(2,1)S(1)}, bf16[1024,1024]{1,0:T(8,128)(2,1)}, u32[]{:S(2)}) copy-start(bf16[1024,1024]{1,0:T(8,128)(2,1)} %q_ref.7) | copy-start | bytes 6291460
  0.6 0.9 copy-start.2
  5.9 8.5 %collective-permute-start = (f32[264,128]{1,0:T(8,128)S(1)}, f32[264,128]{1,0:T(8,128)S(1)}, u32[]{:S(2)}, u32[]{:S(2)}) collective-permute-start(f32[264,128]{1,0:T(8,128)S(1)} %get-tuple-element.61), channel_id=1, source_target_pairs={{0,4},{4,0},{8,12},{12,8},{16,20},{20,16},{24,28},{28,24},{1,5},{5... | collective-permute-start | bytes 405512 | tf_op jit(solution)/shard_map/ppermute | solution.py:865
  8.9 6.5 %collective-permute-start.1 = (f32[264,128]{1,0:T(8,128)S(1)}, f32[264,128]{1,0:T(8,128)S(1)}, u32[]{:S(2)}, u32[]{:S(2)}) collective-permute-start(f32[264,128]{1,0:T(8,128)S(1)} %get-tuple-element.62), channel_id=1, source_target_pairs={{0,8},{4,12},{8,0},{12,4},{16,24},{20,28},{24,16},{28,20},{1,9},{5... | collective-permute-start | bytes 405512 | tf_op jit(solution)/shard_map/ppermute | solution.py:865
  10.5 6.2 %collective-permute-start.2 = (f32[264,128]{1,0:T(8,128)S(1)}, f32[264,128]{1,0:T(8,128)S(1)}, u32[]{:S(2)}, u32[]{:S(2)}) collective-permute-start(f32[264,128]{1,0:T(8,128)S(1)} %get-tuple-element.63), channel_id=1, source_target_pairs={{0,12},{4,8},{8,4},{12,0},{16,28},{20,24},{24,20},{28,16},{1,13},{... | collective-permute-start | bytes 405512 | tf_op jit(solution)/shard_map/ppermute | solution.py:865
  10.5 1.6 %copy-start.3 = (bf16[1024,1024]{1,0:T(8,128)(2,1)S(1)}, bf16[1024,1024]{1,0:T(8,128)(2,1)}, u32[]{:S(2)}) copy-start(bf16[1024,1024]{1,0:T(8,128)(2,1)} %get-tuple-element.57.v_ref) | copy-start | bytes 6291460
  16.8 7.2 %collective-permute-start.3 = (f32[256,128]{1,0:T(8,128)S(1)}, f32[256,128]{1,0:T(8,128)S(1)}, u32[]{:S(2)}, u32[]{:S(2)}) collective-permute-start(f32[256,128]{1,0:T(8,128)S(1)} %get-tuple-element.65.rest_1_), channel_id=1, source_target_pairs={{0,16},{4,20},{8,24},{12,28},{1,17},{5,21},{9,25},{13,29},{2,18},{... | collective-permute-start | bytes 393224 | tf_op jit(solution)/shard_map/ppermute | solution.py:883
  21.4 9.0 %copy-start.1 = (f32[1024]{0:T(1024)S(1)}, f32[1024]{0:T(1024)}, u32[]{:S(2)}) copy-start(f32[1024]{0:T(1024)} %param.9) | copy-start | bytes 12292
  24.0 6.4 %collective-permute-start.6 = (f32[256,128]{1,0:T(8,128)S(1)}, f32[256,128]{1,0:T(8,128)S(1)}, u32[]{:S(2)}, u32[]{:S(2)}) collective-permute-start(f32[256,128]{1,0:T(8,128)S(1)} %get-tuple-element.75), channel_id=1, source_target_pairs={{0,4},{4,0},{8,12},{12,8},{16,20},{20,16},{24,28},{28,24},{1,5},{5... | collective-permute-start | bytes 393224 | tf_op jit(solution)/shard_map/ppermute | solution.py:865
  25.6 7.0 %collective-permute-start.4 = (f32[256,128]{1,0:T(8,128)S(1)}, f32[256,128]{1,0:T(8,128)S(1)}, u32[]{:S(2)}, u32[]{:S(2)}) collective-permute-start(f32[256,128]{1,0:T(8,128)S(1)} %get-tuple-element.72), channel_id=1, source_target_pairs={{0,8},{4,12},{8,0},{12,4},{16,24},{20,28},{24,16},{28,20},{1,9},{5... | collective-permute-start | bytes 393224 | tf_op jit(solution)/shard_map/ppermute | solution.py:865
  28.6 5.9 %collective-permute-start.5 = (f32[256,128]{1,0:T(8,128)S(1)}, f32[256,128]{1,0:T(8,128)S(1)}, u32[]{:S(2)}, u32[]{:S(2)}) collective-permute-start(f32[256,128]{1,0:T(8,128)S(1)} %get-tuple-element.73), channel_id=1, source_target_pairs={{0,12},{4,8},{8,4},{12,0},{16,28},{20,24},{24,20},{28,16},{1,13},{... | collective-permute-start | bytes 393224 | tf_op jit(solution)/shard_map/ppermute | solution.py:865
  36.7 4.4 %collective-permute-start.7 = (bf16[1024,1024]{1,0:T(8,128)(2,1)S(1)}, bf16[1024,1024]{1,0:T(8,128)(2,1)}, u32[]{:S(2)}, u32[]{:S(2)}) collective-permute-start(bf16[1024,1024]{1,0:T(8,128)(2,1)S(1)} %get-tuple-element.78.own_ref.other_ref), channel_id=1, source_target_pairs={{0,1},{1,0},{2,3},{3,2},{4,5},{5,4},{6,7},{7,6},{8,9},{9,8},{10,11... | collective-permute-start | bytes 6291464 | tf_op jit(solution)/shard_map/ppermute | solution.py:868
  38.8 8.8 %collective-permute-start.8 = (bf16[512,256]{1,0:T(8,128)(2,1)S(1)}, bf16[512,256]{1,0:T(8,128)(2,1)S(1)}, u32[]{:S(2)}, u32[]{:S(2)}) collective-permute-start(bf16[512,256]{1,0:T(8,128)(2,1)S(1)} %get-tuple-element.82), channel_id=1, source_target_pairs={{0,4},{4,0},{8,12},{12,8},{16,20},{20,16},{24,28},{28,24},{1,5},{5... | collective-permute-start | bytes 786440 | tf_op jit(solution)/shard_map/ppermute | solution.py:865
  44.8 8.8 %collective-permute-start.9 = (bf16[544,256]{1,0:T(8,128)(2,1)S(1)}, bf16[544,256]{1,0:T(8,128)(2,1)S(1)}, u32[]{:S(2)}, u32[]{:S(2)}) collective-permute-start(bf16[544,256]{1,0:T(8,128)(2,1)S(1)} %get-tuple-element.83), channel_id=1, source_target_pairs={{0,4},{4,0},{8,12},{12,8},{16,20},{20,16},{24,28},{28,24},{1,5},{5... | collective-permute-start | bytes 835592 | tf_op jit(solution)/shard_map/ppermute | solution.py:865
  51.3 13.9 %collective-permute-start.13 = (bf16[512,384]{1,0:T(8,128)(2,1)S(1)}, bf16[512,384]{1,0:T(8,128)(2,1)S(1)}, u32[]{:S(2)}, u32[]{:S(2)}) collective-permute-start(bf16[512,384]{1,0:T(8,128)(2,1)S(1)} %get-tuple-element.91), channel_id=1, source_target_pairs={{0,4},{4,0},{8,12},{12,8},{16,20},{20,16},{24,28},{28,24},{1,5},{5... | collective-permute-start | bytes 1179656 | tf_op jit(solution)/shard_map/ppermute | solution.py:865
  53.7 7.9 %collective-permute-start.10 = (bf16[272,512]{1,0:T(8,128)(2,1)S(1)}, bf16[272,512]{1,0:T(8,128)(2,1)S(1)}, u32[]{:S(2)}, u32[]{:S(2)}) collective-permute-start(bf16[272,512]{1,0:T(8,128)(2,1)S(1)} %get-tuple-element.86), channel_id=1, source_target_pairs={{0,8},{4,12},{8,0},{12,4},{16,24},{20,28},{24,16},{28,20},{1,9},{5... | collective-permute-start | bytes 835592 | tf_op jit(solution)/shard_map/ppermute | solution.py:865
  57.3 10.4 %collective-permute-start.15 = (bf16[512,256]{1,0:T(8,128)(2,1)S(1)}, bf16[512,256]{1,0:T(8,128)(2,1)S(1)}, u32[]{:S(2)}, u32[]{:S(2)}) collective-permute-start(bf16[512,256]{1,0:T(8,128)(2,1)S(1)} %get-tuple-element.95), channel_id=1, source_target_pairs={{0,4},{4,0},{8,12},{12,8},{16,20},{20,16},{24,28},{28,24},{1,5},{5... | collective-permute-start | bytes 786440 | tf_op jit(solution)/shard_map/ppermute | solution.py:865
  61.7 9.8 %collective-permute-start.11 = (bf16[160,512]{1,0:T(8,128)(2,1)S(1)}, bf16[160,512]{1,0:T(8,128)(2,1)S(1)}, u32[]{:S(2)}, u32[]{:S(2)}) collective-permute-start(bf16[160,512]{1,0:T(8,128)(2,1)S(1)} %get-tuple-element.89), channel_id=1, source_target_pairs={{0,16},{4,20},{8,24},{12,28},{16,0},{20,4},{24,8},{28,12},{1,17},{... | collective-permute-start | bytes 491528 | tf_op jit(solution)/shard_map/ppermute | solution.py:865
  65.2 9.1 %collective-permute-start.14 = (bf16[256,384]{1,0:T(8,128)(2,1)S(1)}, bf16[256,384]{1,0:T(8,128)(2,1)S(1)}, u32[]{:S(2)}, u32[]{:S(2)}) collective-permute-start(bf16[256,384]{1,0:T(8,128)(2,1)S(1)} %get-tuple-element.93), channel_id=1, source_target_pairs={{0,8},{4,12},{8,0},{12,4},{16,24},{20,28},{24,16},{28,20},{1,9},{5... | collective-permute-start | bytes 589832 | tf_op jit(solution)/shard_map/ppermute | solution.py:865
  67.8 9.0 %collective-permute-start.16 = (bf16[256,256]{1,0:T(8,128)(2,1)S(1)}, bf16[256,256]{1,0:T(8,128)(2,1)S(1)}, u32[]{:S(2)}, u32[]{:S(2)}) collective-permute-start(bf16[256,256]{1,0:T(8,128)(2,1)S(1)} %get-tuple-element.99), channel_id=1, source_target_pairs={{0,8},{4,12},{8,0},{12,4},{16,24},{20,28},{24,16},{28,20},{1,9},{5... | collective-permute-start | bytes 393224 | tf_op jit(solution)/shard_map/ppermute | solution.py:865
  74.4 7.5 %collective-permute-start.18 = (bf16[128,384]{1,0:T(8,128)(2,1)S(1)}, bf16[128,384]{1,0:T(8,128)(2,1)S(1)}, u32[]{:S(2)}, u32[]{:S(2)}) collective-permute-start(bf16[128,384]{1,0:T(8,128)(2,1)S(1)} %get-tuple-element.102), channel_id=1, source_target_pairs={{0,16},{4,20},{8,24},{12,28},{16,0},{20,4},{24,8},{28,12},{1,17},{... | collective-permute-start | bytes 294920 | tf_op jit(solution)/shard_map/ppermute | solution.py:865
  76.8 6.3 %collective-permute-start.17 = (bf16[128,256]{1,0:T(8,128)(2,1)S(1)}, bf16[128,256]{1,0:T(8,128)(2,1)S(1)}, u32[]{:S(2)}, u32[]{:S(2)}) collective-permute-start(bf16[128,256]{1,0:T(8,128)(2,1)S(1)} %get-tuple-element.101), channel_id=1, source_target_pairs={{0,16},{4,20},{8,24},{12,28},{16,0},{20,4},{24,8},{28,12},{1,17},{... | collective-permute-start | bytes 196616 | tf_op jit(solution)/shard_map/ppermute | solution.py:865
  77.6 7.1 %collective-permute-start.19 = (bf16[128,256]{1,0:T(8,128)(2,1)S(1)}, bf16[128,256]{1,0:T(8,128)(2,1)S(1)}, u32[]{:S(2)}, u32[]{:S(2)}) collective-permute-start(bf16[128,256]{1,0:T(8,128)(2,1)S(1)} %get-tuple-element.104), channel_id=1, source_target_pairs={{0,4},{4,8},{8,12},{12,16},{16,20},{20,24},{24,28},{28,0},{1,5},{5... | collective-permute-start | bytes 196616 | tf_op jit(solution)/shard_map/ppermute | solution.py:876
  79.6 2.5 %collective-permute-start.12 = (f32[8,1024]{1,0:T(8,128)S(1)}, f32[8,1024]{1,0:T(8,128)S(1)}, u32[]{:S(2)}, u32[]{:S(2)}) collective-permute-start(f32[8,1024]{1,0:T(8,128)S(1)} %reduce_sum.9.means_ref), channel_id=1, source_target_pairs={{0,1},{1,0},{2,3},{3,2},{4,5},{5,4},{6,7},{7,6},{8,9},{9,8},{10,11... | collective-permute-start | bytes 98312 | tf_op jit(solution)/shard_map/ppermute | solution.py:868
  79.7 8.0 %collective-permute-start.20 = (bf16[128,256]{1,0:T(8,128)(2,1)S(1)}, bf16[128,256]{1,0:T(8,128)(2,1)S(1)}, u32[]{:S(2)}, u32[]{:S(2)}) collective-permute-start(bf16[128,256]{1,0:T(8,128)(2,1)S(1)} %get-tuple-element.105), channel_id=1, source_target_pairs={{0,8},{4,12},{8,16},{12,20},{16,24},{20,28},{24,0},{28,4},{1,9},{5... | collective-permute-start | bytes 196616 | tf_op jit(solution)/shard_map/ppermute | solution.py:876
  81.8 5.9 %collective-permute-start.21 = (bf16[128,256]{1,0:T(8,128)(2,1)S(1)}, bf16[128,256]{1,0:T(8,128)(2,1)S(1)}, u32[]{:S(2)}, u32[]{:S(2)}) collective-permute-start(bf16[128,256]{1,0:T(8,128)(2,1)S(1)} %get-tuple-element.106), channel_id=1, source_target_pairs={{0,1},{1,0},{2,3},{3,2},{4,5},{5,4},{6,7},{7,6},{8,9},{9,8},{10,11... | collective-permute-start | bytes 196616 | tf_op jit(solution)/shard_map/ppermute | solution.py:868
  82.1 9.1 %collective-permute-start.22 = (bf16[128,256]{1,0:T(8,128)(2,1)S(1)}, bf16[128,256]{1,0:T(8,128)(2,1)S(1)}, u32[]{:S(2)}, u32[]{:S(2)}) collective-permute-start(bf16[128,256]{1,0:T(8,128)(2,1)S(1)} %get-tuple-element.107), channel_id=1, source_target_pairs={{0,12},{4,16},{8,20},{12,24},{16,28},{20,0},{24,4},{28,8},{1,13},{... | collective-permute-start | bytes 196616 | tf_op jit(solution)/shard_map/ppermute | solution.py:876
  83.1 8.1 %collective-permute-start.24 = (bf16[128,256]{1,0:T(8,128)(2,1)S(1)}, bf16[128,256]{1,0:T(8,128)(2,1)S(1)}, u32[]{:S(2)}, u32[]{:S(2)}) collective-permute-start(bf16[128,256]{1,0:T(8,128)(2,1)S(1)} %get-tuple-element.109), channel_id=1, source_target_pairs={{0,1},{1,0},{2,3},{3,2},{4,5},{5,4},{6,7},{7,6},{8,9},{9,8},{10,11... | collective-permute-start | bytes 196616 | tf_op jit(solution)/shard_map/ppermute | solution.py:868
  84.6 6.6 %collective-permute-start.23 = (bf16[128,128]{1,0:T(8,128)(2,1)S(1)}, bf16[128,128]{1,0:T(8,128)(2,1)S(1)}, u32[]{:S(2)}, u32[]{:S(2)}) collective-permute-start(bf16[128,128]{1,0:T(8,128)(2,1)S(1)} %get-tuple-element.108), channel_id=1, source_target_pairs={{0,16},{4,20},{8,24},{12,28},{16,0},{20,4},{24,8},{28,12},{1,17},{... | collective-permute-start | bytes 98312 | tf_op jit(solution)/shard_map/ppermute | solution.py:876

commit v8 on v7

--- a/solution.py
+++ b/solution.py
@@ -824,6 +824,7 @@
         scratch_shapes=[pltpu.VMEM((shards, 2 * width), F32)],
         out_shape=struct((rows, 2 * width), F32),
         compiler_params=params(16),
+        cost_estimate=pl.CostEstimate(flops=1, bytes_accessed=1, transcendentals=0),
         name="cover",
     )(means, others, *values)
 

time: 92.6 us -> 92.6 us (level)
  no operation moved by 1% of the time
where the time goes in v8:
time: 92.6 us; the launch traced here: 92.4 us
  starting transfers between devices  32.6 us (35%)
  Pallas kernels  28.8 us (31%)
  waiting for transfers between devices  26.7 us (29%)
  local copies, waits for them, and re-layouts  3.23 us (3%)
  between operations  0.93 us (1%)
    ppermute x16, waiting for transfers between devices, to_shard(): return lax.ppermute(value, 'ctx', [(a, a ^ apart) for a in range(shards)])  21.5 us
    ppermute x16, starting transfers between devices, to_shard(): return lax.ppermute(value, 'ctx', [(a, a ^ apart) for a in range(shards)])  19.9 us
    pallas_call x4, Pallas kernels, gram_parts(): pl.pallas_call(functools.partial(gram_kernel, rows, blocks, apart), in_sp...  12.5 us
    ppermute x4, starting transfers between devices, forward(): lax.ppermute(value, 'ctx', [(a, (a + step) % shards) for a in range(shard...  7.4 us
    pallas_call x2, Pallas kernels, inner(): pl.pallas_call(functools.partial(inner_loop_kernel, begin, end), in_specs...  4.69 us
    ppermute x1, starting transfers between devices, body(): entered = lax.ppermute(leaving, 'ctx', [(a, a + near) for a in range(near)])  4.65 us
    pallas_call x2, Pallas kernels, finish(): pl.pallas_call(functools.partial(finish_part_kernel, near, part), in_spec...  4.36 us
    pallas_call x1, Pallas kernels, local_states(): pl.pallas_call(functools.partial(states_fetch_kernel, near), in_specs=[hb...  4.35 us
  transfers between devices with their start and end apart: 25, of which 15 were waited for; matrix products, arithmetic and copies ran while one was open for 1% of the time, Pallas kernels for 23%

profile of v8, /device:TPU:0, one launch (start us, length us, event | category | flops | bytes accessed | tf_op | source)
XLA Modules:
  0.0 92.4 jit_solution(17342009160682298935)
XLA Ops:
  0.7 0.9 copy-done.2
  1.5 4.4 %local_states.1 = (f32[4,1024,128]{2,1,0:T(8,128)S(1)}, f32[4,8,128]{2,1,0:T(8,128)S(1)}, f32[32,256]{1,0:T(8,128)S(1)}, f32[264,128]{1,0:T(8,128)S(1)}, f32[264...) custom-call(bf16[1024,1024]{1,0:T(8,128)(2,1)} %k_any.1, ...), custom_call_target="tpu_custom_call" | custom-call | flops 2147483648 | bytes 16777216 | tf_op jit(solution)/shard_map/local_states/pallas_call | solution.py:197
  5.9 3.0 %collective-permute-start = (f32[264,128]{1,0:T(8,128)S(1)}, f32[264,128]{1,0:T(8,128)S(1)}, u32[]{:S(2)}, u32[]{:S(2)}) collective-permute-start(f32[264,128]{1,0:T(8,128)S(1)} %get-tuple-element.61), channel_id=1, source_target_pairs={{0,4},{4,0},{8,12},{12,8},{16,20},{20,16},{24,28},{28,24},{1,5},{5... | collective-permute-start | bytes 405512 | tf_op jit(solution)/shard_map/ppermute | solution.py:866
  8.9 1.6 %collective-permute-start.1 = (f32[264,128]{1,0:T(8,128)S(1)}, f32[264,128]{1,0:T(8,128)S(1)}, u32[]{:S(2)}, u32[]{:S(2)}) collective-permute-start(f32[264,128]{1,0:T(8,128)S(1)} %get-tuple-element.62), channel_id=1, source_target_pairs={{0,8},{4,12},{8,0},{12,4},{16,24},{20,28},{24,16},{28,20},{1,9},{5... | collective-permute-start | bytes 405512 | tf_op jit(solution)/shard_map/ppermute | solution.py:866
  10.5 1.6 %copy-done.3 = bf16[1024,1024]{1,0:T(8,128)(2,1)S(1)} copy-done((bf16[1024,1024]{1,0:T(8,128)(2,1)S(1)}, bf16[1024,1024]{1,0:T(8,128)(2,1)}, u32[]{:S(2)}) %copy-start.3) | copy-done | bytes 2097176
  12.1 2.3 %inner.2 = (f32[1024,1024]{1,0:T(8,128)S(1)}, f32[8,128]{1,0:T(8,128)S(1)}) custom-call(bf16[1024,1024]{1,0:T(8,128)(2,1)S(1)} %copy-done, bf16[1024,1024]{1,0:T(8,128)(2,1)S(1)} %get-tuple-element.56.k_ref, bf16[1024,1024]{1,0:T(8,128)(2,1)S(1)} %copy-done.3, f32[32,256]{1,0:T(8,128)S(1)} %get-tuple-element.58.cumul_ref), custom_call_target="tpu_custom_call" | custom-call | flops 4294967296 | bytes 41943040 | tf_op jit(solution)/shard_map/inner/pallas_call | solution.py:346
  14.4 1.0 %collective-permute-done.1.refs_2_ = f32[264,128]{1,0:T(8,128)S(1)} collective-permute-done((f32[264,128]{1,0:T(8,128)S(1)}, f32[264,128]{1,0:T(8,128)S(1)}, u32[]{:S(2)}, u32[]{:S(2)}) %collective-permute-start.1) | collective-permute-done | bytes 135200 | tf_op jit(solution)/shard_map/ppermute | solution.py:866
  15.4 1.2 %collective-permute-done.2.refs_3_ = f32[264,128]{1,0:T(8,128)S(1)} collective-permute-done((f32[264,128]{1,0:T(8,128)S(1)}, f32[264,128]{1,0:T(8,128)S(1)}, u32[]{:S(2)}, u32[]{:S(2)}) %collective-permute-start.2) | collective-permute-done | bytes 135200 | tf_op jit(solution)/shard_map/ppermute | solution.py:866
  16.7 0.1 chain.1
  16.8 4.6 %collective-permute-start.3 = (f32[256,128]{1,0:T(8,128)S(1)}, f32[256,128]{1,0:T(8,128)S(1)}, u32[]{:S(2)}, u32[]{:S(2)}) collective-permute-start(f32[256,128]{1,0:T(8,128)S(1)} %get-tuple-element.65.rest_1_), channel_id=1, source_target_pairs={{0,16},{4,20},{8,24},{12,28},{1,17},{5,21},{9,25},{13,29},{2,18},{... | collective-permute-start | bytes 393224 | tf_op jit(solution)/shard_map/ppermute | solution.py:884
  21.4 0.0 copy-start.1
  21.4 2.4 %inner.3 = (f32[1024,1024]{1,0:T(8,128)S(1)}, f32[8,128]{1,0:T(8,128)S(1)}) custom-call(bf16[1024,1024]{1,0:T(8,128)(2,1)S(1)} %copy-done, bf16[1024,1024]{1,0:T(8,128)(2,1)S(1)} %get-tuple-element.56.k_ref, bf16[1024,1024]{1,0:T(8,128)(2,1)S(1)} %copy-done.3, f32[32,256]{1,0:T(8,128)S(1)} %get-tuple-element.58.cumul_ref, ...), custom_call_target="tpu_custom_call" | custom-call | flops 4294967296 | bytes 41943040 | tf_op jit(solution)/shard_map/inner/pallas_call | solution.py:346
  23.9 0.1 collective-permute-done.3.entered_ref
  23.9 0.1 spread_states.1
  24.0 1.6 %collective-permute-start.6 = (f32[256,128]{1,0:T(8,128)S(1)}, f32[256,128]{1,0:T(8,128)S(1)}, u32[]{:S(2)}, u32[]{:S(2)}) collective-permute-start(f32[256,128]{1,0:T(8,128)S(1)} %get-tuple-element.75), channel_id=1, source_target_pairs={{0,4},{4,0},{8,12},{12,8},{16,20},{20,16},{24,28},{28,24},{1,5},{5... | collective-permute-start | bytes 393224 | tf_op jit(solution)/shard_map/ppermute | solution.py:866
  25.6 3.0 %collective-permute-start.4 = (f32[256,128]{1,0:T(8,128)S(1)}, f32[256,128]{1,0:T(8,128)S(1)}, u32[]{:S(2)}, u32[]{:S(2)}) collective-permute-start(f32[256,128]{1,0:T(8,128)S(1)} %get-tuple-element.72), channel_id=1, source_target_pairs={{0,8},{4,12},{8,0},{12,4},{16,24},{20,28},{24,16},{28,20},{1,9},{5... | collective-permute-start | bytes 393224 | tf_op jit(solution)/shard_map/ppermute | solution.py:866
  28.6 0.1 collective-permute-start.5
  28.7 1.8 %collective-permute-done.6.rest_1_ = f32[256,128]{1,0:T(8,128)S(1)} collective-permute-done((f32[256,128]{1,0:T(8,128)S(1)}, f32[256,128]{1,0:T(8,128)S(1)}, u32[]{:S(2)}, u32[]{:S(2)}) %collective-permute-start.6) | collective-permute-done | bytes 131104 | tf_op jit(solution)/shard_map/ppermute | solution.py:866
  30.4 2.1 %finish.2 = (bf16[1024,1024]{1,0:T(8,128)(2,1)S(1)}, bf16[16,1024]{1,0:T(8,128)(2,1)S(1)}) custom-call(bf16[1024,1024]{1,0:T(8,128)(2,1)S(1)} %copy-done, f32[1024,1024]{1,0:T(8,128)S(1)} %get-tuple-element.66.raw_ref, f32[4,1024,128]{2,1,0:T(8,128)S(1)} %get-tuple-element.67.entering_ref, f32[4,8,128]{2,1,0:T(8,128)S(1)} %get-tuple-element.68.before_ref, ...), custom_call_target="tpu_custom_call" | custom-call | flops 2147483648 | bytes 41943040 | tf_op jit(solution)/shard_map/finish/pallas_call | solution.py:544
  32.6 1.9 %collective-permute-done.5.rest_1_ = f32[256,128]{1,0:T(8,128)S(1)} collective-permute-done((f32[256,128]{1,0:T(8,128)S(1)}, f32[256,128]{1,0:T(8,128)S(1)}, u32[]{:S(2)}, u32[]{:S(2)}) %collective-permute-start.5) | collective-permute-done | bytes 131104 | tf_op jit(solution)/shard_map/ppermute | solution.py:866
  34.5 2.2 %finish.3 = (bf16[1024,1024]{1,0:T(8,128)(2,1)S(1)}, bf16[16,1024]{1,0:T(8,128)(2,1)S(1)}) custom-call(bf16[1024,1024]{1,0:T(8,128)(2,1)S(1)} %copy-done, f32[1024,1024]{1,0:T(8,128)S(1)} %get-tuple-element.66.raw_ref, f32[4,1024,128]{2,1,0:T(8,128)S(1)} %get-tuple-element.67.entering_ref, f32[4,8,128]{2,1,0:T(8,128)S(1)} %get-tuple-element.68.before_ref, ...), custom_call_target="tpu_custom_call" | custom-call | flops 2147483648 | bytes 41943040 | tf_op jit(solution)/shard_map/finish/pallas_call | solution.py:544
  36.7 0.1 collective-permute-start.7
  36.8 2.0 %gram.4 = (f32[512,256]{1,0:T(8,128)S(1)}, bf16[512,256]{1,0:T(8,128)(2,1)S(1)}) custom-call(bf16[1024,1024]{1,0:T(8,128)(2,1)S(1)} %get-tuple-element.78.own_ref.other_ref, bf16[1024,1024]{1,0:T(8,128)(2,1)S(1)} %get-tuple-element.78.own_ref.other_ref, bf16[16,1024]{1,0:T(8,128)(2,1)S(1)} %get-tuple-element.79.rest_0_), custom_call_target="tpu_custom_call" | custom-call | flops 2147483648 | bytes 16777216 | tf_op jit(solution)/shard_map/gram/pallas_call | solution.py:653
  38.8 0.7 collective-permute-start.8
  39.6 1.5 %collective-permute-done.7.other_ref = bf16[1024,1024]{1,0:T(8,128)(2,1)} collective-permute-done((bf16[1024,1024]{1,0:T(8,128)(2,1)S(1)}, bf16[1024,1024]{1,0:T(8,128)(2,1)}, u32[]{:S(2)}, u32[]{:S(2)}) %collective-permute-start.7) | collective-permute-done | bytes 2097184 | tf_op jit(solution)/shard_map/ppermute | solution.py:869
  41.0 3.8 %gram.5 = (f32[512,256]{1,0:T(8,128)S(1)}, bf16[544,256]{1,0:T(8,128)(2,1)S(1)}) custom-call(bf16[1024,1024]{1,0:T(8,128)(2,1)S(1)} %get-tuple-element.78.own_ref.other_ref, bf16[1024,1024]{1,0:T(8,128)(2,1)} %collective-permute-done.7.other_ref, bf16[32,256]{1,0:T(8,128)(2,1)S(1)} %pad.4.rest_0_.refs_5_, f32[512,256]{1,0:T(8,128)S(1)} %get-tuple-element.80.rest_1_.refs_0_), custom_call_target="tpu_custom_call" | custom-call | flops 2147483648 | bytes 16777216 | tf_op jit(solution)/shard_map/gram/pallas_call | solution.py:653
  44.8 0.7 collective-permute-start.9
  45.5 2.0 %collective-permute-done.8.rest_0_.refs_2_ = bf16[512,256]{1,0:T(8,128)(2,1)S(1)} collective-permute-done((bf16[512,256]{1,0:T(8,128)(2,1)S(1)}, bf16[512,256]{1,0:T(8,128)(2,1)S(1)}, u32[]{:S(2)}, u32[]{:S(2)}) %collective-permute-start.8) | collective-permute-done | bytes 262176 | tf_op jit(solution)/shard_map/ppermute | solution.py:866
  47.6 3.7 %gram.6 = (f32[512,384]{1,0:T(8,128)S(1)}, bf16[512,384]{1,0:T(8,128)(2,1)S(1)}) custom-call(bf16[1024,1024]{1,0:T(8,128)(2,1)S(1)} %get-tuple-element.78.own_ref.other_ref, bf16[1024,1024]{1,0:T(8,128)(2,1)} %collective-permute-done.7.other_ref, bf16[512,256]{1,0:T(8,128)(2,1)S(1)} %collective-permute-done.8.rest_0_.refs_2_), custom_call_target="tpu_custom_call" | custom-call | flops 3221225472 | bytes 16777216 | tf_op jit(solution)/shard_map/gram/pallas_call | solution.py:653
  51.3 0.7 collective-permute-start.13
  52.0 1.6 %collective-permute-done.9.refs_3_ = bf16[544,256]{1,0:T(8,128)(2,1)S(1)} collective-permute-done((bf16[544,256]{1,0:T(8,128)(2,1)S(1)}, bf16[544,256]{1,0:T(8,128)(2,1)S(1)}, u32[]{:S(2)}, u32[]{:S(2)}) %collective-permute-start.9) | collective-permute-done | bytes 278560 | tf_op jit(solution)/shard_map/ppermute | solution.py:866
  53.6 0.1 fold.6
  53.7 0.6 collective-permute-start.10
  54.3 3.0 %gram.7 = (f32[512,256]{1,0:T(8,128)S(1)}, bf16[512,256]{1,0:T(8,128)(2,1)S(1)}) custom-call(bf16[1024,1024]{1,0:T(8,128)(2,1)S(1)} %get-tuple-element.78.own_ref.other_ref, bf16[1024,1024]{1,0:T(8,128)(2,1)} %collective-permute-done.7.other_ref, f32[256,512]{1,0:T(8,128)S(1)} %get-tuple-element.85.refs_0_.refs_2_.rest_0_), custom_call_target="tpu_custom_call" | custom-call | flops 2147483648 | bytes 16777216 | tf_op jit(solution)/shard_map/gram/pallas_call | solution.py:653
  57.3 1.5 %collective-permute-start.15 = (bf16[512,256]{1,0:T(8,128)(2,1)S(1)}, bf16[512,256]{1,0:T(8,128)(2,1)S(1)}, u32[]{:S(2)}, u32[]{:S(2)}) collective-permute-start(bf16[512,256]{1,0:T(8,128)(2,1)S(1)} %get-tuple-element.95), channel_id=1, source_target_pairs={{0,4},{4,0},{8,12},{12,8},{16,20},{20,16},{24,28},{28,24},{1,5},{5... | collective-permute-start | bytes 786440 | tf_op jit(solution)/shard_map/ppermute | solution.py:866
  58.8 2.8 %collective-permute-done.10.refs_1_ = bf16[272,512]{1,0:T(8,128)(2,1)S(1)} collective-permute-done((bf16[272,512]{1,0:T(8,128)(2,1)S(1)}, bf16[272,512]{1,0:T(8,128)(2,1)S(1)}, u32[]{:S(2)}, u32[]{:S(2)}) %collective-permute-start.10) | collective-permute-done | bytes 278560 | tf_op jit(solution)/shard_map/ppermute | solution.py:866
  61.6 0.1 fold.7
  61.7 3.5 %collective-permute-start.11 = (bf16[160,512]{1,0:T(8,128)(2,1)S(1)}, bf16[160,512]{1,0:T(8,128)(2,1)S(1)}, u32[]{:S(2)}, u32[]{:S(2)}) collective-permute-start(bf16[160,512]{1,0:T(8,128)(2,1)S(1)} %get-tuple-element.89), channel_id=1, source_target_pairs={{0,16},{4,20},{8,24},{12,28},{16,0},{20,4},{24,8},{28,12},{1,17},{... | collective-permute-start | bytes 491528 | tf_op jit(solution)/shard_map/ppermute | solution.py:866
  65.2 0.1 fold.8
  65.2 1.3 %collective-permute-start.14 = (bf16[256,384]{1,0:T(8,128)(2,1)S(1)}, bf16[256,384]{1,0:T(8,128)(2,1)S(1)}, u32[]{:S(2)}, u32[]{:S(2)}) collective-permute-start(bf16[256,384]{1,0:T(8,128)(2,1)S(1)} %get-tuple-element.93), channel_id=1, source_target_pairs={{0,8},{4,12},{8,0},{12,4},{16,24},{20,28},{24,16},{28,20},{1,9},{5... | collective-permute-start | bytes 589832 | tf_op jit(solution)/shard_map/ppermute | solution.py:866
  66.6 1.2 %collective-permute-done.15.refs_1_ = bf16[512,256]{1,0:T(8,128)(2,1)S(1)} collective-permute-done((bf16[512,256]{1,0:T(8,128)(2,1)S(1)}, bf16[512,256]{1,0:T(8,128)(2,1)S(1)}, u32[]{:S(2)}, u32[]{:S(2)}) %collective-permute-start.15) | collective-permute-done | bytes 262176 | tf_op jit(solution)/shard_map/ppermute | solution.py:866
  67.8 0.6 collective-permute-start.16
  68.4 3.1 %collective-permute-done.11.other_ref = bf16[160,512]{1,0:T(8,128)(2,1)S(1)} collective-permute-done((bf16[160,512]{1,0:T(8,128)(2,1)S(1)}, bf16[160,512]{1,0:T(8,128)(2,1)S(1)}, u32[]{:S(2)}, u32[]{:S(2)}) %collective-permute-start.11) | collective-permute-done | bytes 163872 | tf_op jit(solution)/shard_map/ppermute | solution.py:866
  71.5 2.8 %collective-permute-done.14.refs_1_ = bf16[256,384]{1,0:T(8,128)(2,1)S(1)} collective-permute-done((bf16[256,384]{1,0:T(8,128)(2,1)S(1)}, bf16[256,384]{1,0:T(8,128)(2,1)S(1)}, u32[]{:S(2)}, u32[]{:S(2)}) %collective-permute-start.14) | collective-permute-done | bytes 196640 | tf_op jit(solution)/shard_map/ppermute | solution.py:866
  74.4 0.3 collective-permute-start.18
  74.6 0.1 close.3
  74.7 2.1 %collective-permute-done.16.refs_1_ = bf16[256,256]{1,0:T(8,128)(2,1)S(1)} collective-permute-done((bf16[256,256]{1,0:T(8,128)(2,1)S(1)}, bf16[256,256]{1,0:T(8,128)(2,1)S(1)}, u32[]{:S(2)}, u32[]{:S(2)}) %collective-permute-start.16) | collective-permute-done | bytes 131104 | tf_op jit(solution)/shard_map/ppermute | solution.py:866
  76.8 0.7 collective-permute-start.17
  77.6 1.9 %collective-permute-start.19 = (bf16[128,256]{1,0:T(8,128)(2,1)S(1)}, bf16[128,256]{1,0:T(8,128)(2,1)S(1)}, u32[]{:S(2)}, u32[]{:S(2)}) collective-permute-start(bf16[128,256]{1,0:T(8,128)(2,1)S(1)} %get-tuple-element.104), channel_id=1, source_target_pairs={{0,4},{4,8},{8,12},{12,16},{16,20},{20,24},{24,28},{28,0},{1,5},{5... | collective-permute-start | bytes 196616 | tf_op jit(solution)/shard_map/ppermute | solution.py:877
  79.5 0.1 reshape.23
  79.5 0.1 reduce_sum.9.means_ref
  79.6 0.1 collective-permute-start.12
  79.7 2.1 %collective-permute-start.20 = (bf16[128,256]{1,0:T(8,128)(2,1)S(1)}, bf16[128,256]{1,0:T(8,128)(2,1)S(1)}, u32[]{:S(2)}, u32[]{:S(2)}) collective-permute-start(bf16[128,256]{1,0:T(8,128)(2,1)S(1)} %get-tuple-element.105), channel_id=1, source_target_pairs={{0,8},{4,12},{8,16},{12,20},{16,24},{20,28},{24,0},{28,4},{1,9},{5... | collective-permute-start | bytes 196616 | tf_op jit(solution)/shard_map/ppermute | solution.py:877
  81.8 0.0 collective-permute-done.18.other_ref
  81.8 0.2 collective-permute-start.21
  82.1 1.0 %collective-permute-start.22 = (bf16[128,256]{1,0:T(8,128)(2,1)S(1)}, bf16[128,256]{1,0:T(8,128)(2,1)S(1)}, u32[]{:S(2)}, u32[]{:S(2)}) collective-permute-start(bf16[128,256]{1,0:T(8,128)(2,1)S(1)} %get-tuple-element.107), channel_id=1, source_target_pairs={{0,12},{4,16},{8,20},{12,24},{16,28},{20,0},{24,4},{28,8},{1,13},{... | collective-permute-start | bytes 196616 | tf_op jit(solution)/shard_map/ppermute | solution.py:877
  83.1 0.2 collective-permute-start.24
  83.3 1.3 %collective-permute-done.19.refs_2_ = bf16[128,256]{1,0:T(8,128)(2,1)S(1)} collective-permute-done((bf16[128,256]{1,0:T(8,128)(2,1)S(1)}, bf16[128,256]{1,0:T(8,128)(2,1)S(1)}, u32[]{:S(2)}, u32[]{:S(2)}) %collective-permute-start.19) | collective-permute-done | bytes 65568 | tf_op jit(solution)/shard_map/ppermute | solution.py:877
  84.6 2.4 %collective-permute-start.23 = (bf16[128,128]{1,0:T(8,128)(2,1)S(1)}, bf16[128,128]{1,0:T(8,128)(2,1)S(1)}, u32[]{:S(2)}, u32[]{:S(2)}) collective-permute-start(bf16[128,128]{1,0:T(8,128)(2,1)S(1)} %get-tuple-element.108), channel_id=1, source_target_pairs={{0,16},{4,20},{8,24},{12,28},{16,0},{20,4},{24,8},{28,12},{1,17},{... | collective-permute-start | bytes 98312 | tf_op jit(solution)/shard_map/ppermute | solution.py:877
  87.1 0.6 copy.7
  87.7 0.0 collective-permute-done.20.refs_3_
  87.7 1.2 %cover.1.begun_ref = f32[128,2048]{1,0:T(8,128)S(1)} custom-call(f32[8,1024]{1,0:T(8,128)S(1)} %reduce_sum.9.means_ref, f32[8,1024]{1,0:T(8,128)S(1)} %collective-permute-done.12.others_ref, f32[128,512]{1,0:T(8,128)S(1)} %get-tuple-element.98.refs_2_.refs_0_, f32[128,256]{1,0:T(8,128)S(1)} %close.5.refs_1_, ...), custom_call_target="tpu_custom_call" | custom-call | flops 1 | bytes 1 | tf_op jit(solution)/shard_map/cover/pallas_call | solution.py:820
  88.9 2.3 %collective-permute-done.23.refs_2_ = bf16[128,128]{1,0:T(8,128)(2,1)S(1)} collective-permute-done((bf16[128,128]{1,0:T(8,128)(2,1)S(1)}, bf16[128,128]{1,0:T(8,128)(2,1)S(1)}, u32[]{:S(2)}, u32[]{:S(2)}) %collective-permute-start.23) | collective-permute-done | bytes 32800 | tf_op jit(solution)/shard_map/ppermute | solution.py:877
  91.2 1.2 %cover_rest.1 = f32[128,2048]{1,0:T(8,128)} custom-call(f32[128,2048]{1,0:T(8,128)S(1)} %cover.1.begun_ref, f32[128,384]{1,0:T(8,128)S(1)} %get-tuple-element.103.rest_0_.refs_0_, bf16[128,256]{1,0:T(8,128)(2,1)S(1)} %collective-permute-done.22.refs_1_, bf16[128,128]{1,0:T(8,128)(2,1)S(1)} %collective-permute-done.23.refs_2_, ...), custom_call_target="tpu_custom_call" | custom-call | tf_op jit(solution)/shard_map/cover_rest/pallas_call | solution.py:848
  (32 shorter events, 0.3 us)
Async XLA Ops:
  0.6 9.9 %copy-start = (bf16[1024,1024]{1,0:T(8,128)(2,1)S(1)}, bf16[1024,1024]{1,0:T(8,128)(2,1)}, u32[]{:S(2)}) copy-start(bf16[1024,1024]{1,0:T(8,128)(2,1)} %q_ref.7) | copy-start | bytes 6291460
  0.6 0.9 copy-start.2
  5.9 8.5 %collective-permute-start = (f32[264,128]{1,0:T(8,128)S(1)}, f32[264,128]{1,0:T(8,128)S(1)}, u32[]{:S(2)}, u32[]{:S(2)}) collective-permute-start(f32[264,128]{1,0:T(8,128)S(1)} %get-tuple-element.61), channel_id=1, source_target_pairs={{0,4},{4,0},{8,12},{12,8},{16,20},{20,16},{24,28},{28,24},{1,5},{5... | collective-permute-start | bytes 405512 | tf_op jit(solution)/shard_map/ppermute | solution.py:866
  8.9 6.5 %collective-permute-start.1 = (f32[264,128]{1,0:T(8,128)S(1)}, f32[264,128]{1,0:T(8,128)S(1)}, u32[]{:S(2)}, u32[]{:S(2)}) collective-permute-start(f32[264,128]{1,0:T(8,128)S(1)} %get-tuple-element.62), channel_id=1, source_target_pairs={{0,8},{4,12},{8,0},{12,4},{16,24},{20,28},{24,16},{28,20},{1,9},{5... | collective-permute-start | bytes 405512 | tf_op jit(solution)/shard_map/ppermute | solution.py:866
  10.5 6.2 %collective-permute-start.2 = (f32[264,128]{1,0:T(8,128)S(1)}, f32[264,128]{1,0:T(8,128)S(1)}, u32[]{:S(2)}, u32[]{:S(2)}) collective-permute-start(f32[264,128]{1,0:T(8,128)S(1)} %get-tuple-element.63), channel_id=1, source_target_pairs={{0,12},{4,8},{8,4},{12,0},{16,28},{20,24},{24,20},{28,16},{1,13},{... | collective-permute-start | bytes 405512 | tf_op jit(solution)/shard_map/ppermute | solution.py:866
  10.5 1.6 %copy-start.3 = (bf16[1024,1024]{1,0:T(8,128)(2,1)S(1)}, bf16[1024,1024]{1,0:T(8,128)(2,1)}, u32[]{:S(2)}) copy-start(bf16[1024,1024]{1,0:T(8,128)(2,1)} %get-tuple-element.57.v_ref) | copy-start | bytes 6291460
  16.8 7.2 %collective-permute-start.3 = (f32[256,128]{1,0:T(8,128)S(1)}, f32[256,128]{1,0:T(8,128)S(1)}, u32[]{:S(2)}, u32[]{:S(2)}) collective-permute-start(f32[256,128]{1,0:T(8,128)S(1)} %get-tuple-element.65.rest_1_), channel_id=1, source_target_pairs={{0,16},{4,20},{8,24},{12,28},{1,17},{5,21},{9,25},{13,29},{2,18},{... | collective-permute-start | bytes 393224 | tf_op jit(solution)/shard_map/ppermute | solution.py:884
  21.4 9.0 %copy-start.1 = (f32[1024]{0:T(1024)S(1)}, f32[1024]{0:T(1024)}, u32[]{:S(2)}) copy-start(f32[1024]{0:T(1024)} %param.9) | copy-start | bytes 12292
  24.0 6.4 %collective-permute-start.6 = (f32[256,128]{1,0:T(8,128)S(1)}, f32[256,128]{1,0:T(8,128)S(1)}, u32[]{:S(2)}, u32[]{:S(2)}) collective-permute-start(f32[256,128]{1,0:T(8,128)S(1)} %get-tuple-element.75), channel_id=1, source_target_pairs={{0,4},{4,0},{8,12},{12,8},{16,20},{20,16},{24,28},{28,24},{1,5},{5... | collective-permute-start | bytes 393224 | tf_op jit(solution)/shard_map/ppermute | solution.py:866
  25.6 7.0 %collective-permute-start.4 = (f32[256,128]{1,0:T(8,128)S(1)}, f32[256,128]{1,0:T(8,128)S(1)}, u32[]{:S(2)}, u32[]{:S(2)}) collective-permute-start(f32[256,128]{1,0:T(8,128)S(1)} %get-tuple-element.72), channel_id=1, source_target_pairs={{0,8},{4,12},{8,0},{12,4},{16,24},{20,28},{24,16},{28,20},{1,9},{5... | collective-permute-start | bytes 393224 | tf_op jit(solution)/shard_map/ppermute | solution.py:866
  28.6 5.9 %collective-permute-start.5 = (f32[256,128]{1,0:T(8,128)S(1)}, f32[256,128]{1,0:T(8,128)S(1)}, u32[]{:S(2)}, u32[]{:S(2)}) collective-permute-start(f32[256,128]{1,0:T(8,128)S(1)} %get-tuple-element.73), channel_id=1, source_target_pairs={{0,12},{4,8},{8,4},{12,0},{16,28},{20,24},{24,20},{28,16},{1,13},{... | collective-permute-start | bytes 393224 | tf_op jit(solution)/shard_map/ppermute | solution.py:866
  36.7 4.4 %collective-permute-start.7 = (bf16[1024,1024]{1,0:T(8,128)(2,1)S(1)}, bf16[1024,1024]{1,0:T(8,128)(2,1)}, u32[]{:S(2)}, u32[]{:S(2)}) collective-permute-start(bf16[1024,1024]{1,0:T(8,128)(2,1)S(1)} %get-tuple-element.78.own_ref.other_ref), channel_id=1, source_target_pairs={{0,1},{1,0},{2,3},{3,2},{4,5},{5,4},{6,7},{7,6},{8,9},{9,8},{10,11... | collective-permute-start | bytes 6291464 | tf_op jit(solution)/shard_map/ppermute | solution.py:869
  38.8 8.8 %collective-permute-start.8 = (bf16[512,256]{1,0:T(8,128)(2,1)S(1)}, bf16[512,256]{1,0:T(8,128)(2,1)S(1)}, u32[]{:S(2)}, u32[]{:S(2)}) collective-permute-start(bf16[512,256]{1,0:T(8,128)(2,1)S(1)} %get-tuple-element.82), channel_id=1, source_target_pairs={{0,4},{4,0},{8,12},{12,8},{16,20},{20,16},{24,28},{28,24},{1,5},{5... | collective-permute-start | bytes 786440 | tf_op jit(solution)/shard_map/ppermute | solution.py:866
  44.8 8.8 %collective-permute-start.9 = (bf16[544,256]{1,0:T(8,128)(2,1)S(1)}, bf16[544,256]{1,0:T(8,128)(2,1)S(1)}, u32[]{:S(2)}, u32[]{:S(2)}) collective-permute-start(bf16[544,256]{1,0:T(8,128)(2,1)S(1)} %get-tuple-element.83), channel_id=1, source_target_pairs={{0,4},{4,0},{8,12},{12,8},{16,20},{20,16},{24,28},{28,24},{1,5},{5... | collective-permute-start | bytes 835592 | tf_op jit(solution)/shard_map/ppermute | solution.py:866
  51.3 13.9 %collective-permute-start.13 = (bf16[512,384]{1,0:T(8,128)(2,1)S(1)}, bf16[512,384]{1,0:T(8,128)(2,1)S(1)}, u32[]{:S(2)}, u32[]{:S(2)}) collective-permute-start(bf16[512,384]{1,0:T(8,128)(2,1)S(1)} %get-tuple-element.91), channel_id=1, source_target_pairs={{0,4},{4,0},{8,12},{12,8},{16,20},{20,16},{24,28},{28,24},{1,5},{5... | collective-permute-start | bytes 1179656 | tf_op jit(solution)/shard_map/ppermute | solution.py:866
  53.7 7.9 %collective-permute-start.10 = (bf16[272,512]{1,0:T(8,128)(2,1)S(1)}, bf16[272,512]{1,0:T(8,128)(2,1)S(1)}, u32[]{:S(2)}, u32[]{:S(2)}) collective-permute-start(bf16[272,512]{1,0:T(8,128)(2,1)S(1)} %get-tuple-element.86), channel_id=1, source_target_pairs={{0,8},{4,12},{8,0},{12,4},{16,24},{20,28},{24,16},{28,20},{1,9},{5... | collective-permute-start | bytes 835592 | tf_op jit(solution)/shard_map/ppermute | solution.py:866
  57.3 10.4 %collective-permute-start.15 = (bf16[512,256]{1,0:T(8,128)(2,1)S(1)}, bf16[512,256]{1,0:T(8,128)(2,1)S(1)}, u32[]{:S(2)}, u32[]{:S(2)}) collective-permute-start(bf16[512,256]{1,0:T(8,128)(2,1)S(1)} %get-tuple-element.95), channel_id=1, source_target_pairs={{0,4},{4,0},{8,12},{12,8},{16,20},{20,16},{24,28},{28,24},{1,5},{5... | collective-permute-start | bytes 786440 | tf_op jit(solution)/shard_map/ppermute | solution.py:866
  61.7 9.8 %collective-permute-start.11 = (bf16[160,512]{1,0:T(8,128)(2,1)S(1)}, bf16[160,512]{1,0:T(8,128)(2,1)S(1)}, u32[]{:S(2)}, u32[]{:S(2)}) collective-permute-start(bf16[160,512]{1,0:T(8,128)(2,1)S(1)} %get-tuple-element.89), channel_id=1, source_target_pairs={{0,16},{4,20},{8,24},{12,28},{16,0},{20,4},{24,8},{28,12},{1,17},{... | collective-permute-start | bytes 491528 | tf_op jit(solution)/shard_map/ppermute | solution.py:866
  65.2 9.1 %collective-permute-start.14 = (bf16[256,384]{1,0:T(8,128)(2,1)S(1)}, bf16[256,384]{1,0:T(8,128)(2,1)S(1)}, u32[]{:S(2)}, u32[]{:S(2)}) collective-permute-start(bf16[256,384]{1,0:T(8,128)(2,1)S(1)} %get-tuple-element.93), channel_id=1, source_target_pairs={{0,8},{4,12},{8,0},{12,4},{16,24},{20,28},{24,16},{28,20},{1,9},{5... | collective-permute-start | bytes 589832 | tf_op jit(solution)/shard_map/ppermute | solution.py:866
  67.8 9.0 %collective-permute-start.16 = (bf16[256,256]{1,0:T(8,128)(2,1)S(1)}, bf16[256,256]{1,0:T(8,128)(2,1)S(1)}, u32[]{:S(2)}, u32[]{:S(2)}) collective-permute-start(bf16[256,256]{1,0:T(8,128)(2,1)S(1)} %get-tuple-element.99), channel_id=1, source_target_pairs={{0,8},{4,12},{8,0},{12,4},{16,24},{20,28},{24,16},{28,20},{1,9},{5... | collective-permute-start | bytes 393224 | tf_op jit(solution)/shard_map/ppermute | solution.py:866
  74.4 7.5 %collective-permute-start.18 = (bf16[128,384]{1,0:T(8,128)(2,1)S(1)}, bf16[128,384]{1,0:T(8,128)(2,1)S(1)}, u32[]{:S(2)}, u32[]{:S(2)}) collective-permute-start(bf16[128,384]{1,0:T(8,128)(2,1)S(1)} %get-tuple-element.102), channel_id=1, source_target_pairs={{0,16},{4,20},{8,24},{12,28},{16,0},{20,4},{24,8},{28,12},{1,17},{... | collective-permute-start | bytes 294920 | tf_op jit(solution)/shard_map/ppermute | solution.py:866
  76.8 6.3 %collective-permute-start.17 = (bf16[128,256]{1,0:T(8,128)(2,1)S(1)}, bf16[128,256]{1,0:T(8,128)(2,1)S(1)}, u32[]{:S(2)}, u32[]{:S(2)}) collective-permute-start(bf16[128,256]{1,0:T(8,128)(2,1)S(1)} %get-tuple-element.101), channel_id=1, source_target_pairs={{0,16},{4,20},{8,24},{12,28},{16,0},{20,4},{24,8},{28,12},{1,17},{... | collective-permute-start | bytes 196616 | tf_op jit(solution)/shard_map/ppermute | solution.py:866
  77.6 7.1 %collective-permute-start.19 = (bf16[128,256]{1,0:T(8,128)(2,1)S(1)}, bf16[128,256]{1,0:T(8,128)(2,1)S(1)}, u32[]{:S(2)}, u32[]{:S(2)}) collective-permute-start(bf16[128,256]{1,0:T(8,128)(2,1)S(1)} %get-tuple-element.104), channel_id=1, source_target_pairs={{0,4},{4,8},{8,12},{12,16},{16,20},{20,24},{24,28},{28,0},{1,5},{5... | collective-permute-start | bytes 196616 | tf_op jit(solution)/shard_map/ppermute | solution.py:877
  79.6 2.5 %collective-permute-start.12 = (f32[8,1024]{1,0:T(8,128)S(1)}, f32[8,1024]{1,0:T(8,128)S(1)}, u32[]{:S(2)}, u32[]{:S(2)}) collective-permute-start(f32[8,1024]{1,0:T(8,128)S(1)} %reduce_sum.9.means_ref), channel_id=1, source_target_pairs={{0,1},{1,0},{2,3},{3,2},{4,5},{5,4},{6,7},{7,6},{8,9},{9,8},{10,11... | collective-permute-start | bytes 98312 | tf_op jit(solution)/shard_map/ppermute | solution.py:869
  79.7 8.0 %collective-permute-start.20 = (bf16[128,256]{1,0:T(8,128)(2,1)S(1)}, bf16[128,256]{1,0:T(8,128)(2,1)S(1)}, u32[]{:S(2)}, u32[]{:S(2)}) collective-permute-start(bf16[128,256]{1,0:T(8,128)(2,1)S(1)} %get-tuple-element.105), channel_id=1, source_target_pairs={{0,8},{4,12},{8,16},{12,20},{16,24},{20,28},{24,0},{28,4},{1,9},{5... | collective-permute-start | bytes 196616 | tf_op jit(solution)/shard_map/ppermute | solution.py:877
  81.8 5.9 %collective-permute-start.21 = (bf16[128,256]{1,0:T(8,128)(2,1)S(1)}, bf16[128,256]{1,0:T(8,128)(2,1)S(1)}, u32[]{:S(2)}, u32[]{:S(2)}) collective-permute-start(bf16[128,256]{1,0:T(8,128)(2,1)S(1)} %get-tuple-element.106), channel_id=1, source_target_pairs={{0,1},{1,0},{2,3},{3,2},{4,5},{5,4},{6,7},{7,6},{8,9},{9,8},{10,11... | collective-permute-start | bytes 196616 | tf_op jit(solution)/shard_map/ppermute | solution.py:869
  82.1 9.1 %collective-permute-start.22 = (bf16[128,256]{1,0:T(8,128)(2,1)S(1)}, bf16[128,256]{1,0:T(8,128)(2,1)S(1)}, u32[]{:S(2)}, u32[]{:S(2)}) collective-permute-start(bf16[128,256]{1,0:T(8,128)(2,1)S(1)} %get-tuple-element.107), channel_id=1, source_target_pairs={{0,12},{4,16},{8,20},{12,24},{16,28},{20,0},{24,4},{28,8},{1,13},{... | collective-permute-start | bytes 196616 | tf_op jit(solution)/shard_map/ppermute | solution.py:877
  83.1 8.1 %collective-permute-start.24 = (bf16[128,256]{1,0:T(8,128)(2,1)S(1)}, bf16[128,256]{1,0:T(8,128)(2,1)S(1)}, u32[]{:S(2)}, u32[]{:S(2)}) collective-permute-start(bf16[128,256]{1,0:T(8,128)(2,1)S(1)} %get-tuple-element.109), channel_id=1, source_target_pairs={{0,1},{1,0},{2,3},{3,2},{4,5},{5,4},{6,7},{7,6},{8,9},{9,8},{10,11... | collective-permute-start | bytes 196616 | tf_op jit(solution)/shard_map/ppermute | solution.py:869
  84.6 6.6 %collective-permute-start.23 = (bf16[128,128]{1,0:T(8,128)(2,1)S(1)}, bf16[128,128]{1,0:T(8,128)(2,1)S(1)}, u32[]{:S(2)}, u32[]{:S(2)}) collective-permute-start(bf16[128,128]{1,0:T(8,128)(2,1)S(1)} %get-tuple-element.108), channel_id=1, source_target_pairs={{0,16},{4,20},{8,24},{12,28},{16,0},{20,4},{24,8},{28,12},{1,17},{... | collective-permute-start | bytes 98312 | tf_op jit(solution)/shard_map/ppermute | solution.py:877
